TPU v7x, 256 devices: a whole 4x4x8 slice. The times are simulated.
256 devices in a mesh: cam: 8 (over x, y_hi), brick: 32 (over z, y_lo, core).
Axes of the slice: x: 4, y: 4 (y_hi: 2, y_lo: 2; y = y_hi * 2 + y_lo), z: 8, core: 2. Of those that a mesh axis runs over, the one named last changes fastest.
Arguments:
- raw_frames: bfloat16 [512, 256, 2048], P(('cam', 'brick')), may hold values from 2.4 to 12
- frame_order: int32 [256, 2], P(('cam', 'brick')), may hold values from 0 to 1, each once within a row
- dark_frame: bfloat16 [256, 2048], replicated, may hold values from 0 to 0.5
- flat_gain: bfloat16 [256, 2048], replicated, may hold values from 0.75 to 1.25
- stripe_band: float32 [9, 2048], replicated, may hold values from -0.015 to 0.015
- shear_offset: int32 [512], P('cam'), may hold values from 0 to 511
- shear_fraction: float32 [512], P('cam'), may hold values from 0 to 1
- band_index: int32 [512], replicated, may hold values from 0 to 7
- psf_bank: float32 [8, 13], replicated, may hold values from 0.2 to 1
- lateral_psf: float32 [9], replicated, may hold values from 0.2 to 1
Outputs:
- restored: bfloat16 [512, 256, 2048], P('cam', 'brick')
Inputs may be any that keep to these rules, and one draw needn't show every extreme that they name: Each row of frame_order names every number of 0 to 1 once.
All inputs are finite; a program needn't handle non-finite values.
Results may differ from a plain program's by a relative error of at most 0.005.
Values may be sent and summed in bfloat16 or wider, within the bound.
No kernel may reach another device: no remote copies, remote signals or barrier semaphores. Data moves between devices by JAX's collectives and lax.ppermute only.
A program may use at most 128 MiB of HBM per device.

v0:
```python
import functools

import jax
import jax.numpy as jnp
from jax import lax
from jax.experimental import pallas as pl
from jax.experimental.pallas import tpu as pltpu
from jax.sharding import PartitionSpec as P

SHEAR = 512
ITERS = 2
BACKGROUND = 1.0

LANES = 128
TILE = 256
BLOCK_ROWS = 64
MARGIN = SHEAR + LANES
R = 4
VMEM = 50 * 1024 * 1024


def frame_kernel(
    order_ref, offset_ref, fraction_ref,
    raw_prev, raw_main, raw_next,
    dark_prev, dark_main, dark_next,
    gain_prev, gain_main, gain_next,
    band_ref, out0_ref, out1_ref, scratch,
):
    step = pl.program_id(0)
    steps = pl.num_programs(0)
    columns = raw_main.shape[-1]
    tiles = columns // LANES
    rows = BLOCK_ROWS + 16
    brick = lax.axis_index("brick")
    f32 = jnp.float32

    @pl.when(step == 0)
    def _():
        scratch[:, :, :MARGIN] = jnp.zeros((2, BLOCK_ROWS, MARGIN), f32)

    has_prev = (step > 0).astype(f32)
    has_next = (step < steps - 1).astype(f32)

    for place in range(2):
        frame = jnp.where(order_ref[0, 0] == place, 0, 1)

        def destripe(tile, _):
            cols = pl.ds(pl.multiple_of(tile * LANES, LANES), LANES)

            def flat(raw, dark, gain):
                return (raw[frame, :, cols].astype(f32) - dark[:, cols].astype(f32)) * gain[
                    :, cols
                ].astype(f32)

            above = flat(raw_prev, dark_prev, gain_prev)[8:16] * has_prev
            below = flat(raw_next, dark_next, gain_next)[0:8] * has_next
            here = flat(raw_main, dark_main, gain_main)
            f = jnp.concatenate([above, here, below], axis=0)
            after = pltpu.roll(f, rows - 1, 0)
            before = pltpu.roll(f, 1, 0)
            band = band_ref[:, cols]

            def three(k):
                return band[k : k + 1] * before + band[k + 1 : k + 2] * f + band[k + 2 : k + 3] * after

            out = (
                f
                + three(3)
                + pltpu.roll(three(6), rows - 3, 0)
                + pltpu.roll(three(0), 3, 0)
            )
            scratch[place, :, pl.ds(pl.multiple_of(MARGIN + tile * LANES, LANES), LANES)] = out[
                8 : 8 + BLOCK_ROWS
            ]
            return 0

        lax.fori_loop(0, tiles, destripe, 0)

    lane = lax.broadcasted_iota(jnp.int32, (BLOCK_ROWS, LANES), 1)
    bricks = BLOCK_ROWS // 8
    upper = lax.broadcasted_iota(jnp.int32, (bricks, 8, LANES), 1) < 4
    amounts = [offset_ref[brick * 2 + place] for place in range(2)]
    weights = [fraction_ref[brick * 2 + place] for place in range(2)]

    def turned(place, tile):
        whole = amounts[place] // LANES
        part = amounts[place] % LANES
        start = MARGIN + (tile - whole) * LANES
        x = scratch[place, :, pl.ds(pl.multiple_of(start, LANES), LANES)]
        return pltpu.roll(x, part, 1), pltpu.roll(x, (part + 1) % LANES, 1)

    def deskew(tile, carry):
        values = []
        following = []
        for place in range(2):
            part = amounts[place] % LANES
            now = turned(place, tile)
            last = carry[place]
            near = jnp.where(lane < part, last[0], now[0])
            far = jnp.where(lane < part + 1, last[1], now[1])
            mixed = (1.0 - weights[place]) * near + weights[place] * far
            values.append(mixed.reshape(bricks, 8, LANES))
            following.append(now)
        cols = pl.ds(pl.multiple_of(tile * LANES, LANES), LANES)
        out0 = jnp.where(upper, values[0], pltpu.roll(values[1], 4, 1))
        out1 = jnp.where(upper, pltpu.roll(values[0], 4, 1), values[1])
        out0_ref[:, :, cols] = out0.astype(jnp.bfloat16)
        out1_ref[:, :, cols] = out1.astype(jnp.bfloat16)
        return tuple(following)

    lax.fori_loop(0, tiles, deskew, tuple(turned(place, -1) for place in range(2)))


def frame_side(raw, order, dark, gain, band, offset, fraction):
    _, frame_rows, columns = raw.shape
    steps = frame_rows // BLOCK_ROWS
    bricks = frame_rows // 8
    per = BLOCK_ROWS // 16
    last = frame_rows // 16 - 1
    smem = pl.BlockSpec(memory_space=pltpu.SMEM)

    def three(lead):
        zeros = (0,) * len(lead)
        return [
            pl.BlockSpec(lead + (16, columns), lambda i: zeros + (jnp.maximum(per * i - 1, 0), 0)),
            pl.BlockSpec(lead + (BLOCK_ROWS, columns), lambda i: zeros + (i, 0)),
            pl.BlockSpec(lead + (16, columns), lambda i: zeros + (jnp.minimum(per * i + per, last), 0)),
        ]

    piece = jax.ShapeDtypeStruct((bricks, 8, columns), jnp.bfloat16)
    piece_spec = pl.BlockSpec((BLOCK_ROWS // 8, 8, columns), lambda i: (i, 0, 0))
    return pl.pallas_call(
        frame_kernel,
        grid=(steps,),
        in_specs=[smem, smem, smem]
        + three((2,)) + three(()) + three(())
        + [pl.BlockSpec(band.shape, lambda i: (0, 0))],
        out_specs=[piece_spec, piece_spec],
        out_shape=[piece, piece],
        scratch_shapes=[pltpu.VMEM((2, BLOCK_ROWS, MARGIN + columns), jnp.float32)],
        compiler_params=pltpu.CompilerParams(vmem_limit_bytes=VMEM),
        cost_estimate=pl.CostEstimate(flops=30_000_000, bytes_accessed=6_500_000, transcendentals=0),
        name="frame_side",
    )(order, offset, fraction, raw, raw, raw, dark, dark, dark, gain, gain, gain, band)


def bands_kernel(taps, lat_taps, psf_ref, lateral_ref, index_ref, g_ref, gt_ref, tl_ref, tm_ref):
    size = g_ref.shape[0]
    f32 = jnp.float32
    index = index_ref[...]
    raw = []
    for tap in range(taps):
        value = jnp.zeros(index.shape, f32)
        for kernel in range(psf_ref.shape[0]):
            value = jnp.where(index == kernel, psf_ref[kernel, tap], value)
        raw.append(value)
    total = functools.reduce(lambda a, b: a + b, raw)
    total = jnp.where(total > 0.0, total, 1.0)
    row = lax.broadcasted_iota(jnp.int32, (size, size), 0)
    col = lax.broadcasted_iota(jnp.int32, (size, size), 1)
    gap = row - col
    adjoint = jnp.zeros((size, size), f32)
    for tap in range(taps):
        adjoint = jnp.where(gap == R * (tap - taps // 2), raw[tap] / total, adjoint)
    gt_ref[...] = adjoint.astype(jnp.bfloat16)
    g_ref[...] = adjoint.T.astype(jnp.bfloat16)

    lateral_total = lateral_ref[0]
    for tap in range(1, lat_taps):
        lateral_total = lateral_total + lateral_ref[tap]
    k = lax.broadcasted_iota(jnp.int32, tl_ref.shape, 0)
    j = lax.broadcasted_iota(jnp.int32, tl_ref.shape, 1)
    place = k - LANES - j + lat_taps // 2
    forward = jnp.zeros(tl_ref.shape, f32)
    backward = jnp.zeros(tl_ref.shape, f32)
    for tap in range(lat_taps):
        forward = jnp.where(place == tap, lateral_ref[tap], forward)
        backward = jnp.where(place == lat_taps - 1 - tap, lateral_ref[tap], backward)
    scale = jnp.full((1, TILE), lateral_total, f32)
    tl_ref[...] = (forward / scale).astype(jnp.bfloat16)
    tm_ref[...] = (backward / scale).astype(jnp.bfloat16)


def bands(psf_bank, lateral_psf, band_index, planes, halo):
    spread = jnp.pad(band_index, (halo, halo), constant_values=-1)
    first = lax.axis_index("cam") * planes
    mine = lax.dynamic_slice_in_dim(spread, first, planes + 2 * halo, 0)
    size = (planes + 2 * halo) * R
    index = jnp.broadcast_to(mine[:, None], (planes + 2 * halo, R)).reshape(1, size)
    smem = pl.BlockSpec(memory_space=pltpu.SMEM)
    vmem = pl.BlockSpec(memory_space=pltpu.VMEM)
    square = jax.ShapeDtypeStruct((size, size), jnp.bfloat16)
    strip = jax.ShapeDtypeStruct((TILE + 2 * LANES, TILE), jnp.bfloat16)
    return pl.pallas_call(
        functools.partial(bands_kernel, psf_bank.shape[1], lateral_psf.shape[0]),
        in_specs=[smem, smem, vmem],
        out_specs=[vmem] * 4,
        out_shape=[square, square, strip, strip],
        compiler_params=pltpu.CompilerParams(vmem_limit_bytes=VMEM),
        cost_estimate=pl.CostEstimate(flops=10_000_000, bytes_accessed=2_000_000, transcendentals=0),
        name="bands",
    )(psf_bank, lateral_psf, index)


def restore_kernel(half, merge, *refs):
    low, centre, high, g, gt, tl, tm = refs[:7]
    earlier = refs[7] if merge else None
    out, mf, ef, mb, qb, pad = refs[7 + merge :]
    f32 = jnp.float32
    bf16 = jnp.bfloat16
    size, columns = mf.shape
    tiles = columns // TILE
    edge = low.shape[0] * low.shape[1]

    pad[:, :LANES] = jnp.zeros((size, LANES), bf16)
    pad[:, LANES + columns :] = jnp.zeros((size, LANES), bf16)

    def at(tile, shift=0, width=TILE):
        return pl.ds(pl.multiple_of(tile * TILE + shift, LANES), width)

    def every(body):
        lax.fori_loop(0, tiles, lambda tile, _: body(tile), None)

    def load(tile):
        cols = at(tile)
        parts = [
            ref[:, :, cols].astype(f32).reshape(-1, TILE) for ref in (low, centre, high)
        ]
        whole = jnp.concatenate(parts, axis=0)
        mf[:, cols] = whole
        mb[:, cols] = whole.astype(bf16)
        qb[:, cols] = jnp.zeros((size, TILE), bf16)

    every(load)

    def span(reach):
        lo = reach * half * R // 16 * 16
        return slice(lo, size - lo)

    for sweep in range(ITERS):
        rows = span(2 * sweep + 1)
        inner = span(2 * sweep + 2)
        final = sweep == ITERS - 1

        def axial(tile):
            r = jnp.dot(g[rows, :], mb[:, at(tile)], preferred_element_type=f32)
            pad[rows, at(tile, LANES)] = r.astype(bf16)

        def ratio(tile):
            cols = at(tile)
            b = jnp.dot(pad[rows, at(tile, 0, TILE + 2 * LANES)], tl[...], preferred_element_type=f32)
            qb[rows, cols] = (mf[rows, cols] / (b + BACKGROUND)).astype(bf16)

        def axial_back(tile):
            r = jnp.dot(gt[inner, :], qb[:, at(tile)], preferred_element_type=f32)
            pad[inner, at(tile, LANES)] = r.astype(bf16)

        def update(tile):
            cols = at(tile)
            d = jnp.dot(pad[inner, at(tile, 0, TILE + 2 * LANES)], tm[...], preferred_element_type=f32)
            source = mf if sweep == 0 else ef
            e = source[inner, cols] * d
            if not final:
                ef[inner, cols] = e
                mb[inner, cols] = e.astype(bf16)
            elif not merge:
                out[:, cols] = e.astype(bf16)
            else:
                v1 = e.reshape(-1, 8, TILE)
                v0 = earlier[:, cols].astype(f32).reshape(-1, 8, TILE)
                upper = lax.broadcasted_iota(jnp.int32, v0.shape, 1) < 4
                even = jnp.where(upper, v0, pltpu.roll(v1, 4, 1))
                odd = jnp.where(upper, pltpu.roll(v0, 4, 1), v1)
                both = jnp.stack([even, odd], axis=1).reshape(-1, 8, TILE)
                out[:, :, cols] = both.astype(bf16)

        every(axial)
        every(ratio)
        every(axial_back)
        every(update)


def restore(low, centre, high, matrices, earlier, half):
    columns = centre.shape[-1]
    planes = centre.shape[0] * 2
    size = (low.shape[0] + centre.shape[0] + high.shape[0]) * centre.shape[1]
    merge = earlier is not None
    vmem = pl.BlockSpec(memory_space=pltpu.VMEM)
    shape = (planes, 8, columns) if merge else (planes * R, columns)
    operands = (low, centre, high, *matrices) + ((earlier,) if merge else ())
    return pl.pallas_call(
        functools.partial(restore_kernel, half, merge),
        in_specs=[vmem] * len(operands),
        out_specs=vmem,
        out_shape=jax.ShapeDtypeStruct(shape, jnp.bfloat16),
        scratch_shapes=[
            pltpu.VMEM((size, columns), jnp.float32),
            pltpu.VMEM((size, columns), jnp.float32),
            pltpu.VMEM((size, columns), jnp.bfloat16),
            pltpu.VMEM((size, columns), jnp.bfloat16),
            pltpu.VMEM((size, columns + 2 * LANES), jnp.bfloat16),
        ],
        compiler_params=pltpu.CompilerParams(vmem_limit_bytes=VMEM),
        cost_estimate=pl.CostEstimate(
            flops=7_000_000_000, bytes_accessed=8_000_000, transcendentals=0
        ),
        name="restore",
    )(*operands)


def local(
    raw_frames,
    frame_order,
    dark_frame,
    flat_gain,
    stripe_band,
    shear_offset,
    shear_fraction,
    band_index,
    psf_bank,
    lateral_psf,
):
    half = psf_bank.shape[1] // 2
    planes = shear_offset.shape[0]
    halo = 2 * ITERS * half
    pieces = frame_side(
        raw_frames, frame_order, dark_frame, flat_gain, stripe_band, shear_offset, shear_fraction
    )
    count = lax.axis_size("cam")
    forward = [(i, i + 1) for i in range(count - 1)]
    backward = [(i + 1, i) for i in range(count - 1)]
    matrices = bands(psf_bank, lateral_psf, band_index, planes, halo)
    depth = halo // 2
    result = None
    for piece in pieces:
        centre = lax.all_to_all(piece, "brick", split_axis=0, concat_axis=0, tiled=True)
        low = lax.ppermute(centre[-depth:], "cam", forward)
        high = lax.ppermute(centre[:depth], "cam", backward)
        result = restore(low, centre, high, matrices, result, half)
    return result


def solution(mesh):
    placed = (
        P(("cam", "brick"), None, None),
        P(("cam", "brick"), None),
        P(),
        P(),
        P(),
        P("cam"),
        P("cam"),
        P(),
        P(),
        P(),
    )
    return jax.shard_map(
        local, mesh=mesh, in_specs=placed, out_specs=P("cam", "brick", None), check_vma=False
    )
```

profile of v0, /device:TPU:125, one launch (start us, length us, event | category | flops | bytes accessed | tf_op | source)
XLA Modules:
  0.0 144.4 jit_solution(14688051173441225063)
XLA Ops:
  0.0 1.2 copy-done
  1.2 0.9 copy-done.1
  2.1 0.7 copy-done.2
  2.8 0.7 copy-done.3
  3.4 0.7 copy-done.4
  4.1 16.2 %frame_side.1 = (bf16[32,8,2048]{2,1,0:T(8,128)(2,1)S(1)}, bf16[32,8,2048]{2,1,0:T(8,128)(2,1)}) custom-call(s32[1,2]{1,0:T(1,128)S(1)} %copy-done.2, s32[64]{0:T(128)S(1)} %copy-done.3, f32[64]{0:T(128)S(1)} %copy-done.4, bf16[2,256,2048]{2,1,0:T(8,128)(2,1)} %raw_next.1, bf16[2,256,2048]{2,1,0:T(8,128)(2,1)} %raw_next.1, bf16[2,256,2048]{2,1,0:T(8,128)(2,1)} %raw_next.1, ...), custom_call_target="tpu_custom_call" | custom-call | flops 30000000 | bytes 6500000 | tf_op jit(solution)/shard_map/frame_side/pallas_call | solution.py:132
  20.3 0.0 copy-start.6
  20.4 34.5 %all_to_all.10.refs_1_ = bf16[32,8,2048]{2,1,0:T(8,128)(2,1)S(1)} all-to-all(bf16[32,8,2048]{2,1,0:T(8,128)(2,1)S(1)} %get-tuple-element.16), channel_id=1, replica_groups=mesh['cam'=8,'brick'=32] {'brick'}, dimensions={0} | all-to-all | bytes 2097152 | tf_op jit(solution)/shard_map/all_to_all | solution.py:336
  54.9 7.4 %all-to-all-start = ((bf16[32,8,2048]{2,1,0:T(8,128)(2,1)}), bf16[32,8,2048]{2,1,0:T(8,128)(2,1)S(1)}, u32[]{:S(2)}, u32[]{:S(2)}) async-start(bf16[32,8,2048]{2,1,0:T(8,128)(2,1)} %get-tuple-element.11), calls=%async_computation | async-start | bytes 2097152 | tf_op jit(solution)/shard_map/all_to_all | solution.py:336
  62.3 0.0 copy-done.9
  62.4 0.1 pad_dynamic-slice_fusion
  62.4 0.1 broadcast_in_dim.2
  62.5 0.1 reshape.4.index_ref
  62.6 0.0 copy-done.5
  62.6 0.0 copy-done.6
  62.7 1.5 %bands.1 = (bf16[448,448]{1,0:T(8,128)(2,1)S(1)}, bf16[448,448]{1,0:T(8,128)(2,1)S(1)}, bf16[512,256]{1,0:T(8,128)(2,1)S(1)}, bf16[512,256]{1,0:T(8,128)(2,1)S(1)}) custom-call(f32[8,13]{1,0:T(8,128)S(1)} %copy-done.5, f32[9]{0:T(128)S(1)} %copy-done.6, s32[1,448]{1,0:T(1,128)S(1)} %reshape.4.index_ref), custom_call_target="tpu_custom_call" | custom-call | flops 10000000 | bytes 2000000 | tf_op jit(solution)/shard_map/bands/pallas_call | solution.py:194
  64.2 1.0 fusion
  65.2 0.0 copy-done.8
  65.2 2.9 %collective-permute-start.3 = (bf16[12,8,2048]{2,1,0:T(8,128)(2,1)}, bf16[12,8,2048]{2,1,0:T(8,128)(2,1)S(1)}, u32[]{:S(2)}, u32[]{:S(2)}) collective-permute-start(bf16[12,8,2048]{2,1,0:T(8,128)(2,1)} %get-tuple-element.17), channel_id=1, source_target_pairs={{32,0},{64,32},{96,64},{128,96},{160,128},{192,160},{224,192},{33,... | collective-permute-start | bytes 1179656 | tf_op jit(solution)/shard_map/ppermute | solution.py:338
  68.1 4.8 %collective-permute-start.2 = (bf16[12,8,2048]{2,1,0:T(8,128)(2,1)}, bf16[12,8,2048]{2,1,0:T(8,128)(2,1)S(1)}, u32[]{:S(2)}, u32[]{:S(2)}) collective-permute-start(bf16[12,8,2048]{2,1,0:T(8,128)(2,1)} %get-tuple-element.18), channel_id=1, source_target_pairs={{0,32},{32,64},{64,96},{96,128},{128,160},{160,192},{192,224},{1,3... | collective-permute-start | bytes 1179656 | tf_op jit(solution)/shard_map/ppermute | solution.py:337
  72.9 15.4 %all-to-all-done.refs_1_ = bf16[32,8,2048]{2,1,0:T(8,128)(2,1)S(1)} async-done(((bf16[32,8,2048]{2,1,0:T(8,128)(2,1)}), bf16[32,8,2048]{2,1,0:T(8,128)(2,1)S(1)}, u32[]{:S(2)}, u32[]{:S(2)}) %all-to-all-start) | async-done | bytes 1048608 | tf_op jit(solution)/shard_map/all_to_all | solution.py:336
  88.3 0.1 fusion.1
  88.4 2.8 %collective-permute-start.1 = (bf16[12,8,2048]{2,1,0:T(8,128)(2,1)S(1)}, bf16[12,8,2048]{2,1,0:T(8,128)(2,1)S(1)}, u32[]{:S(2)}, u32[]{:S(2)}) collective-permute-start(bf16[12,8,2048]{2,1,0:T(8,128)(2,1)S(1)} %get-tuple-element.19), channel_id=1, source_target_pairs={{32,0},{64,32},{96,64},{128,96},{160,128},{192,160},{224,192},{33,... | collective-permute-start | bytes 1179656 | tf_op jit(solution)/shard_map/ppermute | solution.py:338
  91.2 4.8 %collective-permute-start = (bf16[12,8,2048]{2,1,0:T(8,128)(2,1)S(1)}, bf16[12,8,2048]{2,1,0:T(8,128)(2,1)S(1)}, u32[]{:S(2)}, u32[]{:S(2)}) collective-permute-start(bf16[12,8,2048]{2,1,0:T(8,128)(2,1)S(1)} %get-tuple-element.20), channel_id=1, source_target_pairs={{0,32},{32,64},{64,96},{96,128},{128,160},{160,192},{192,224},{1,3... | collective-permute-start | bytes 1179656 | tf_op jit(solution)/shard_map/ppermute | solution.py:337
  96.1 0.0 collective-permute-done.3.refs_2_
  96.1 8.6 %collective-permute-done.2.refs_0_ = bf16[12,8,2048]{2,1,0:T(8,128)(2,1)S(1)} collective-permute-done((bf16[12,8,2048]{2,1,0:T(8,128)(2,1)}, bf16[12,8,2048]{2,1,0:T(8,128)(2,1)S(1)}, u32[]{:S(2)}, u32[]{:S(2)}) %collective-permute-start.2) | collective-permute-done | bytes 393248 | tf_op jit(solution)/shard_map/ppermute | solution.py:337
  104.7 18.7 %restore.2.refs_7_ = bf16[256,2048]{1,0:T(8,128)(2,1)S(1)} custom-call(bf16[12,8,2048]{2,1,0:T(8,128)(2,1)S(1)} %collective-permute-done.2.refs_0_, bf16[32,8,2048]{2,1,0:T(8,128)(2,1)} %copy-done.8, bf16[12,8,2048]{2,1,0:T(8,128)(2,1)S(1)} %collective-permute-done.3.refs_2_, bf16[448,448]{1,0:T(8,128)(2,1)S(1)} %get-tuple-element.12.refs_3_, ...), custom_call_target="tpu_custom_call" | custom-call | flops 7000000000 | bytes 8000000 | tf_op jit(solution)/shard_map/restore/pallas_call | solution.py:291
  123.4 0.0 copy-start.7
  123.4 1.0 copy-done.7
  124.4 0.0 collective-permute-done.1.refs_2_
  124.4 0.0 collective-permute-done.refs_0_
  124.4 20.1 %restore.3 = bf16[64,8,2048]{2,1,0:T(8,128)(2,1)} custom-call(bf16[12,8,2048]{2,1,0:T(8,128)(2,1)S(1)} %collective-permute-done.refs_0_, bf16[32,8,2048]{2,1,0:T(8,128)(2,1)S(1)} %all-to-all-done.refs_1_, bf16[12,8,2048]{2,1,0:T(8,128)(2,1)S(1)} %collective-permute-done.1.refs_2_, bf16[448,448]{1,0:T(8,128)(2,1)S(1)} %get-tuple-element.12.refs_3_, ...), custom_call_target="tpu_custom_call" | custom-call | flops 7000000000 | bytes 8000000 | tf_op jit(solution)/shard_map/restore/pallas_call | solution.py:291
  (8 shorter events, 0.0 us)
Async XLA Ops:
  0.0 1.2 copy-start
  1.2 0.9 copy-start.1
  2.1 0.7 copy-start.2
  2.8 0.7 copy-start.3
  3.4 0.7 copy-start.4
  20.3 42.0 %copy-start.9 = (s32[512]{0:T(512)S(1)}, s32[512]{0:T(512)}, u32[]{:S(2)}) copy-start(s32[512]{0:T(512)} %param.17) | copy-start | bytes 6148
  20.3 42.3 %copy-start.5 = (f32[8,13]{1,0:T(8,128)S(1)}, f32[8,13]{1,0:T(8,128)}, u32[]{:S(2)}) copy-start(f32[8,13]{1,0:T(8,128)} %psf_ref.1) | copy-start | bytes 1252
  20.3 42.3 %copy-start.6 = (f32[9]{0:T(128)S(1)}, f32[9]{0:T(128)}, u32[]{:S(2)}) copy-start(f32[9]{0:T(128)} %lateral_ref.1) | copy-start | bytes 112
  54.9 10.3 %copy-start.8 = (bf16[32,8,2048]{2,1,0:T(8,128)(2,1)}, bf16[32,8,2048]{2,1,0:T(8,128)(2,1)S(1)}, u32[]{:S(2)}) copy-start(bf16[32,8,2048]{2,1,0:T(8,128)(2,1)S(1)} %all_to_all.10.refs_1_) | copy-start | bytes 3145732
  54.9 33.4 %all-to-all-start = ((bf16[32,8,2048]{2,1,0:T(8,128)(2,1)}), bf16[32,8,2048]{2,1,0:T(8,128)(2,1)S(1)}, u32[]{:S(2)}, u32[]{:S(2)}) async-start(bf16[32,8,2048]{2,1,0:T(8,128)(2,1)} %get-tuple-element.11), calls=%async_computation | async-start | bytes 2097152 | tf_op jit(solution)/shard_map/all_to_all | solution.py:336
  65.2 30.9 %collective-permute-start.3 = (bf16[12,8,2048]{2,1,0:T(8,128)(2,1)}, bf16[12,8,2048]{2,1,0:T(8,128)(2,1)S(1)}, u32[]{:S(2)}, u32[]{:S(2)}) collective-permute-start(bf16[12,8,2048]{2,1,0:T(8,128)(2,1)} %get-tuple-element.17), channel_id=1, source_target_pairs={{32,0},{64,32},{96,64},{128,96},{160,128},{192,160},{224,192},{33,... | collective-permute-start | bytes 1179656 | tf_op jit(solution)/shard_map/ppermute | solution.py:338
  68.1 36.7 %collective-permute-start.2 = (bf16[12,8,2048]{2,1,0:T(8,128)(2,1)}, bf16[12,8,2048]{2,1,0:T(8,128)(2,1)S(1)}, u32[]{:S(2)}, u32[]{:S(2)}) collective-permute-start(bf16[12,8,2048]{2,1,0:T(8,128)(2,1)} %get-tuple-element.18), channel_id=1, source_target_pairs={{0,32},{32,64},{64,96},{96,128},{128,160},{160,192},{192,224},{1,3... | collective-permute-start | bytes 1179656 | tf_op jit(solution)/shard_map/ppermute | solution.py:337
  88.4 36.0 %collective-permute-start.1 = (bf16[12,8,2048]{2,1,0:T(8,128)(2,1)S(1)}, bf16[12,8,2048]{2,1,0:T(8,128)(2,1)S(1)}, u32[]{:S(2)}, u32[]{:S(2)}) collective-permute-start(bf16[12,8,2048]{2,1,0:T(8,128)(2,1)S(1)} %get-tuple-element.19), channel_id=1, source_target_pairs={{32,0},{64,32},{96,64},{128,96},{160,128},{192,160},{224,192},{33,... | collective-permute-start | bytes 1179656 | tf_op jit(solution)/shard_map/ppermute | solution.py:338
  91.2 33.1 %collective-permute-start = (bf16[12,8,2048]{2,1,0:T(8,128)(2,1)S(1)}, bf16[12,8,2048]{2,1,0:T(8,128)(2,1)S(1)}, u32[]{:S(2)}, u32[]{:S(2)}) collective-permute-start(bf16[12,8,2048]{2,1,0:T(8,128)(2,1)S(1)} %get-tuple-element.20), channel_id=1, source_target_pairs={{0,32},{32,64},{64,96},{96,128},{128,160},{160,192},{192,224},{1,3... | collective-permute-start | bytes 1179656 | tf_op jit(solution)/shard_map/ppermute | solution.py:337
  123.4 1.0 copy-start.7
where the time goes:
time: 145 us; the launch traced here: 144 us
  Pallas kernels  56.5 us (39%)
  blocking collectives  34.5 us (24%)
  waiting for transfers between devices  24 us (17%)
  starting transfers between devices  22.8 us (16%)
  local copies, waits for them, and re-layouts  6.41 us (4%)
    pallas_call x2, Pallas kernels, restore(): pl.pallas_call(functools.partial(restore_kernel, half, merge), in_specs=[...  38.7 us
    all_to_all x1, blocking collectives, local(): lax.all_to_all(piece, 'brick', split_axis=0, concat_axis=0, tiled=True)  34.5 us
    pallas_call x1, Pallas kernels, frame_side(): pl.pallas_call(frame_kernel, grid=(steps,), in_specs=[smem, smem, smem] +...  16.2 us
    all_to_all x1, waiting for transfers between devices, local(): lax.all_to_all(piece, 'brick', split_axis=0, concat_axis=0, tiled=True)  15.4 us
    ppermute x2, starting transfers between devices, local(): low = lax.ppermute(centre[-depth:], 'cam', forward)  9.67 us
    ppermute x2, waiting for transfers between devices, local(): low = lax.ppermute(centre[-depth:], 'cam', forward)  8.63 us
    all_to_all x1, starting transfers between devices, local(): lax.all_to_all(piece, 'brick', split_axis=0, concat_axis=0, tiled=True)  7.44 us
    ppermute x2, starting transfers between devices, local(): high = lax.ppermute(centre[:depth], 'cam', backward)  5.69 us
  transfers between devices with their start and end apart: 5, of which 2 were waited for; matrix products, arithmetic and copies ran while one was open for 1% of the time, Pallas kernels for 14%

commit v1 on v0

v1 whole, which is shorter than its diff:
```python
import functools

import jax
import jax.numpy as jnp
from jax import lax
from jax.experimental import pallas as pl
from jax.experimental.pallas import tpu as pltpu
from jax.sharding import PartitionSpec as P

SHEAR = 512
ITERS = 2
BACKGROUND = 1.0

LANES = 128
TILE = 256
ROWS = 8
BLOCK_ROWS = 64
LEAD = SHEAR // LANES + 1
SPLIT = 1280
VMEM = 60 * 1024 * 1024
GROUP = 20
SPAN = 32


def frame_kernel(
    first, count,
    order_ref, offset_ref, fraction_ref,
    raw_prev, raw_main, raw_next,
    dark_prev, dark_main, dark_next,
    gain_prev, gain_main, gain_next,
    band_ref, out_ref, scratch,
):
    step = pl.program_id(0)
    steps = pl.num_programs(0)
    rows = BLOCK_ROWS + 16
    brick = lax.axis_index("brick")
    f32 = jnp.float32
    bf16 = jnp.bfloat16
    base = first - LEAD

    @pl.when(step == 0)
    def _():
        if base < 0:
            scratch[:, :, : -base * LANES] = jnp.zeros((2, BLOCK_ROWS, -base * LANES), f32)

    has_prev = (step > 0).astype(f32)
    has_next = (step < steps - 1).astype(f32)
    frames = [jnp.where(order_ref[0, 0] == place, 0, 1) for place in range(2)]

    for tile in range(max(base, 0), first + count):
        cols = pl.ds(tile * LANES, LANES)
        band = band_ref[:, cols]
        levels = []
        for part, keep in ((0, slice(8, 16)), (1, slice(None)), (2, slice(0, 8))):
            dark = (dark_prev, dark_main, dark_next)[part][:, cols].astype(f32)[keep]
            gain = (gain_prev, gain_main, gain_next)[part][:, cols].astype(f32)[keep]
            if part != 1:
                gain = gain * (has_prev, None, has_next)[part]
            levels.append((dark, gain, keep))
        for place in range(2):
            f = jnp.concatenate(
                [
                    (raw[frames[place], :, cols].astype(f32)[keep] - dark) * gain
                    for raw, (dark, gain, keep) in zip((raw_prev, raw_main, raw_next), levels)
                ],
                axis=0,
            )
            after = pltpu.roll(f, rows - 1, 0)
            before = pltpu.roll(f, 1, 0)

            def three(k):
                return band[k : k + 1] * before + band[k + 1 : k + 2] * f + band[k + 2 : k + 3] * after

            out = (
                f
                + three(3)
                + pltpu.roll(three(6), rows - 3, 0)
                + pltpu.roll(three(0), 3, 0)
            )[8 : 8 + BLOCK_ROWS]
            scratch[place, :, pl.ds((tile - base) * LANES, LANES)] = out.astype(bf16).astype(f32)

    lane = lax.broadcasted_iota(jnp.int32, (BLOCK_ROWS, LANES), 1)
    bricks = BLOCK_ROWS // ROWS
    for place in range(2):
        amount = offset_ref[brick * 2 + place]
        weight = fraction_ref[brick * 2 + place]
        whole = amount // LANES
        part = amount % LANES
        near_mask = lane < part
        far_mask = lane < part + 1

        def turned(tile):
            start = (tile - base - whole) * LANES
            x = scratch[place, :, pl.ds(pl.multiple_of(start, LANES), LANES)]
            return (1.0 - weight) * pltpu.roll(x, part, 1), weight * pltpu.roll(x, (part + 1) % LANES, 1)

        last = turned(first - 1)
        for tile in range(first, first + count):
            now = turned(tile)
            mixed = jnp.where(near_mask, last[0], now[0]) + jnp.where(far_mask, last[1], now[1])
            last = now
            out_ref[:, place * ROWS : (place + 1) * ROWS, pl.ds((tile - first) * LANES, LANES)] = (
                mixed.reshape(bricks, ROWS, LANES).astype(bf16)
            )


def frame_side(raw, order, dark, gain, band, offset, fraction, lo, hi):
    _, frame_rows, columns = raw.shape
    steps = frame_rows // BLOCK_ROWS
    bricks = frame_rows // ROWS
    per = BLOCK_ROWS // 16
    last = frame_rows // 16 - 1
    smem = pl.BlockSpec(memory_space=pltpu.SMEM)
    first, count = lo // LANES, (hi - lo) // LANES

    def three(lead):
        zeros = (0,) * len(lead)
        return [
            pl.BlockSpec(lead + (16, columns), lambda i: zeros + (jnp.maximum(per * i - 1, 0), 0)),
            pl.BlockSpec(lead + (BLOCK_ROWS, columns), lambda i: zeros + (i, 0)),
            pl.BlockSpec(lead + (16, columns), lambda i: zeros + (jnp.minimum(per * i + per, last), 0)),
        ]

    return pl.pallas_call(
        functools.partial(frame_kernel, first, count),
        grid=(steps,),
        in_specs=[smem, smem, smem]
        + three((2,)) + three(()) + three(())
        + [pl.BlockSpec(band.shape, lambda i: (0, 0))],
        out_specs=pl.BlockSpec((BLOCK_ROWS // ROWS, 2 * ROWS, hi - lo), lambda i: (i, 0, 0)),
        out_shape=jax.ShapeDtypeStruct((bricks, 2 * ROWS, hi - lo), jnp.bfloat16),
        scratch_shapes=[pltpu.VMEM((2, BLOCK_ROWS, (LEAD + count) * LANES), jnp.float32)],
        compiler_params=pltpu.CompilerParams(vmem_limit_bytes=VMEM),
        cost_estimate=pl.CostEstimate(
            flops=8_000_000_000, bytes_accessed=6_500_000, transcendentals=0
        ),
        name="frame_side",
    )(order, offset, fraction, raw, raw, raw, dark, dark, dark, gain, gain, gain, band)


def stages(planes, half):
    total = planes + 4 * ITERS * half
    plan = []
    for reach in range(1, 2 * ITERS + 1):
        lo, hi = reach * half, total - reach * half
        plan.append([(at, min(GROUP, hi - at)) for at in range(lo, hi, GROUP)])
    return plan


def bands_kernel(taps, lat_taps, plan, psf_ref, lateral_ref, index_ref, g_ref, gt_ref, tl_ref, tm_ref):
    f32 = jnp.float32
    bf16 = jnp.bfloat16
    half = taps // 2
    width = SPAN * ROWS
    index = index_ref[...]
    raw = []
    for tap in range(taps):
        value = jnp.zeros(index.shape, f32)
        for kernel in range(psf_ref.shape[0]):
            value = jnp.where(index == kernel, psf_ref[kernel, tap], value)
        raw.append(value)
    total = functools.reduce(lambda a, b: a + b, raw)
    total = jnp.where(total > 0.0, total, 1.0)
    unit = [value / total for value in raw]
    row = lax.broadcasted_iota(jnp.int32, (width, width), 0)
    col = lax.broadcasted_iota(jnp.int32, (width, width), 1)

    def banded(start, gap, order):
        m = jnp.zeros((width, width), f32)
        for tap in range(taps):
            values = unit[tap][:, start * ROWS : start * ROWS + width]
            m = jnp.where(gap == ROWS * order(tap), values, m)
        return m

    slot = [0, 0]
    for number, groups in enumerate(plan):
        for at, _ in groups:
            if number % 2 == 0:
                m = banded(at, row - col, lambda tap: tap).T
                g_ref[slot[0]] = m[: GROUP * ROWS].astype(bf16)
            else:
                m = banded(at - half, col - row, lambda tap: 2 * half - tap)
                gt_ref[slot[1]] = m[: GROUP * ROWS].astype(bf16)
            slot[number % 2] += 1

    lateral_total = lateral_ref[0]
    for tap in range(1, lat_taps):
        lateral_total = lateral_total + lateral_ref[tap]
    k = lax.broadcasted_iota(jnp.int32, tl_ref.shape, 0)
    j = lax.broadcasted_iota(jnp.int32, tl_ref.shape, 1)
    place = k - LANES - j + lat_taps // 2
    forward = jnp.zeros(tl_ref.shape, f32)
    backward = jnp.zeros(tl_ref.shape, f32)
    for tap in range(lat_taps):
        forward = jnp.where(place == tap, lateral_ref[tap], forward)
        backward = jnp.where(place == lat_taps - 1 - tap, lateral_ref[tap], backward)
    scale = jnp.full((1, TILE), lateral_total, f32)
    tl_ref[...] = (forward / scale).astype(bf16)
    tm_ref[...] = (backward / scale).astype(bf16)


def bands(psf_bank, lateral_psf, band_index, planes, halo):
    half = psf_bank.shape[1] // 2
    plan = stages(planes, half)
    spread = jnp.pad(band_index, (halo, halo + SPAN), constant_values=-1)
    first = lax.axis_index("cam") * planes
    length = planes + 2 * halo + SPAN
    mine = lax.dynamic_slice_in_dim(spread, first, length, 0)
    index = jnp.broadcast_to(mine[:, None], (length, ROWS)).reshape(1, length * ROWS)
    smem = pl.BlockSpec(memory_space=pltpu.SMEM)
    vmem = pl.BlockSpec(memory_space=pltpu.VMEM)
    counts = [sum(len(groups) for groups in plan[kind::2]) for kind in range(2)]
    strip = jax.ShapeDtypeStruct((TILE + 2 * LANES, TILE), jnp.bfloat16)
    return pl.pallas_call(
        functools.partial(bands_kernel, psf_bank.shape[1], lateral_psf.shape[0], plan),
        in_specs=[smem, smem, vmem],
        out_specs=[vmem] * 4,
        out_shape=[
            jax.ShapeDtypeStruct((n, GROUP * ROWS, SPAN * ROWS), jnp.bfloat16) for n in counts
        ]
        + [strip, strip],
        compiler_params=pltpu.CompilerParams(vmem_limit_bytes=VMEM),
        cost_estimate=pl.CostEstimate(
            flops=2_000_000_000, bytes_accessed=2_000_000, transcendentals=0
        ),
        name="bands",
    )(psf_bank, lateral_psf, index)


def restore_kernel(plan, kept, *refs):
    later = kept is not None
    sources = [refs[3 * i : 3 * i + 3] for i in range(2 if later else 1)]
    refs = refs[3 * len(sources) :]
    g, gt, tl, tm = refs[:4]
    earlier = refs[4] if later else None
    out, mf, ef, mb, qb, pad, pad_back = refs[4 + later :]
    f32 = jnp.float32
    bf16 = jnp.bfloat16
    size, columns = mf.shape
    tiles = columns // TILE

    for buffer in (pad, pad_back):
        buffer[:, :LANES] = jnp.zeros((size, LANES), bf16)
        buffer[:, LANES + columns :] = jnp.zeros((size, LANES), bf16)

    at_column = 0
    for source in sources:
        width = source[1].shape[-1]
        at_row = 0
        for ref in source:
            height = ref.shape[0] * ref.shape[1]
            for col in range(0, width, TILE):
                whole = ref[:, :, col : col + TILE].reshape(height, TILE)
                there = slice(at_column + col, at_column + col + TILE)
                mb[at_row : at_row + height, there] = whole
                mf[at_row : at_row + height, there] = whole.astype(f32)
            at_row += height
        at_column += width

    def columns_of(tile):
        return slice(tile * TILE, (tile + 1) * TILE)

    def within(tile):
        return slice(LANES + tile * TILE, LANES + (tile + 1) * TILE)

    def around(tile):
        return slice(tile * TILE, (tile + 1) * TILE + 2 * LANES)

    half = plan[0][0][0]

    def rows_of(groups):
        return slice(groups[0][0] * ROWS, (groups[-1][0] + groups[-1][1]) * ROWS)

    def axial(matrices, skip, groups, source, target, tile):
        for number, (first, count) in enumerate(groups):
            low = (first - half) * ROWS
            high = (first + count + half) * ROWS
            r = jnp.dot(
                matrices[skip + number, : count * ROWS, : high - low],
                source[low:high, columns_of(tile)],
                preferred_element_type=f32,
            )
            target[first * ROWS : (first + count) * ROWS, within(tile)] = r.astype(bf16)

    for sweep in range(ITERS):
        ahead, back = plan[2 * sweep], plan[2 * sweep + 1]
        outer, inner = rows_of(ahead), rows_of(back)
        skip_ahead = sum(len(groups) for groups in plan[0 : 2 * sweep : 2])
        skip_back = sum(len(groups) for groups in plan[1 : 2 * sweep : 2])
        final = sweep == ITERS - 1

        def ratio(tile):
            cols = columns_of(tile)
            b = jnp.dot(pad[outer, around(tile)], tl[...], preferred_element_type=f32) + BACKGROUND
            guess = pl.reciprocal(b, approx=True)
            guess = guess * (2.0 - b * guess)
            qb[outer, cols] = (mf[outer, cols] * guess).astype(bf16)

        def update(tile):
            cols = columns_of(tile)
            d = jnp.dot(pad_back[inner, around(tile)], tm[...], preferred_element_type=f32)
            e = (mf if sweep == 0 else ef)[inner, cols] * d
            if not final:
                ef[inner, cols] = e
                mb[inner, cols] = e.astype(bf16)
                return
            e = e.reshape(-1, ROWS, TILE).astype(bf16)
            if not later:
                lo, hi = tile * TILE, min((tile + 1) * TILE, out.shape[-1])
                if hi > lo:
                    out[:, :, lo:hi] = e[:, :, : hi - lo]
            else:
                cut = kept if tile == 0 else 0
                start = out.shape[-1] - columns + tile * TILE
                out[:, :, start + cut : start + TILE] = e[:, :, cut:]

        for step in range(tiles + 5):
            if step < tiles:
                axial(g, skip_ahead, ahead, mb, pad, step)
            if 0 <= step - 2 < tiles:
                ratio(step - 2)
            if 0 <= step - 3 < tiles:
                axial(gt, skip_back, back, qb, pad_back, step - 3)
            if 0 <= step - 5 < tiles:
                update(step - 5)

    if later:
        out[:, :, : earlier.shape[-1]] = earlier[...]


def restore(parts, matrices, earlier, plan, columns):
    later = earlier is not None
    planes = plan[-1][-1][0] + plan[-1][-1][1] - plan[-1][0][0]
    height = sum(part.shape[0] * part.shape[1] for part in parts[0])
    operands, specs, width = [], [], 0
    for number, part in enumerate(parts):
        kept = 2 * LANES if number < len(parts) - 1 else part[0].shape[-1]
        for array in part:
            block = array.shape[:2] + (kept,)
            index = (0, 0, array.shape[-1] // kept - 1)
            operands.append(array)
            specs.append(pl.BlockSpec(block, lambda i, index=index: index))
        width += kept

    def whole(array):
        return pl.BlockSpec(array.shape, lambda i: (0,) * len(array.shape))

    for array in (*matrices, *([earlier] if later else [])):
        operands.append(array)
        specs.append(whole(array))
    result = jax.ShapeDtypeStruct((planes, ROWS, columns if later else width - LANES), jnp.bfloat16)
    return pl.pallas_call(
        functools.partial(restore_kernel, plan, LANES if later else None),
        grid=(1,),
        in_specs=specs,
        out_specs=whole(result),
        out_shape=result,
        scratch_shapes=[
            pltpu.VMEM((height, width), jnp.float32),
            pltpu.VMEM((height, width), jnp.float32),
            pltpu.VMEM((height, width), jnp.bfloat16),
            pltpu.VMEM((height, width), jnp.bfloat16),
            pltpu.VMEM((height, width + 2 * LANES), jnp.bfloat16),
            pltpu.VMEM((height, width + 2 * LANES), jnp.bfloat16),
        ],
        compiler_params=pltpu.CompilerParams(vmem_limit_bytes=VMEM),
        cost_estimate=pl.CostEstimate(
            flops=7_000_000_000, bytes_accessed=8_000_000, transcendentals=0
        ),
        name="restore",
    )(*operands)


def local(
    raw_frames,
    frame_order,
    dark_frame,
    flat_gain,
    stripe_band,
    shear_offset,
    shear_fraction,
    band_index,
    psf_bank,
    lateral_psf,
):
    half = psf_bank.shape[1] // 2
    planes = shear_offset.shape[0]
    columns = raw_frames.shape[-1]
    halo = 2 * ITERS * half
    plan = stages(planes, half)
    count = lax.axis_size("cam")
    forward = [(i, i + 1) for i in range(count - 1)]
    backward = [(i + 1, i) for i in range(count - 1)]
    matrices = bands(psf_bank, lateral_psf, band_index, planes, halo)
    depth = halo // 2
    result = None
    parts = []
    for lo, hi in ((0, SPLIT), (SPLIT, columns)):
        piece = frame_side(
            raw_frames, frame_order, dark_frame, flat_gain, stripe_band, shear_offset,
            shear_fraction, lo, hi,
        )
        centre = lax.all_to_all(piece, "brick", split_axis=0, concat_axis=0, tiled=True)
        if result is not None:
            centre, result = lax.optimization_barrier((centre, result))
        low = lax.ppermute(centre[-depth:], "cam", forward)
        high = lax.ppermute(centre[:depth], "cam", backward)
        parts.append((low, centre, high))
        result = restore(parts, matrices, result, plan, columns)
    return result


def solution(mesh):
    placed = (
        P(("cam", "brick"), None, None),
        P(("cam", "brick"), None),
        P(),
        P(),
        P(),
        P("cam"),
        P("cam"),
        P(),
        P(),
        P(),
    )
    return jax.shard_map(
        local, mesh=mesh, in_specs=placed, out_specs=P("cam", "brick", None), check_vma=False
    )
```

time: 145 us -> 131 us (0.903)
  the two profiles are of different devices: /device:TPU:125 before, /device:TPU:14 now
where the time goes in v1:
time: 131 us; the launch traced here: 130 us
  waiting for transfers between devices  58.9 us (45%)
  Pallas kernels  38.2 us (29%)
  starting transfers between devices  29.5 us (23%)
  local copies, waits for them, and re-layouts  3.4 us (3%)
    ppermute x2, waiting for transfers between devices, local(): high = lax.ppermute(centre[:depth], 'cam', backward)  32.8 us
    all_to_all x2, waiting for transfers between devices, local(): lax.all_to_all(piece, 'brick', split_axis=0, concat_axis=0, tiled=True)  26 us
    pallas_call x2, Pallas kernels, restore(): pl.pallas_call(functools.partial(restore_kernel, plan, LANES if later els...  18.5 us
    pallas_call x2, Pallas kernels, frame_side(): pl.pallas_call(functools.partial(frame_kernel, first, count), grid=(steps...  15.7 us
    all_to_all x2, starting transfers between devices, local(): lax.all_to_all(piece, 'brick', split_axis=0, concat_axis=0, tiled=True)  14.4 us
    ppermute x2, starting transfers between devices, local(): high = lax.ppermute(centre[:depth], 'cam', backward)  8.61 us
    ppermute x2, starting transfers between devices, local(): low = lax.ppermute(centre[-depth:], 'cam', forward)  6.52 us
    pallas_call x1, Pallas kernels, bands(): pl.pallas_call(functools.partial(bands_kernel, psf_bank.shape[1], lateral...  3.92 us
  transfers between devices with their start and end apart: 6, of which 3 were waited for; matrix products, arithmetic and copies ran while one was open for 1% of the time, Pallas kernels for 16%

profile of v1, /device:TPU:14, one launch (start us, length us, event | category | flops | bytes accessed | tf_op | source)
XLA Modules:
  0.0 130.0 jit_solution(2598557914572873974)
XLA Ops:
  0.0 8.0 %frame_side.2 = bf16[32,16,1280]{2,1,0:T(8,128)(2,1)} custom-call(s32[1,2]{1,0:T(1,128)} %order_ref.3, s32[64]{0:T(128)} %offset_ref.3, f32[64]{0:T(128)} %fraction_ref.3, bf16[2,256,2048]{2,1,0:T(8,128)(2,1)} %raw_next.3, bf16[2,256,2048]{2,1,0:T(8,128)(2,1)} %raw_next.3, bf16[2,256,2048]{2,1,0:T(8,128)(2,1)} %raw_next.3, bf16[256,2048]{1,0:T(8,128)(2,1)} %dark_next.3, ...), custom_call_target="tpu_custom_call" | custom-call | flops 8000000000 | bytes 6500000 | tf_op jit(solution)/shard_map/frame_side/pallas_call | solution.py:124
  8.0 10.1 %all-to-all-start = ((bf16[32,16,1280]{2,1,0:T(8,128)(2,1)}), bf16[32,16,1280]{2,1,0:T(8,128)(2,1)S(1)}, u32[]{:S(2)}, u32[]{:S(2)}) async-start(bf16[32,16,1280]{2,1,0:T(8,128)(2,1)} %frame_side.2), calls=%async_computation | async-start | bytes 2621440 | tf_op jit(solution)/shard_map/all_to_all | solution.py:403
  18.1 7.7 %frame_side.3 = bf16[32,16,768]{2,1,0:T(8,128)(2,1)} custom-call(s32[1,2]{1,0:T(1,128)} %order_ref.3, s32[64]{0:T(128)} %offset_ref.3, f32[64]{0:T(128)} %fraction_ref.3, bf16[2,256,2048]{2,1,0:T(8,128)(2,1)} %raw_next.3, bf16[2,256,2048]{2,1,0:T(8,128)(2,1)} %raw_next.3, bf16[2,256,2048]{2,1,0:T(8,128)(2,1)} %raw_next.3, bf16[256,2048]{1,0:T(8,128)(2,1)} %dark_next.3, ...), custom_call_target="tpu_custom_call" | custom-call | flops 8000000000 | bytes 6500000 | tf_op jit(solution)/shard_map/frame_side/pallas_call | solution.py:124
  25.8 26.0 %all-to-all-done.refs_1_ = bf16[32,16,1280]{2,1,0:T(8,128)(2,1)S(1)} async-done(((bf16[32,16,1280]{2,1,0:T(8,128)(2,1)}), bf16[32,16,1280]{2,1,0:T(8,128)(2,1)S(1)}, u32[]{:S(2)}, u32[]{:S(2)}) %all-to-all-start) | async-done | bytes 1310752 | tf_op jit(solution)/shard_map/all_to_all | solution.py:403
  51.8 0.0 copy-start
  51.8 4.3 %all-to-all-start.1 = ((bf16[32,16,768]{2,1,0:T(8,128)(2,1)}), bf16[32,16,768]{2,1,0:T(8,128)(2,1)S(1)}, u32[]{:S(2)}, u32[]{:S(2)}) async-start(bf16[32,16,768]{2,1,0:T(8,128)(2,1)} %frame_side.3), calls=%async_computation.1 | async-start | bytes 1572864 | tf_op jit(solution)/shard_map/all_to_all | solution.py:403
  56.1 0.0 copy-start.2
  56.2 0.1 fusion
  56.2 0.0 copy-done
  56.2 4.5 %collective-permute-start.1 = (bf16[12,16,1280]{2,1,0:T(8,128)(2,1)S(1)}, bf16[12,16,1280]{2,1,0:T(8,128)(2,1)S(1)}, u32[]{:S(2)}, u32[]{:S(2)}) collective-permute-start(bf16[12,16,1280]{2,1,0:T(8,128)(2,1)S(1)} %get-tuple-element.17), channel_id=1, source_target_pairs={{32,0},{64,32},{96,64},{128,96},{160,128},{192,160},{224,192},{33,... | collective-permute-start | bytes 1474568 | tf_op jit(solution)/shard_map/ppermute | solution.py:407
  60.7 3.1 %collective-permute-start = (bf16[12,16,1280]{2,1,0:T(8,128)(2,1)S(1)}, bf16[12,16,1280]{2,1,0:T(8,128)(2,1)S(1)}, u32[]{:S(2)}, u32[]{:S(2)}) collective-permute-start(bf16[12,16,1280]{2,1,0:T(8,128)(2,1)S(1)} %get-tuple-element.18), channel_id=1, source_target_pairs={{0,32},{32,64},{64,96},{96,128},{128,160},{160,192},{192,224},{1,3... | collective-permute-start | bytes 1474568 | tf_op jit(solution)/shard_map/ppermute | solution.py:406
  63.8 0.0 copy-done.2
  63.8 0.1 pad_dynamic-slice_fusion
  63.9 0.1 broadcast_in_dim.2
  64.0 0.7 reshape.4.index_ref
  64.7 3.9 %bands.1 = (bf16[9,160,256]{2,1,0:T(8,128)(2,1)}, bf16[9,160,256]{2,1,0:T(8,128)(2,1)}, bf16[512,256]{1,0:T(8,128)(2,1)}, bf16[512,256]{1,0:T(8,128)(2,1)}) custom-call(f32[8,13]{1,0:T(8,128)} %psf_ref.1, f32[9]{0:T(128)} %lateral_ref.1, s32[1,1152]{1,0:T(1,128)} %reshape.4.index_ref), custom_call_target="tpu_custom_call" | custom-call | flops 2000000000 | bytes 2000000 | tf_op jit(solution)/shard_map/bands/pallas_call | solution.py:214
  68.6 22.2 %collective-permute-done.1.refs_2_ = bf16[12,16,1280]{2,1,0:T(8,128)(2,1)S(1)} collective-permute-done((bf16[12,16,1280]{2,1,0:T(8,128)(2,1)S(1)}, bf16[12,16,1280]{2,1,0:T(8,128)(2,1)S(1)}, u32[]{:S(2)}, u32[]{:S(2)}) %collective-permute-start.1) | collective-permute-done | bytes 491552 | tf_op jit(solution)/shard_map/ppermute | solution.py:407
  90.8 0.0 copy-start.3
  90.8 0.0 collective-permute-done.refs_0_
  90.8 0.0 copy-start.4
  90.8 0.8 copy-done.3
  91.6 0.2 copy-done.4
  91.8 9.4 %restore.2.refs_10_ = bf16[64,8,1152]{2,1,0:T(8,128)(2,1)} custom-call(bf16[12,16,1280]{2,1,0:T(8,128)(2,1)} %copy-done.4, bf16[32,16,1280]{2,1,0:T(8,128)(2,1)} %copy-done, bf16[12,16,1280]{2,1,0:T(8,128)(2,1)} %copy-done.3, bf16[9,160,256]{2,1,0:T(8,128)(2,1)} %get-tuple-element.11.refs_3_.refs_6_, bf16[9,160,256]{2,1,0:T(8,128)(2,1)} %get-tuple-element.12.refs_4_.refs_7_, ...), custom_call_target="tpu_custom_call" | custom-call | flops 7000000000 | bytes 8000000 | tf_op jit(solution)/shard_map/restore/pallas_call | solution.py:352
  101.1 0.0 all-to-all-done.1.refs_4_
  101.2 4.1 %collective-permute-start.3 = (bf16[12,16,768]{2,1,0:T(8,128)(2,1)S(1)}, bf16[12,16,768]{2,1,0:T(8,128)(2,1)S(1)}, u32[]{:S(2)}, u32[]{:S(2)}) collective-permute-start(bf16[12,16,768]{2,1,0:T(8,128)(2,1)S(1)} %get-tuple-element.19), channel_id=1, source_target_pairs={{32,0},{64,32},{96,64},{128,96},{160,128},{192,160},{224,192},{33,... | collective-permute-start | bytes 884744 | tf_op jit(solution)/shard_map/ppermute | solution.py:407
  105.3 3.4 %collective-permute-start.2 = (bf16[12,16,768]{2,1,0:T(8,128)(2,1)S(1)}, bf16[12,16,768]{2,1,0:T(8,128)(2,1)S(1)}, u32[]{:S(2)}, u32[]{:S(2)}) collective-permute-start(bf16[12,16,768]{2,1,0:T(8,128)(2,1)S(1)} %get-tuple-element.20), channel_id=1, source_target_pairs={{0,32},{32,64},{64,96},{96,128},{128,160},{160,192},{192,224},{1,3... | collective-permute-start | bytes 884744 | tf_op jit(solution)/shard_map/ppermute | solution.py:406
  108.8 10.7 %collective-permute-done.3.refs_5_ = bf16[12,16,768]{2,1,0:T(8,128)(2,1)S(1)} collective-permute-done((bf16[12,16,768]{2,1,0:T(8,128)(2,1)S(1)}, bf16[12,16,768]{2,1,0:T(8,128)(2,1)S(1)}, u32[]{:S(2)}, u32[]{:S(2)}) %collective-permute-start.3) | collective-permute-done | bytes 294944 | tf_op jit(solution)/shard_map/ppermute | solution.py:407
  119.4 0.0 collective-permute-done.2.refs_3_
  119.4 0.0 copy-done.1
  119.4 0.7 copy-done.5
  120.1 0.7 copy-done.6
  120.9 9.2 %restore.3 = bf16[64,8,2048]{2,1,0:T(8,128)(2,1)} custom-call(bf16[12,16,1280]{2,1,0:T(8,128)(2,1)} %copy-done.4, bf16[32,16,1280]{2,1,0:T(8,128)(2,1)} %copy-done, bf16[12,16,1280]{2,1,0:T(8,128)(2,1)} %copy-done.3, bf16[12,16,768]{2,1,0:T(8,128)(2,1)} %copy-done.6, bf16[32,16,768]{2,1,0:T(8,128)(2,1)} %copy-done.1, bf16[12,16,768]{2,1,0:T(8,128)(2,1)} %copy-done.5, ...), custom_call_target="tpu_custom_call" | custom-call | flops 7000000000 | bytes 8000000 | tf_op jit(solution)/shard_map/restore/pallas_call | solution.py:352
  (4 shorter events, 0.0 us)
Async XLA Ops:
  8.0 43.8 %all-to-all-start = ((bf16[32,16,1280]{2,1,0:T(8,128)(2,1)}), bf16[32,16,1280]{2,1,0:T(8,128)(2,1)S(1)}, u32[]{:S(2)}, u32[]{:S(2)}) async-start(bf16[32,16,1280]{2,1,0:T(8,128)(2,1)} %frame_side.2), calls=%async_computation | async-start | bytes 2621440 | tf_op jit(solution)/shard_map/all_to_all | solution.py:403
  51.8 4.4 %copy-start = (bf16[32,16,1280]{2,1,0:T(8,128)(2,1)}, bf16[32,16,1280]{2,1,0:T(8,128)(2,1)S(1)}, u32[]{:S(2)}) copy-start(bf16[32,16,1280]{2,1,0:T(8,128)(2,1)S(1)} %all-to-all-done.refs_1_) | copy-start | bytes 3932164
  51.8 49.3 %all-to-all-start.1 = ((bf16[32,16,768]{2,1,0:T(8,128)(2,1)}), bf16[32,16,768]{2,1,0:T(8,128)(2,1)S(1)}, u32[]{:S(2)}, u32[]{:S(2)}) async-start(bf16[32,16,768]{2,1,0:T(8,128)(2,1)} %frame_side.3), calls=%async_computation.1 | async-start | bytes 1572864 | tf_op jit(solution)/shard_map/all_to_all | solution.py:403
  56.1 7.7 %copy-start.2 = (s32[512]{0:T(512)S(1)}, s32[512]{0:T(512)}, u32[]{:S(2)}) copy-start(s32[512]{0:T(512)} %param.17) | copy-start | bytes 6148
  56.2 34.5 %collective-permute-start.1 = (bf16[12,16,1280]{2,1,0:T(8,128)(2,1)S(1)}, bf16[12,16,1280]{2,1,0:T(8,128)(2,1)S(1)}, u32[]{:S(2)}, u32[]{:S(2)}) collective-permute-start(bf16[12,16,1280]{2,1,0:T(8,128)(2,1)S(1)} %get-tuple-element.17), channel_id=1, source_target_pairs={{32,0},{64,32},{96,64},{128,96},{160,128},{192,160},{224,192},{33,... | collective-permute-start | bytes 1474568 | tf_op jit(solution)/shard_map/ppermute | solution.py:407
  60.7 30.1 %collective-permute-start = (bf16[12,16,1280]{2,1,0:T(8,128)(2,1)S(1)}, bf16[12,16,1280]{2,1,0:T(8,128)(2,1)S(1)}, u32[]{:S(2)}, u32[]{:S(2)}) collective-permute-start(bf16[12,16,1280]{2,1,0:T(8,128)(2,1)S(1)} %get-tuple-element.18), channel_id=1, source_target_pairs={{0,32},{32,64},{64,96},{96,128},{128,160},{160,192},{192,224},{1,3... | collective-permute-start | bytes 1474568 | tf_op jit(solution)/shard_map/ppermute | solution.py:406
  90.8 0.8 copy-start.3
  90.8 1.0 copy-start.4
  101.1 18.3 %copy-start.1 = (bf16[32,16,768]{2,1,0:T(8,128)(2,1)}, bf16[32,16,768]{2,1,0:T(8,128)(2,1)S(1)}, u32[]{:S(2)}) copy-start(bf16[32,16,768]{2,1,0:T(8,128)(2,1)S(1)} %all-to-all-done.1.refs_4_) | copy-start | bytes 2359300
  101.2 18.3 %collective-permute-start.3 = (bf16[12,16,768]{2,1,0:T(8,128)(2,1)S(1)}, bf16[12,16,768]{2,1,0:T(8,128)(2,1)S(1)}, u32[]{:S(2)}, u32[]{:S(2)}) collective-permute-start(bf16[12,16,768]{2,1,0:T(8,128)(2,1)S(1)} %get-tuple-element.19), channel_id=1, source_target_pairs={{32,0},{64,32},{96,64},{128,96},{160,128},{192,160},{224,192},{33,... | collective-permute-start | bytes 884744 | tf_op jit(solution)/shard_map/ppermute | solution.py:407
  105.3 14.1 %collective-permute-start.2 = (bf16[12,16,768]{2,1,0:T(8,128)(2,1)S(1)}, bf16[12,16,768]{2,1,0:T(8,128)(2,1)S(1)}, u32[]{:S(2)}, u32[]{:S(2)}) collective-permute-start(bf16[12,16,768]{2,1,0:T(8,128)(2,1)S(1)} %get-tuple-element.20), channel_id=1, source_target_pairs={{0,32},{32,64},{64,96},{96,128},{128,160},{160,192},{192,224},{1,3... | collective-permute-start | bytes 884744 | tf_op jit(solution)/shard_map/ppermute | solution.py:406
  119.4 0.7 copy-start.5
  120.1 0.7 copy-start.6

commit v2 on v1

--- a/solution.py
+++ b/solution.py
@@ -401,8 +401,6 @@
             shear_fraction, lo, hi,
         )
         centre = lax.all_to_all(piece, "brick", split_axis=0, concat_axis=0, tiled=True)
-        if result is not None:
-            centre, result = lax.optimization_barrier((centre, result))
         low = lax.ppermute(centre[-depth:], "cam", forward)
         high = lax.ppermute(centre[:depth], "cam", backward)
         parts.append((low, centre, high))

time: 131 us -> 118 us (0.901)
  waiting for transfers between devices: 58.9 us -> 47.6 us
    ppermute x2, waiting for transfers between devices: 32.8 us -> 10.5 us  [local(): high = lax.ppermute(centre[:depth], 'cam', backward)]
    all_to_all x2, waiting for transfers between devices: 26 us -> 37 us  [local(): lax.all_to_all(piece, 'brick', split_axis=0, concat_axis=0, tiled=True)]
  transfers between devices with their start and end apart: 6 -> 6, of which waited for: 3 -> 3; matrix products, arithmetic and copies ran while one was open for 1% -> 1% of each run, Pallas kernels for 16% -> 18%
where the time goes in v2:
time: 118 us
  waiting for transfers between devices  47.6 us (40%)
  Pallas kernels  38.2 us (32%)
  starting transfers between devices  29.3 us (25%)
  local copies, waits for them, and re-layouts  2.69 us (2%)
    all_to_all x2, waiting for transfers between devices, local(): lax.all_to_all(piece, 'brick', split_axis=0, concat_axis=0, tiled=True)  37 us
    pallas_call x2, Pallas kernels, restore(): pl.pallas_call(functools.partial(restore_kernel, plan, LANES if later els...  18.5 us
    pallas_call x2, Pallas kernels, frame_side(): pl.pallas_call(functools.partial(frame_kernel, first, count), grid=(steps...  15.7 us
    all_to_all x2, starting transfers between devices, local(): lax.all_to_all(piece, 'brick', split_axis=0, concat_axis=0, tiled=True)  14.4 us
    ppermute x2, waiting for transfers between devices, local(): high = lax.ppermute(centre[:depth], 'cam', backward)  10.5 us
    ppermute x2, starting transfers between devices, local(): high = lax.ppermute(centre[:depth], 'cam', backward)  8.94 us
    ppermute x2, starting transfers between devices, local(): low = lax.ppermute(centre[-depth:], 'cam', forward)  5.98 us
    pallas_call x1, Pallas kernels, bands(): pl.pallas_call(functools.partial(bands_kernel, psf_bank.shape[1], lateral...  3.92 us
  transfers between devices with their start and end apart: 6, of which 3 were waited for; matrix products, arithmetic and copies ran while one was open for 1% of the time, Pallas kernels for 18%

profile of v2, /device:TPU:14, one launch (start us, length us, event | category | flops | bytes accessed | tf_op | source)
XLA Modules:
  0.0 117.8 jit_solution(4291349969055502409)
XLA Ops:
  0.0 8.0 %frame_side.2 = bf16[32,16,1280]{2,1,0:T(8,128)(2,1)} custom-call(s32[1,2]{1,0:T(1,128)} %order_ref.3, s32[64]{0:T(128)} %offset_ref.3, f32[64]{0:T(128)} %fraction_ref.3, bf16[2,256,2048]{2,1,0:T(8,128)(2,1)} %raw_next.3, bf16[2,256,2048]{2,1,0:T(8,128)(2,1)} %raw_next.3, bf16[2,256,2048]{2,1,0:T(8,128)(2,1)} %raw_next.3, bf16[256,2048]{1,0:T(8,128)(2,1)} %dark_next.3, ...), custom_call_target="tpu_custom_call" | custom-call | flops 8000000000 | bytes 6500000 | tf_op jit(solution)/shard_map/frame_side/pallas_call | solution.py:124
  8.0 10.1 %all-to-all-start = ((bf16[32,16,1280]{2,1,0:T(8,128)(2,1)}), bf16[32,16,1280]{2,1,0:T(8,128)(2,1)S(1)}, u32[]{:S(2)}, u32[]{:S(2)}) async-start(bf16[32,16,1280]{2,1,0:T(8,128)(2,1)} %frame_side.2), calls=%async_computation | async-start | bytes 2621440 | tf_op jit(solution)/shard_map/all_to_all | solution.py:403
  18.1 7.7 %frame_side.3 = bf16[32,16,768]{2,1,0:T(8,128)(2,1)} custom-call(s32[1,2]{1,0:T(1,128)} %order_ref.3, s32[64]{0:T(128)} %offset_ref.3, f32[64]{0:T(128)} %fraction_ref.3, bf16[2,256,2048]{2,1,0:T(8,128)(2,1)} %raw_next.3, bf16[2,256,2048]{2,1,0:T(8,128)(2,1)} %raw_next.3, bf16[2,256,2048]{2,1,0:T(8,128)(2,1)} %raw_next.3, bf16[256,2048]{1,0:T(8,128)(2,1)} %dark_next.3, ...), custom_call_target="tpu_custom_call" | custom-call | flops 8000000000 | bytes 6500000 | tf_op jit(solution)/shard_map/frame_side/pallas_call | solution.py:124
  25.8 26.0 %all-to-all-done.refs_1_ = bf16[32,16,1280]{2,1,0:T(8,128)(2,1)S(1)} async-done(((bf16[32,16,1280]{2,1,0:T(8,128)(2,1)}), bf16[32,16,1280]{2,1,0:T(8,128)(2,1)S(1)}, u32[]{:S(2)}, u32[]{:S(2)}) %all-to-all-start) | async-done | bytes 1310752 | tf_op jit(solution)/shard_map/all_to_all | solution.py:403
  51.8 4.3 %all-to-all-start.1 = ((bf16[32,16,768]{2,1,0:T(8,128)(2,1)}), bf16[32,16,768]{2,1,0:T(8,128)(2,1)S(1)}, u32[]{:S(2)}, u32[]{:S(2)}) async-start(bf16[32,16,768]{2,1,0:T(8,128)(2,1)} %frame_side.3), calls=%async_computation.1 | async-start | bytes 1572864 | tf_op jit(solution)/shard_map/all_to_all | solution.py:403
  56.1 0.0 copy-start.2
  56.2 0.1 fusion
  56.2 0.0 copy-done
  56.2 4.5 %collective-permute-start.1 = (bf16[12,16,1280]{2,1,0:T(8,128)(2,1)S(1)}, bf16[12,16,1280]{2,1,0:T(8,128)(2,1)S(1)}, u32[]{:S(2)}, u32[]{:S(2)}) collective-permute-start(bf16[12,16,1280]{2,1,0:T(8,128)(2,1)S(1)} %get-tuple-element.13), channel_id=1, source_target_pairs={{32,0},{64,32},{96,64},{128,96},{160,128},{192,160},{224,192},{33,... | collective-permute-start | bytes 1474568 | tf_op jit(solution)/shard_map/ppermute | solution.py:405
  60.7 2.9 %collective-permute-start = (bf16[12,16,1280]{2,1,0:T(8,128)(2,1)S(1)}, bf16[12,16,1280]{2,1,0:T(8,128)(2,1)S(1)}, u32[]{:S(2)}, u32[]{:S(2)}) collective-permute-start(bf16[12,16,1280]{2,1,0:T(8,128)(2,1)S(1)} %get-tuple-element.14), channel_id=1, source_target_pairs={{0,32},{32,64},{64,96},{96,128},{128,160},{160,192},{192,224},{1,3... | collective-permute-start | bytes 1474568 | tf_op jit(solution)/shard_map/ppermute | solution.py:404
  63.6 0.0 copy-done.2
  63.6 0.1 pad_dynamic-slice_fusion
  63.7 0.1 broadcast_in_dim.2
  63.8 0.7 reshape.4.index_ref
  64.5 3.9 %bands.1 = (bf16[9,160,256]{2,1,0:T(8,128)(2,1)}, bf16[9,160,256]{2,1,0:T(8,128)(2,1)}, bf16[512,256]{1,0:T(8,128)(2,1)}, bf16[512,256]{1,0:T(8,128)(2,1)}) custom-call(f32[8,13]{1,0:T(8,128)} %psf_ref.1, f32[9]{0:T(128)} %lateral_ref.1, s32[1,1152]{1,0:T(1,128)} %reshape.4.index_ref), custom_call_target="tpu_custom_call" | custom-call | flops 2000000000 | bytes 2000000 | tf_op jit(solution)/shard_map/bands/pallas_call | solution.py:214
  68.5 11.0 %all-to-all-done.1.refs_4_ = bf16[32,16,768]{2,1,0:T(8,128)(2,1)S(1)} async-done(((bf16[32,16,768]{2,1,0:T(8,128)(2,1)}), bf16[32,16,768]{2,1,0:T(8,128)(2,1)S(1)}, u32[]{:S(2)}, u32[]{:S(2)}) %all-to-all-start.1) | async-done | bytes 786464 | tf_op jit(solution)/shard_map/all_to_all | solution.py:403
  79.5 0.0 copy-start.1
  79.5 4.5 %collective-permute-start.3 = (bf16[12,16,768]{2,1,0:T(8,128)(2,1)S(1)}, bf16[12,16,768]{2,1,0:T(8,128)(2,1)S(1)}, u32[]{:S(2)}, u32[]{:S(2)}) collective-permute-start(bf16[12,16,768]{2,1,0:T(8,128)(2,1)S(1)} %get-tuple-element.15), channel_id=1, source_target_pairs={{32,0},{64,32},{96,64},{128,96},{160,128},{192,160},{224,192},{33,... | collective-permute-start | bytes 884744 | tf_op jit(solution)/shard_map/ppermute | solution.py:405
  84.0 3.1 %collective-permute-start.2 = (bf16[12,16,768]{2,1,0:T(8,128)(2,1)S(1)}, bf16[12,16,768]{2,1,0:T(8,128)(2,1)}, u32[]{:S(2)}, u32[]{:S(2)}) collective-permute-start(bf16[12,16,768]{2,1,0:T(8,128)(2,1)S(1)} %get-tuple-element.16), channel_id=1, source_target_pairs={{0,32},{32,64},{64,96},{96,128},{128,160},{160,192},{192,224},{1,3... | collective-permute-start | bytes 884744 | tf_op jit(solution)/shard_map/ppermute | solution.py:404
  87.1 10.5 %collective-permute-done.1.refs_2_ = bf16[12,16,1280]{2,1,0:T(8,128)(2,1)S(1)} collective-permute-done((bf16[12,16,1280]{2,1,0:T(8,128)(2,1)S(1)}, bf16[12,16,1280]{2,1,0:T(8,128)(2,1)S(1)}, u32[]{:S(2)}, u32[]{:S(2)}) %collective-permute-start.1) | collective-permute-done | bytes 491552 | tf_op jit(solution)/shard_map/ppermute | solution.py:405
  97.6 0.0 copy-start.3
  97.6 0.0 collective-permute-done.refs_0_
  97.6 0.0 copy-start.4
  97.6 0.8 copy-done.3
  98.4 0.2 copy-done.4
  98.6 9.4 %restore.2.refs_10_ = bf16[64,8,1152]{2,1,0:T(8,128)(2,1)} custom-call(bf16[12,16,1280]{2,1,0:T(8,128)(2,1)} %copy-done.4, bf16[32,16,1280]{2,1,0:T(8,128)(2,1)} %copy-done, bf16[12,16,1280]{2,1,0:T(8,128)(2,1)} %copy-done.3, bf16[9,160,256]{2,1,0:T(8,128)(2,1)} %get-tuple-element.9.refs_3_.refs_6_, bf16[9,160,256]{2,1,0:T(8,128)(2,1)} %get-tuple-element.10.refs_4_.refs_7_, ...), custom_call_target="tpu_custom_call" | custom-call | flops 7000000000 | bytes 8000000 | tf_op jit(solution)/shard_map/restore/pallas_call | solution.py:352
  107.9 0.0 copy-done.1
  108.0 0.0 collective-permute-done.3.refs_5_
  108.0 0.0 copy-start.5
  108.0 0.0 collective-permute-done.2.refs_3_
  108.0 0.7 copy-done.5
  108.7 9.2 %restore.3 = bf16[64,8,2048]{2,1,0:T(8,128)(2,1)} custom-call(bf16[12,16,1280]{2,1,0:T(8,128)(2,1)} %copy-done.4, bf16[32,16,1280]{2,1,0:T(8,128)(2,1)} %copy-done, bf16[12,16,1280]{2,1,0:T(8,128)(2,1)} %copy-done.3, bf16[12,16,768]{2,1,0:T(8,128)(2,1)} %collective-permute-done.2.refs_3_, bf16[32,16,768]{2,1,0:T(8,128)(2,1)} %copy-done.1, ...), custom_call_target="tpu_custom_call" | custom-call | flops 7000000000 | bytes 8000000 | tf_op jit(solution)/shard_map/restore/pallas_call | solution.py:352
  (2 shorter events, 0.0 us)
Async XLA Ops:
  8.0 43.8 %all-to-all-start = ((bf16[32,16,1280]{2,1,0:T(8,128)(2,1)}), bf16[32,16,1280]{2,1,0:T(8,128)(2,1)S(1)}, u32[]{:S(2)}, u32[]{:S(2)}) async-start(bf16[32,16,1280]{2,1,0:T(8,128)(2,1)} %frame_side.2), calls=%async_computation | async-start | bytes 2621440 | tf_op jit(solution)/shard_map/all_to_all | solution.py:403
  51.8 4.4 %copy-start = (bf16[32,16,1280]{2,1,0:T(8,128)(2,1)}, bf16[32,16,1280]{2,1,0:T(8,128)(2,1)S(1)}, u32[]{:S(2)}) copy-start(bf16[32,16,1280]{2,1,0:T(8,128)(2,1)S(1)} %all-to-all-done.refs_1_) | copy-start | bytes 3932164
  51.8 27.6 %all-to-all-start.1 = ((bf16[32,16,768]{2,1,0:T(8,128)(2,1)}), bf16[32,16,768]{2,1,0:T(8,128)(2,1)S(1)}, u32[]{:S(2)}, u32[]{:S(2)}) async-start(bf16[32,16,768]{2,1,0:T(8,128)(2,1)} %frame_side.3), calls=%async_computation.1 | async-start | bytes 1572864 | tf_op jit(solution)/shard_map/all_to_all | solution.py:403
  56.1 7.5 %copy-start.2 = (s32[512]{0:T(512)S(1)}, s32[512]{0:T(512)}, u32[]{:S(2)}) copy-start(s32[512]{0:T(512)} %param.17) | copy-start | bytes 6148
  56.2 41.3 %collective-permute-start.1 = (bf16[12,16,1280]{2,1,0:T(8,128)(2,1)S(1)}, bf16[12,16,1280]{2,1,0:T(8,128)(2,1)S(1)}, u32[]{:S(2)}, u32[]{:S(2)}) collective-permute-start(bf16[12,16,1280]{2,1,0:T(8,128)(2,1)S(1)} %get-tuple-element.13), channel_id=1, source_target_pairs={{32,0},{64,32},{96,64},{128,96},{160,128},{192,160},{224,192},{33,... | collective-permute-start | bytes 1474568 | tf_op jit(solution)/shard_map/ppermute | solution.py:405
  60.7 36.9 %collective-permute-start = (bf16[12,16,1280]{2,1,0:T(8,128)(2,1)S(1)}, bf16[12,16,1280]{2,1,0:T(8,128)(2,1)S(1)}, u32[]{:S(2)}, u32[]{:S(2)}) collective-permute-start(bf16[12,16,1280]{2,1,0:T(8,128)(2,1)S(1)} %get-tuple-element.14), channel_id=1, source_target_pairs={{0,32},{32,64},{64,96},{96,128},{128,160},{160,192},{192,224},{1,3... | collective-permute-start | bytes 1474568 | tf_op jit(solution)/shard_map/ppermute | solution.py:404
  79.5 28.5 %copy-start.1 = (bf16[32,16,768]{2,1,0:T(8,128)(2,1)}, bf16[32,16,768]{2,1,0:T(8,128)(2,1)S(1)}, u32[]{:S(2)}) copy-start(bf16[32,16,768]{2,1,0:T(8,128)(2,1)S(1)} %all-to-all-done.1.refs_4_) | copy-start | bytes 2359300
  79.5 28.4 %collective-permute-start.3 = (bf16[12,16,768]{2,1,0:T(8,128)(2,1)S(1)}, bf16[12,16,768]{2,1,0:T(8,128)(2,1)S(1)}, u32[]{:S(2)}, u32[]{:S(2)}) collective-permute-start(bf16[12,16,768]{2,1,0:T(8,128)(2,1)S(1)} %get-tuple-element.15), channel_id=1, source_target_pairs={{32,0},{64,32},{96,64},{128,96},{160,128},{192,160},{224,192},{33,... | collective-permute-start | bytes 884744 | tf_op jit(solution)/shard_map/ppermute | solution.py:405
  84.0 24.0 %collective-permute-start.2 = (bf16[12,16,768]{2,1,0:T(8,128)(2,1)S(1)}, bf16[12,16,768]{2,1,0:T(8,128)(2,1)}, u32[]{:S(2)}, u32[]{:S(2)}) collective-permute-start(bf16[12,16,768]{2,1,0:T(8,128)(2,1)S(1)} %get-tuple-element.16), channel_id=1, source_target_pairs={{0,32},{32,64},{64,96},{96,128},{128,160},{160,192},{192,224},{1,3... | collective-permute-start | bytes 884744 | tf_op jit(solution)/shard_map/ppermute | solution.py:404
  97.6 0.8 copy-start.3
  97.6 1.0 copy-start.4
  108.0 0.7 copy-start.5

commit v3 on v2

--- a/solution.py
+++ b/solution.py
@@ -18,6 +18,8 @@
 LEAD = SHEAR // LANES + 1
 SPLIT = 1280
 VMEM = 60 * 1024 * 1024
+BANDS_VMEM = 20 * 1024 * 1024
+RESTORE_VMEM = 42 * 1024 * 1024
 GROUP = 20
 SPAN = 32
 
@@ -139,15 +141,29 @@
 
 
 def stages(planes, half):
-    total = planes + 4 * ITERS * half
-    plan = []
-    for reach in range(1, 2 * ITERS + 1):
-        lo, hi = reach * half, total - reach * half
-        plan.append([(at, min(GROUP, hi - at)) for at in range(lo, hi, GROUP)])
-    return plan
-
-
-def bands_kernel(taps, lat_taps, plan, psf_ref, lateral_ref, index_ref, g_ref, gt_ref, tl_ref, tm_ref):
+    halo = 2 * ITERS * half
+    total = planes + 2 * halo
+
+    def cut(lo, hi, most):
+        parts = -(-(hi - lo) // most)
+        size = -(-(hi - lo) // (2 * parts)) * 2
+        return [(at, min(size, hi - at)) for at in range(lo, hi, size)]
+
+    inner, outer = [], []
+    for stage in range(1, 2 * ITERS + 1):
+        reach = stage * half
+        lo, hi = halo + reach, total - halo - reach
+        inner.append([cut(lo, hi, GROUP)])
+        outer.append([cut(reach, lo, GROUP), cut(hi, total - reach, GROUP)])
+    return inner, outer
+
+
+def flat(stage):
+    return [group for groups in stage for group in groups]
+
+
+def bands_kernel(taps, lat_taps, plans, psf_ref, lateral_ref, index_ref, *outs):
+    matrices, (tl_ref, tm_ref) = outs[:-2], outs[-2:]
     f32 = jnp.float32
     bf16 = jnp.bfloat16
     half = taps // 2
@@ -172,16 +188,18 @@
             m = jnp.where(gap == ROWS * order(tap), values, m)
         return m
 
-    slot = [0, 0]
-    for number, groups in enumerate(plan):
-        for at, _ in groups:
-            if number % 2 == 0:
-                m = banded(at, row - col, lambda tap: tap).T
-                g_ref[slot[0]] = m[: GROUP * ROWS].astype(bf16)
-            else:
-                m = banded(at - half, col - row, lambda tap: 2 * half - tap)
-                gt_ref[slot[1]] = m[: GROUP * ROWS].astype(bf16)
-            slot[number % 2] += 1
+    for which, plan in enumerate(plans):
+        slot = [0, 0]
+        for number, stage in enumerate(plan):
+            kind = number % 2
+            target = matrices[2 * which + kind]
+            for at, _ in flat(stage):
+                if kind == 0:
+                    m = banded(at, row - col, lambda tap: tap).T
+                else:
+                    m = banded(at - half, col - row, lambda tap: 2 * half - tap)
+                target[slot[kind]] = m[: GROUP * ROWS].astype(bf16)
+                slot[kind] += 1
 
     lateral_total = lateral_ref[0]
     for tap in range(1, lat_taps):
@@ -200,8 +218,7 @@
 
 
 def bands(psf_bank, lateral_psf, band_index, planes, halo):
-    half = psf_bank.shape[1] // 2
-    plan = stages(planes, half)
+    plans = stages(planes, psf_bank.shape[1] // 2)
     spread = jnp.pad(band_index, (halo, halo + SPAN), constant_values=-1)
     first = lax.axis_index("cam") * planes
     length = planes + 2 * halo + SPAN
@@ -209,17 +226,19 @@
     index = jnp.broadcast_to(mine[:, None], (length, ROWS)).reshape(1, length * ROWS)
     smem = pl.BlockSpec(memory_space=pltpu.SMEM)
     vmem = pl.BlockSpec(memory_space=pltpu.VMEM)
-    counts = [sum(len(groups) for groups in plan[kind::2]) for kind in range(2)]
+    counts = [
+        sum(len(flat(stage)) for stage in plan[kind::2]) for plan in plans for kind in range(2)
+    ]
     strip = jax.ShapeDtypeStruct((TILE + 2 * LANES, TILE), jnp.bfloat16)
     return pl.pallas_call(
-        functools.partial(bands_kernel, psf_bank.shape[1], lateral_psf.shape[0], plan),
+        functools.partial(bands_kernel, psf_bank.shape[1], lateral_psf.shape[0], plans),
         in_specs=[smem, smem, vmem],
-        out_specs=[vmem] * 4,
+        out_specs=[vmem] * 6,
         out_shape=[
             jax.ShapeDtypeStruct((n, GROUP * ROWS, SPAN * ROWS), jnp.bfloat16) for n in counts
         ]
         + [strip, strip],
-        compiler_params=pltpu.CompilerParams(vmem_limit_bytes=VMEM),
+        compiler_params=pltpu.CompilerParams(vmem_limit_bytes=BANDS_VMEM),
         cost_estimate=pl.CostEstimate(
             flops=2_000_000_000, bytes_accessed=2_000_000, transcendentals=0
         ),
@@ -227,16 +246,25 @@
     )(psf_bank, lateral_psf, index)
 
 
-def restore_kernel(plan, kept, *refs):
-    later = kept is not None
-    sources = [refs[3 * i : 3 * i + 3] for i in range(2 if later else 1)]
-    refs = refs[3 * len(sources) :]
+def restore_kernel(plan, inside, counts, merge, cut, *refs):
+    parts = []
+    for count in counts:
+        parts.append(refs[:count])
+        refs = refs[count:]
     g, gt, tl, tm = refs[:4]
-    earlier = refs[4] if later else None
-    out, mf, ef, mb, qb, pad, pad_back = refs[4 + later :]
+    refs = refs[4:]
     f32 = jnp.float32
     bf16 = jnp.bfloat16
+    half = plan[0][0][0][0] if not inside else plan[1][0][0][0] - plan[0][0][0][0]
+    halo = 2 * ITERS * half
+    if inside:
+        out, q_out, e_out, mf, ef, mb, qb, pad, pad_back = refs
+    else:
+        q_in, e_in, middle = refs[:3]
+        earlier = refs[3] if merge else None
+        out, mf, ef, mb, qb, pad, pad_back = refs[3 + merge :]
     size, columns = mf.shape
+    total = size // ROWS
     tiles = columns // TILE
 
     for buffer in (pad, pad_back):
@@ -244,10 +272,10 @@
         buffer[:, LANES + columns :] = jnp.zeros((size, LANES), bf16)
 
     at_column = 0
-    for source in sources:
-        width = source[1].shape[-1]
-        at_row = 0
-        for ref in source:
+    for part in parts:
+        width = part[0].shape[-1]
+        at_row = halo * ROWS if inside else 0
+        for ref in part:
             height = ref.shape[0] * ref.shape[1]
             for col in range(0, width, TILE):
                 whole = ref[:, :, col : col + TILE].reshape(height, TILE)
@@ -257,6 +285,19 @@
             at_row += height
         at_column += width
 
+    q_rows = slice((halo + half) * ROWS, (total - halo - half) * ROWS)
+    e_width = half * (2 * ITERS - 2) * ROWS
+    e_low = (halo + 2 * half) * ROWS
+    e_high = (total - halo - 2 * half) * ROWS - e_width
+    if not inside:
+        qb[q_rows, :] = q_in[...]
+        for number, start in enumerate((e_low, e_high)):
+            e = e_in[number * e_width : (number + 1) * e_width, :]
+            ef[start : start + e_width, :] = e
+            mb[start : start + e_width, :] = e.astype(bf16)
+        for lo in range(0, out.shape[-1] if not merge else 0, LANES):
+            out[half * 4 : out.shape[0] - half * 4, :, lo : lo + LANES] = middle[:, :, lo : lo + LANES]
+
     def columns_of(tile):
         return slice(tile * TILE, (tile + 1) * TILE)
 
@@ -266,13 +307,11 @@
     def around(tile):
         return slice(tile * TILE, (tile + 1) * TILE + 2 * LANES)
 
-    half = plan[0][0][0]
-
     def rows_of(groups):
         return slice(groups[0][0] * ROWS, (groups[-1][0] + groups[-1][1]) * ROWS)
 
-    def axial(matrices, skip, groups, source, target, tile):
-        for number, (first, count) in enumerate(groups):
+    def axial(matrices, skip, stage, source, target, tile):
+        for number, (first, count) in enumerate(flat(stage)):
             low = (first - half) * ROWS
             high = (first + count + half) * ROWS
             r = jnp.dot(
@@ -284,35 +323,36 @@
 
     for sweep in range(ITERS):
         ahead, back = plan[2 * sweep], plan[2 * sweep + 1]
-        outer, inner = rows_of(ahead), rows_of(back)
-        skip_ahead = sum(len(groups) for groups in plan[0 : 2 * sweep : 2])
-        skip_back = sum(len(groups) for groups in plan[1 : 2 * sweep : 2])
+        skip_ahead = sum(len(flat(stage)) for stage in plan[0 : 2 * sweep : 2])
+        skip_back = sum(len(flat(stage)) for stage in plan[1 : 2 * sweep : 2])
         final = sweep == ITERS - 1
 
         def ratio(tile):
             cols = columns_of(tile)
-            b = jnp.dot(pad[outer, around(tile)], tl[...], preferred_element_type=f32) + BACKGROUND
-            guess = pl.reciprocal(b, approx=True)
-            guess = guess * (2.0 - b * guess)
-            qb[outer, cols] = (mf[outer, cols] * guess).astype(bf16)
+            for groups in ahead:
+                rows = rows_of(groups)
+                b = jnp.dot(pad[rows, around(tile)], tl[...], preferred_element_type=f32) + BACKGROUND
+                guess = pl.reciprocal(b, approx=True)
+                guess = guess * (2.0 - b * guess)
+                qb[rows, cols] = (mf[rows, cols] * guess).astype(bf16)
 
         def update(tile):
             cols = columns_of(tile)
-            d = jnp.dot(pad_back[inner, around(tile)], tm[...], preferred_element_type=f32)
-            e = (mf if sweep == 0 else ef)[inner, cols] * d
-            if not final:
-                ef[inner, cols] = e
-                mb[inner, cols] = e.astype(bf16)
-                return
-            e = e.reshape(-1, ROWS, TILE).astype(bf16)
-            if not later:
-                lo, hi = tile * TILE, min((tile + 1) * TILE, out.shape[-1])
-                if hi > lo:
-                    out[:, :, lo:hi] = e[:, :, : hi - lo]
-            else:
-                cut = kept if tile == 0 else 0
-                start = out.shape[-1] - columns + tile * TILE
-                out[:, :, start + cut : start + TILE] = e[:, :, cut:]
+            for groups in back:
+                rows = rows_of(groups)
+                d = jnp.dot(pad_back[rows, around(tile)], tm[...], preferred_element_type=f32)
+                e = (mf if sweep == 0 else ef)[rows, cols] * d
+                if not final:
+                    ef[rows, cols] = e
+                    mb[rows, cols] = e.astype(bf16)
+                    continue
+                e = e.reshape(-1, ROWS, TILE).astype(bf16)
+                first = groups[0][0] - plan[-1][0][0][0]
+                start = (out.shape[-1] - columns if cut else 0) + tile * TILE
+                drop = cut if tile == 0 else 0
+                keep = min(TILE, out.shape[-1] - start)
+                if keep > drop:
+                    out[first : first + e.shape[0], :, start + drop : start + keep] = e[:, :, drop:keep]
 
         for step in range(tiles + 5):
             if step < tiles:
@@ -324,14 +364,18 @@
             if 0 <= step - 5 < tiles:
                 update(step - 5)
 
-    if later:
-        out[:, :, : earlier.shape[-1]] = earlier[...]
-
-
-def restore(parts, matrices, earlier, plan, columns):
-    later = earlier is not None
-    planes = plan[-1][-1][0] + plan[-1][-1][1] - plan[-1][0][0]
-    height = sum(part.shape[0] * part.shape[1] for part in parts[0])
+    if inside:
+        q_out[...] = qb[q_rows, :]
+        e_out[:e_width, :] = ef[e_low : e_low + e_width, :]
+        e_out[e_width:, :] = ef[e_high : e_high + e_width, :]
+    elif merge:
+        kept = earlier.shape[-1]
+        out[:, :, :kept] = earlier[...]
+        out[half * 4 : out.shape[0] - half * 4, :, kept:] = middle[:, :, columns - (out.shape[-1] - kept) :]
+
+
+def restore(parts, matrices, state, earlier, plan, inside, planes, half, columns):
+    merge = earlier is not None
     operands, specs, width = [], [], 0
     for number, part in enumerate(parts):
         kept = 2 * LANES if number < len(parts) - 1 else part[0].shape[-1]
@@ -345,29 +389,41 @@
     def whole(array):
         return pl.BlockSpec(array.shape, lambda i: (0,) * len(array.shape))
 
-    for array in (*matrices, *([earlier] if later else [])):
+    for array in (*matrices, *state, *([earlier] if merge else [])):
         operands.append(array)
         specs.append(whole(array))
-    result = jax.ShapeDtypeStruct((planes, ROWS, columns if later else width - LANES), jnp.bfloat16)
+    halo = 2 * ITERS * half
+    height = (planes + 2 * halo) * ROWS
+    bf16 = jnp.bfloat16
+    if inside:
+        cut = 0
+        results = [
+            jax.ShapeDtypeStruct((planes - 2 * halo, ROWS, width), bf16),
+            jax.ShapeDtypeStruct(((planes - 2 * half) * ROWS, width), bf16),
+            jax.ShapeDtypeStruct((2 * half * (2 * ITERS - 2) * ROWS, width), jnp.float32),
+        ]
+    else:
+        cut = LANES if merge else 0
+        results = [jax.ShapeDtypeStruct((planes, ROWS, columns if merge else width - LANES), bf16)]
     return pl.pallas_call(
-        functools.partial(restore_kernel, plan, LANES if later else None),
+        functools.partial(restore_kernel, plan, inside, [len(part) for part in parts], merge, cut),
         grid=(1,),
         in_specs=specs,
-        out_specs=whole(result),
-        out_shape=result,
+        out_specs=[whole(result) for result in results],
+        out_shape=results,
         scratch_shapes=[
             pltpu.VMEM((height, width), jnp.float32),
             pltpu.VMEM((height, width), jnp.float32),
-            pltpu.VMEM((height, width), jnp.bfloat16),
-            pltpu.VMEM((height, width), jnp.bfloat16),
-            pltpu.VMEM((height, width + 2 * LANES), jnp.bfloat16),
-            pltpu.VMEM((height, width + 2 * LANES), jnp.bfloat16),
+            pltpu.VMEM((height, width), bf16),
+            pltpu.VMEM((height, width), bf16),
+            pltpu.VMEM((height, width + 2 * LANES), bf16),
+            pltpu.VMEM((height, width + 2 * LANES), bf16),
         ],
-        compiler_params=pltpu.CompilerParams(vmem_limit_bytes=VMEM),
+        compiler_params=pltpu.CompilerParams(vmem_limit_bytes=RESTORE_VMEM),
         cost_estimate=pl.CostEstimate(
-            flops=7_000_000_000, bytes_accessed=8_000_000, transcendentals=0
+            flops=5_000_000_000, bytes_accessed=8_000_000, transcendentals=0
         ),
-        name="restore",
+        name="inside" if inside else "ends",
     )(*operands)
 
 
@@ -387,14 +443,17 @@
     planes = shear_offset.shape[0]
     columns = raw_frames.shape[-1]
     halo = 2 * ITERS * half
-    plan = stages(planes, half)
+    inner, outer = stages(planes, half)
     count = lax.axis_size("cam")
     forward = [(i, i + 1) for i in range(count - 1)]
     backward = [(i + 1, i) for i in range(count - 1)]
-    matrices = bands(psf_bank, lateral_psf, band_index, planes, halo)
+    *axial, forward_lateral, backward_lateral = bands(psf_bank, lateral_psf, band_index, planes, halo)
+    inner_matrices = (*axial[:2], forward_lateral, backward_lateral)
+    outer_matrices = (*axial[2:], forward_lateral, backward_lateral)
     depth = halo // 2
     result = None
     parts = []
+    centres = []
     for lo, hi in ((0, SPLIT), (SPLIT, columns)):
         piece = frame_side(
             raw_frames, frame_order, dark_frame, flat_gain, stripe_band, shear_offset,
@@ -403,8 +462,15 @@
         centre = lax.all_to_all(piece, "brick", split_axis=0, concat_axis=0, tiled=True)
         low = lax.ppermute(centre[-depth:], "cam", forward)
         high = lax.ppermute(centre[:depth], "cam", backward)
+        centres.append((centre,))
         parts.append((low, centre, high))
-        result = restore(parts, matrices, result, plan, columns)
+        middle, quotients, estimates = restore(
+            centres, inner_matrices, (), None, inner, True, planes, half, columns
+        )
+        (result,) = restore(
+            parts, outer_matrices, (quotients, estimates, middle), result, outer, False, planes, half,
+            columns,
+        )
     return result
 
 

time: 118 us -> 116 us (0.983)
  Pallas kernels: 38.2 us -> 32.8 us
  starting transfers between devices: 29.3 us -> 30.9 us
    pallas_call x2 -> x4, Pallas kernels: 18.5 us -> 14 us  [restore(): pl.pallas_call(functools.partial(restore_kernel, plan, inside, [len(part)...]
    ppermute x2, waiting for transfers between devices: 0.01 us -> 3.35 us  [local(): low = lax.ppermute(centre[-depth:], 'cam', forward)]
    all_to_all x2, waiting for transfers between devices: 37 us -> 34.4 us  [local(): lax.all_to_all(piece, 'brick', split_axis=0, concat_axis=0, tiled=True)]
    ppermute x2, starting transfers between devices: 5.98 us -> 8.42 us  [local(): low = lax.ppermute(centre[-depth:], 'cam', forward)]
  transfers between devices with their start and end apart: 6 -> 6, of which waited for: 3 -> 4; matrix products, arithmetic and copies ran while one was open for 1% -> 1% of each run, Pallas kernels for 18% -> 18%
where the time goes in v3:
time: 116 us
  waiting for transfers between devices  48.2 us (42%)
  Pallas kernels  32.8 us (28%)
  starting transfers between devices  30.9 us (27%)
  local copies, waits for them, and re-layouts  3.44 us (3%)
    all_to_all x2, waiting for transfers between devices, local(): lax.all_to_all(piece, 'brick', split_axis=0, concat_axis=0, tiled=True)  34.4 us
    pallas_call x2, Pallas kernels, frame_side(): pl.pallas_call(functools.partial(frame_kernel, first, count), grid=(steps...  15.8 us
    all_to_all x2, starting transfers between devices, local(): lax.all_to_all(piece, 'brick', split_axis=0, concat_axis=0, tiled=True)  14.1 us
    pallas_call x4, Pallas kernels, restore(): pl.pallas_call(functools.partial(restore_kernel, plan, inside, [len(part)...  14 us
    ppermute x2, waiting for transfers between devices, local(): high = lax.ppermute(centre[:depth], 'cam', backward)  10.4 us
    ppermute x2, starting transfers between devices, local(): low = lax.ppermute(centre[-depth:], 'cam', forward)  8.42 us
    ppermute x2, starting transfers between devices, local(): high = lax.ppermute(centre[:depth], 'cam', backward)  8.37 us
    ppermute x2, waiting for transfers between devices, local(): low = lax.ppermute(centre[-depth:], 'cam', forward)  3.35 us
  transfers between devices with their start and end apart: 6, of which 4 were waited for; matrix products, arithmetic and copies ran while one was open for 1% of the time, Pallas kernels for 18%

profile of v3, /device:TPU:14, one launch (start us, length us, event | category | flops | bytes accessed | tf_op | source)
XLA Modules:
  0.0 115.6 jit_solution(17157835813932211377)
XLA Ops:
  0.0 7.7 %frame_side.3 = bf16[32,16,768]{2,1,0:T(8,128)(2,1)} custom-call(s32[1,2]{1,0:T(1,128)} %order_ref.3, s32[64]{0:T(128)} %offset_ref.3, f32[64]{0:T(128)} %fraction_ref.3, bf16[2,256,2048]{2,1,0:T(8,128)(2,1)} %raw_next.3, bf16[2,256,2048]{2,1,0:T(8,128)(2,1)} %raw_next.3, bf16[2,256,2048]{2,1,0:T(8,128)(2,1)} %raw_next.3, bf16[256,2048]{1,0:T(8,128)(2,1)} %dark_next.3, ...), custom_call_target="tpu_custom_call" | custom-call | flops 8000000000 | bytes 6500000 | tf_op jit(solution)/shard_map/frame_side/pallas_call | solution.py:126
  7.7 10.1 %all-to-all-start.1 = ((bf16[32,16,768]{2,1,0:T(8,128)(2,1)}), bf16[32,16,768]{2,1,0:T(8,128)(2,1)S(1)}, u32[]{:S(2)}, u32[]{:S(2)}) async-start(bf16[32,16,768]{2,1,0:T(8,128)(2,1)} %frame_side.3), calls=%async_computation.1 | async-start | bytes 1572864 | tf_op jit(solution)/shard_map/all_to_all | solution.py:462
  17.8 8.1 %frame_side.2 = bf16[32,16,1280]{2,1,0:T(8,128)(2,1)} custom-call(s32[1,2]{1,0:T(1,128)} %order_ref.3, s32[64]{0:T(128)} %offset_ref.3, f32[64]{0:T(128)} %fraction_ref.3, bf16[2,256,2048]{2,1,0:T(8,128)(2,1)} %raw_next.3, bf16[2,256,2048]{2,1,0:T(8,128)(2,1)} %raw_next.3, bf16[2,256,2048]{2,1,0:T(8,128)(2,1)} %raw_next.3, bf16[256,2048]{1,0:T(8,128)(2,1)} %dark_next.3, ...), custom_call_target="tpu_custom_call" | custom-call | flops 8000000000 | bytes 6500000 | tf_op jit(solution)/shard_map/frame_side/pallas_call | solution.py:126
  25.9 0.0 copy-start
  25.9 0.0 copy-start.1
  25.9 15.2 %all-to-all-done.1.refs_1_.refs_4_ = bf16[32,16,768]{2,1,0:T(8,128)(2,1)S(1)} async-done(((bf16[32,16,768]{2,1,0:T(8,128)(2,1)}), bf16[32,16,768]{2,1,0:T(8,128)(2,1)S(1)}, u32[]{:S(2)}, u32[]{:S(2)}) %all-to-all-start.1) | async-done | bytes 786464 | tf_op jit(solution)/shard_map/all_to_all | solution.py:462
  41.1 4.0 %all-to-all-start = ((bf16[32,16,1280]{2,1,0:T(8,128)(2,1)}), bf16[32,16,1280]{2,1,0:T(8,128)(2,1)S(1)}, u32[]{:S(2)}, u32[]{:S(2)}) async-start(bf16[32,16,1280]{2,1,0:T(8,128)(2,1)} %frame_side.2), calls=%async_computation | async-start | bytes 2621440 | tf_op jit(solution)/shard_map/all_to_all | solution.py:462
  45.1 0.0 copy-done.12
  45.2 0.1 pad_dynamic-slice_fusion
  45.2 0.1 broadcast_in_dim.2
  45.3 0.1 reshape.4.index_ref
  45.5 3.0 %bands.1 = (bf16[5,160,256]{2,1,0:T(8,128)(2,1)S(1)}, bf16[3,160,256]{2,1,0:T(8,128)(2,1)S(1)}, bf16[8,160,256]{2,1,0:T(8,128)(2,1)S(1)}, bf16[8,160,256]{2,1,0:...) custom-call(f32[8,13]{1,0:T(8,128)S(1)} %copy-done, f32[9]{0:T(128)S(1)} %copy-done.1, ...), custom_call_target="tpu_custom_call" | custom-call | flops 2000000000 | bytes 2000000 | tf_op jit(solution)/shard_map/bands/pallas_call | solution.py:233
  48.5 0.7 copy-done.6
  49.2 0.7 copy-done.8
  49.9 0.7 copy-done.10
  50.6 0.9 fusion.1
  51.6 4.2 %collective-permute-start.2 = (bf16[12,16,768]{2,1,0:T(8,128)(2,1)}, bf16[12,16,768]{2,1,0:T(8,128)(2,1)S(1)}, u32[]{:S(2)}, u32[]{:S(2)}) collective-permute-start(bf16[12,16,768]{2,1,0:T(8,128)(2,1)} %get-tuple-element.32), channel_id=1, source_target_pairs={{0,32},{32,64},{64,96},{96,128},{128,160},{160,192},{192,224},{1,3... | collective-permute-start | bytes 884744 | tf_op jit(solution)/shard_map/ppermute | solution.py:463
  55.8 0.0 copy-done.2
  55.8 0.0 copy-done.4
  55.8 4.0 %collective-permute-start.3 = (bf16[12,16,768]{2,1,0:T(8,128)(2,1)}, bf16[12,16,768]{2,1,0:T(8,128)(2,1)S(1)}, u32[]{:S(2)}, u32[]{:S(2)}) collective-permute-start(bf16[12,16,768]{2,1,0:T(8,128)(2,1)} %get-tuple-element.31), channel_id=1, source_target_pairs={{32,0},{64,32},{96,64},{128,96},{160,128},{192,160},{224,192},{33,... | collective-permute-start | bytes 884744 | tf_op jit(solution)/shard_map/ppermute | solution.py:464
  59.8 19.2 %all-to-all-done.refs_0_.refs_1_ = bf16[32,16,1280]{2,1,0:T(8,128)(2,1)S(1)} async-done(((bf16[32,16,1280]{2,1,0:T(8,128)(2,1)}), bf16[32,16,1280]{2,1,0:T(8,128)(2,1)S(1)}, u32[]{:S(2)}, u32[]{:S(2)}) %all-to-all-start) | async-done | bytes 1310752 | tf_op jit(solution)/shard_map/all_to_all | solution.py:462
  79.0 0.1 fusion
  79.1 4.2 %collective-permute-start = (bf16[12,16,1280]{2,1,0:T(8,128)(2,1)S(1)}, bf16[12,16,1280]{2,1,0:T(8,128)(2,1)S(1)}, u32[]{:S(2)}, u32[]{:S(2)}) collective-permute-start(bf16[12,16,1280]{2,1,0:T(8,128)(2,1)S(1)} %get-tuple-element.30), channel_id=1, source_target_pairs={{0,32},{32,64},{64,96},{96,128},{128,160},{160,192},{192,224},{1,3... | collective-permute-start | bytes 1474568 | tf_op jit(solution)/shard_map/ppermute | solution.py:463
  83.3 4.3 %collective-permute-start.1 = (bf16[12,16,1280]{2,1,0:T(8,128)(2,1)S(1)}, bf16[12,16,1280]{2,1,0:T(8,128)(2,1)S(1)}, u32[]{:S(2)}, u32[]{:S(2)}) collective-permute-start(bf16[12,16,1280]{2,1,0:T(8,128)(2,1)S(1)} %get-tuple-element.29), channel_id=1, source_target_pairs={{32,0},{64,32},{96,64},{128,96},{160,128},{192,160},{224,192},{33,... | collective-permute-start | bytes 1474568 | tf_op jit(solution)/shard_map/ppermute | solution.py:464
  87.7 3.2 %inside.3 = (bf16[16,8,1280]{2,1,0:T(8,128)(2,1)S(1)}, bf16[416,1280]{1,0:T(8,128)(2,1)S(1)}, f32[192,1280]{1,0:T(8,128)S(1)}) custom-call(bf16[32,16,1280]{2,1,0:T(8,128)(2,1)S(1)} %all-to-all-done.refs_0_.refs_1_, bf16[5,160,256]{2,1,0:T(8,128)(2,1)S(1)} %copy-done.5, bf16[3,160,256]{2,1,0:T(8,128)(2,1)S(1)} %copy-done.11, bf16[512,256]{1,0:T(8,128)(2,1)S(1)} %copy-done.7, ...), custom_call_target="tpu_custom_call" | custom-call | flops 5000000000 | bytes 8000000 | tf_op jit(solution)/shard_map/inside/pallas_call | solution.py:408
  90.9 2.5 %inside.2 = (bf16[16,8,1024]{2,1,0:T(8,128)(2,1)S(1)}, bf16[416,1024]{1,0:T(8,128)(2,1)S(1)}, f32[192,1024]{1,0:T(8,128)S(1)}) custom-call(bf16[32,16,1280]{2,1,0:T(8,128)(2,1)S(1)} %all-to-all-done.refs_0_.refs_1_, bf16[32,16,768]{2,1,0:T(8,128)(2,1)S(1)} %all-to-all-done.1.refs_1_.refs_4_, bf16[5,160,256]{2,1,0:T(8,128)(2,1)S(1)} %copy-done.5, ...), custom_call_target="tpu_custom_call" | custom-call | flops 5000000000 | bytes 8000000 | tf_op jit(solution)/shard_map/inside/pallas_call | solution.py:408
  93.5 3.3 %collective-permute-done.refs_0_ = bf16[12,16,1280]{2,1,0:T(8,128)(2,1)S(1)} collective-permute-done((bf16[12,16,1280]{2,1,0:T(8,128)(2,1)S(1)}, bf16[12,16,1280]{2,1,0:T(8,128)(2,1)S(1)}, u32[]{:S(2)}, u32[]{:S(2)}) %collective-permute-start) | collective-permute-done | bytes 491552 | tf_op jit(solution)/shard_map/ppermute | solution.py:463
  96.8 10.4 %collective-permute-done.1.refs_2_ = bf16[12,16,1280]{2,1,0:T(8,128)(2,1)S(1)} collective-permute-done((bf16[12,16,1280]{2,1,0:T(8,128)(2,1)S(1)}, bf16[12,16,1280]{2,1,0:T(8,128)(2,1)S(1)}, u32[]{:S(2)}, u32[]{:S(2)}) %collective-permute-start.1) | collective-permute-done | bytes 491552 | tf_op jit(solution)/shard_map/ppermute | solution.py:464
  107.3 3.8 %ends.2.refs_13_ = bf16[64,8,1152]{2,1,0:T(8,128)(2,1)S(1)} custom-call(bf16[12,16,1280]{2,1,0:T(8,128)(2,1)S(1)} %collective-permute-done.refs_0_, bf16[32,16,1280]{2,1,0:T(8,128)(2,1)S(1)} %all-to-all-done.refs_0_.refs_1_, bf16[12,16,1280]{2,1,0:T(8,128)(2,1)S(1)} %collective-permute-done.1.refs_2_, ...), custom_call_target="tpu_custom_call" | custom-call | flops 5000000000 | bytes 8000000 | tf_op jit(solution)/shard_map/ends/pallas_call | solution.py:408
  111.1 0.0 collective-permute-done.2.refs_3_
  111.1 0.0 collective-permute-done.3.refs_5_
  111.1 4.5 %ends.3 = bf16[64,8,2048]{2,1,0:T(8,128)(2,1)} custom-call(bf16[12,16,1280]{2,1,0:T(8,128)(2,1)S(1)} %collective-permute-done.refs_0_, bf16[32,16,1280]{2,1,0:T(8,128)(2,1)S(1)} %all-to-all-done.refs_0_.refs_1_, bf16[12,16,1280]{2,1,0:T(8,128)(2,1)S(1)} %collective-permute-done.1.refs_2_, bf16[12,16,768]{2,1,0:T(8,128)(2,1)S(1)} %collective-permute-done.2.refs_3_, ...), custom_call_target="tpu_custom_call" | custom-call | flops 5000000000 | bytes 8000000 | tf_op jit(solution)/shard_map/ends/pallas_call | solution.py:408
  (18 shorter events, 0.0 us)
Async XLA Ops:
  7.7 33.4 %all-to-all-start.1 = ((bf16[32,16,768]{2,1,0:T(8,128)(2,1)}), bf16[32,16,768]{2,1,0:T(8,128)(2,1)S(1)}, u32[]{:S(2)}, u32[]{:S(2)}) async-start(bf16[32,16,768]{2,1,0:T(8,128)(2,1)} %frame_side.3), calls=%async_computation.1 | async-start | bytes 1572864 | tf_op jit(solution)/shard_map/all_to_all | solution.py:462
  25.9 19.3 %copy-start.12 = (s32[512]{0:T(512)S(1)}, s32[512]{0:T(512)}, u32[]{:S(2)}) copy-start(s32[512]{0:T(512)} %param.17) | copy-start | bytes 6148
  25.9 19.6 %copy-start = (f32[8,13]{1,0:T(8,128)S(1)}, f32[8,13]{1,0:T(8,128)}, u32[]{:S(2)}) copy-start(f32[8,13]{1,0:T(8,128)} %psf_ref.1) | copy-start | bytes 1252
  25.9 19.6 %copy-start.1 = (f32[9]{0:T(128)S(1)}, f32[9]{0:T(128)}, u32[]{:S(2)}) copy-start(f32[9]{0:T(128)} %lateral_ref.1) | copy-start | bytes 112
  41.1 37.9 %all-to-all-start = ((bf16[32,16,1280]{2,1,0:T(8,128)(2,1)}), bf16[32,16,1280]{2,1,0:T(8,128)(2,1)S(1)}, u32[]{:S(2)}, u32[]{:S(2)}) async-start(bf16[32,16,1280]{2,1,0:T(8,128)(2,1)} %frame_side.2), calls=%async_computation | async-start | bytes 2621440 | tf_op jit(solution)/shard_map/all_to_all | solution.py:462
  48.5 0.7 copy-start.6
  49.2 0.7 copy-start.8
  49.9 0.7 copy-start.10
  50.6 5.1 %copy-start.2 = (bf16[8,160,256]{2,1,0:T(8,128)(2,1)}, bf16[8,160,256]{2,1,0:T(8,128)(2,1)S(1)}, u32[]{:S(2)}) copy-start(bf16[8,160,256]{2,1,0:T(8,128)(2,1)S(1)} %get-tuple-element.18.refs_4_.refs_7_) | copy-start | bytes 1966084
  50.6 5.2 %copy-start.4 = (bf16[5,160,256]{2,1,0:T(8,128)(2,1)}, bf16[5,160,256]{2,1,0:T(8,128)(2,1)S(1)}, u32[]{:S(2)}) copy-start(bf16[5,160,256]{2,1,0:T(8,128)(2,1)S(1)} %get-tuple-element.21.refs_2_.refs_1_) | copy-start | bytes 1228804
  51.6 59.5 %collective-permute-start.2 = (bf16[12,16,768]{2,1,0:T(8,128)(2,1)}, bf16[12,16,768]{2,1,0:T(8,128)(2,1)S(1)}, u32[]{:S(2)}, u32[]{:S(2)}) collective-permute-start(bf16[12,16,768]{2,1,0:T(8,128)(2,1)} %get-tuple-element.32), channel_id=1, source_target_pairs={{0,32},{32,64},{64,96},{96,128},{128,160},{160,192},{192,224},{1,3... | collective-permute-start | bytes 884744 | tf_op jit(solution)/shard_map/ppermute | solution.py:463
  55.8 55.3 %collective-permute-start.3 = (bf16[12,16,768]{2,1,0:T(8,128)(2,1)}, bf16[12,16,768]{2,1,0:T(8,128)(2,1)S(1)}, u32[]{:S(2)}, u32[]{:S(2)}) collective-permute-start(bf16[12,16,768]{2,1,0:T(8,128)(2,1)} %get-tuple-element.31), channel_id=1, source_target_pairs={{32,0},{64,32},{96,64},{128,96},{160,128},{192,160},{224,192},{33,... | collective-permute-start | bytes 884744 | tf_op jit(solution)/shard_map/ppermute | solution.py:464
  79.0 8.7 %copy-start.5 = (bf16[5,160,256]{2,1,0:T(8,128)(2,1)S(1)}, bf16[5,160,256]{2,1,0:T(8,128)(2,1)}, u32[]{:S(2)}) copy-start(bf16[5,160,256]{2,1,0:T(8,128)(2,1)} %copy-done.4) | copy-start | bytes 1228804
  79.0 8.7 %copy-start.7 = (bf16[512,256]{1,0:T(8,128)(2,1)S(1)}, bf16[512,256]{1,0:T(8,128)(2,1)}, u32[]{:S(2)}) copy-start(bf16[512,256]{1,0:T(8,128)(2,1)} %copy-done.6) | copy-start | bytes 786436
  79.0 8.7 %copy-start.9 = (bf16[512,256]{1,0:T(8,128)(2,1)S(1)}, bf16[512,256]{1,0:T(8,128)(2,1)}, u32[]{:S(2)}) copy-start(bf16[512,256]{1,0:T(8,128)(2,1)} %copy-done.8) | copy-start | bytes 786436
  79.0 8.7 %copy-start.11 = (bf16[3,160,256]{2,1,0:T(8,128)(2,1)S(1)}, bf16[3,160,256]{2,1,0:T(8,128)(2,1)}, u32[]{:S(2)}) copy-start(bf16[3,160,256]{2,1,0:T(8,128)(2,1)} %copy-done.10) | copy-start | bytes 737284
  79.1 17.7 %collective-permute-start = (bf16[12,16,1280]{2,1,0:T(8,128)(2,1)S(1)}, bf16[12,16,1280]{2,1,0:T(8,128)(2,1)S(1)}, u32[]{:S(2)}, u32[]{:S(2)}) collective-permute-start(bf16[12,16,1280]{2,1,0:T(8,128)(2,1)S(1)} %get-tuple-element.30), channel_id=1, source_target_pairs={{0,32},{32,64},{64,96},{96,128},{128,160},{160,192},{192,224},{1,3... | collective-permute-start | bytes 1474568 | tf_op jit(solution)/shard_map/ppermute | solution.py:463
  83.3 23.9 %collective-permute-start.1 = (bf16[12,16,1280]{2,1,0:T(8,128)(2,1)S(1)}, bf16[12,16,1280]{2,1,0:T(8,128)(2,1)S(1)}, u32[]{:S(2)}, u32[]{:S(2)}) collective-permute-start(bf16[12,16,1280]{2,1,0:T(8,128)(2,1)S(1)} %get-tuple-element.29), channel_id=1, source_target_pairs={{32,0},{64,32},{96,64},{128,96},{160,128},{192,160},{224,192},{33,... | collective-permute-start | bytes 1474568 | tf_op jit(solution)/shard_map/ppermute | solution.py:464
  90.9 16.3 %copy-start.3 = (bf16[8,160,256]{2,1,0:T(8,128)(2,1)S(1)}, bf16[8,160,256]{2,1,0:T(8,128)(2,1)}, u32[]{:S(2)}) copy-start(bf16[8,160,256]{2,1,0:T(8,128)(2,1)} %copy-done.2) | copy-start | bytes 1966084

commit v4 on v3

--- a/solution.py
+++ b/solution.py
@@ -451,14 +451,21 @@
     inner_matrices = (*axial[:2], forward_lateral, backward_lateral)
     outer_matrices = (*axial[2:], forward_lateral, backward_lateral)
     depth = halo // 2
+    first_piece = frame_side(
+        raw_frames, frame_order, dark_frame, flat_gain, stripe_band, shear_offset, shear_fraction, 0, SPLIT
+    )
+    first_piece, later_order = lax.optimization_barrier((first_piece, frame_order))
+    second_piece = frame_side(
+        raw_frames, later_order, dark_frame, flat_gain, stripe_band, shear_offset, shear_fraction,
+        SPLIT, columns,
+    )
+    second_piece, inner_matrices, outer_matrices = lax.optimization_barrier(
+        (second_piece, inner_matrices, outer_matrices)
+    )
     result = None
     parts = []
     centres = []
-    for lo, hi in ((0, SPLIT), (SPLIT, columns)):
-        piece = frame_side(
-            raw_frames, frame_order, dark_frame, flat_gain, stripe_band, shear_offset,
-            shear_fraction, lo, hi,
-        )
+    for piece in (first_piece, second_piece):
         centre = lax.all_to_all(piece, "brick", split_axis=0, concat_axis=0, tiled=True)
         low = lax.ppermute(centre[-depth:], "cam", forward)
         high = lax.ppermute(centre[:depth], "cam", backward)

time: 116 us -> 132 us (1.14)
  blocking collectives: 0 us -> 33.2 us
  starting transfers between devices: 30.9 us -> 20.8 us
  waiting for transfers between devices: 48.2 us -> 38.5 us
  local copies, waits for them, and re-layouts: 3.44 us -> 5.66 us
    all_to_all x0 -> x1, blocking collectives: none -> 33.2 us  [local(): lax.all_to_all(piece, 'brick', split_axis=0, concat_axis=0, tiled=True)]
    all_to_all x2 -> x1, starting transfers between devices: 14.1 us -> 4.01 us  [local(): lax.all_to_all(piece, 'brick', split_axis=0, concat_axis=0, tiled=True)]
    all_to_all x2 -> x1, waiting for transfers between devices: 34.4 us -> 24.8 us  [local(): lax.all_to_all(piece, 'brick', split_axis=0, concat_axis=0, tiled=True)]
    unnamed x26, local copies, waits for them, and re-layouts: 2.16 us -> 3.77 us
  transfers between devices with their start and end apart: 6 -> 5, of which waited for: 4 -> 3; matrix products, arithmetic and copies ran while one was open for 1% -> 1% of each run, Pallas kernels for 18% -> 7%
where the time goes in v4:
time: 132 us; the launch traced here: 131 us
  waiting for transfers between devices  38.5 us (29%)
  blocking collectives  33.2 us (25%)
  Pallas kernels  32.8 us (25%)
  starting transfers between devices  20.8 us (16%)
  local copies, waits for them, and re-layouts  5.66 us (4%)
    all_to_all x1, blocking collectives, local(): lax.all_to_all(piece, 'brick', split_axis=0, concat_axis=0, tiled=True)  33.2 us
    all_to_all x1, waiting for transfers between devices, local(): lax.all_to_all(piece, 'brick', split_axis=0, concat_axis=0, tiled=True)  24.8 us
    pallas_call x2, Pallas kernels, frame_side(): pl.pallas_call(functools.partial(frame_kernel, first, count), grid=(steps...  15.8 us
    pallas_call x4, Pallas kernels, restore(): pl.pallas_call(functools.partial(restore_kernel, plan, inside, [len(part)...  14 us
    ppermute x2, waiting for transfers between devices, local(): high = lax.ppermute(centre[:depth], 'cam', backward)  10.4 us
    ppermute x2, starting transfers between devices, local(): low = lax.ppermute(centre[-depth:], 'cam', forward)  9.29 us
    ppermute x2, starting transfers between devices, local(): high = lax.ppermute(centre[:depth], 'cam', backward)  7.5 us
    all_to_all x1, starting transfers between devices, local(): lax.all_to_all(piece, 'brick', split_axis=0, concat_axis=0, tiled=True)  4.01 us
  transfers between devices with their start and end apart: 5, of which 3 were waited for; matrix products, arithmetic and copies ran while one was open for 1% of the time, Pallas kernels for 7%

profile of v4, /device:TPU:14, one launch (start us, length us, event | category | flops | bytes accessed | tf_op | source)
XLA Modules:
  0.0 131.2 jit_solution(11765192702947039549)
XLA Ops:
  0.0 0.8 pad_dynamic-slice_fusion
  0.8 0.1 broadcast_in_dim.2
  0.8 0.1 reshape.4.index_ref
  1.0 8.1 %frame_side.2 = bf16[32,16,1280]{2,1,0:T(8,128)(2,1)} custom-call(s32[1,2]{1,0:T(1,128)} %order_ref.2, s32[64]{0:T(128)} %offset_ref.3, f32[64]{0:T(128)} %fraction_ref.3, bf16[2,256,2048]{2,1,0:T(8,128)(2,1)} %raw_next.3, bf16[2,256,2048]{2,1,0:T(8,128)(2,1)} %raw_next.3, bf16[2,256,2048]{2,1,0:T(8,128)(2,1)} %raw_next.3, bf16[256,2048]{1,0:T(8,128)(2,1)} %dark_next.3, ...), custom_call_target="tpu_custom_call" | custom-call | flops 8000000000 | bytes 6500000 | tf_op jit(solution)/shard_map/frame_side/pallas_call | solution.py:126
  9.0 0.0 copy-start.1
  9.0 7.7 %frame_side.3 = bf16[32,16,768]{2,1,0:T(8,128)(2,1)} custom-call(s32[1,2]{1,0:T(1,128)} %order_ref.2, s32[64]{0:T(128)} %offset_ref.3, f32[64]{0:T(128)} %fraction_ref.3, bf16[2,256,2048]{2,1,0:T(8,128)(2,1)} %raw_next.3, bf16[2,256,2048]{2,1,0:T(8,128)(2,1)} %raw_next.3, bf16[2,256,2048]{2,1,0:T(8,128)(2,1)} %raw_next.3, bf16[256,2048]{1,0:T(8,128)(2,1)} %dark_next.3, ...), custom_call_target="tpu_custom_call" | custom-call | flops 8000000000 | bytes 6500000 | tf_op jit(solution)/shard_map/frame_side/pallas_call | solution.py:126
  16.8 0.0 copy-done
  16.8 0.0 copy-done.1
  16.8 3.0 %bands.1 = (bf16[5,160,256]{2,1,0:T(8,128)(2,1)S(1)}, bf16[3,160,256]{2,1,0:T(8,128)(2,1)S(1)}, bf16[8,160,256]{2,1,0:T(8,128)(2,1)S(1)}, bf16[8,160,256]{2,1,0:...) custom-call(f32[8,13]{1,0:T(8,128)S(1)} %copy-done, f32[9]{0:T(128)S(1)} %copy-done.1, ...), custom_call_target="tpu_custom_call" | custom-call | flops 2000000000 | bytes 2000000 | tf_op jit(solution)/shard_map/bands/pallas_call | solution.py:233
  19.8 0.9 copy-done.2
  20.7 0.8 copy-done.4
  21.5 0.7 copy-done.6
  22.2 0.7 copy-done.8
  22.9 0.7 copy-done.10
  23.6 0.0 copy-done.12
  23.6 33.2 %all_to_all.10.refs_1_.refs_4_ = bf16[32,16,768]{2,1,0:T(8,128)(2,1)S(1)} all-to-all(bf16[32,16,768]{2,1,0:T(8,128)(2,1)S(1)} %copy-done.12), channel_id=1, replica_groups=mesh['cam'=8,'brick'=32] {'brick'}, dimensions={0} | all-to-all | bytes 1572864 | tf_op jit(solution)/shard_map/all_to_all | solution.py:469
  56.8 4.0 %all-to-all-start = ((bf16[32,16,1280]{2,1,0:T(8,128)(2,1)}), bf16[32,16,1280]{2,1,0:T(8,128)(2,1)S(1)}, u32[]{:S(2)}, u32[]{:S(2)}) async-start(bf16[32,16,1280]{2,1,0:T(8,128)(2,1)} %frame_side.2), calls=%async_computation | async-start | bytes 2621440 | tf_op jit(solution)/shard_map/all_to_all | solution.py:469
  60.8 0.9 fusion.1
  61.7 4.2 %collective-permute-start.2 = (bf16[12,16,768]{2,1,0:T(8,128)(2,1)}, bf16[12,16,768]{2,1,0:T(8,128)(2,1)S(1)}, u32[]{:S(2)}, u32[]{:S(2)}) collective-permute-start(bf16[12,16,768]{2,1,0:T(8,128)(2,1)} %get-tuple-element.54), channel_id=1, source_target_pairs={{0,32},{32,64},{64,96},{96,128},{128,160},{160,192},{192,224},{1,3... | collective-permute-start | bytes 884744 | tf_op jit(solution)/shard_map/ppermute | solution.py:470
  65.9 4.0 %collective-permute-start.3 = (bf16[12,16,768]{2,1,0:T(8,128)(2,1)}, bf16[12,16,768]{2,1,0:T(8,128)(2,1)S(1)}, u32[]{:S(2)}, u32[]{:S(2)}) collective-permute-start(bf16[12,16,768]{2,1,0:T(8,128)(2,1)} %get-tuple-element.53), channel_id=1, source_target_pairs={{32,0},{64,32},{96,64},{128,96},{160,128},{192,160},{224,192},{33,... | collective-permute-start | bytes 884744 | tf_op jit(solution)/shard_map/ppermute | solution.py:471
  69.9 24.8 %all-to-all-done.refs_0_.refs_1_ = bf16[32,16,1280]{2,1,0:T(8,128)(2,1)S(1)} async-done(((bf16[32,16,1280]{2,1,0:T(8,128)(2,1)}), bf16[32,16,1280]{2,1,0:T(8,128)(2,1)S(1)}, u32[]{:S(2)}, u32[]{:S(2)}) %all-to-all-start) | async-done | bytes 1310752 | tf_op jit(solution)/shard_map/all_to_all | solution.py:469
  94.7 0.1 fusion
  94.8 5.1 %collective-permute-start = (bf16[12,16,1280]{2,1,0:T(8,128)(2,1)S(1)}, bf16[12,16,1280]{2,1,0:T(8,128)(2,1)S(1)}, u32[]{:S(2)}, u32[]{:S(2)}) collective-permute-start(bf16[12,16,1280]{2,1,0:T(8,128)(2,1)S(1)} %get-tuple-element.52), channel_id=1, source_target_pairs={{0,32},{32,64},{64,96},{96,128},{128,160},{160,192},{192,224},{1,3... | collective-permute-start | bytes 1474568 | tf_op jit(solution)/shard_map/ppermute | solution.py:470
  99.9 3.5 %collective-permute-start.1 = (bf16[12,16,1280]{2,1,0:T(8,128)(2,1)S(1)}, bf16[12,16,1280]{2,1,0:T(8,128)(2,1)S(1)}, u32[]{:S(2)}, u32[]{:S(2)}) collective-permute-start(bf16[12,16,1280]{2,1,0:T(8,128)(2,1)S(1)} %get-tuple-element.51), channel_id=1, source_target_pairs={{32,0},{64,32},{96,64},{128,96},{160,128},{192,160},{224,192},{33,... | collective-permute-start | bytes 1474568 | tf_op jit(solution)/shard_map/ppermute | solution.py:471
  103.4 3.2 %inside.3 = (bf16[16,8,1280]{2,1,0:T(8,128)(2,1)S(1)}, bf16[416,1280]{1,0:T(8,128)(2,1)S(1)}, f32[192,1280]{1,0:T(8,128)S(1)}) custom-call(bf16[32,16,1280]{2,1,0:T(8,128)(2,1)S(1)} %all-to-all-done.refs_0_.refs_1_, bf16[5,160,256]{2,1,0:T(8,128)(2,1)S(1)} %copy-done.5, bf16[3,160,256]{2,1,0:T(8,128)(2,1)S(1)} %copy-done.11, bf16[512,256]{1,0:T(8,128)(2,1)S(1)} %copy-done.7, ...), custom_call_target="tpu_custom_call" | custom-call | flops 5000000000 | bytes 8000000 | tf_op jit(solution)/shard_map/inside/pallas_call | solution.py:408
  106.6 2.5 %inside.2 = (bf16[16,8,1024]{2,1,0:T(8,128)(2,1)S(1)}, bf16[416,1024]{1,0:T(8,128)(2,1)S(1)}, f32[192,1024]{1,0:T(8,128)S(1)}) custom-call(bf16[32,16,1280]{2,1,0:T(8,128)(2,1)S(1)} %all-to-all-done.refs_0_.refs_1_, bf16[32,16,768]{2,1,0:T(8,128)(2,1)S(1)} %all_to_all.10.refs_1_.refs_4_, bf16[5,160,256]{2,1,0:T(8,128)(2,1)S(1)} %copy-done.5, ...), custom_call_target="tpu_custom_call" | custom-call | flops 5000000000 | bytes 8000000 | tf_op jit(solution)/shard_map/inside/pallas_call | solution.py:408
  109.1 3.3 %collective-permute-done.refs_0_ = bf16[12,16,1280]{2,1,0:T(8,128)(2,1)S(1)} collective-permute-done((bf16[12,16,1280]{2,1,0:T(8,128)(2,1)S(1)}, bf16[12,16,1280]{2,1,0:T(8,128)(2,1)S(1)}, u32[]{:S(2)}, u32[]{:S(2)}) %collective-permute-start) | collective-permute-done | bytes 491552 | tf_op jit(solution)/shard_map/ppermute | solution.py:470
  112.5 10.4 %collective-permute-done.1.refs_2_ = bf16[12,16,1280]{2,1,0:T(8,128)(2,1)S(1)} collective-permute-done((bf16[12,16,1280]{2,1,0:T(8,128)(2,1)S(1)}, bf16[12,16,1280]{2,1,0:T(8,128)(2,1)S(1)}, u32[]{:S(2)}, u32[]{:S(2)}) %collective-permute-start.1) | collective-permute-done | bytes 491552 | tf_op jit(solution)/shard_map/ppermute | solution.py:471
  122.9 3.8 %ends.2.refs_13_ = bf16[64,8,1152]{2,1,0:T(8,128)(2,1)S(1)} custom-call(bf16[12,16,1280]{2,1,0:T(8,128)(2,1)S(1)} %collective-permute-done.refs_0_, bf16[32,16,1280]{2,1,0:T(8,128)(2,1)S(1)} %all-to-all-done.refs_0_.refs_1_, bf16[12,16,1280]{2,1,0:T(8,128)(2,1)S(1)} %collective-permute-done.1.refs_2_, ...), custom_call_target="tpu_custom_call" | custom-call | flops 5000000000 | bytes 8000000 | tf_op jit(solution)/shard_map/ends/pallas_call | solution.py:408
  126.7 0.0 collective-permute-done.2.refs_3_
  126.8 0.0 collective-permute-done.3.refs_5_
  126.8 4.5 %ends.3 = bf16[64,8,2048]{2,1,0:T(8,128)(2,1)} custom-call(bf16[12,16,1280]{2,1,0:T(8,128)(2,1)S(1)} %collective-permute-done.refs_0_, bf16[32,16,1280]{2,1,0:T(8,128)(2,1)S(1)} %all-to-all-done.refs_0_.refs_1_, bf16[12,16,1280]{2,1,0:T(8,128)(2,1)S(1)} %collective-permute-done.1.refs_2_, bf16[12,16,768]{2,1,0:T(8,128)(2,1)S(1)} %collective-permute-done.2.refs_3_, ...), custom_call_target="tpu_custom_call" | custom-call | flops 5000000000 | bytes 8000000 | tf_op jit(solution)/shard_map/ends/pallas_call | solution.py:408
  (17 shorter events, 0.0 us)
Async XLA Ops:
  9.0 7.7 %copy-start = (f32[8,13]{1,0:T(8,128)S(1)}, f32[8,13]{1,0:T(8,128)}, u32[]{:S(2)}) copy-start(f32[8,13]{1,0:T(8,128)} %psf_ref.1) | copy-start | bytes 1252
  9.0 7.7 %copy-start.1 = (f32[9]{0:T(128)S(1)}, f32[9]{0:T(128)}, u32[]{:S(2)}) copy-start(f32[9]{0:T(128)} %lateral_ref.1) | copy-start | bytes 112
  16.8 6.8 %copy-start.12 = (bf16[32,16,768]{2,1,0:T(8,128)(2,1)S(1)}, bf16[32,16,768]{2,1,0:T(8,128)(2,1)}, u32[]{:S(2)}) copy-start(bf16[32,16,768]{2,1,0:T(8,128)(2,1)} %frame_side.3) | copy-start | bytes 2359300
  19.8 0.9 copy-start.2
  20.7 0.8 copy-start.4
  21.5 0.7 copy-start.6
  22.2 0.7 copy-start.8
  22.9 0.7 copy-start.10
  56.8 37.9 %all-to-all-start = ((bf16[32,16,1280]{2,1,0:T(8,128)(2,1)}), bf16[32,16,1280]{2,1,0:T(8,128)(2,1)S(1)}, u32[]{:S(2)}, u32[]{:S(2)}) async-start(bf16[32,16,1280]{2,1,0:T(8,128)(2,1)} %frame_side.2), calls=%async_computation | async-start | bytes 2621440 | tf_op jit(solution)/shard_map/all_to_all | solution.py:469
  61.7 65.1 %collective-permute-start.2 = (bf16[12,16,768]{2,1,0:T(8,128)(2,1)}, bf16[12,16,768]{2,1,0:T(8,128)(2,1)S(1)}, u32[]{:S(2)}, u32[]{:S(2)}) collective-permute-start(bf16[12,16,768]{2,1,0:T(8,128)(2,1)} %get-tuple-element.54), channel_id=1, source_target_pairs={{0,32},{32,64},{64,96},{96,128},{128,160},{160,192},{192,224},{1,3... | collective-permute-start | bytes 884744 | tf_op jit(solution)/shard_map/ppermute | solution.py:470
  65.9 60.9 %collective-permute-start.3 = (bf16[12,16,768]{2,1,0:T(8,128)(2,1)}, bf16[12,16,768]{2,1,0:T(8,128)(2,1)S(1)}, u32[]{:S(2)}, u32[]{:S(2)}) collective-permute-start(bf16[12,16,768]{2,1,0:T(8,128)(2,1)} %get-tuple-element.53), channel_id=1, source_target_pairs={{32,0},{64,32},{96,64},{128,96},{160,128},{192,160},{224,192},{33,... | collective-permute-start | bytes 884744 | tf_op jit(solution)/shard_map/ppermute | solution.py:471
  94.7 8.7 %copy-start.5 = (bf16[5,160,256]{2,1,0:T(8,128)(2,1)S(1)}, bf16[5,160,256]{2,1,0:T(8,128)(2,1)}, u32[]{:S(2)}) copy-start(bf16[5,160,256]{2,1,0:T(8,128)(2,1)} %copy-done.4) | copy-start | bytes 1228804
  94.7 8.7 %copy-start.7 = (bf16[512,256]{1,0:T(8,128)(2,1)S(1)}, bf16[512,256]{1,0:T(8,128)(2,1)}, u32[]{:S(2)}) copy-start(bf16[512,256]{1,0:T(8,128)(2,1)} %copy-done.6) | copy-start | bytes 786436
  94.7 8.7 %copy-start.9 = (bf16[512,256]{1,0:T(8,128)(2,1)S(1)}, bf16[512,256]{1,0:T(8,128)(2,1)}, u32[]{:S(2)}) copy-start(bf16[512,256]{1,0:T(8,128)(2,1)} %copy-done.8) | copy-start | bytes 786436
  94.7 8.7 %copy-start.11 = (bf16[3,160,256]{2,1,0:T(8,128)(2,1)S(1)}, bf16[3,160,256]{2,1,0:T(8,128)(2,1)}, u32[]{:S(2)}) copy-start(bf16[3,160,256]{2,1,0:T(8,128)(2,1)} %copy-done.10) | copy-start | bytes 737284
  94.8 17.7 %collective-permute-start = (bf16[12,16,1280]{2,1,0:T(8,128)(2,1)S(1)}, bf16[12,16,1280]{2,1,0:T(8,128)(2,1)S(1)}, u32[]{:S(2)}, u32[]{:S(2)}) collective-permute-start(bf16[12,16,1280]{2,1,0:T(8,128)(2,1)S(1)} %get-tuple-element.52), channel_id=1, source_target_pairs={{0,32},{32,64},{64,96},{96,128},{128,160},{160,192},{192,224},{1,3... | collective-permute-start | bytes 1474568 | tf_op jit(solution)/shard_map/ppermute | solution.py:470
  99.9 23.0 %collective-permute-start.1 = (bf16[12,16,1280]{2,1,0:T(8,128)(2,1)S(1)}, bf16[12,16,1280]{2,1,0:T(8,128)(2,1)S(1)}, u32[]{:S(2)}, u32[]{:S(2)}) collective-permute-start(bf16[12,16,1280]{2,1,0:T(8,128)(2,1)S(1)} %get-tuple-element.51), channel_id=1, source_target_pairs={{32,0},{64,32},{96,64},{128,96},{160,128},{192,160},{224,192},{33,... | collective-permute-start | bytes 1474568 | tf_op jit(solution)/shard_map/ppermute | solution.py:471
  106.6 16.3 %copy-start.3 = (bf16[8,160,256]{2,1,0:T(8,128)(2,1)S(1)}, bf16[8,160,256]{2,1,0:T(8,128)(2,1)}, u32[]{:S(2)}) copy-start(bf16[8,160,256]{2,1,0:T(8,128)(2,1)} %copy-done.2) | copy-start | bytes 1966084

commit v5 on v4

--- a/solution.py
+++ b/solution.py
@@ -459,14 +459,16 @@
         raw_frames, later_order, dark_frame, flat_gain, stripe_band, shear_offset, shear_fraction,
         SPLIT, columns,
     )
-    second_piece, inner_matrices, outer_matrices = lax.optimization_barrier(
-        (second_piece, inner_matrices, outer_matrices)
-    )
     result = None
     parts = []
     centres = []
-    for piece in (first_piece, second_piece):
+    for number in range(2):
+        piece = second_piece if number else first_piece
         centre = lax.all_to_all(piece, "brick", split_axis=0, concat_axis=0, tiled=True)
+        if number == 0:
+            centre, second_piece, inner_matrices, outer_matrices = lax.optimization_barrier(
+                (centre, second_piece, inner_matrices, outer_matrices)
+            )
         low = lax.ppermute(centre[-depth:], "cam", forward)
         high = lax.ppermute(centre[:depth], "cam", backward)
         centres.append((centre,))

time: 132 us -> 121 us (0.917)
  blocking collectives: 33.2 us -> 0 us
  starting transfers between devices: 20.8 us -> 31.8 us
  waiting for transfers between devices: 38.5 us -> 47.5 us
  local copies, waits for them, and re-layouts: 5.66 us -> 8.14 us
    all_to_all x1 -> x0, blocking collectives: 33.2 us -> none  [local(): lax.all_to_all(piece, 'brick', split_axis=0, concat_axis=0, tiled=True)]
    all_to_all x1 -> x2, starting transfers between devices: 4.01 us -> 14.5 us  [local(): lax.all_to_all(piece, 'brick', split_axis=0, concat_axis=0, tiled=True)]
    ppermute x2, waiting for transfers between devices: 3.35 us -> 12.7 us  [local(): low = lax.ppermute(centre[-depth:], 'cam', forward)]
    all_to_all x1 -> x2, waiting for transfers between devices: 24.8 us -> 18.8 us  [local(): lax.all_to_all(piece, 'brick', split_axis=0, concat_axis=0, tiled=True)]
    ppermute x2, waiting for transfers between devices: 10.4 us -> 16 us  [local(): high = lax.ppermute(centre[:depth], 'cam', backward)]
    unnamed x26 -> x40, local copies, waits for them, and re-layouts: 3.77 us -> 7.75 us
    ppermute x2, starting transfers between devices: 7.5 us -> 11 us  [local(): high = lax.ppermute(centre[:depth], 'cam', backward)]
    ppermute x2, starting transfers between devices: 9.29 us -> 6.26 us  [local(): low = lax.ppermute(centre[-depth:], 'cam', forward)]
  transfers between devices with their start and end apart: 5 -> 6, of which waited for: 3 -> 4; matrix products, arithmetic and copies ran while one was open for 1% -> 0% of each run, Pallas kernels for 7% -> 17%
where the time goes in v5:
time: 121 us; the launch traced here: 120 us
  waiting for transfers between devices  47.5 us (39%)
  Pallas kernels  32.8 us (27%)
  starting transfers between devices  31.8 us (26%)
  local copies, waits for them, and re-layouts  8.14 us (7%)
    all_to_all x2, waiting for transfers between devices, local(): lax.all_to_all(piece, 'brick', split_axis=0, concat_axis=0, tiled=True)  18.8 us
    ppermute x2, waiting for transfers between devices, local(): high = lax.ppermute(centre[:depth], 'cam', backward)  16 us
    pallas_call x2, Pallas kernels, frame_side(): pl.pallas_call(functools.partial(frame_kernel, first, count), grid=(steps...  15.7 us
    all_to_all x2, starting transfers between devices, local(): lax.all_to_all(piece, 'brick', split_axis=0, concat_axis=0, tiled=True)  14.5 us
    pallas_call x4, Pallas kernels, restore(): pl.pallas_call(functools.partial(restore_kernel, plan, inside, [len(part)...  14 us
    ppermute x2, waiting for transfers between devices, local(): low = lax.ppermute(centre[-depth:], 'cam', forward)  12.7 us
    ppermute x2, starting transfers between devices, local(): high = lax.ppermute(centre[:depth], 'cam', backward)  11 us
    unnamed x40, local copies, waits for them, and re-layouts  7.75 us
  transfers between devices with their start and end apart: 6, of which 4 were waited for; matrix products, arithmetic and copies ran while one was open for 0% of the time, Pallas kernels for 17%

profile of v5, /device:TPU:14, one launch (start us, length us, event | category | flops | bytes accessed | tf_op | source)
XLA Modules:
  0.0 120.5 jit_solution(5389313316028306060)
XLA Ops:
  0.0 8.0 %frame_side.2 = bf16[32,16,1280]{2,1,0:T(8,128)(2,1)} custom-call(s32[1,2]{1,0:T(1,128)} %order_ref.2, s32[64]{0:T(128)} %offset_ref.3, f32[64]{0:T(128)} %fraction_ref.3, bf16[2,256,2048]{2,1,0:T(8,128)(2,1)} %raw_next.3, bf16[2,256,2048]{2,1,0:T(8,128)(2,1)} %raw_next.3, bf16[2,256,2048]{2,1,0:T(8,128)(2,1)} %raw_next.3, bf16[256,2048]{1,0:T(8,128)(2,1)} %dark_next.3, ...), custom_call_target="tpu_custom_call" | custom-call | flops 8000000000 | bytes 6500000 | tf_op jit(solution)/shard_map/frame_side/pallas_call | solution.py:126
  8.0 0.0 copy-start
  8.1 0.0 copy-start.1
  8.1 10.2 %all-to-all-start = ((bf16[32,16,1280]{2,1,0:T(8,128)(2,1)}), bf16[32,16,1280]{2,1,0:T(8,128)(2,1)S(1)}, u32[]{:S(2)}, u32[]{:S(2)}) async-start(bf16[32,16,1280]{2,1,0:T(8,128)(2,1)} %frame_side.2), calls=%async_computation | async-start | bytes 2621440 | tf_op jit(solution)/shard_map/all_to_all | solution.py:467
  18.3 0.1 pad_dynamic-slice_fusion
  18.4 0.1 broadcast_in_dim.2
  18.5 0.1 reshape.4.index_ref
  18.6 3.0 %bands.1 = (bf16[5,160,256]{2,1,0:T(8,128)(2,1)S(1)}, bf16[3,160,256]{2,1,0:T(8,128)(2,1)S(1)}, bf16[8,160,256]{2,1,0:T(8,128)(2,1)S(1)}, bf16[8,160,256]{2,1,0:...) custom-call(f32[8,13]{1,0:T(8,128)S(1)} %copy-done, f32[9]{0:T(128)S(1)} %copy-done.1, ...), custom_call_target="tpu_custom_call" | custom-call | flops 2000000000 | bytes 2000000 | tf_op jit(solution)/shard_map/bands/pallas_call | solution.py:233
  21.7 0.9 copy-done.4
  22.5 0.8 copy-done.7
  23.4 0.7 copy-done.10
  24.1 0.7 copy-done.13
  24.8 0.7 copy-done.16
  25.5 7.7 %frame_side.3 = bf16[32,16,768]{2,1,0:T(8,128)(2,1)} custom-call(s32[1,2]{1,0:T(1,128)} %order_ref.2, s32[64]{0:T(128)} %offset_ref.3, f32[64]{0:T(128)} %fraction_ref.3, bf16[2,256,2048]{2,1,0:T(8,128)(2,1)} %raw_next.3, bf16[2,256,2048]{2,1,0:T(8,128)(2,1)} %raw_next.3, bf16[2,256,2048]{2,1,0:T(8,128)(2,1)} %raw_next.3, bf16[256,2048]{1,0:T(8,128)(2,1)} %dark_next.3, ...), custom_call_target="tpu_custom_call" | custom-call | flops 8000000000 | bytes 6500000 | tf_op jit(solution)/shard_map/frame_side/pallas_call | solution.py:126
  33.2 18.8 %all-to-all-done.refs_0_.refs_1_ = bf16[32,16,1280]{2,1,0:T(8,128)(2,1)S(1)} async-done(((bf16[32,16,1280]{2,1,0:T(8,128)(2,1)}), bf16[32,16,1280]{2,1,0:T(8,128)(2,1)S(1)}, u32[]{:S(2)}, u32[]{:S(2)}) %all-to-all-start) | async-done | bytes 1310752 | tf_op jit(solution)/shard_map/all_to_all | solution.py:467
  52.0 4.3 %all-to-all-start.1 = ((bf16[32,16,768]{2,1,0:T(8,128)(2,1)}), bf16[32,16,768]{2,1,0:T(8,128)(2,1)S(1)}, u32[]{:S(2)}, u32[]{:S(2)}) async-start(bf16[32,16,768]{2,1,0:T(8,128)(2,1)} %frame_side.3), calls=%async_computation.1 | async-start | bytes 1572864 | tf_op jit(solution)/shard_map/all_to_all | solution.py:467
  56.4 0.1 fusion
  56.5 4.3 %collective-permute-start = (bf16[12,16,1280]{2,1,0:T(8,128)(2,1)S(1)}, bf16[12,16,1280]{2,1,0:T(8,128)(2,1)S(1)}, u32[]{:S(2)}, u32[]{:S(2)}) collective-permute-start(bf16[12,16,1280]{2,1,0:T(8,128)(2,1)S(1)} %get-tuple-element.54), channel_id=1, source_target_pairs={{0,32},{32,64},{64,96},{96,128},{128,160},{160,192},{192,224},{1,3... | collective-permute-start | bytes 1474568 | tf_op jit(solution)/shard_map/ppermute | solution.py:472
  60.8 4.4 %collective-permute-start.1 = (bf16[12,16,1280]{2,1,0:T(8,128)(2,1)S(1)}, bf16[12,16,1280]{2,1,0:T(8,128)(2,1)S(1)}, u32[]{:S(2)}, u32[]{:S(2)}) collective-permute-start(bf16[12,16,1280]{2,1,0:T(8,128)(2,1)S(1)} %get-tuple-element.53), channel_id=1, source_target_pairs={{32,0},{64,32},{96,64},{128,96},{160,128},{192,160},{224,192},{33,... | collective-permute-start | bytes 1474568 | tf_op jit(solution)/shard_map/ppermute | solution.py:473
  65.2 3.2 %inside.3 = (bf16[16,8,1280]{2,1,0:T(8,128)(2,1)S(1)}, bf16[416,1280]{1,0:T(8,128)(2,1)S(1)}, f32[192,1280]{1,0:T(8,128)S(1)}) custom-call(bf16[32,16,1280]{2,1,0:T(8,128)(2,1)S(1)} %all-to-all-done.refs_0_.refs_1_, bf16[5,160,256]{2,1,0:T(8,128)(2,1)S(1)} %get-tuple-element.43.refs_2_.refs_1_, bf16[3,160,256]{2,1,0:T(8,128)(2,1)S(1)} %copy-done.17, ...), custom_call_target="tpu_custom_call" | custom-call | flops 5000000000 | bytes 8000000 | tf_op jit(solution)/shard_map/inside/pallas_call | solution.py:408
  68.4 12.7 %collective-permute-done.refs_0_ = bf16[12,16,1280]{2,1,0:T(8,128)(2,1)S(1)} collective-permute-done((bf16[12,16,1280]{2,1,0:T(8,128)(2,1)S(1)}, bf16[12,16,1280]{2,1,0:T(8,128)(2,1)S(1)}, u32[]{:S(2)}, u32[]{:S(2)}) %collective-permute-start) | collective-permute-done | bytes 491552 | tf_op jit(solution)/shard_map/ppermute | solution.py:472
  81.1 10.4 %collective-permute-done.1.refs_2_ = bf16[12,16,1280]{2,1,0:T(8,128)(2,1)S(1)} collective-permute-done((bf16[12,16,1280]{2,1,0:T(8,128)(2,1)S(1)}, bf16[12,16,1280]{2,1,0:T(8,128)(2,1)S(1)}, u32[]{:S(2)}, u32[]{:S(2)}) %collective-permute-start.1) | collective-permute-done | bytes 491552 | tf_op jit(solution)/shard_map/ppermute | solution.py:473
  91.5 3.8 %ends.2.refs_13_ = bf16[64,8,1152]{2,1,0:T(8,128)(2,1)S(1)} custom-call(bf16[12,16,1280]{2,1,0:T(8,128)(2,1)S(1)} %collective-permute-done.refs_0_, bf16[32,16,1280]{2,1,0:T(8,128)(2,1)S(1)} %all-to-all-done.refs_0_.refs_1_, bf16[12,16,1280]{2,1,0:T(8,128)(2,1)S(1)} %collective-permute-done.1.refs_2_, bf16[8,160,256]{2,1,0:T(8,128)(2,1)S(1)} %copy-done.5, ...), custom_call_target="tpu_custom_call" | custom-call | flops 5000000000 | bytes 8000000 | tf_op jit(solution)/shard_map/ends/pallas_call | solution.py:408
  95.4 1.0 copy-done.2
  96.4 1.9 %collective-permute-start.2 = (bf16[12,16,768]{2,1,0:T(8,128)(2,1)S(1)}, bf16[12,16,768]{2,1,0:T(8,128)(2,1)S(1)}, u32[]{:S(2)}, u32[]{:S(2)}) collective-permute-start(bf16[12,16,768]{2,1,0:T(8,128)(2,1)S(1)} %get-tuple-element.56), channel_id=1, source_target_pairs={{0,32},{32,64},{64,96},{96,128},{128,160},{160,192},{192,224},{1,3... | collective-permute-start | bytes 884744 | tf_op jit(solution)/shard_map/ppermute | solution.py:472
  98.4 6.7 %collective-permute-start.3 = (bf16[12,16,768]{2,1,0:T(8,128)(2,1)S(1)}, bf16[12,16,768]{2,1,0:T(8,128)(2,1)S(1)}, u32[]{:S(2)}, u32[]{:S(2)}) collective-permute-start(bf16[12,16,768]{2,1,0:T(8,128)(2,1)S(1)} %get-tuple-element.55), channel_id=1, source_target_pairs={{32,0},{64,32},{96,64},{128,96},{160,128},{192,160},{224,192},{33,... | collective-permute-start | bytes 884744 | tf_op jit(solution)/shard_map/ppermute | solution.py:473
  105.1 0.9 copy-done.12
  106.0 0.9 copy-done.15
  107.0 0.9 copy-done.18
  107.9 2.5 %inside.2 = (bf16[16,8,1024]{2,1,0:T(8,128)(2,1)S(1)}, bf16[416,1024]{1,0:T(8,128)(2,1)S(1)}, f32[192,1024]{1,0:T(8,128)S(1)}) custom-call(bf16[32,16,1280]{2,1,0:T(8,128)(2,1)S(1)} %all-to-all-done.refs_0_.refs_1_, bf16[32,16,768]{2,1,0:T(8,128)(2,1)S(1)} %all-to-all-done.1.refs_1_.refs_4_, bf16[5,160,256]{2,1,0:T(8,128)(2,1)S(1)} %get-tuple-element.43.refs_2_.refs_1_, ...), custom_call_target="tpu_custom_call" | custom-call | flops 5000000000 | bytes 8000000 | tf_op jit(solution)/shard_map/inside/pallas_call | solution.py:408
  110.5 5.5 %collective-permute-done.3.refs_5_ = bf16[12,16,768]{2,1,0:T(8,128)(2,1)S(1)} collective-permute-done((bf16[12,16,768]{2,1,0:T(8,128)(2,1)S(1)}, bf16[12,16,768]{2,1,0:T(8,128)(2,1)S(1)}, u32[]{:S(2)}, u32[]{:S(2)}) %collective-permute-start.3) | collective-permute-done | bytes 294944 | tf_op jit(solution)/shard_map/ppermute | solution.py:473
  116.0 4.5 %ends.3 = bf16[64,8,2048]{2,1,0:T(8,128)(2,1)} custom-call(bf16[12,16,1280]{2,1,0:T(8,128)(2,1)S(1)} %collective-permute-done.refs_0_, bf16[32,16,1280]{2,1,0:T(8,128)(2,1)S(1)} %all-to-all-done.refs_0_.refs_1_, bf16[12,16,1280]{2,1,0:T(8,128)(2,1)S(1)} %collective-permute-done.1.refs_2_, bf16[12,16,768]{2,1,0:T(8,128)(2,1)S(1)} %collective-permute-done.2.refs_3_, ...), custom_call_target="tpu_custom_call" | custom-call | flops 5000000000 | bytes 8000000 | tf_op jit(solution)/shard_map/ends/pallas_call | solution.py:408
  (32 shorter events, 0.1 us)
Async XLA Ops:
  8.0 10.3 %copy-start.19 = (s32[512]{0:T(512)S(1)}, s32[512]{0:T(512)}, u32[]{:S(2)}) copy-start(s32[512]{0:T(512)} %param.17) | copy-start | bytes 6148
  8.0 10.6 %copy-start = (f32[8,13]{1,0:T(8,128)S(1)}, f32[8,13]{1,0:T(8,128)}, u32[]{:S(2)}) copy-start(f32[8,13]{1,0:T(8,128)} %psf_ref.1) | copy-start | bytes 1252
  8.1 10.6 %copy-start.1 = (f32[9]{0:T(128)S(1)}, f32[9]{0:T(128)}, u32[]{:S(2)}) copy-start(f32[9]{0:T(128)} %lateral_ref.1) | copy-start | bytes 112
  8.1 44.0 %all-to-all-start = ((bf16[32,16,1280]{2,1,0:T(8,128)(2,1)}), bf16[32,16,1280]{2,1,0:T(8,128)(2,1)S(1)}, u32[]{:S(2)}, u32[]{:S(2)}) async-start(bf16[32,16,1280]{2,1,0:T(8,128)(2,1)} %frame_side.2), calls=%async_computation | async-start | bytes 2621440 | tf_op jit(solution)/shard_map/all_to_all | solution.py:467
  21.7 0.9 copy-start.4
  22.5 0.8 copy-start.7
  23.4 0.7 copy-start.10
  24.1 0.7 copy-start.13
  24.8 0.7 copy-start.16
  52.0 44.4 %all-to-all-start.1 = ((bf16[32,16,768]{2,1,0:T(8,128)(2,1)}), bf16[32,16,768]{2,1,0:T(8,128)(2,1)S(1)}, u32[]{:S(2)}, u32[]{:S(2)}) async-start(bf16[32,16,768]{2,1,0:T(8,128)(2,1)} %frame_side.3), calls=%async_computation.1 | async-start | bytes 1572864 | tf_op jit(solution)/shard_map/all_to_all | solution.py:467
  56.3 8.8 %copy-start.11 = (bf16[512,256]{1,0:T(8,128)(2,1)S(1)}, bf16[512,256]{1,0:T(8,128)(2,1)}, u32[]{:S(2)}) copy-start(bf16[512,256]{1,0:T(8,128)(2,1)} %copy-done.10) | copy-start | bytes 786436
  56.4 8.8 %copy-start.14 = (bf16[512,256]{1,0:T(8,128)(2,1)S(1)}, bf16[512,256]{1,0:T(8,128)(2,1)}, u32[]{:S(2)}) copy-start(bf16[512,256]{1,0:T(8,128)(2,1)} %copy-done.13) | copy-start | bytes 786436
  56.4 8.8 %copy-start.17 = (bf16[3,160,256]{2,1,0:T(8,128)(2,1)S(1)}, bf16[3,160,256]{2,1,0:T(8,128)(2,1)}, u32[]{:S(2)}) copy-start(bf16[3,160,256]{2,1,0:T(8,128)(2,1)} %copy-done.16) | copy-start | bytes 737284
  56.5 24.7 %collective-permute-start = (bf16[12,16,1280]{2,1,0:T(8,128)(2,1)S(1)}, bf16[12,16,1280]{2,1,0:T(8,128)(2,1)S(1)}, u32[]{:S(2)}, u32[]{:S(2)}) collective-permute-start(bf16[12,16,1280]{2,1,0:T(8,128)(2,1)S(1)} %get-tuple-element.54), channel_id=1, source_target_pairs={{0,32},{32,64},{64,96},{96,128},{128,160},{160,192},{192,224},{1,3... | collective-permute-start | bytes 1474568 | tf_op jit(solution)/shard_map/ppermute | solution.py:472
  60.8 30.7 %copy-start.5 = (bf16[8,160,256]{2,1,0:T(8,128)(2,1)S(1)}, bf16[8,160,256]{2,1,0:T(8,128)(2,1)}, u32[]{:S(2)}) copy-start(bf16[8,160,256]{2,1,0:T(8,128)(2,1)} %copy-done.4) | copy-start | bytes 1966084
  60.8 30.7 %copy-start.8 = (bf16[8,160,256]{2,1,0:T(8,128)(2,1)S(1)}, bf16[8,160,256]{2,1,0:T(8,128)(2,1)}, u32[]{:S(2)}) copy-start(bf16[8,160,256]{2,1,0:T(8,128)(2,1)} %copy-done.7) | copy-start | bytes 1966084
  60.8 30.7 %collective-permute-start.1 = (bf16[12,16,1280]{2,1,0:T(8,128)(2,1)S(1)}, bf16[12,16,1280]{2,1,0:T(8,128)(2,1)S(1)}, u32[]{:S(2)}, u32[]{:S(2)}) collective-permute-start(bf16[12,16,1280]{2,1,0:T(8,128)(2,1)S(1)} %get-tuple-element.53), channel_id=1, source_target_pairs={{32,0},{64,32},{96,64},{128,96},{160,128},{192,160},{224,192},{33,... | collective-permute-start | bytes 1474568 | tf_op jit(solution)/shard_map/ppermute | solution.py:473
  95.4 1.0 copy-start.2
  96.4 14.0 %collective-permute-start.2 = (bf16[12,16,768]{2,1,0:T(8,128)(2,1)S(1)}, bf16[12,16,768]{2,1,0:T(8,128)(2,1)S(1)}, u32[]{:S(2)}, u32[]{:S(2)}) collective-permute-start(bf16[12,16,768]{2,1,0:T(8,128)(2,1)S(1)} %get-tuple-element.56), channel_id=1, source_target_pairs={{0,32},{32,64},{64,96},{96,128},{128,160},{160,192},{192,224},{1,3... | collective-permute-start | bytes 884744 | tf_op jit(solution)/shard_map/ppermute | solution.py:472
  98.4 17.6 %copy-start.3 = (bf16[64,8,1152]{2,1,0:T(8,128)(2,1)S(1)}, bf16[64,8,1152]{2,1,0:T(8,128)(2,1)}, u32[]{:S(2)}) copy-start(bf16[64,8,1152]{2,1,0:T(8,128)(2,1)} %copy-done.2) | copy-start | bytes 3538948
  98.4 17.6 %copy-start.6 = (bf16[8,160,256]{2,1,0:T(8,128)(2,1)S(1)}, bf16[8,160,256]{2,1,0:T(8,128)(2,1)}, u32[]{:S(2)}) copy-start(bf16[8,160,256]{2,1,0:T(8,128)(2,1)} %copy-done.4) | copy-start | bytes 1966084
  98.4 17.6 %copy-start.9 = (bf16[8,160,256]{2,1,0:T(8,128)(2,1)S(1)}, bf16[8,160,256]{2,1,0:T(8,128)(2,1)}, u32[]{:S(2)}) copy-start(bf16[8,160,256]{2,1,0:T(8,128)(2,1)} %copy-done.7) | copy-start | bytes 1966084
  98.4 17.6 %collective-permute-start.3 = (bf16[12,16,768]{2,1,0:T(8,128)(2,1)S(1)}, bf16[12,16,768]{2,1,0:T(8,128)(2,1)S(1)}, u32[]{:S(2)}, u32[]{:S(2)}) collective-permute-start(bf16[12,16,768]{2,1,0:T(8,128)(2,1)S(1)} %get-tuple-element.55), channel_id=1, source_target_pairs={{32,0},{64,32},{96,64},{128,96},{160,128},{192,160},{224,192},{33,... | collective-permute-start | bytes 884744 | tf_op jit(solution)/shard_map/ppermute | solution.py:473
  105.1 1.0 copy-start.12
  106.0 0.9 copy-start.15
  107.0 0.9 copy-start.18

commit v6 on v4

--- a/solution.py
+++ b/solution.py
@@ -459,26 +459,35 @@
         raw_frames, later_order, dark_frame, flat_gain, stripe_band, shear_offset, shear_fraction,
         SPLIT, columns,
     )
-    second_piece, inner_matrices, outer_matrices = lax.optimization_barrier(
-        (second_piece, inner_matrices, outer_matrices)
-    )
-    result = None
-    parts = []
-    centres = []
-    for piece in (first_piece, second_piece):
-        centre = lax.all_to_all(piece, "brick", split_axis=0, concat_axis=0, tiled=True)
+    def exchange(piece):
+        return lax.all_to_all(piece, "brick", split_axis=0, concat_axis=0, tiled=True)
+
+    def with_halo(centre):
         low = lax.ppermute(centre[-depth:], "cam", forward)
         high = lax.ppermute(centre[:depth], "cam", backward)
-        centres.append((centre,))
-        parts.append((low, centre, high))
+        return low, centre, high
+
+    def inside(centres):
         middle, quotients, estimates = restore(
             centres, inner_matrices, (), None, inner, True, planes, half, columns
         )
-        (result,) = restore(
-            parts, outer_matrices, (quotients, estimates, middle), result, outer, False, planes, half,
-            columns,
-        )
-    return result
+        return quotients, estimates, middle
+
+    def ends(parts, state, earlier):
+        return restore(
+            parts, outer_matrices, state, earlier, outer, False, planes, half, columns
+        )[0]
+
+    first, second_piece, inner_matrices, outer_matrices = lax.optimization_barrier(
+        (exchange(first_piece), second_piece, inner_matrices, outer_matrices)
+    )
+    first_part = with_halo(first)
+    first_state = inside([(first,)])
+    second, first_state = lax.optimization_barrier((exchange(second_piece), first_state))
+    second_part = with_halo(second)
+    second_state = inside([(first,), (second,)])
+    result = ends([first_part], first_state, None)
+    return ends([first_part, second_part], second_state, result)
 
 
 def solution(mesh):

time: 132 us -> 109 us (0.83)
  blocking collectives: 33.2 us -> 0 us
  starting transfers between devices: 20.8 us -> 29.7 us
  local copies, waits for them, and re-layouts: 5.66 us -> 10.7 us
  waiting for transfers between devices: 38.5 us -> 35.5 us
    all_to_all x1 -> x0, blocking collectives: 33.2 us -> none  [local(): lax.all_to_all(piece, 'brick', split_axis=0, concat_axis=0, tiled=True)]
    all_to_all x1 -> x2, starting transfers between devices: 4.01 us -> 14.5 us  [exchange(): lax.all_to_all(piece, 'brick', split_axis=0, concat_axis=0, tiled=True)]
    ppermute x4, waiting for transfers between devices: 13.8 us -> 7.41 us  [the longest x2 7.4 us: with_halo(): high = lax.ppermute(centre[:depth], 'cam', backward)]
    unnamed x26 -> x44, local copies, waits for them, and re-layouts: 3.77 us -> 9.34 us
    all_to_all x1 -> x2, waiting for transfers between devices: 24.8 us -> 28.1 us  [exchange(): lax.all_to_all(piece, 'brick', split_axis=0, concat_axis=0, tiled=True)]
    ppermute x4, starting transfers between devices: 16.8 us -> 15.2 us  [the longest x2 8.93 us: with_halo(): high = lax.ppermute(centre[:depth], 'cam', backward)]
  transfers between devices with their start and end apart: 5 -> 6, of which waited for: 3 -> 4; matrix products, arithmetic and copies ran while one was open for 1% -> 1% of each run, Pallas kernels for 7% -> 18%
where the time goes in v6:
time: 109 us; the launch traced here: 108 us
  waiting for transfers between devices  35.5 us (33%)
  Pallas kernels  32.3 us (30%)
  starting transfers between devices  29.7 us (27%)
  local copies, waits for them, and re-layouts  10.7 us (10%)
    all_to_all x2, waiting for transfers between devices, exchange(): lax.all_to_all(piece, 'brick', split_axis=0, concat_axis=0, tiled=True)  28.1 us
    pallas_call x2, Pallas kernels, frame_side(): pl.pallas_call(functools.partial(frame_kernel, first, count), grid=(steps...  15.2 us
    all_to_all x2, starting transfers between devices, exchange(): lax.all_to_all(piece, 'brick', split_axis=0, concat_axis=0, tiled=True)  14.5 us
    pallas_call x4, Pallas kernels, restore(): pl.pallas_call(functools.partial(restore_kernel, plan, inside, [len(part)...  14 us
    unnamed x44, local copies, waits for them, and re-layouts  9.34 us
    ppermute x2, starting transfers between devices, with_halo(): high = lax.ppermute(centre[:depth], 'cam', backward)  8.93 us
    ppermute x2, waiting for transfers between devices, with_halo(): high = lax.ppermute(centre[:depth], 'cam', backward)  7.4 us
    ppermute x2, starting transfers between devices, with_halo(): low = lax.ppermute(centre[-depth:], 'cam', forward)  6.24 us
  transfers between devices with their start and end apart: 6, of which 4 were waited for; matrix products, arithmetic and copies ran while one was open for 1% of the time, Pallas kernels for 18%

profile of v6, /device:TPU:14, one launch (start us, length us, event | category | flops | bytes accessed | tf_op | source)
XLA Modules:
  0.0 108.4 jit_solution(16357016525215886481)
XLA Ops:
  0.0 7.8 %frame_side.2 = bf16[32,16,1280]{2,1,0:T(8,128)(2,1)} custom-call(s32[1,2]{1,0:T(1,128)} %order_ref.2, s32[64]{0:T(128)} %offset_ref.3, f32[64]{0:T(128)} %fraction_ref.3, bf16[2,256,2048]{2,1,0:T(8,128)(2,1)} %raw_next.3, bf16[2,256,2048]{2,1,0:T(8,128)(2,1)} %raw_next.3, bf16[2,256,2048]{2,1,0:T(8,128)(2,1)} %raw_next.3, bf16[256,2048]{1,0:T(8,128)(2,1)} %dark_next.3, ...), custom_call_target="tpu_custom_call" | custom-call | flops 8000000000 | bytes 6500000 | tf_op jit(solution)/shard_map/frame_side/pallas_call | solution.py:126
  7.8 10.2 %all-to-all-start = ((bf16[32,16,1280]{2,1,0:T(8,128)(2,1)}), bf16[32,16,1280]{2,1,0:T(8,128)(2,1)S(1)}, u32[]{:S(2)}, u32[]{:S(2)}) async-start(bf16[32,16,1280]{2,1,0:T(8,128)(2,1)} %frame_side.2), calls=%async_computation | async-start | bytes 2621440 | tf_op jit(solution)/shard_map/all_to_all | solution.py:463
  18.0 0.1 pad_dynamic-slice_fusion
  18.1 0.1 broadcast_in_dim.2
  18.2 0.1 reshape.4.index_ref
  18.3 3.0 %bands.1 = (bf16[5,160,256]{2,1,0:T(8,128)(2,1)S(1)}, bf16[3,160,256]{2,1,0:T(8,128)(2,1)S(1)}, bf16[8,160,256]{2,1,0:T(8,128)(2,1)S(1)}, bf16[8,160,256]{2,1,0:...) custom-call(f32[8,13]{1,0:T(8,128)S(1)} %copy-done, f32[9]{0:T(128)S(1)} %copy-done.1, ...), custom_call_target="tpu_custom_call" | custom-call | flops 2000000000 | bytes 2000000 | tf_op jit(solution)/shard_map/bands/pallas_call | solution.py:233
  21.4 0.8 copy-done.2
  22.2 0.8 copy-done.4
  23.1 0.7 copy-done.10
  23.8 0.7 copy-done.13
  24.5 0.7 copy-done.16
  25.2 7.4 %frame_side.3 = bf16[32,16,768]{2,1,0:T(8,128)(2,1)} custom-call(s32[1,2]{1,0:T(1,128)} %order_ref.2, s32[64]{0:T(128)} %offset_ref.3, f32[64]{0:T(128)} %fraction_ref.3, bf16[2,256,2048]{2,1,0:T(8,128)(2,1)} %raw_next.3, bf16[2,256,2048]{2,1,0:T(8,128)(2,1)} %raw_next.3, bf16[2,256,2048]{2,1,0:T(8,128)(2,1)} %raw_next.3, bf16[256,2048]{1,0:T(8,128)(2,1)} %dark_next.3, ...), custom_call_target="tpu_custom_call" | custom-call | flops 8000000000 | bytes 6500000 | tf_op jit(solution)/shard_map/frame_side/pallas_call | solution.py:126
  32.6 19.1 %all-to-all-done.refs_0_.refs_1_ = bf16[32,16,1280]{2,1,0:T(8,128)(2,1)S(1)} async-done(((bf16[32,16,1280]{2,1,0:T(8,128)(2,1)}), bf16[32,16,1280]{2,1,0:T(8,128)(2,1)S(1)}, u32[]{:S(2)}, u32[]{:S(2)}) %all-to-all-start) | async-done | bytes 1310752 | tf_op jit(solution)/shard_map/all_to_all | solution.py:463
  51.8 4.3 %all-to-all-start.1 = ((bf16[32,16,768]{2,1,0:T(8,128)(2,1)}), bf16[32,16,768]{2,1,0:T(8,128)(2,1)S(1)}, u32[]{:S(2)}, u32[]{:S(2)}) async-start(bf16[32,16,768]{2,1,0:T(8,128)(2,1)} %frame_side.3), calls=%async_computation.1 | async-start | bytes 1572864 | tf_op jit(solution)/shard_map/all_to_all | solution.py:463
  56.1 1.0 fusion
  57.1 4.5 %collective-permute-start.1 = (bf16[12,16,1280]{2,1,0:T(8,128)(2,1)}, bf16[12,16,1280]{2,1,0:T(8,128)(2,1)S(1)}, u32[]{:S(2)}, u32[]{:S(2)}) collective-permute-start(bf16[12,16,1280]{2,1,0:T(8,128)(2,1)} %get-tuple-element.61), channel_id=1, source_target_pairs={{32,0},{64,32},{96,64},{128,96},{160,128},{192,160},{224,192},{33,... | collective-permute-start | bytes 1474568 | tf_op jit(solution)/shard_map/ppermute | solution.py:467
  61.6 2.9 %collective-permute-start = (bf16[12,16,1280]{2,1,0:T(8,128)(2,1)}, bf16[12,16,1280]{2,1,0:T(8,128)(2,1)S(1)}, u32[]{:S(2)}, u32[]{:S(2)}) collective-permute-start(bf16[12,16,1280]{2,1,0:T(8,128)(2,1)} %get-tuple-element.62), channel_id=1, source_target_pairs={{0,32},{32,64},{64,96},{96,128},{128,160},{160,192},{192,224},{1,3... | collective-permute-start | bytes 1474568 | tf_op jit(solution)/shard_map/ppermute | solution.py:466
  64.5 3.2 %inside.2 = (bf16[16,8,1280]{2,1,0:T(8,128)(2,1)S(1)}, bf16[416,1280]{1,0:T(8,128)(2,1)S(1)}, f32[192,1280]{1,0:T(8,128)S(1)}) custom-call(bf16[32,16,1280]{2,1,0:T(8,128)(2,1)S(1)} %all-to-all-done.refs_0_.refs_1_, bf16[5,160,256]{2,1,0:T(8,128)(2,1)S(1)} %get-tuple-element.43.refs_1_.refs_2_, bf16[3,160,256]{2,1,0:T(8,128)(2,1)S(1)} %copy-done.17, ...), custom_call_target="tpu_custom_call" | custom-call | flops 5000000000 | bytes 8000000 | tf_op jit(solution)/shard_map/inside/pallas_call | solution.py:408
  67.7 1.0 copy-done.6
  68.7 0.9 copy-done.8
  69.7 0.7 copy-done.19
  70.4 9.0 %all-to-all-done.1.refs_1_.refs_4_ = bf16[32,16,768]{2,1,0:T(8,128)(2,1)S(1)} async-done(((bf16[32,16,768]{2,1,0:T(8,128)(2,1)}), bf16[32,16,768]{2,1,0:T(8,128)(2,1)S(1)}, u32[]{:S(2)}, u32[]{:S(2)}) %all-to-all-start.1) | async-done | bytes 786464 | tf_op jit(solution)/shard_map/all_to_all | solution.py:463
  79.4 4.5 %collective-permute-start.3 = (bf16[12,16,768]{2,1,0:T(8,128)(2,1)S(1)}, bf16[12,16,768]{2,1,0:T(8,128)(2,1)S(1)}, u32[]{:S(2)}, u32[]{:S(2)}) collective-permute-start(bf16[12,16,768]{2,1,0:T(8,128)(2,1)S(1)} %get-tuple-element.63), channel_id=1, source_target_pairs={{32,0},{64,32},{96,64},{128,96},{160,128},{192,160},{224,192},{33,... | collective-permute-start | bytes 884744 | tf_op jit(solution)/shard_map/ppermute | solution.py:467
  84.0 3.3 %collective-permute-start.2 = (bf16[12,16,768]{2,1,0:T(8,128)(2,1)S(1)}, bf16[12,16,768]{2,1,0:T(8,128)(2,1)S(1)}, u32[]{:S(2)}, u32[]{:S(2)}) collective-permute-start(bf16[12,16,768]{2,1,0:T(8,128)(2,1)S(1)} %get-tuple-element.64), channel_id=1, source_target_pairs={{0,32},{32,64},{64,96},{96,128},{128,160},{160,192},{192,224},{1,3... | collective-permute-start | bytes 884744 | tf_op jit(solution)/shard_map/ppermute | solution.py:466
  87.3 0.9 copy-done.12
  88.3 0.9 copy-done.15
  89.2 0.9 copy-done.18
  90.2 2.5 %inside.3 = (bf16[16,8,1024]{2,1,0:T(8,128)(2,1)S(1)}, bf16[416,1024]{1,0:T(8,128)(2,1)S(1)}, f32[192,1024]{1,0:T(8,128)S(1)}) custom-call(bf16[32,16,1280]{2,1,0:T(8,128)(2,1)S(1)} %all-to-all-done.refs_0_.refs_1_, bf16[32,16,768]{2,1,0:T(8,128)(2,1)S(1)} %all-to-all-done.1.refs_1_.refs_4_, bf16[5,160,256]{2,1,0:T(8,128)(2,1)S(1)} %get-tuple-element.43.refs_1_.refs_2_, ...), custom_call_target="tpu_custom_call" | custom-call | flops 5000000000 | bytes 8000000 | tf_op jit(solution)/shard_map/inside/pallas_call | solution.py:408
  92.7 5.3 %collective-permute-done.1.refs_2_ = bf16[12,16,1280]{2,1,0:T(8,128)(2,1)S(1)} collective-permute-done((bf16[12,16,1280]{2,1,0:T(8,128)(2,1)}, bf16[12,16,1280]{2,1,0:T(8,128)(2,1)S(1)}, u32[]{:S(2)}, u32[]{:S(2)}) %collective-permute-start.1) | collective-permute-done | bytes 491552 | tf_op jit(solution)/shard_map/ppermute | solution.py:467
  98.0 3.8 %ends.2.refs_13_ = bf16[64,8,1152]{2,1,0:T(8,128)(2,1)S(1)} custom-call(bf16[12,16,1280]{2,1,0:T(8,128)(2,1)S(1)} %collective-permute-done.refs_0_, bf16[32,16,1280]{2,1,0:T(8,128)(2,1)S(1)} %all-to-all-done.refs_0_.refs_1_, bf16[12,16,1280]{2,1,0:T(8,128)(2,1)S(1)} %collective-permute-done.1.refs_2_, bf16[8,160,256]{2,1,0:T(8,128)(2,1)S(1)} %copy-done.3, ...), custom_call_target="tpu_custom_call" | custom-call | flops 5000000000 | bytes 8000000 | tf_op jit(solution)/shard_map/ends/pallas_call | solution.py:408
  101.8 2.2 %collective-permute-done.3.refs_5_ = bf16[12,16,768]{2,1,0:T(8,128)(2,1)S(1)} collective-permute-done((bf16[12,16,768]{2,1,0:T(8,128)(2,1)S(1)}, bf16[12,16,768]{2,1,0:T(8,128)(2,1)S(1)}, u32[]{:S(2)}, u32[]{:S(2)}) %collective-permute-start.3) | collective-permute-done | bytes 294944 | tf_op jit(solution)/shard_map/ppermute | solution.py:467
  104.0 4.5 %ends.3 = bf16[64,8,2048]{2,1,0:T(8,128)(2,1)} custom-call(bf16[12,16,1280]{2,1,0:T(8,128)(2,1)S(1)} %collective-permute-done.refs_0_, bf16[32,16,1280]{2,1,0:T(8,128)(2,1)S(1)} %all-to-all-done.refs_0_.refs_1_, bf16[12,16,1280]{2,1,0:T(8,128)(2,1)S(1)} %collective-permute-done.1.refs_2_, bf16[12,16,768]{2,1,0:T(8,128)(2,1)S(1)} %collective-permute-done.2.refs_3_, ...), custom_call_target="tpu_custom_call" | custom-call | flops 5000000000 | bytes 8000000 | tf_op jit(solution)/shard_map/ends/pallas_call | solution.py:408
  (36 shorter events, 0.1 us)
Async XLA Ops:
  7.8 10.3 %copy-start.21 = (s32[512]{0:T(512)S(1)}, s32[512]{0:T(512)}, u32[]{:S(2)}) copy-start(s32[512]{0:T(512)} %param.17) | copy-start | bytes 6148
  7.8 10.6 %copy-start = (f32[8,13]{1,0:T(8,128)S(1)}, f32[8,13]{1,0:T(8,128)}, u32[]{:S(2)}) copy-start(f32[8,13]{1,0:T(8,128)} %psf_ref.1) | copy-start | bytes 1252
  7.8 10.6 %copy-start.1 = (f32[9]{0:T(128)S(1)}, f32[9]{0:T(128)}, u32[]{:S(2)}) copy-start(f32[9]{0:T(128)} %lateral_ref.1) | copy-start | bytes 112
  7.8 44.0 %all-to-all-start = ((bf16[32,16,1280]{2,1,0:T(8,128)(2,1)}), bf16[32,16,1280]{2,1,0:T(8,128)(2,1)S(1)}, u32[]{:S(2)}, u32[]{:S(2)}) async-start(bf16[32,16,1280]{2,1,0:T(8,128)(2,1)} %frame_side.2), calls=%async_computation | async-start | bytes 2621440 | tf_op jit(solution)/shard_map/all_to_all | solution.py:463
  21.4 0.8 copy-start.2
  22.2 0.8 copy-start.4
  23.1 0.7 copy-start.10
  23.8 0.7 copy-start.13
  24.5 0.7 copy-start.16
  51.8 27.6 %all-to-all-start.1 = ((bf16[32,16,768]{2,1,0:T(8,128)(2,1)}), bf16[32,16,768]{2,1,0:T(8,128)(2,1)S(1)}, u32[]{:S(2)}, u32[]{:S(2)}) async-start(bf16[32,16,768]{2,1,0:T(8,128)(2,1)} %frame_side.3), calls=%async_computation.1 | async-start | bytes 1572864 | tf_op jit(solution)/shard_map/all_to_all | solution.py:463
  56.1 8.4 %copy-start.11 = (bf16[512,256]{1,0:T(8,128)(2,1)S(1)}, bf16[512,256]{1,0:T(8,128)(2,1)}, u32[]{:S(2)}) copy-start(bf16[512,256]{1,0:T(8,128)(2,1)} %copy-done.10) | copy-start | bytes 786436
  56.1 8.4 %copy-start.14 = (bf16[512,256]{1,0:T(8,128)(2,1)S(1)}, bf16[512,256]{1,0:T(8,128)(2,1)}, u32[]{:S(2)}) copy-start(bf16[512,256]{1,0:T(8,128)(2,1)} %copy-done.13) | copy-start | bytes 786436
  56.1 8.4 %copy-start.17 = (bf16[3,160,256]{2,1,0:T(8,128)(2,1)S(1)}, bf16[3,160,256]{2,1,0:T(8,128)(2,1)}, u32[]{:S(2)}) copy-start(bf16[3,160,256]{2,1,0:T(8,128)(2,1)} %copy-done.16) | copy-start | bytes 737284
  57.1 40.8 %collective-permute-start.1 = (bf16[12,16,1280]{2,1,0:T(8,128)(2,1)}, bf16[12,16,1280]{2,1,0:T(8,128)(2,1)S(1)}, u32[]{:S(2)}, u32[]{:S(2)}) collective-permute-start(bf16[12,16,1280]{2,1,0:T(8,128)(2,1)} %get-tuple-element.61), channel_id=1, source_target_pairs={{32,0},{64,32},{96,64},{128,96},{160,128},{192,160},{224,192},{33,... | collective-permute-start | bytes 1474568 | tf_op jit(solution)/shard_map/ppermute | solution.py:467
  61.6 36.4 %collective-permute-start = (bf16[12,16,1280]{2,1,0:T(8,128)(2,1)}, bf16[12,16,1280]{2,1,0:T(8,128)(2,1)S(1)}, u32[]{:S(2)}, u32[]{:S(2)}) collective-permute-start(bf16[12,16,1280]{2,1,0:T(8,128)(2,1)} %get-tuple-element.62), channel_id=1, source_target_pairs={{0,32},{32,64},{64,96},{96,128},{128,160},{160,192},{192,224},{1,3... | collective-permute-start | bytes 1474568 | tf_op jit(solution)/shard_map/ppermute | solution.py:466
  67.7 1.0 copy-start.6
  68.7 0.9 copy-start.8
  69.7 0.7 copy-start.19
  79.4 24.5 %collective-permute-start.3 = (bf16[12,16,768]{2,1,0:T(8,128)(2,1)S(1)}, bf16[12,16,768]{2,1,0:T(8,128)(2,1)S(1)}, u32[]{:S(2)}, u32[]{:S(2)}) collective-permute-start(bf16[12,16,768]{2,1,0:T(8,128)(2,1)S(1)} %get-tuple-element.63), channel_id=1, source_target_pairs={{32,0},{64,32},{96,64},{128,96},{160,128},{192,160},{224,192},{33,... | collective-permute-start | bytes 884744 | tf_op jit(solution)/shard_map/ppermute | solution.py:467
  83.9 14.0 %copy-start.3 = (bf16[8,160,256]{2,1,0:T(8,128)(2,1)S(1)}, bf16[8,160,256]{2,1,0:T(8,128)(2,1)}, u32[]{:S(2)}) copy-start(bf16[8,160,256]{2,1,0:T(8,128)(2,1)} %copy-done.2) | copy-start | bytes 1966084
  83.9 14.0 %copy-start.5 = (bf16[8,160,256]{2,1,0:T(8,128)(2,1)S(1)}, bf16[8,160,256]{2,1,0:T(8,128)(2,1)}, u32[]{:S(2)}) copy-start(bf16[8,160,256]{2,1,0:T(8,128)(2,1)} %copy-done.4) | copy-start | bytes 1966084
  83.9 14.0 %copy-start.7 = (bf16[416,1280]{1,0:T(8,128)(2,1)S(1)}, bf16[416,1280]{1,0:T(8,128)(2,1)}, u32[]{:S(2)}) copy-start(bf16[416,1280]{1,0:T(8,128)(2,1)} %copy-done.6) | copy-start | bytes 3194884
  84.0 14.0 %copy-start.9 = (f32[192,1280]{1,0:T(8,128)S(1)}, f32[192,1280]{1,0:T(8,128)}, u32[]{:S(2)}) copy-start(f32[192,1280]{1,0:T(8,128)} %copy-done.8) | copy-start | bytes 2949124
  84.0 20.0 %collective-permute-start.2 = (bf16[12,16,768]{2,1,0:T(8,128)(2,1)S(1)}, bf16[12,16,768]{2,1,0:T(8,128)(2,1)S(1)}, u32[]{:S(2)}, u32[]{:S(2)}) collective-permute-start(bf16[12,16,768]{2,1,0:T(8,128)(2,1)S(1)} %get-tuple-element.64), channel_id=1, source_target_pairs={{0,32},{32,64},{64,96},{96,128},{128,160},{160,192},{192,224},{1,3... | collective-permute-start | bytes 884744 | tf_op jit(solution)/shard_map/ppermute | solution.py:466
  87.3 1.0 copy-start.12
  88.3 0.9 copy-start.15
  89.2 0.9 copy-start.18
  90.2 7.8 %copy-start.20 = (bf16[16,8,1280]{2,1,0:T(8,128)(2,1)S(1)}, bf16[16,8,1280]{2,1,0:T(8,128)(2,1)}, u32[]{:S(2)}) copy-start(bf16[16,8,1280]{2,1,0:T(8,128)(2,1)} %copy-done.19) | copy-start | bytes 983044

commit v7 on v6

--- a/solution.py
+++ b/solution.py
@@ -16,7 +16,7 @@
 ROWS = 8
 BLOCK_ROWS = 64
 LEAD = SHEAR // LANES + 1
-SPLIT = 1280
+SPLIT = 1024
 VMEM = 60 * 1024 * 1024
 BANDS_VMEM = 20 * 1024 * 1024
 RESTORE_VMEM = 42 * 1024 * 1024
@@ -30,7 +30,7 @@
     raw_prev, raw_main, raw_next,
     dark_prev, dark_main, dark_next,
     gain_prev, gain_main, gain_next,
-    band_ref, out_ref, scratch,
+    band_ref, out_ref, scratch, level,
 ):
     step = pl.program_id(0)
     steps = pl.num_programs(0)
@@ -49,36 +49,30 @@
     has_next = (step < steps - 1).astype(f32)
     frames = [jnp.where(order_ref[0, 0] == place, 0, 1) for place in range(2)]
 
-    for tile in range(max(base, 0), first + count):
+    used = range(max(base, 0), first + count)
+    for tile in used:
         cols = pl.ds(tile * LANES, LANES)
-        band = band_ref[:, cols]
-        levels = []
-        for part, keep in ((0, slice(8, 16)), (1, slice(None)), (2, slice(0, 8))):
+        for part, keep, start in ((0, slice(8, 16), 0), (1, slice(None), 8), (2, slice(0, 8), rows - 8)):
             dark = (dark_prev, dark_main, dark_next)[part][:, cols].astype(f32)[keep]
             gain = (gain_prev, gain_main, gain_next)[part][:, cols].astype(f32)[keep]
             if part != 1:
                 gain = gain * (has_prev, None, has_next)[part]
-            levels.append((dark, gain, keep))
+            raw = (raw_prev, raw_main, raw_next)[part]
+            for place in range(2):
+                f = (raw[frames[place], :, cols].astype(f32)[keep] - dark) * gain
+                level[place, tile - used[0], start : start + f.shape[0], :] = f
+
+    zero = jnp.minimum(step, 0)
+    taps = band_ref.shape[0]
+    for tile in used:
+        band = band_ref[:, pl.ds(tile * LANES, LANES)]
         for place in range(2):
-            f = jnp.concatenate(
-                [
-                    (raw[frames[place], :, cols].astype(f32)[keep] - dark) * gain
-                    for raw, (dark, gain, keep) in zip((raw_prev, raw_main, raw_next), levels)
-                ],
-                axis=0,
-            )
-            after = pltpu.roll(f, rows - 1, 0)
-            before = pltpu.roll(f, 1, 0)
-
-            def three(k):
-                return band[k : k + 1] * before + band[k + 1 : k + 2] * f + band[k + 2 : k + 3] * after
-
-            out = (
-                f
-                + three(3)
-                + pltpu.roll(three(6), rows - 3, 0)
-                + pltpu.roll(three(0), 3, 0)
-            )[8 : 8 + BLOCK_ROWS]
+            here = tile - used[0]
+            out = level[place, here, 8 : 8 + BLOCK_ROWS, :] * (1.0 + band[taps // 2 : taps // 2 + 1])
+            for tap in range(taps):
+                if tap != taps // 2:
+                    shifted = level[place, here, pl.ds(zero + 8 + tap - taps // 2, BLOCK_ROWS), :]
+                    out = out + band[tap : tap + 1] * shifted
             scratch[place, :, pl.ds((tile - base) * LANES, LANES)] = out.astype(bf16).astype(f32)
 
     lane = lax.broadcasted_iota(jnp.int32, (BLOCK_ROWS, LANES), 1)
@@ -131,7 +125,10 @@
         + [pl.BlockSpec(band.shape, lambda i: (0, 0))],
         out_specs=pl.BlockSpec((BLOCK_ROWS // ROWS, 2 * ROWS, hi - lo), lambda i: (i, 0, 0)),
         out_shape=jax.ShapeDtypeStruct((bricks, 2 * ROWS, hi - lo), jnp.bfloat16),
-        scratch_shapes=[pltpu.VMEM((2, BLOCK_ROWS, (LEAD + count) * LANES), jnp.float32)],
+        scratch_shapes=[
+            pltpu.VMEM((2, BLOCK_ROWS, (LEAD + count) * LANES), jnp.float32),
+            pltpu.VMEM((2, min(first, LEAD) + count, BLOCK_ROWS + 16, LANES), jnp.float32),
+        ],
         compiler_params=pltpu.CompilerParams(vmem_limit_bytes=VMEM),
         cost_estimate=pl.CostEstimate(
             flops=8_000_000_000, bytes_accessed=6_500_000, transcendentals=0

time: 109 us -> 109 us (level); the launches traced: 108 us -> 107 us
  local copies, waits for them, and re-layouts: 10.7 us -> 14.5 us
  waiting for transfers between devices: 35.5 us -> 32 us
  Pallas kernels: 32.3 us -> 30.8 us
    unnamed x44 -> x48, local copies, waits for them, and re-layouts: 9.34 us -> 13.3 us
    ppermute x2, waiting for transfers between devices: 7.4 us -> 4.85 us  [with_halo(): high = lax.ppermute(centre[:depth], 'cam', backward)]
    pallas_call x2, Pallas kernels: 15.2 us -> 13.7 us  [frame_side(): pl.pallas_call(functools.partial(frame_kernel, first, count), grid=(steps...]
  transfers between devices with their start and end apart: 6 -> 6, of which waited for: 4 -> 3; matrix products, arithmetic and copies ran while one was open for 1% -> 1% of each run, Pallas kernels for 18% -> 18%
where the time goes in v7:
time: 109 us; the launch traced here: 107 us
  waiting for transfers between devices  32 us (29%)
  Pallas kernels  30.8 us (28%)
  starting transfers between devices  29.2 us (27%)
  local copies, waits for them, and re-layouts  14.5 us (13%)
    all_to_all x2, waiting for transfers between devices, exchange(): lax.all_to_all(piece, 'brick', split_axis=0, concat_axis=0, tiled=True)  27.1 us
    all_to_all x2, starting transfers between devices, exchange(): lax.all_to_all(piece, 'brick', split_axis=0, concat_axis=0, tiled=True)  14.2 us
    pallas_call x4, Pallas kernels, restore(): pl.pallas_call(functools.partial(restore_kernel, plan, inside, [len(part)...  14.1 us
    pallas_call x2, Pallas kernels, frame_side(): pl.pallas_call(functools.partial(frame_kernel, first, count), grid=(steps...  13.7 us
    unnamed x48, local copies, waits for them, and re-layouts  13.3 us
    ppermute x2, starting transfers between devices, with_halo(): high = lax.ppermute(centre[:depth], 'cam', backward)  8.93 us
    ppermute x2, starting transfers between devices, with_halo(): low = lax.ppermute(centre[-depth:], 'cam', forward)  6.11 us
    ppermute x2, waiting for transfers between devices, with_halo(): high = lax.ppermute(centre[:depth], 'cam', backward)  4.85 us
  transfers between devices with their start and end apart: 6, of which 3 were waited for; matrix products, arithmetic and copies ran while one was open for 1% of the time, Pallas kernels for 18%

profile of v7, /device:TPU:14, one launch (start us, length us, event | category | flops | bytes accessed | tf_op | source)
XLA Modules:
  0.0 106.9 jit_solution(8787548699380371321)
XLA Ops:
  0.0 6.5 %frame_side.2 = bf16[32,16,1024]{2,1,0:T(8,128)(2,1)} custom-call(s32[1,2]{1,0:T(1,128)} %order_ref.2, s32[64]{0:T(128)} %offset_ref.3, f32[64]{0:T(128)} %fraction_ref.3, bf16[2,256,2048]{2,1,0:T(8,128)(2,1)} %raw_next.3, bf16[2,256,2048]{2,1,0:T(8,128)(2,1)} %raw_next.3, bf16[2,256,2048]{2,1,0:T(8,128)(2,1)} %raw_next.3, bf16[256,2048]{1,0:T(8,128)(2,1)} %dark_next.3, ...), custom_call_target="tpu_custom_call" | custom-call | flops 8000000000 | bytes 6500000 | tf_op jit(solution)/shard_map/frame_side/pallas_call | solution.py:120
  6.5 10.2 %all-to-all-start = ((bf16[32,16,1024]{2,1,0:T(8,128)(2,1)}), bf16[32,16,1024]{2,1,0:T(8,128)(2,1)S(1)}, u32[]{:S(2)}, u32[]{:S(2)}) async-start(bf16[32,16,1024]{2,1,0:T(8,128)(2,1)} %frame_side.2), calls=%async_computation | async-start | bytes 2097152 | tf_op jit(solution)/shard_map/all_to_all | solution.py:460
  17.1 3.0 %bands.1 = (bf16[5,160,256]{2,1,0:T(8,128)(2,1)S(1)}, bf16[3,160,256]{2,1,0:T(8,128)(2,1)S(1)}, bf16[8,160,256]{2,1,0:T(8,128)(2,1)S(1)}, bf16[8,160,256]{2,1,0:...) custom-call(f32[8,13]{1,0:T(8,128)S(1)} %copy-done, f32[9]{0:T(128)S(1)} %copy-done.1, ...), custom_call_target="tpu_custom_call" | custom-call | flops 2000000000 | bytes 2000000 | tf_op jit(solution)/shard_map/bands/pallas_call | solution.py:230
  20.1 0.8 copy-done.2
  21.0 0.8 copy-done.4
  21.7 0.7 copy-done.11
  22.5 0.7 copy-done.18
  23.2 7.2 %frame_side.3 = bf16[32,16,1024]{2,1,0:T(8,128)(2,1)} custom-call(s32[1,2]{1,0:T(1,128)} %order_ref.2, s32[64]{0:T(128)} %offset_ref.3, f32[64]{0:T(128)} %fraction_ref.3, bf16[2,256,2048]{2,1,0:T(8,128)(2,1)} %raw_next.3, bf16[2,256,2048]{2,1,0:T(8,128)(2,1)} %raw_next.3, bf16[2,256,2048]{2,1,0:T(8,128)(2,1)} %raw_next.3, bf16[256,2048]{1,0:T(8,128)(2,1)} %dark_next.3, ...), custom_call_target="tpu_custom_call" | custom-call | flops 8000000000 | bytes 6500000 | tf_op jit(solution)/shard_map/frame_side/pallas_call | solution.py:120
  30.4 15.3 %all-to-all-done.refs_0_.refs_1_ = bf16[32,16,1024]{2,1,0:T(8,128)(2,1)S(1)} async-done(((bf16[32,16,1024]{2,1,0:T(8,128)(2,1)}), bf16[32,16,1024]{2,1,0:T(8,128)(2,1)S(1)}, u32[]{:S(2)}, u32[]{:S(2)}) %all-to-all-start) | async-done | bytes 1048608 | tf_op jit(solution)/shard_map/all_to_all | solution.py:460
  45.7 4.0 %all-to-all-start.1 = ((bf16[32,16,1024]{2,1,0:T(8,128)(2,1)}), bf16[32,16,1024]{2,1,0:T(8,128)(2,1)S(1)}, u32[]{:S(2)}, u32[]{:S(2)}) async-start(bf16[32,16,1024]{2,1,0:T(8,128)(2,1)} %frame_side.3), calls=%async_computation.1 | async-start | bytes 2097152 | tf_op jit(solution)/shard_map/all_to_all | solution.py:460
  49.7 0.9 fusion.1
  50.7 4.5 %collective-permute-start.1 = (bf16[12,16,1024]{2,1,0:T(8,128)(2,1)}, bf16[12,16,1024]{2,1,0:T(8,128)(2,1)S(1)}, u32[]{:S(2)}, u32[]{:S(2)}) collective-permute-start(bf16[12,16,1024]{2,1,0:T(8,128)(2,1)} %get-tuple-element.63), channel_id=1, source_target_pairs={{32,0},{64,32},{96,64},{128,96},{160,128},{192,160},{224,192},{33,... | collective-permute-start | bytes 1179656 | tf_op jit(solution)/shard_map/ppermute | solution.py:464
  55.1 2.9 %collective-permute-start = (bf16[12,16,1024]{2,1,0:T(8,128)(2,1)}, bf16[12,16,1024]{2,1,0:T(8,128)(2,1)S(1)}, u32[]{:S(2)}, u32[]{:S(2)}) collective-permute-start(bf16[12,16,1024]{2,1,0:T(8,128)(2,1)} %get-tuple-element.64), channel_id=1, source_target_pairs={{0,32},{32,64},{64,96},{96,128},{128,160},{160,192},{192,224},{1,3... | collective-permute-start | bytes 1179656 | tf_op jit(solution)/shard_map/ppermute | solution.py:463
  58.0 1.0 copy-done.5
  59.0 0.9 copy-done.12
  60.0 0.9 copy-done.15
  60.9 0.9 copy-done.19
  61.9 2.5 %inside.2 = (bf16[16,8,1024]{2,1,0:T(8,128)(2,1)S(1)}, bf16[416,1024]{1,0:T(8,128)(2,1)S(1)}, f32[192,1024]{1,0:T(8,128)S(1)}) custom-call(bf16[32,16,1024]{2,1,0:T(8,128)(2,1)S(1)} %all-to-all-done.refs_0_.refs_1_, bf16[5,160,256]{2,1,0:T(8,128)(2,1)S(1)} %copy-done.5, bf16[3,160,256]{2,1,0:T(8,128)(2,1)S(1)} %copy-done.19, ...), custom_call_target="tpu_custom_call" | custom-call | flops 5000000000 | bytes 8000000 | tf_op jit(solution)/shard_map/inside/pallas_call | solution.py:405
  64.4 0.9 copy-done.7
  65.3 0.9 copy-done.9
  66.2 0.7 copy-done.21
  66.9 11.8 %all-to-all-done.1.refs_1_.refs_4_ = bf16[32,16,1024]{2,1,0:T(8,128)(2,1)S(1)} async-done(((bf16[32,16,1024]{2,1,0:T(8,128)(2,1)}), bf16[32,16,1024]{2,1,0:T(8,128)(2,1)S(1)}, u32[]{:S(2)}, u32[]{:S(2)}) %all-to-all-start.1) | async-done | bytes 1048608 | tf_op jit(solution)/shard_map/all_to_all | solution.py:460
  78.8 4.5 %collective-permute-start.3 = (bf16[12,16,1024]{2,1,0:T(8,128)(2,1)S(1)}, bf16[12,16,1024]{2,1,0:T(8,128)(2,1)S(1)}, u32[]{:S(2)}, u32[]{:S(2)}) collective-permute-start(bf16[12,16,1024]{2,1,0:T(8,128)(2,1)S(1)} %get-tuple-element.61), channel_id=1, source_target_pairs={{32,0},{64,32},{96,64},{128,96},{160,128},{192,160},{224,192},{33,... | collective-permute-start | bytes 1179656 | tf_op jit(solution)/shard_map/ppermute | solution.py:464
  83.3 3.2 %collective-permute-start.2 = (bf16[12,16,1024]{2,1,0:T(8,128)(2,1)S(1)}, bf16[12,16,1024]{2,1,0:T(8,128)(2,1)S(1)}, u32[]{:S(2)}, u32[]{:S(2)}) collective-permute-start(bf16[12,16,1024]{2,1,0:T(8,128)(2,1)S(1)} %get-tuple-element.62), channel_id=1, source_target_pairs={{0,32},{32,64},{64,96},{96,128},{128,160},{160,192},{192,224},{1,3... | collective-permute-start | bytes 1179656 | tf_op jit(solution)/shard_map/ppermute | solution.py:463
  86.5 1.0 copy-done.6
  87.5 0.9 copy-done.13
  88.5 0.9 copy-done.16
  89.4 0.9 copy-done.20
  90.4 3.2 %inside.3 = (bf16[16,8,1280]{2,1,0:T(8,128)(2,1)S(1)}, bf16[416,1280]{1,0:T(8,128)(2,1)S(1)}, f32[192,1280]{1,0:T(8,128)S(1)}) custom-call(bf16[32,16,1024]{2,1,0:T(8,128)(2,1)S(1)} %all-to-all-done.refs_0_.refs_1_, bf16[32,16,1024]{2,1,0:T(8,128)(2,1)S(1)} %all-to-all-done.1.refs_1_.refs_4_, bf16[5,160,256]{2,1,0:T(8,128)(2,1)S(1)} %copy-done.6, ...), custom_call_target="tpu_custom_call" | custom-call | flops 5000000000 | bytes 8000000 | tf_op jit(solution)/shard_map/inside/pallas_call | solution.py:405
  93.7 3.2 %ends.2.refs_13_ = bf16[64,8,896]{2,1,0:T(8,128)(2,1)S(1)} custom-call(bf16[12,16,1024]{2,1,0:T(8,128)(2,1)S(1)} %collective-permute-done.refs_0_, bf16[32,16,1024]{2,1,0:T(8,128)(2,1)S(1)} %all-to-all-done.refs_0_.refs_1_, bf16[12,16,1024]{2,1,0:T(8,128)(2,1)S(1)} %collective-permute-done.1.refs_2_, ...), custom_call_target="tpu_custom_call" | custom-call | flops 5000000000 | bytes 8000000 | tf_op jit(solution)/shard_map/ends/pallas_call | solution.py:405
  96.9 4.8 %collective-permute-done.3.refs_5_ = bf16[12,16,1024]{2,1,0:T(8,128)(2,1)S(1)} collective-permute-done((bf16[12,16,1024]{2,1,0:T(8,128)(2,1)S(1)}, bf16[12,16,1024]{2,1,0:T(8,128)(2,1)S(1)}, u32[]{:S(2)}, u32[]{:S(2)}) %collective-permute-start.3) | collective-permute-done | bytes 393248 | tf_op jit(solution)/shard_map/ppermute | solution.py:464
  101.7 5.2 %ends.3 = bf16[64,8,2048]{2,1,0:T(8,128)(2,1)} custom-call(bf16[12,16,1024]{2,1,0:T(8,128)(2,1)S(1)} %collective-permute-done.refs_0_, bf16[32,16,1024]{2,1,0:T(8,128)(2,1)S(1)} %all-to-all-done.refs_0_.refs_1_, bf16[12,16,1024]{2,1,0:T(8,128)(2,1)S(1)} %collective-permute-done.1.refs_2_, bf16[12,16,1024]{2,1,0:T(8,128)(2,1)S(1)} %collective-permute-done.2.refs_3_, ...), custom_call_target="tpu_custom_call" | custom-call | flops 5000000000 | bytes 8000000 | tf_op jit(solution)/shard_map/ends/pallas_call | solution.py:405
  (40 shorter events, 0.4 us)
Async XLA Ops:
  6.5 10.3 %copy-start.23 = (s32[512]{0:T(512)S(1)}, s32[512]{0:T(512)}, u32[]{:S(2)}) copy-start(s32[512]{0:T(512)} %param.17) | copy-start | bytes 6148
  6.5 10.6 %copy-start = (f32[8,13]{1,0:T(8,128)S(1)}, f32[8,13]{1,0:T(8,128)}, u32[]{:S(2)}) copy-start(f32[8,13]{1,0:T(8,128)} %psf_ref.1) | copy-start | bytes 1252
  6.5 10.6 %copy-start.1 = (f32[9]{0:T(128)S(1)}, f32[9]{0:T(128)}, u32[]{:S(2)}) copy-start(f32[9]{0:T(128)} %lateral_ref.1) | copy-start | bytes 112
  6.5 39.2 %all-to-all-start = ((bf16[32,16,1024]{2,1,0:T(8,128)(2,1)}), bf16[32,16,1024]{2,1,0:T(8,128)(2,1)S(1)}, u32[]{:S(2)}, u32[]{:S(2)}) async-start(bf16[32,16,1024]{2,1,0:T(8,128)(2,1)} %frame_side.2), calls=%async_computation | async-start | bytes 2097152 | tf_op jit(solution)/shard_map/all_to_all | solution.py:460
  20.1 0.8 copy-start.2
  21.0 0.8 copy-start.4
  21.7 0.7 copy-start.11
  22.5 0.7 copy-start.18
  23.2 7.2 %copy-start.14 = (bf16[512,256]{1,0:T(8,128)(2,1)}, bf16[512,256]{1,0:T(8,128)(2,1)S(1)}, u32[]{:S(2)}) copy-start(bf16[512,256]{1,0:T(8,128)(2,1)S(1)} %get-tuple-element.54.refs_4_.refs_5_.refs_6_.refs_9_) | copy-start | bytes 786436
  45.7 33.0 %all-to-all-start.1 = ((bf16[32,16,1024]{2,1,0:T(8,128)(2,1)}), bf16[32,16,1024]{2,1,0:T(8,128)(2,1)S(1)}, u32[]{:S(2)}, u32[]{:S(2)}) async-start(bf16[32,16,1024]{2,1,0:T(8,128)(2,1)} %frame_side.3), calls=%async_computation.1 | async-start | bytes 2097152 | tf_op jit(solution)/shard_map/all_to_all | solution.py:460
  50.7 43.0 %collective-permute-start.1 = (bf16[12,16,1024]{2,1,0:T(8,128)(2,1)}, bf16[12,16,1024]{2,1,0:T(8,128)(2,1)S(1)}, u32[]{:S(2)}, u32[]{:S(2)}) collective-permute-start(bf16[12,16,1024]{2,1,0:T(8,128)(2,1)} %get-tuple-element.63), channel_id=1, source_target_pairs={{32,0},{64,32},{96,64},{128,96},{160,128},{192,160},{224,192},{33,... | collective-permute-start | bytes 1179656 | tf_op jit(solution)/shard_map/ppermute | solution.py:464
  55.1 38.5 %collective-permute-start = (bf16[12,16,1024]{2,1,0:T(8,128)(2,1)}, bf16[12,16,1024]{2,1,0:T(8,128)(2,1)S(1)}, u32[]{:S(2)}, u32[]{:S(2)}) collective-permute-start(bf16[12,16,1024]{2,1,0:T(8,128)(2,1)} %get-tuple-element.64), channel_id=1, source_target_pairs={{0,32},{32,64},{64,96},{96,128},{128,160},{160,192},{192,224},{1,3... | collective-permute-start | bytes 1179656 | tf_op jit(solution)/shard_map/ppermute | solution.py:463
  58.0 1.0 copy-start.5
  59.0 0.9 copy-start.12
  60.0 0.9 copy-start.15
  60.9 0.9 copy-start.19
  64.4 0.9 copy-start.7
  65.3 0.9 copy-start.9
  66.2 0.7 copy-start.21
  78.8 22.9 %collective-permute-start.3 = (bf16[12,16,1024]{2,1,0:T(8,128)(2,1)S(1)}, bf16[12,16,1024]{2,1,0:T(8,128)(2,1)S(1)}, u32[]{:S(2)}, u32[]{:S(2)}) collective-permute-start(bf16[12,16,1024]{2,1,0:T(8,128)(2,1)S(1)} %get-tuple-element.61), channel_id=1, source_target_pairs={{32,0},{64,32},{96,64},{128,96},{160,128},{192,160},{224,192},{33,... | collective-permute-start | bytes 1179656 | tf_op jit(solution)/shard_map/ppermute | solution.py:464
  83.3 10.3 %copy-start.3 = (bf16[8,160,256]{2,1,0:T(8,128)(2,1)S(1)}, bf16[8,160,256]{2,1,0:T(8,128)(2,1)}, u32[]{:S(2)}) copy-start(bf16[8,160,256]{2,1,0:T(8,128)(2,1)} %copy-done.2) | copy-start | bytes 1966084
  83.3 18.4 %collective-permute-start.2 = (bf16[12,16,1024]{2,1,0:T(8,128)(2,1)S(1)}, bf16[12,16,1024]{2,1,0:T(8,128)(2,1)S(1)}, u32[]{:S(2)}, u32[]{:S(2)}) collective-permute-start(bf16[12,16,1024]{2,1,0:T(8,128)(2,1)S(1)} %get-tuple-element.62), channel_id=1, source_target_pairs={{0,32},{32,64},{64,96},{96,128},{128,160},{160,192},{192,224},{1,3... | collective-permute-start | bytes 1179656 | tf_op jit(solution)/shard_map/ppermute | solution.py:463
  86.5 1.0 copy-start.6
  87.5 0.9 copy-start.13
  88.5 0.9 copy-start.16
  89.4 0.9 copy-start.20
  90.4 3.3 %copy-start.8 = (bf16[416,1024]{1,0:T(8,128)(2,1)S(1)}, bf16[416,1024]{1,0:T(8,128)(2,1)}, u32[]{:S(2)}) copy-start(bf16[416,1024]{1,0:T(8,128)(2,1)} %copy-done.7) | copy-start | bytes 2555908
  90.4 3.3 %copy-start.10 = (f32[192,1024]{1,0:T(8,128)S(1)}, f32[192,1024]{1,0:T(8,128)}, u32[]{:S(2)}) copy-start(f32[192,1024]{1,0:T(8,128)} %copy-done.9) | copy-start | bytes 2359300
  90.4 3.3 %copy-start.17 = (bf16[512,256]{1,0:T(8,128)(2,1)S(1)}, bf16[512,256]{1,0:T(8,128)(2,1)}, u32[]{:S(2)}) copy-start(bf16[512,256]{1,0:T(8,128)(2,1)} %copy-done.14) | copy-start | bytes 786436
  90.4 3.3 %copy-start.22 = (bf16[16,8,1024]{2,1,0:T(8,128)(2,1)S(1)}, bf16[16,8,1024]{2,1,0:T(8,128)(2,1)}, u32[]{:S(2)}) copy-start(bf16[16,8,1024]{2,1,0:T(8,128)(2,1)} %copy-done.21) | copy-start | bytes 786436

commit v8 on v7

--- a/solution.py
+++ b/solution.py
@@ -19,7 +19,8 @@
 SPLIT = 1024
 VMEM = 60 * 1024 * 1024
 BANDS_VMEM = 20 * 1024 * 1024
-RESTORE_VMEM = 42 * 1024 * 1024
+RESTORE_VMEM = 30 * 1024 * 1024
+LATER_VMEM = 20 * 1024 * 1024
 GROUP = 20
 SPAN = 32
 
@@ -108,6 +109,8 @@
     last = frame_rows // 16 - 1
     smem = pl.BlockSpec(memory_space=pltpu.SMEM)
     first, count = lo // LANES, (hi - lo) // LANES
+    if lo == 0:
+        columns = hi
 
     def three(lead):
         zeros = (0,) * len(lead)
@@ -122,14 +125,14 @@
         grid=(steps,),
         in_specs=[smem, smem, smem]
         + three((2,)) + three(()) + three(())
-        + [pl.BlockSpec(band.shape, lambda i: (0, 0))],
+        + [pl.BlockSpec((band.shape[0], columns), lambda i: (0, 0))],
         out_specs=pl.BlockSpec((BLOCK_ROWS // ROWS, 2 * ROWS, hi - lo), lambda i: (i, 0, 0)),
         out_shape=jax.ShapeDtypeStruct((bricks, 2 * ROWS, hi - lo), jnp.bfloat16),
         scratch_shapes=[
             pltpu.VMEM((2, BLOCK_ROWS, (LEAD + count) * LANES), jnp.float32),
             pltpu.VMEM((2, min(first, LEAD) + count, BLOCK_ROWS + 16, LANES), jnp.float32),
         ],
-        compiler_params=pltpu.CompilerParams(vmem_limit_bytes=VMEM),
+        compiler_params=pltpu.CompilerParams(vmem_limit_bytes=VMEM if lo == 0 else LATER_VMEM),
         cost_estimate=pl.CostEstimate(
             flops=8_000_000_000, bytes_accessed=6_500_000, transcendentals=0
         ),
@@ -243,7 +246,7 @@
     )(psf_bank, lateral_psf, index)
 
 
-def restore_kernel(plan, inside, counts, merge, cut, *refs):
+def restore_kernel(plan, inside, counts, cut, *refs):
     parts = []
     for count in counts:
         parts.append(refs[:count])
@@ -254,12 +257,15 @@
     bf16 = jnp.bfloat16
     half = plan[0][0][0][0] if not inside else plan[1][0][0][0] - plan[0][0][0][0]
     halo = 2 * ITERS * half
+    if not inside:
+        q_in, e_in = refs[:2]
+        refs = refs[2:]
+    buffers = refs[-8:]
+    mf, ef, mb, qb, pad, pad_back, done, sems = buffers
     if inside:
-        out, q_out, e_out, mf, ef, mb, qb, pad, pad_back = refs
+        canvas, q_out, e_out = refs[-11:-8]
     else:
-        q_in, e_in, middle = refs[:3]
-        earlier = refs[3] if merge else None
-        out, mf, ef, mb, qb, pad, pad_back = refs[3 + merge :]
+        canvas = refs[-9]
     size, columns = mf.shape
     total = size // ROWS
     tiles = columns // TILE
@@ -270,12 +276,13 @@
 
     at_column = 0
     for part in parts:
-        width = part[0].shape[-1]
+        width = part[0].shape[-1] if part is parts[-1] else 2 * LANES
+        skip = part[0].shape[-1] - width
         at_row = halo * ROWS if inside else 0
         for ref in part:
             height = ref.shape[0] * ref.shape[1]
             for col in range(0, width, TILE):
-                whole = ref[:, :, col : col + TILE].reshape(height, TILE)
+                whole = ref[:, :, skip + col : skip + col + TILE].reshape(height, TILE)
                 there = slice(at_column + col, at_column + col + TILE)
                 mb[at_row : at_row + height, there] = whole
                 mf[at_row : at_row + height, there] = whole.astype(f32)
@@ -292,8 +299,11 @@
             e = e_in[number * e_width : (number + 1) * e_width, :]
             ef[start : start + e_width, :] = e
             mb[start : start + e_width, :] = e.astype(bf16)
-        for lo in range(0, out.shape[-1] if not merge else 0, LANES):
-            out[half * 4 : out.shape[0] - half * 4, :, lo : lo + LANES] = middle[:, :, lo : lo + LANES]
+
+    copies = []
+    base = canvas.shape[-1] - columns if cut else 0
+    limit = canvas.shape[-1] if cut else columns - LANES
+    top = ITERS * 2 * half
 
     def columns_of(tile):
         return slice(tile * TILE, (tile + 1) * TILE)
@@ -343,13 +353,21 @@
                     ef[rows, cols] = e
                     mb[rows, cols] = e.astype(bf16)
                     continue
-                e = e.reshape(-1, ROWS, TILE).astype(bf16)
-                first = groups[0][0] - plan[-1][0][0][0]
-                start = (out.shape[-1] - columns if cut else 0) + tile * TILE
+                start = base + tile * TILE
                 drop = cut if tile == 0 else 0
-                keep = min(TILE, out.shape[-1] - start)
+                keep = min(TILE, limit - start)
                 if keep > drop:
-                    out[first : first + e.shape[0], :, start + drop : start + keep] = e[:, :, drop:keep]
+                    first, count = groups[0][0] - top, e.shape[0] // ROWS
+                    where = (slice(first, first + count), slice(None))
+                    here = slice(tile * TILE + drop, tile * TILE + keep)
+                    done[where + (here,)] = e.reshape(-1, ROWS, TILE)[:, :, drop:keep].astype(bf16)
+                    copy = pltpu.make_async_copy(
+                        done.at[where + (here,)],
+                        canvas.at[where + (slice(start + drop, start + keep),)],
+                        sems.at[len(copies)],
+                    )
+                    copy.start()
+                    copies.append(copy)
 
         for step in range(tiles + 5):
             if step < tiles:
@@ -365,49 +383,39 @@
         q_out[...] = qb[q_rows, :]
         e_out[:e_width, :] = ef[e_low : e_low + e_width, :]
         e_out[e_width:, :] = ef[e_high : e_high + e_width, :]
-    elif merge:
-        kept = earlier.shape[-1]
-        out[:, :, :kept] = earlier[...]
-        out[half * 4 : out.shape[0] - half * 4, :, kept:] = middle[:, :, columns - (out.shape[-1] - kept) :]
-
-
-def restore(parts, matrices, state, earlier, plan, inside, planes, half, columns):
-    merge = earlier is not None
-    operands, specs, width = [], [], 0
-    for number, part in enumerate(parts):
-        kept = 2 * LANES if number < len(parts) - 1 else part[0].shape[-1]
-        for array in part:
-            block = array.shape[:2] + (kept,)
-            index = (0, 0, array.shape[-1] // kept - 1)
-            operands.append(array)
-            specs.append(pl.BlockSpec(block, lambda i, index=index: index))
-        width += kept
-
-    def whole(array):
-        return pl.BlockSpec(array.shape, lambda i: (0,) * len(array.shape))
-
-    for array in (*matrices, *state, *([earlier] if merge else [])):
-        operands.append(array)
-        specs.append(whole(array))
+    for copy in copies:
+        copy.wait()
+
+
+def restore(parts, matrices, state, canvas, plan, inside, planes, half, columns):
+    later = len(parts) > 1
+    width = parts[-1][0].shape[-1] + (2 * LANES if later else 0)
     halo = 2 * ITERS * half
     height = (planes + 2 * halo) * ROWS
     bf16 = jnp.bfloat16
+    vmem = pl.BlockSpec(memory_space=pltpu.VMEM)
+    hbm = pl.BlockSpec(memory_space=pltpu.HBM)
+    operands = [array for part in parts for array in part] + [*matrices, *state]
+    specs = [vmem] * len(operands)
+    aliases = {}
+    if canvas is not None:
+        aliases = {len(operands): 0}
+        operands.append(canvas)
+        specs.append(hbm)
+    results = [jax.ShapeDtypeStruct((planes, ROWS, columns), bf16)]
     if inside:
-        cut = 0
-        results = [
-            jax.ShapeDtypeStruct((planes - 2 * halo, ROWS, width), bf16),
+        results += [
             jax.ShapeDtypeStruct(((planes - 2 * half) * ROWS, width), bf16),
             jax.ShapeDtypeStruct((2 * half * (2 * ITERS - 2) * ROWS, width), jnp.float32),
         ]
-    else:
-        cut = LANES if merge else 0
-        results = [jax.ShapeDtypeStruct((planes, ROWS, columns if merge else width - LANES), bf16)]
     return pl.pallas_call(
-        functools.partial(restore_kernel, plan, inside, [len(part) for part in parts], merge, cut),
-        grid=(1,),
+        functools.partial(
+            restore_kernel, plan, inside, [len(part) for part in parts], LANES if later else 0
+        ),
         in_specs=specs,
-        out_specs=[whole(result) for result in results],
+        out_specs=[hbm] + [vmem] * (len(results) - 1),
         out_shape=results,
+        input_output_aliases=aliases,
         scratch_shapes=[
             pltpu.VMEM((height, width), jnp.float32),
             pltpu.VMEM((height, width), jnp.float32),
@@ -415,6 +423,8 @@
             pltpu.VMEM((height, width), bf16),
             pltpu.VMEM((height, width + 2 * LANES), bf16),
             pltpu.VMEM((height, width + 2 * LANES), bf16),
+            pltpu.VMEM((planes, ROWS, width), bf16),
+            pltpu.SemaphoreType.DMA((2 * (width // TILE),)),
         ],
         compiler_params=pltpu.CompilerParams(vmem_limit_bytes=RESTORE_VMEM),
         cost_estimate=pl.CostEstimate(
@@ -464,27 +474,25 @@
         high = lax.ppermute(centre[:depth], "cam", backward)
         return low, centre, high
 
-    def inside(centres):
-        middle, quotients, estimates = restore(
-            centres, inner_matrices, (), None, inner, True, planes, half, columns
+    def inside(centres, canvas):
+        canvas, *state = restore(
+            centres, inner_matrices, (), canvas, inner, True, planes, half, columns
         )
-        return quotients, estimates, middle
-
-    def ends(parts, state, earlier):
-        return restore(
-            parts, outer_matrices, state, earlier, outer, False, planes, half, columns
-        )[0]
+        return canvas, state
+
+    def ends(parts, state, canvas):
+        return restore(parts, outer_matrices, state, canvas, outer, False, planes, half, columns)[0]
 
     first, second_piece, inner_matrices, outer_matrices = lax.optimization_barrier(
         (exchange(first_piece), second_piece, inner_matrices, outer_matrices)
     )
     first_part = with_halo(first)
-    first_state = inside([(first,)])
+    canvas, first_state = inside([(first,)], None)
     second, first_state = lax.optimization_barrier((exchange(second_piece), first_state))
     second_part = with_halo(second)
-    second_state = inside([(first,), (second,)])
-    result = ends([first_part], first_state, None)
-    return ends([first_part, second_part], second_state, result)
+    canvas, second_state = inside([(first,), (second,)], canvas)
+    canvas = ends([first_part], first_state, canvas)
+    return ends([first_part, second_part], second_state, canvas)
 
 
 def solution(mesh):

time: 109 us -> 108 us (level)
  starting transfers between devices: 29.2 us -> 30.9 us
  waiting for transfers between devices: 32 us -> 30.4 us
    pallas_call x2, Pallas kernels: 13.7 us -> 11.7 us  [frame_side(): pl.pallas_call(functools.partial(frame_kernel, first, count), grid=(steps...]
    ppermute x2, starting transfers between devices: 6.11 us -> 7.81 us  [with_halo(): low = lax.ppermute(centre[-depth:], 'cam', forward)]
    pallas_call x4, Pallas kernels: 14.1 us -> 15.6 us  [restore(): pl.pallas_call(functools.partial(restore_kernel, plan, inside, [len(part)...]
    ppermute x2, waiting for transfers between devices: 4.85 us -> 3.61 us  [with_halo(): high = lax.ppermute(centre[:depth], 'cam', backward)]
    unnamed x48 -> x56, local copies, waits for them, and re-layouts: 13.3 us -> 13.2 us
  transfers between devices with their start and end apart: 6 -> 6, of which waited for: 3 -> 3; matrix products, arithmetic and copies ran while one was open for 1% -> 1% of each run, Pallas kernels for 18% -> 19%
where the time goes in v8:
time: 108 us; the launch traced here: 107 us
  starting transfers between devices  30.9 us (29%)
  waiting for transfers between devices  30.4 us (28%)
  Pallas kernels  30.3 us (28%)
  local copies, waits for them, and re-layouts  14.5 us (13%)
    all_to_all x2, waiting for transfers between devices, exchange(): lax.all_to_all(piece, 'brick', split_axis=0, concat_axis=0, tiled=True)  26.8 us
    pallas_call x4, Pallas kernels, restore(): pl.pallas_call(functools.partial(restore_kernel, plan, inside, [len(part)...  15.6 us
    all_to_all x2, starting transfers between devices, exchange(): lax.all_to_all(piece, 'brick', split_axis=0, concat_axis=0, tiled=True)  14.2 us
    unnamed x56, local copies, waits for them, and re-layouts  13.2 us
    pallas_call x2, Pallas kernels, frame_side(): pl.pallas_call(functools.partial(frame_kernel, first, count), grid=(steps...  11.7 us
    ppermute x2, starting transfers between devices, with_halo(): high = lax.ppermute(centre[:depth], 'cam', backward)  8.85 us
    ppermute x2, starting transfers between devices, with_halo(): low = lax.ppermute(centre[-depth:], 'cam', forward)  7.81 us
    ppermute x2, waiting for transfers between devices, with_halo(): high = lax.ppermute(centre[:depth], 'cam', backward)  3.61 us
  transfers between devices with their start and end apart: 6, of which 3 were waited for; matrix products, arithmetic and copies ran while one was open for 1% of the time, Pallas kernels for 19%

profile of v8, /device:TPU:14, one launch (start us, length us, event | category | flops | bytes accessed | tf_op | source)
XLA Modules:
  0.0 106.6 jit_solution(11257416769676778567)
XLA Ops:
  0.0 5.8 %frame_side.2 = bf16[32,16,1024]{2,1,0:T(8,128)(2,1)} custom-call(s32[1,2]{1,0:T(1,128)} %order_ref.2, s32[64]{0:T(128)} %offset_ref.3, f32[64]{0:T(128)} %fraction_ref.3, bf16[2,256,2048]{2,1,0:T(8,128)(2,1)} %raw_next.3, bf16[2,256,2048]{2,1,0:T(8,128)(2,1)} %raw_next.3, bf16[2,256,2048]{2,1,0:T(8,128)(2,1)} %raw_next.3, bf16[256,2048]{1,0:T(8,128)(2,1)} %dark_next.3, ...), custom_call_target="tpu_custom_call" | custom-call | flops 8000000000 | bytes 6500000 | tf_op jit(solution)/shard_map/frame_side/pallas_call | solution.py:123
  5.8 10.2 %all-to-all-start = ((bf16[32,16,1024]{2,1,0:T(8,128)(2,1)}), bf16[32,16,1024]{2,1,0:T(8,128)(2,1)S(1)}, u32[]{:S(2)}, u32[]{:S(2)}) async-start(bf16[32,16,1024]{2,1,0:T(8,128)(2,1)} %frame_side.2), calls=%async_computation | async-start | bytes 2097152 | tf_op jit(solution)/shard_map/all_to_all | solution.py:470
  16.4 3.0 %bands.1 = (bf16[5,160,256]{2,1,0:T(8,128)(2,1)S(1)}, bf16[3,160,256]{2,1,0:T(8,128)(2,1)S(1)}, bf16[8,160,256]{2,1,0:T(8,128)(2,1)S(1)}, bf16[8,160,256]{2,1,0:...) custom-call(f32[8,13]{1,0:T(8,128)S(1)} %copy-done.4, f32[9]{0:T(128)S(1)} %copy-done.5, ...), custom_call_target="tpu_custom_call" | custom-call | flops 2000000000 | bytes 2000000 | tf_op jit(solution)/shard_map/bands/pallas_call | solution.py:233
  19.5 0.8 copy-done.9
  20.3 0.7 copy-done.15
  21.1 0.7 copy-done.18
  21.8 0.7 copy-done.21
  22.5 0.7 copy-done.24
  23.2 5.9 %frame_side.3 = bf16[32,16,1024]{2,1,0:T(8,128)(2,1)} custom-call(s32[1,2]{1,0:T(1,128)S(1)} %copy-done.6, s32[64]{0:T(128)S(1)} %copy-done.7, f32[64]{0:T(128)S(1)} %copy-done.8, bf16[2,256,2048]{2,1,0:T(8,128)(2,1)S(1)} %copy-done, bf16[2,256,2048]{2,1,0:T(8,128)(2,1)S(1)} %copy-done, bf16[2,256,2048]{2,1,0:T(8,128)(2,1)S(1)} %copy-done, ...), custom_call_target="tpu_custom_call" | custom-call | flops 8000000000 | bytes 6500000 | tf_op jit(solution)/shard_map/frame_side/pallas_call | solution.py:123
  29.2 15.8 %all-to-all-done.refs_0_.refs_1_ = bf16[32,16,1024]{2,1,0:T(8,128)(2,1)S(1)} async-done(((bf16[32,16,1024]{2,1,0:T(8,128)(2,1)}), bf16[32,16,1024]{2,1,0:T(8,128)(2,1)S(1)}, u32[]{:S(2)}, u32[]{:S(2)}) %all-to-all-start) | async-done | bytes 1048608 | tf_op jit(solution)/shard_map/all_to_all | solution.py:470
  45.0 4.0 %all-to-all-start.1 = ((bf16[32,16,1024]{2,1,0:T(8,128)(2,1)}), bf16[32,16,1024]{2,1,0:T(8,128)(2,1)S(1)}, u32[]{:S(2)}, u32[]{:S(2)}) async-start(bf16[32,16,1024]{2,1,0:T(8,128)(2,1)} %frame_side.3), calls=%async_computation.1 | async-start | bytes 2097152 | tf_op jit(solution)/shard_map/all_to_all | solution.py:470
  49.0 0.9 fusion.1
  49.9 4.2 %collective-permute-start = (bf16[12,16,1024]{2,1,0:T(8,128)(2,1)}, bf16[12,16,1024]{2,1,0:T(8,128)(2,1)S(1)}, u32[]{:S(2)}, u32[]{:S(2)}) collective-permute-start(bf16[12,16,1024]{2,1,0:T(8,128)(2,1)} %get-tuple-element.62), channel_id=1, source_target_pairs={{0,32},{32,64},{64,96},{96,128},{128,160},{160,192},{192,224},{1,3... | collective-permute-start | bytes 1179656 | tf_op jit(solution)/shard_map/ppermute | solution.py:473
  54.1 4.0 %collective-permute-start.1 = (bf16[12,16,1024]{2,1,0:T(8,128)(2,1)}, bf16[12,16,1024]{2,1,0:T(8,128)(2,1)S(1)}, u32[]{:S(2)}, u32[]{:S(2)}) collective-permute-start(bf16[12,16,1024]{2,1,0:T(8,128)(2,1)} %get-tuple-element.61), channel_id=1, source_target_pairs={{32,0},{64,32},{96,64},{128,96},{160,128},{192,160},{224,192},{33,... | collective-permute-start | bytes 1179656 | tf_op jit(solution)/shard_map/ppermute | solution.py:474
  58.2 1.0 copy-done.16
  59.2 0.9 copy-done.19
  60.1 0.9 copy-done.22
  61.1 0.9 copy-done.25
  62.0 3.2 %inside.2 = (bf16[64,8,2048]{2,1,0:T(8,128)(2,1)}, bf16[416,1024]{1,0:T(8,128)(2,1)S(1)}, f32[192,1024]{1,0:T(8,128)S(1)}) custom-call(bf16[32,16,1024]{2,1,0:T(8,128)(2,1)S(1)} %all-to-all-done.refs_0_.refs_1_, bf16[5,160,256]{2,1,0:T(8,128)(2,1)S(1)} %copy-done.16, bf16[3,160,256]{2,1,0:T(8,128)(2,1)S(1)} %copy-done.25, bf16[512,256]{1,0:T(8,128)(2,1)S(1)} %copy-done.19, ...), custom_call_target="tpu_custom_call" | custom-call | flops 5000000000 | bytes 8000000 | tf_op jit(solution)/shard_map/inside/pallas_call | solution.py:411
  65.2 0.9 copy-done.11
  66.1 0.9 copy-done.13
  67.0 11.0 %all-to-all-done.1.refs_1_.refs_4_ = bf16[32,16,1024]{2,1,0:T(8,128)(2,1)S(1)} async-done(((bf16[32,16,1024]{2,1,0:T(8,128)(2,1)}), bf16[32,16,1024]{2,1,0:T(8,128)(2,1)S(1)}, u32[]{:S(2)}, u32[]{:S(2)}) %all-to-all-start.1) | async-done | bytes 1048608 | tf_op jit(solution)/shard_map/all_to_all | solution.py:470
  78.1 3.6 %collective-permute-start.2 = (bf16[12,16,1024]{2,1,0:T(8,128)(2,1)S(1)}, bf16[12,16,1024]{2,1,0:T(8,128)(2,1)S(1)}, u32[]{:S(2)}, u32[]{:S(2)}) collective-permute-start(bf16[12,16,1024]{2,1,0:T(8,128)(2,1)S(1)} %get-tuple-element.60), channel_id=1, source_target_pairs={{0,32},{32,64},{64,96},{96,128},{128,160},{160,192},{192,224},{1,3... | collective-permute-start | bytes 1179656 | tf_op jit(solution)/shard_map/ppermute | solution.py:473
  81.7 4.8 %collective-permute-start.3 = (bf16[12,16,1024]{2,1,0:T(8,128)(2,1)S(1)}, bf16[12,16,1024]{2,1,0:T(8,128)(2,1)S(1)}, u32[]{:S(2)}, u32[]{:S(2)}) collective-permute-start(bf16[12,16,1024]{2,1,0:T(8,128)(2,1)S(1)} %get-tuple-element.59), channel_id=1, source_target_pairs={{32,0},{64,32},{96,64},{128,96},{160,128},{192,160},{224,192},{33,... | collective-permute-start | bytes 1179656 | tf_op jit(solution)/shard_map/ppermute | solution.py:474
  86.5 1.0 copy-done.17
  87.5 0.9 copy-done.20
  88.5 0.9 copy-done.23
  89.4 0.9 copy-done.26
  90.4 3.9 %inside.3 = (bf16[64,8,2048]{2,1,0:T(8,128)(2,1)}, bf16[416,1280]{1,0:T(8,128)(2,1)S(1)}, f32[192,1280]{1,0:T(8,128)S(1)}) custom-call(bf16[32,16,1024]{2,1,0:T(8,128)(2,1)S(1)} %all-to-all-done.refs_0_.refs_1_, bf16[32,16,1024]{2,1,0:T(8,128)(2,1)S(1)} %all-to-all-done.1.refs_1_.refs_4_, ...), custom_call_target="tpu_custom_call", output_to_operand_aliasing={{0}: (6, {})} | custom-call | flops 5000000000 | bytes 8000000 | tf_op jit(solution)/shard_map/inside/pallas_call | solution.py:411
  94.4 3.9 %ends.2.refs_12_ = bf16[64,8,2048]{2,1,0:T(8,128)(2,1)} custom-call(bf16[12,16,1024]{2,1,0:T(8,128)(2,1)S(1)} %collective-permute-done.refs_0_, bf16[32,16,1024]{2,1,0:T(8,128)(2,1)S(1)} %all-to-all-done.refs_0_.refs_1_, bf16[12,16,1024]{2,1,0:T(8,128)(2,1)S(1)} %collective-permute-done.1.refs_2_, ...), custom_call_target="tpu_custom_call", output_to_operand_aliasing={{}: (9, {})} | custom-call | flops 5000000000 | bytes 8000000 | tf_op jit(solution)/shard_map/ends/pallas_call | solution.py:411
  98.3 3.6 %collective-permute-done.3.refs_5_ = bf16[12,16,1024]{2,1,0:T(8,128)(2,1)S(1)} collective-permute-done((bf16[12,16,1024]{2,1,0:T(8,128)(2,1)S(1)}, bf16[12,16,1024]{2,1,0:T(8,128)(2,1)S(1)}, u32[]{:S(2)}, u32[]{:S(2)}) %collective-permute-start.3) | collective-permute-done | bytes 393248 | tf_op jit(solution)/shard_map/ppermute | solution.py:474
  101.9 4.6 %ends.3 = bf16[64,8,2048]{2,1,0:T(8,128)(2,1)} custom-call(bf16[12,16,1024]{2,1,0:T(8,128)(2,1)S(1)} %collective-permute-done.refs_0_, bf16[32,16,1024]{2,1,0:T(8,128)(2,1)S(1)} %all-to-all-done.refs_0_.refs_1_, bf16[12,16,1024]{2,1,0:T(8,128)(2,1)S(1)} %collective-permute-done.1.refs_2_, ...), custom_call_target="tpu_custom_call", output_to_operand_aliasing={{}: (12, {})} | custom-call | flops 5000000000 | bytes 8000000 | tf_op jit(solution)/shard_map/ends/pallas_call | solution.py:411
  (48 shorter events, 0.5 us)
Async XLA Ops:
  5.8 10.3 %copy-start.27 = (s32[512]{0:T(512)S(1)}, s32[512]{0:T(512)}, u32[]{:S(2)}) copy-start(s32[512]{0:T(512)} %param.17) | copy-start | bytes 6148
  5.8 10.6 %copy-start.4 = (f32[8,13]{1,0:T(8,128)S(1)}, f32[8,13]{1,0:T(8,128)}, u32[]{:S(2)}) copy-start(f32[8,13]{1,0:T(8,128)} %psf_ref.1) | copy-start | bytes 1252
  5.8 10.6 %copy-start.5 = (f32[9]{0:T(128)S(1)}, f32[9]{0:T(128)}, u32[]{:S(2)}) copy-start(f32[9]{0:T(128)} %lateral_ref.1) | copy-start | bytes 112
  5.8 39.2 %all-to-all-start = ((bf16[32,16,1024]{2,1,0:T(8,128)(2,1)}), bf16[32,16,1024]{2,1,0:T(8,128)(2,1)S(1)}, u32[]{:S(2)}, u32[]{:S(2)}) async-start(bf16[32,16,1024]{2,1,0:T(8,128)(2,1)} %frame_side.2), calls=%async_computation | async-start | bytes 2097152 | tf_op jit(solution)/shard_map/all_to_all | solution.py:470
  16.4 6.8 %copy-start = (bf16[2,256,2048]{2,1,0:T(8,128)(2,1)S(1)}, bf16[2,256,2048]{2,1,0:T(8,128)(2,1)}, u32[]{:S(2)}) copy-start(bf16[2,256,2048]{2,1,0:T(8,128)(2,1)} %raw_next.3) | copy-start | bytes 6291460
  16.4 6.8 %copy-start.1 = (bf16[256,2048]{1,0:T(8,128)(2,1)S(1)}, bf16[256,2048]{1,0:T(8,128)(2,1)}, u32[]{:S(2)}) copy-start(bf16[256,2048]{1,0:T(8,128)(2,1)} %dark_next.3) | copy-start | bytes 3145732
  16.4 6.8 %copy-start.2 = (bf16[256,2048]{1,0:T(8,128)(2,1)S(1)}, bf16[256,2048]{1,0:T(8,128)(2,1)}, u32[]{:S(2)}) copy-start(bf16[256,2048]{1,0:T(8,128)(2,1)} %gain_next.3) | copy-start | bytes 3145732
  16.4 6.8 %copy-start.3 = (f32[9,2048]{1,0:T(8,128)S(1)}, f32[9,2048]{1,0:T(8,128)}, u32[]{:S(2)}) copy-start(f32[9,2048]{1,0:T(8,128)} %band_ref.3) | copy-start | bytes 221188
  16.4 6.8 %copy-start.6 = (s32[1,2]{1,0:T(1,128)S(1)}, s32[1,2]{1,0:T(1,128)}, u32[]{:S(2)}) copy-start(s32[1,2]{1,0:T(1,128)} %order_ref.2) | copy-start | bytes 28
  16.4 6.8 %copy-start.7 = (s32[64]{0:T(128)S(1)}, s32[64]{0:T(128)}, u32[]{:S(2)}) copy-start(s32[64]{0:T(128)} %offset_ref.3) | copy-start | bytes 772
  16.4 6.8 %copy-start.8 = (f32[64]{0:T(128)S(1)}, f32[64]{0:T(128)}, u32[]{:S(2)}) copy-start(f32[64]{0:T(128)} %fraction_ref.3) | copy-start | bytes 772
  19.5 0.8 copy-start.9
  20.3 0.7 copy-start.15
  21.8 0.7 copy-start.21
  45.0 33.0 %all-to-all-start.1 = ((bf16[32,16,1024]{2,1,0:T(8,128)(2,1)}), bf16[32,16,1024]{2,1,0:T(8,128)(2,1)S(1)}, u32[]{:S(2)}, u32[]{:S(2)}) async-start(bf16[32,16,1024]{2,1,0:T(8,128)(2,1)} %frame_side.3), calls=%async_computation.1 | async-start | bytes 2097152 | tf_op jit(solution)/shard_map/all_to_all | solution.py:470
  49.9 44.4 %collective-permute-start = (bf16[12,16,1024]{2,1,0:T(8,128)(2,1)}, bf16[12,16,1024]{2,1,0:T(8,128)(2,1)S(1)}, u32[]{:S(2)}, u32[]{:S(2)}) collective-permute-start(bf16[12,16,1024]{2,1,0:T(8,128)(2,1)} %get-tuple-element.62), channel_id=1, source_target_pairs={{0,32},{32,64},{64,96},{96,128},{128,160},{160,192},{192,224},{1,3... | collective-permute-start | bytes 1179656 | tf_op jit(solution)/shard_map/ppermute | solution.py:473
  54.1 40.2 %collective-permute-start.1 = (bf16[12,16,1024]{2,1,0:T(8,128)(2,1)}, bf16[12,16,1024]{2,1,0:T(8,128)(2,1)S(1)}, u32[]{:S(2)}, u32[]{:S(2)}) collective-permute-start(bf16[12,16,1024]{2,1,0:T(8,128)(2,1)} %get-tuple-element.61), channel_id=1, source_target_pairs={{32,0},{64,32},{96,64},{128,96},{160,128},{192,160},{224,192},{33,... | collective-permute-start | bytes 1179656 | tf_op jit(solution)/shard_map/ppermute | solution.py:474
  58.2 1.0 copy-start.16
  59.2 0.9 copy-start.19
  60.1 0.9 copy-start.22
  61.1 0.9 copy-start.25
  65.2 0.9 copy-start.11
  66.1 0.9 copy-start.13
  78.1 20.2 %collective-permute-start.2 = (bf16[12,16,1024]{2,1,0:T(8,128)(2,1)S(1)}, bf16[12,16,1024]{2,1,0:T(8,128)(2,1)S(1)}, u32[]{:S(2)}, u32[]{:S(2)}) collective-permute-start(bf16[12,16,1024]{2,1,0:T(8,128)(2,1)S(1)} %get-tuple-element.60), channel_id=1, source_target_pairs={{0,32},{32,64},{64,96},{96,128},{128,160},{160,192},{192,224},{1,3... | collective-permute-start | bytes 1179656 | tf_op jit(solution)/shard_map/ppermute | solution.py:473
  81.7 20.2 %collective-permute-start.3 = (bf16[12,16,1024]{2,1,0:T(8,128)(2,1)S(1)}, bf16[12,16,1024]{2,1,0:T(8,128)(2,1)S(1)}, u32[]{:S(2)}, u32[]{:S(2)}) collective-permute-start(bf16[12,16,1024]{2,1,0:T(8,128)(2,1)S(1)} %get-tuple-element.59), channel_id=1, source_target_pairs={{32,0},{64,32},{96,64},{128,96},{160,128},{192,160},{224,192},{33,... | collective-permute-start | bytes 1179656 | tf_op jit(solution)/shard_map/ppermute | solution.py:474
  86.5 1.0 copy-start.17
  87.5 0.9 copy-start.20
  88.5 0.9 copy-start.23
  89.4 0.9 copy-start.26
  90.4 4.0 %copy-start.10 = (bf16[8,160,256]{2,1,0:T(8,128)(2,1)S(1)}, bf16[8,160,256]{2,1,0:T(8,128)(2,1)}, u32[]{:S(2)}) copy-start(bf16[8,160,256]{2,1,0:T(8,128)(2,1)} %copy-done.9) | copy-start | bytes 1966084
  90.4 4.0 %copy-start.12 = (bf16[416,1024]{1,0:T(8,128)(2,1)S(1)}, bf16[416,1024]{1,0:T(8,128)(2,1)}, u32[]{:S(2)}) copy-start(bf16[416,1024]{1,0:T(8,128)(2,1)} %copy-done.11) | copy-start | bytes 2555908
  90.4 4.0 %copy-start.14 = (f32[192,1024]{1,0:T(8,128)S(1)}, f32[192,1024]{1,0:T(8,128)}, u32[]{:S(2)}) copy-start(f32[192,1024]{1,0:T(8,128)} %copy-done.13) | copy-start | bytes 2359300
  (2 other events, 1.4 us)

commit v9 on v8

--- a/solution.py
+++ b/solution.py
@@ -16,7 +16,7 @@
 ROWS = 8
 BLOCK_ROWS = 64
 LEAD = SHEAR // LANES + 1
-SPLIT = 1024
+CUTS = (1024, 1792)
 VMEM = 60 * 1024 * 1024
 BANDS_VMEM = 20 * 1024 * 1024
 RESTORE_VMEM = 30 * 1024 * 1024
@@ -246,7 +246,7 @@
     )(psf_bank, lateral_psf, index)
 
 
-def restore_kernel(plan, inside, counts, cut, *refs):
+def restore_kernel(plan, inside, counts, base, cut, limit, *refs):
     parts = []
     for count in counts:
         parts.append(refs[:count])
@@ -301,8 +301,6 @@
             mb[start : start + e_width, :] = e.astype(bf16)
 
     copies = []
-    base = canvas.shape[-1] - columns if cut else 0
-    limit = canvas.shape[-1] if cut else columns - LANES
     top = ITERS * 2 * half
 
     def columns_of(tile):
@@ -387,7 +385,7 @@
         copy.wait()
 
 
-def restore(parts, matrices, state, canvas, plan, inside, planes, half, columns):
+def restore(parts, matrices, state, canvas, plan, inside, planes, half, columns, hi):
     later = len(parts) > 1
     width = parts[-1][0].shape[-1] + (2 * LANES if later else 0)
     halo = 2 * ITERS * half
@@ -410,7 +408,8 @@
         ]
     return pl.pallas_call(
         functools.partial(
-            restore_kernel, plan, inside, [len(part) for part in parts], LANES if later else 0
+            restore_kernel, plan, inside, [len(part) for part in parts],
+            hi - width, LANES if later else 0, hi if hi == columns else hi - LANES,
         ),
         in_specs=specs,
         out_specs=[hbm] + [vmem] * (len(results) - 1),
@@ -458,14 +457,16 @@
     inner_matrices = (*axial[:2], forward_lateral, backward_lateral)
     outer_matrices = (*axial[2:], forward_lateral, backward_lateral)
     depth = halo // 2
-    first_piece = frame_side(
-        raw_frames, frame_order, dark_frame, flat_gain, stripe_band, shear_offset, shear_fraction, 0, SPLIT
-    )
-    first_piece, later_order = lax.optimization_barrier((first_piece, frame_order))
-    second_piece = frame_side(
-        raw_frames, later_order, dark_frame, flat_gain, stripe_band, shear_offset, shear_fraction,
-        SPLIT, columns,
-    )
+    edges = (0, *CUTS, columns)
+    pieces = []
+    order = frame_order
+    for lo, hi in zip(edges[:-1], edges[1:]):
+        piece = frame_side(
+            raw_frames, order, dark_frame, flat_gain, stripe_band, shear_offset, shear_fraction, lo, hi
+        )
+        piece, order = lax.optimization_barrier((piece, order))
+        pieces.append(piece)
+
     def exchange(piece):
         return lax.all_to_all(piece, "brick", split_axis=0, concat_axis=0, tiled=True)
 
@@ -474,25 +475,38 @@
         high = lax.ppermute(centre[:depth], "cam", backward)
         return low, centre, high
 
-    def inside(centres, canvas):
+    def inside(centres, canvas, hi):
         canvas, *state = restore(
-            centres, inner_matrices, (), canvas, inner, True, planes, half, columns
+            centres, inner_matrices, (), canvas, inner, True, planes, half, columns, hi
         )
         return canvas, state
 
-    def ends(parts, state, canvas):
-        return restore(parts, outer_matrices, state, canvas, outer, False, planes, half, columns)[0]
-
-    first, second_piece, inner_matrices, outer_matrices = lax.optimization_barrier(
-        (exchange(first_piece), second_piece, inner_matrices, outer_matrices)
-    )
-    first_part = with_halo(first)
-    canvas, first_state = inside([(first,)], None)
-    second, first_state = lax.optimization_barrier((exchange(second_piece), first_state))
-    second_part = with_halo(second)
-    canvas, second_state = inside([(first,), (second,)], canvas)
-    canvas = ends([first_part], first_state, canvas)
-    return ends([first_part, second_part], second_state, canvas)
+    def ends(parts, state, canvas, hi):
+        return restore(
+            parts, outer_matrices, state, canvas, outer, False, planes, half, columns, hi
+        )[0]
+
+    parts, states, canvas = [], [], None
+    inner_matrices, outer_matrices = tuple(inner_matrices), tuple(outer_matrices)
+    for number, hi in enumerate(edges[1:]):
+        centre = exchange(pieces[number])
+        following = pieces[number + 1 : number + 2]
+        if number == 0:
+            centre, following, inner_matrices, outer_matrices = lax.optimization_barrier(
+                (centre, following, inner_matrices, outer_matrices)
+            )
+        else:
+            centre, following, states[-1] = lax.optimization_barrier((centre, following, states[-1]))
+        pieces[number + 1 : number + 2] = following
+        parts.append(with_halo(centre))
+        centres = [(part[1],) for part in parts[-2:]]
+        if number > 1:
+            canvas = ends(parts[:-1][-3:-1], states[-2], canvas, edges[number - 1])
+        canvas, state = inside(centres, canvas, hi)
+        states.append(state)
+    last = len(parts) - 1
+    canvas = ends(parts[-3:-1], states[-2], canvas, edges[last])
+    return ends(parts[-2:], states[-1], canvas, columns)
 
 
 def solution(mesh):

time: 108 us -> 120 us (1.11)
  waiting for transfers between devices: 30.4 us -> 15.5 us
  starting transfers between devices: 30.9 us -> 45.4 us
  Pallas kernels: 30.3 us -> 37.2 us
  local copies, waits for them, and re-layouts: 14.5 us -> 20.5 us
    all_to_all x2 -> x3, waiting for transfers between devices: 26.8 us -> 15.5 us  [exchange(): lax.all_to_all(piece, 'brick', split_axis=0, concat_axis=0, tiled=True)]
    ppermute x2 -> x3, starting transfers between devices: 8.85 us -> 15.2 us  [with_halo(): high = lax.ppermute(centre[:depth], 'cam', backward)]
    all_to_all x2 -> x3, starting transfers between devices: 14.2 us -> 20.3 us  [exchange(): lax.all_to_all(piece, 'brick', split_axis=0, concat_axis=0, tiled=True)]
    unnamed x56 -> x88, local copies, waits for them, and re-layouts: 13.2 us -> 18.3 us
    pallas_call x4 -> x6, Pallas kernels: 15.6 us -> 19.3 us  [restore(): pl.pallas_call(functools.partial(restore_kernel, plan, inside, [len(part)...]
    ppermute x2 -> x3, waiting for transfers between devices: 3.61 us -> 0.01 us  [with_halo(): high = lax.ppermute(centre[:depth], 'cam', backward)]
    pallas_call x2 -> x3, Pallas kernels: 11.7 us -> 14.9 us  [frame_side(): pl.pallas_call(functools.partial(frame_kernel, first, count), grid=(steps...]
    ppermute x2 -> x3, starting transfers between devices: 7.81 us -> 9.94 us  [with_halo(): low = lax.ppermute(centre[-depth:], 'cam', forward)]
  transfers between devices with their start and end apart: 6 -> 9, of which waited for: 3 -> 2; matrix products, arithmetic and copies ran while one was open for 1% -> 2% of each run, Pallas kernels for 19% -> 24%
where the time goes in v9:
time: 120 us; the launch traced here: 119 us
  starting transfers between devices  45.4 us (38%)
  Pallas kernels  37.2 us (31%)
  local copies, waits for them, and re-layouts  20.5 us (17%)
  waiting for transfers between devices  15.5 us (13%)
    all_to_all x3, starting transfers between devices, exchange(): lax.all_to_all(piece, 'brick', split_axis=0, concat_axis=0, tiled=True)  20.3 us
    pallas_call x6, Pallas kernels, restore(): pl.pallas_call(functools.partial(restore_kernel, plan, inside, [len(part)...  19.3 us
    unnamed x88, local copies, waits for them, and re-layouts  18.3 us
    all_to_all x3, waiting for transfers between devices, exchange(): lax.all_to_all(piece, 'brick', split_axis=0, concat_axis=0, tiled=True)  15.5 us
    ppermute x3, starting transfers between devices, with_halo(): high = lax.ppermute(centre[:depth], 'cam', backward)  15.2 us
    pallas_call x3, Pallas kernels, frame_side(): pl.pallas_call(functools.partial(frame_kernel, first, count), grid=(steps...  14.9 us
    ppermute x3, starting transfers between devices, with_halo(): low = lax.ppermute(centre[-depth:], 'cam', forward)  9.94 us
    pallas_call x1, Pallas kernels, bands(): pl.pallas_call(functools.partial(bands_kernel, psf_bank.shape[1], lateral...  3.03 us
  transfers between devices with their start and end apart: 9, of which 2 were waited for; matrix products, arithmetic and copies ran while one was open for 2% of the time, Pallas kernels for 24%

profile of v9, /device:TPU:14, one launch (start us, length us, event | category | flops | bytes accessed | tf_op | source)
XLA Modules:
  0.0 119.4 jit_solution(14767666001693183349)
XLA Ops:
  0.0 5.8 %frame_side.3 = bf16[32,16,1024]{2,1,0:T(8,128)(2,1)} custom-call(s32[1,2]{1,0:T(1,128)} %order_ref.3, s32[64]{0:T(128)} %offset_ref.5, f32[64]{0:T(128)} %fraction_ref.5, bf16[2,256,2048]{2,1,0:T(8,128)(2,1)} %raw_next.5, bf16[2,256,2048]{2,1,0:T(8,128)(2,1)} %raw_next.5, bf16[2,256,2048]{2,1,0:T(8,128)(2,1)} %raw_next.5, bf16[256,2048]{1,0:T(8,128)(2,1)} %dark_next.5, ...), custom_call_target="tpu_custom_call" | custom-call | flops 8000000000 | bytes 6500000 | tf_op jit(solution)/shard_map/frame_side/pallas_call | solution.py:123
  5.8 10.2 %all-to-all-start = ((bf16[32,16,1024]{2,1,0:T(8,128)(2,1)}), bf16[32,16,1024]{2,1,0:T(8,128)(2,1)S(1)}, u32[]{:S(2)}, u32[]{:S(2)}) async-start(bf16[32,16,1024]{2,1,0:T(8,128)(2,1)} %frame_side.3), calls=%async_computation | async-start | bytes 2097152 | tf_op jit(solution)/shard_map/all_to_all | solution.py:471
  16.4 1.2 %copy-done.2 = bf16[256,2048]{1,0:T(8,128)(2,1)S(1)} copy-done((bf16[256,2048]{1,0:T(8,128)(2,1)S(1)}, bf16[256,2048]{1,0:T(8,128)(2,1)}, u32[]{:S(2)}) %copy-start.2) | copy-done | bytes 1048600
  17.6 1.2 %copy-done.4 = bf16[256,2048]{1,0:T(8,128)(2,1)S(1)} copy-done((bf16[256,2048]{1,0:T(8,128)(2,1)S(1)}, bf16[256,2048]{1,0:T(8,128)(2,1)}, u32[]{:S(2)}) %copy-start.4) | copy-done | bytes 1048600
  18.9 5.3 %frame_side.4 = bf16[32,16,768]{2,1,0:T(8,128)(2,1)} custom-call(s32[1,2]{1,0:T(1,128)S(1)} %copy-done.9, s32[64]{0:T(128)S(1)} %copy-done.10, f32[64]{0:T(128)S(1)} %copy-done.11, bf16[2,256,2048]{2,1,0:T(8,128)(2,1)S(1)} %copy-done, bf16[2,256,2048]{2,1,0:T(8,128)(2,1)S(1)} %copy-done, bf16[2,256,2048]{2,1,0:T(8,128)(2,1)S(1)} %copy-done, ...), custom_call_target="tpu_custom_call" | custom-call | flops 8000000000 | bytes 6500000 | tf_op jit(solution)/shard_map/frame_side/pallas_call | solution.py:123
  24.2 3.0 %bands.1 = (bf16[5,160,256]{2,1,0:T(8,128)(2,1)S(1)}, bf16[3,160,256]{2,1,0:T(8,128)(2,1)S(1)}, bf16[8,160,256]{2,1,0:T(8,128)(2,1)S(1)}, bf16[8,160,256]{2,1,0:...) custom-call(f32[8,13]{1,0:T(8,128)S(1)} %copy-done.7, f32[9]{0:T(128)S(1)} %copy-done.8, ...), custom_call_target="tpu_custom_call" | custom-call | flops 2000000000 | bytes 2000000 | tf_op jit(solution)/shard_map/bands/pallas_call | solution.py:233
  31.8 13.2 %all-to-all-done.refs_0_.refs_1_ = bf16[32,16,1024]{2,1,0:T(8,128)(2,1)S(1)} async-done(((bf16[32,16,1024]{2,1,0:T(8,128)(2,1)}), bf16[32,16,1024]{2,1,0:T(8,128)(2,1)S(1)}, u32[]{:S(2)}, u32[]{:S(2)}) %all-to-all-start) | async-done | bytes 1048608 | tf_op jit(solution)/shard_map/all_to_all | solution.py:471
  45.0 4.0 %all-to-all-start.1 = ((bf16[32,16,768]{2,1,0:T(8,128)(2,1)}), bf16[32,16,768]{2,1,0:T(8,128)(2,1)S(1)}, u32[]{:S(2)}, u32[]{:S(2)}) async-start(bf16[32,16,768]{2,1,0:T(8,128)(2,1)} %frame_side.4), calls=%async_computation.1 | async-start | bytes 1572864 | tf_op jit(solution)/shard_map/all_to_all | solution.py:471
  49.0 1.6 %copy-done.1 = bf16[2,256,2048]{2,1,0:T(8,128)(2,1)S(1)} copy-done((bf16[2,256,2048]{2,1,0:T(8,128)(2,1)S(1)}, bf16[2,256,2048]{2,1,0:T(8,128)(2,1)}, u32[]{:S(2)}) %copy-start.1) | copy-done | bytes 2097176
  50.6 1.2 %copy-done.5 = bf16[256,2048]{1,0:T(8,128)(2,1)S(1)} copy-done((bf16[256,2048]{1,0:T(8,128)(2,1)S(1)}, bf16[256,2048]{1,0:T(8,128)(2,1)}, u32[]{:S(2)}) %copy-start.5) | copy-done | bytes 1048600
  51.8 3.8 %frame_side.5 = bf16[32,16,256]{2,1,0:T(8,128)(2,1)} custom-call(s32[1,2]{1,0:T(1,128)S(1)} %copy-done.9, s32[64]{0:T(128)S(1)} %copy-done.10, f32[64]{0:T(128)S(1)} %copy-done.11, bf16[2,256,2048]{2,1,0:T(8,128)(2,1)S(1)} %copy-done.1, bf16[2,256,2048]{2,1,0:T(8,128)(2,1)S(1)} %copy-done.1, bf16[2,256,2048]{2,1,0:T(8,128)(2,1)S(1)} %copy-done.1, ...), custom_call_target="tpu_custom_call" | custom-call | flops 8000000000 | bytes 6500000 | tf_op jit(solution)/shard_map/frame_side/pallas_call | solution.py:123
  55.7 1.0 fusion
  56.6 4.2 %collective-permute-start.4 = (bf16[12,16,1024]{2,1,0:T(8,128)(2,1)}, bf16[12,16,1024]{2,1,0:T(8,128)(2,1)S(1)}, u32[]{:S(2)}, u32[]{:S(2)}) collective-permute-start(bf16[12,16,1024]{2,1,0:T(8,128)(2,1)} %get-tuple-element.80), channel_id=1, source_target_pairs={{0,32},{32,64},{64,96},{96,128},{128,160},{160,192},{192,224},{1,3... | collective-permute-start | bytes 1179656 | tf_op jit(solution)/shard_map/ppermute | solution.py:474
  60.8 4.2 %collective-permute-start.5 = (bf16[12,16,1024]{2,1,0:T(8,128)(2,1)}, bf16[12,16,1024]{2,1,0:T(8,128)(2,1)S(1)}, u32[]{:S(2)}, u32[]{:S(2)}) collective-permute-start(bf16[12,16,1024]{2,1,0:T(8,128)(2,1)} %get-tuple-element.79), channel_id=1, source_target_pairs={{32,0},{64,32},{96,64},{128,96},{160,128},{192,160},{224,192},{33,... | collective-permute-start | bytes 1179656 | tf_op jit(solution)/shard_map/ppermute | solution.py:475
  65.1 3.2 %inside.3 = (bf16[64,8,2048]{2,1,0:T(8,128)(2,1)}, bf16[416,1024]{1,0:T(8,128)(2,1)S(1)}, f32[192,1024]{1,0:T(8,128)S(1)}) custom-call(bf16[32,16,1024]{2,1,0:T(8,128)(2,1)S(1)} %all-to-all-done.refs_0_.refs_1_, bf16[5,160,256]{2,1,0:T(8,128)(2,1)S(1)} %copy-done.27, bf16[3,160,256]{2,1,0:T(8,128)(2,1)S(1)} %copy-done.40, bf16[512,256]{1,0:T(8,128)(2,1)S(1)} %copy-done.31, ...), custom_call_target="tpu_custom_call" | custom-call | flops 5000000000 | bytes 8000000 | tf_op jit(solution)/shard_map/inside/pallas_call | solution.py:409
  70.1 2.3 %all-to-all-done.1.refs_1_.refs_0_.refs_4_ = bf16[32,16,768]{2,1,0:T(8,128)(2,1)S(1)} async-done(((bf16[32,16,768]{2,1,0:T(8,128)(2,1)}), bf16[32,16,768]{2,1,0:T(8,128)(2,1)S(1)}, u32[]{:S(2)}, u32[]{:S(2)}) %all-to-all-start.1) | async-done | bytes 786464 | tf_op jit(solution)/shard_map/all_to_all | solution.py:471
  72.4 6.1 %all-to-all-start.2 = ((bf16[32,16,256]{2,1,0:T(8,128)(2,1)}), bf16[32,16,256]{2,1,0:T(8,128)(2,1)S(1)}, u32[]{:S(2)}, u32[]{:S(2)}) async-start(bf16[32,16,256]{2,1,0:T(8,128)(2,1)} %frame_side.5), calls=%async_computation.2 | async-start | bytes 524288 | tf_op jit(solution)/shard_map/all_to_all | solution.py:471
  78.5 0.9 copy-done.37
  79.5 0.9 copy-done.41
  80.4 3.2 %inside.4 = (bf16[64,8,2048]{2,1,0:T(8,128)(2,1)}, bf16[416,1024]{1,0:T(8,128)(2,1)S(1)}, f32[192,1024]{1,0:T(8,128)S(1)}) custom-call(bf16[32,16,1024]{2,1,0:T(8,128)(2,1)S(1)} %all-to-all-done.refs_0_.refs_1_, bf16[32,16,768]{2,1,0:T(8,128)(2,1)S(1)} %all-to-all-done.1.refs_1_.refs_0_.refs_4_, ...), custom_call_target="tpu_custom_call", output_to_operand_aliasing={{0}: (6, {})} | custom-call | flops 5000000000 | bytes 8000000 | tf_op jit(solution)/shard_map/inside/pallas_call | solution.py:409
  85.5 3.3 %collective-permute-start = (bf16[12,16,768]{2,1,0:T(8,128)(2,1)}, bf16[12,16,768]{2,1,0:T(8,128)(2,1)S(1)}, u32[]{:S(2)}, u32[]{:S(2)}) collective-permute-start(bf16[12,16,768]{2,1,0:T(8,128)(2,1)} %get-tuple-element.82), channel_id=1, source_target_pairs={{0,32},{32,64},{64,96},{96,128},{128,160},{160,192},{192,224},{1,3... | collective-permute-start | bytes 884744 | tf_op jit(solution)/shard_map/ppermute | solution.py:474
  88.8 4.9 %collective-permute-start.1 = (bf16[12,16,768]{2,1,0:T(8,128)(2,1)}, bf16[12,16,768]{2,1,0:T(8,128)(2,1)S(1)}, u32[]{:S(2)}, u32[]{:S(2)}) collective-permute-start(bf16[12,16,768]{2,1,0:T(8,128)(2,1)} %get-tuple-element.81), channel_id=1, source_target_pairs={{32,0},{64,32},{96,64},{128,96},{160,128},{192,160},{224,192},{33,... | collective-permute-start | bytes 884744 | tf_op jit(solution)/shard_map/ppermute | solution.py:475
  93.8 3.9 %ends.3.refs_6_ = bf16[64,8,2048]{2,1,0:T(8,128)(2,1)} custom-call(bf16[12,16,1024]{2,1,0:T(8,128)(2,1)S(1)} %collective-permute-done.4.refs_0_, bf16[32,16,1024]{2,1,0:T(8,128)(2,1)S(1)} %all-to-all-done.refs_0_.refs_1_, bf16[12,16,1024]{2,1,0:T(8,128)(2,1)S(1)} %collective-permute-done.5.refs_2_, ...), custom_call_target="tpu_custom_call", output_to_operand_aliasing={{}: (9, {})} | custom-call | flops 5000000000 | bytes 8000000 | tf_op jit(solution)/shard_map/ends/pallas_call | solution.py:409
  97.7 2.4 %collective-permute-start.2 = (bf16[12,16,256]{2,1,0:T(8,128)(2,1)S(1)}, bf16[12,16,256]{2,1,0:T(8,128)(2,1)S(1)}, u32[]{:S(2)}, u32[]{:S(2)}) collective-permute-start(bf16[12,16,256]{2,1,0:T(8,128)(2,1)S(1)} %get-tuple-element.84), channel_id=1, source_target_pairs={{0,32},{32,64},{64,96},{96,128},{128,160},{160,192},{192,224},{1,3... | collective-permute-start | bytes 294920 | tf_op jit(solution)/shard_map/ppermute | solution.py:474
  100.2 6.1 %collective-permute-start.3 = (bf16[12,16,256]{2,1,0:T(8,128)(2,1)S(1)}, bf16[12,16,256]{2,1,0:T(8,128)(2,1)S(1)}, u32[]{:S(2)}, u32[]{:S(2)}) collective-permute-start(bf16[12,16,256]{2,1,0:T(8,128)(2,1)S(1)} %get-tuple-element.83), channel_id=1, source_target_pairs={{32,0},{64,32},{96,64},{128,96},{160,128},{192,160},{224,192},{33,... | collective-permute-start | bytes 294920 | tf_op jit(solution)/shard_map/ppermute | solution.py:475
  106.3 1.0 copy-done.29
  107.3 0.9 copy-done.34
  108.2 0.9 copy-done.38
  109.2 0.9 copy-done.42
  110.1 2.5 %inside.5 = (bf16[64,8,2048]{2,1,0:T(8,128)(2,1)}, bf16[416,512]{1,0:T(8,128)(2,1)S(1)}, f32[192,512]{1,0:T(8,128)S(1)}) custom-call(bf16[32,16,768]{2,1,0:T(8,128)(2,1)S(1)} %all-to-all-done.1.refs_1_.refs_0_.refs_4_, bf16[32,16,256]{2,1,0:T(8,128)(2,1)S(1)} %all-to-all-done.2.refs_1_.refs_4_, ...), custom_call_target="tpu_custom_call", output_to_operand_aliasing={{0}: (6, {})} | custom-call | flops 5000000000 | bytes 8000000 | tf_op jit(solution)/shard_map/inside/pallas_call | solution.py:409
  112.7 3.8 %ends.4.refs_12_ = bf16[64,8,2048]{2,1,0:T(8,128)(2,1)} custom-call(bf16[12,16,1024]{2,1,0:T(8,128)(2,1)S(1)} %collective-permute-done.4.refs_0_, bf16[32,16,1024]{2,1,0:T(8,128)(2,1)S(1)} %all-to-all-done.refs_0_.refs_1_, bf16[12,16,1024]{2,1,0:T(8,128)(2,1)S(1)} %collective-permute-done.5.refs_2_, ...), custom_call_target="tpu_custom_call", output_to_operand_aliasing={{}: (12, {})} | custom-call | flops 5000000000 | bytes 8000000 | tf_op jit(solution)/shard_map/ends/pallas_call | solution.py:409
  116.6 2.6 %ends.5 = bf16[64,8,2048]{2,1,0:T(8,128)(2,1)} custom-call(bf16[12,16,768]{2,1,0:T(8,128)(2,1)S(1)} %collective-permute-done.refs_3_.refs_0_, bf16[32,16,768]{2,1,0:T(8,128)(2,1)S(1)} %all-to-all-done.1.refs_1_.refs_0_.refs_4_, bf16[12,16,768]{2,1,0:T(8,128)(2,1)S(1)} %collective-permute-done.1.refs_5_.refs_2_, ...), custom_call_target="tpu_custom_call", output_to_operand_aliasing={{}: (12, {})} | custom-call | flops 5000000000 | bytes 8000000 | tf_op jit(solution)/shard_map/ends/pallas_call | solution.py:409
  (90 shorter events, 8.6 us)
Async XLA Ops:
  0.0 16.1 %copy-start.43 = (s32[512]{0:T(512)S(1)}, s32[512]{0:T(512)}, u32[]{:S(2)}) copy-start(s32[512]{0:T(512)} %param.17) | copy-start | bytes 6148
  5.8 10.6 %copy-start = (bf16[2,256,2048]{2,1,0:T(8,128)(2,1)S(1)}, bf16[2,256,2048]{2,1,0:T(8,128)(2,1)}, u32[]{:S(2)}) copy-start(bf16[2,256,2048]{2,1,0:T(8,128)(2,1)} %raw_next.5) | copy-start | bytes 6291460
  5.8 10.6 %copy-start.6 = (f32[9,2048]{1,0:T(8,128)S(1)}, f32[9,2048]{1,0:T(8,128)}, u32[]{:S(2)}) copy-start(f32[9,2048]{1,0:T(8,128)} %band_ref.5) | copy-start | bytes 221188
  5.8 10.6 %copy-start.9 = (s32[1,2]{1,0:T(1,128)S(1)}, s32[1,2]{1,0:T(1,128)}, u32[]{:S(2)}) copy-start(s32[1,2]{1,0:T(1,128)} %order_ref.3) | copy-start | bytes 28
  5.8 10.6 %copy-start.10 = (s32[64]{0:T(128)S(1)}, s32[64]{0:T(128)}, u32[]{:S(2)}) copy-start(s32[64]{0:T(128)} %offset_ref.5) | copy-start | bytes 772
  5.8 10.6 %copy-start.11 = (f32[64]{0:T(128)S(1)}, f32[64]{0:T(128)}, u32[]{:S(2)}) copy-start(f32[64]{0:T(128)} %fraction_ref.5) | copy-start | bytes 772
  5.8 39.2 %all-to-all-start = ((bf16[32,16,1024]{2,1,0:T(8,128)(2,1)}), bf16[32,16,1024]{2,1,0:T(8,128)(2,1)S(1)}, u32[]{:S(2)}, u32[]{:S(2)}) async-start(bf16[32,16,1024]{2,1,0:T(8,128)(2,1)} %frame_side.3), calls=%async_computation | async-start | bytes 2097152 | tf_op jit(solution)/shard_map/all_to_all | solution.py:471
  24.2 24.8 %copy-start.3 = (bf16[256,2048]{1,0:T(8,128)(2,1)S(1)}, bf16[256,2048]{1,0:T(8,128)(2,1)}, u32[]{:S(2)}) copy-start(bf16[256,2048]{1,0:T(8,128)(2,1)} %dark_next.5) | copy-start | bytes 3145732
  45.0 27.4 %all-to-all-start.1 = ((bf16[32,16,768]{2,1,0:T(8,128)(2,1)}), bf16[32,16,768]{2,1,0:T(8,128)(2,1)S(1)}, u32[]{:S(2)}, u32[]{:S(2)}) async-start(bf16[32,16,768]{2,1,0:T(8,128)(2,1)} %frame_side.4), calls=%async_computation.1 | async-start | bytes 1572864 | tf_op jit(solution)/shard_map/all_to_all | solution.py:471
  51.8 13.2 %copy-start.27 = (bf16[5,160,256]{2,1,0:T(8,128)(2,1)S(1)}, bf16[5,160,256]{2,1,0:T(8,128)(2,1)}, u32[]{:S(2)}) copy-start(bf16[5,160,256]{2,1,0:T(8,128)(2,1)} %copy-done.26) | copy-start | bytes 1228804
  51.8 13.2 %copy-start.31 = (bf16[512,256]{1,0:T(8,128)(2,1)S(1)}, bf16[512,256]{1,0:T(8,128)(2,1)}, u32[]{:S(2)}) copy-start(bf16[512,256]{1,0:T(8,128)(2,1)} %copy-done.30) | copy-start | bytes 786436
  51.8 13.2 %copy-start.36 = (bf16[512,256]{1,0:T(8,128)(2,1)S(1)}, bf16[512,256]{1,0:T(8,128)(2,1)}, u32[]{:S(2)}) copy-start(bf16[512,256]{1,0:T(8,128)(2,1)} %copy-done.35) | copy-start | bytes 786436
  51.8 13.2 %copy-start.40 = (bf16[3,160,256]{2,1,0:T(8,128)(2,1)S(1)}, bf16[3,160,256]{2,1,0:T(8,128)(2,1)}, u32[]{:S(2)}) copy-start(bf16[3,160,256]{2,1,0:T(8,128)(2,1)} %copy-done.39) | copy-start | bytes 737284
  56.6 37.1 %collective-permute-start.4 = (bf16[12,16,1024]{2,1,0:T(8,128)(2,1)}, bf16[12,16,1024]{2,1,0:T(8,128)(2,1)S(1)}, u32[]{:S(2)}, u32[]{:S(2)}) collective-permute-start(bf16[12,16,1024]{2,1,0:T(8,128)(2,1)} %get-tuple-element.80), channel_id=1, source_target_pairs={{0,32},{32,64},{64,96},{96,128},{128,160},{160,192},{192,224},{1,3... | collective-permute-start | bytes 1179656 | tf_op jit(solution)/shard_map/ppermute | solution.py:474
  60.8 17.7 %copy-start.28 = (bf16[5,160,256]{2,1,0:T(8,128)(2,1)S(1)}, bf16[5,160,256]{2,1,0:T(8,128)(2,1)}, u32[]{:S(2)}) copy-start(bf16[5,160,256]{2,1,0:T(8,128)(2,1)} %copy-done.26) | copy-start | bytes 1228804
  60.8 17.7 %copy-start.32 = (bf16[512,256]{1,0:T(8,128)(2,1)S(1)}, bf16[512,256]{1,0:T(8,128)(2,1)}, u32[]{:S(2)}) copy-start(bf16[512,256]{1,0:T(8,128)(2,1)} %copy-done.30) | copy-start | bytes 786436
  60.8 32.9 %collective-permute-start.5 = (bf16[12,16,1024]{2,1,0:T(8,128)(2,1)}, bf16[12,16,1024]{2,1,0:T(8,128)(2,1)S(1)}, u32[]{:S(2)}, u32[]{:S(2)}) collective-permute-start(bf16[12,16,1024]{2,1,0:T(8,128)(2,1)} %get-tuple-element.79), channel_id=1, source_target_pairs={{32,0},{64,32},{96,64},{128,96},{160,128},{192,160},{224,192},{33,... | collective-permute-start | bytes 1179656 | tf_op jit(solution)/shard_map/ppermute | solution.py:475
  72.4 25.3 %all-to-all-start.2 = ((bf16[32,16,256]{2,1,0:T(8,128)(2,1)}), bf16[32,16,256]{2,1,0:T(8,128)(2,1)S(1)}, u32[]{:S(2)}, u32[]{:S(2)}) async-start(bf16[32,16,256]{2,1,0:T(8,128)(2,1)} %frame_side.5), calls=%async_computation.2 | async-start | bytes 524288 | tf_op jit(solution)/shard_map/all_to_all | solution.py:471
  80.4 13.3 %copy-start.17 = (bf16[8,160,256]{2,1,0:T(8,128)(2,1)S(1)}, bf16[8,160,256]{2,1,0:T(8,128)(2,1)}, u32[]{:S(2)}) copy-start(bf16[8,160,256]{2,1,0:T(8,128)(2,1)} %copy-done.16) | copy-start | bytes 1966084
  80.4 13.4 %copy-start.20 = (bf16[8,160,256]{2,1,0:T(8,128)(2,1)S(1)}, bf16[8,160,256]{2,1,0:T(8,128)(2,1)}, u32[]{:S(2)}) copy-start(bf16[8,160,256]{2,1,0:T(8,128)(2,1)} %copy-done.19) | copy-start | bytes 1966084
  80.4 13.4 %copy-start.23 = (bf16[416,1024]{1,0:T(8,128)(2,1)S(1)}, bf16[416,1024]{1,0:T(8,128)(2,1)}, u32[]{:S(2)}) copy-start(bf16[416,1024]{1,0:T(8,128)(2,1)} %copy-done.22) | copy-start | bytes 2555908
  80.4 13.4 %copy-start.25 = (f32[192,1024]{1,0:T(8,128)S(1)}, f32[192,1024]{1,0:T(8,128)}, u32[]{:S(2)}) copy-start(f32[192,1024]{1,0:T(8,128)} %copy-done.24) | copy-start | bytes 2359300
  80.4 13.4 %copy-start.33 = (bf16[512,256]{1,0:T(8,128)(2,1)S(1)}, bf16[512,256]{1,0:T(8,128)(2,1)}, u32[]{:S(2)}) copy-start(bf16[512,256]{1,0:T(8,128)(2,1)} %copy-done.30) | copy-start | bytes 786436
  84.5 9.2 %copy-start.12 = (bf16[416,1024]{1,0:T(8,128)(2,1)}, bf16[416,1024]{1,0:T(8,128)(2,1)S(1)}, u32[]{:S(2)}) copy-start(bf16[416,1024]{1,0:T(8,128)(2,1)S(1)} %get-tuple-element.76.refs_10_) | copy-start | bytes 2555908
  85.5 27.2 %collective-permute-start = (bf16[12,16,768]{2,1,0:T(8,128)(2,1)}, bf16[12,16,768]{2,1,0:T(8,128)(2,1)S(1)}, u32[]{:S(2)}, u32[]{:S(2)}) collective-permute-start(bf16[12,16,768]{2,1,0:T(8,128)(2,1)} %get-tuple-element.82), channel_id=1, source_target_pairs={{0,32},{32,64},{64,96},{96,128},{128,160},{160,192},{192,224},{1,3... | collective-permute-start | bytes 884744 | tf_op jit(solution)/shard_map/ppermute | solution.py:474
  88.8 23.9 %collective-permute-start.1 = (bf16[12,16,768]{2,1,0:T(8,128)(2,1)}, bf16[12,16,768]{2,1,0:T(8,128)(2,1)S(1)}, u32[]{:S(2)}, u32[]{:S(2)}) collective-permute-start(bf16[12,16,768]{2,1,0:T(8,128)(2,1)} %get-tuple-element.81), channel_id=1, source_target_pairs={{32,0},{64,32},{96,64},{128,96},{160,128},{192,160},{224,192},{33,... | collective-permute-start | bytes 884744 | tf_op jit(solution)/shard_map/ppermute | solution.py:475
  97.7 18.8 %collective-permute-start.2 = (bf16[12,16,256]{2,1,0:T(8,128)(2,1)S(1)}, bf16[12,16,256]{2,1,0:T(8,128)(2,1)S(1)}, u32[]{:S(2)}, u32[]{:S(2)}) collective-permute-start(bf16[12,16,256]{2,1,0:T(8,128)(2,1)S(1)} %get-tuple-element.84), channel_id=1, source_target_pairs={{0,32},{32,64},{64,96},{96,128},{128,160},{160,192},{192,224},{1,3... | collective-permute-start | bytes 294920 | tf_op jit(solution)/shard_map/ppermute | solution.py:474
  100.2 12.5 %copy-start.13 = (bf16[416,1024]{1,0:T(8,128)(2,1)S(1)}, bf16[416,1024]{1,0:T(8,128)(2,1)}, u32[]{:S(2)}) copy-start(bf16[416,1024]{1,0:T(8,128)(2,1)} %copy-done.12) | copy-start | bytes 2555908
  100.2 12.5 %copy-start.15 = (f32[192,1024]{1,0:T(8,128)S(1)}, f32[192,1024]{1,0:T(8,128)}, u32[]{:S(2)}) copy-start(f32[192,1024]{1,0:T(8,128)} %copy-done.14) | copy-start | bytes 2359300
  100.2 12.5 %copy-start.18 = (bf16[8,160,256]{2,1,0:T(8,128)(2,1)S(1)}, bf16[8,160,256]{2,1,0:T(8,128)(2,1)}, u32[]{:S(2)}) copy-start(bf16[8,160,256]{2,1,0:T(8,128)(2,1)} %copy-done.16) | copy-start | bytes 1966084
  100.2 12.5 %copy-start.21 = (bf16[8,160,256]{2,1,0:T(8,128)(2,1)S(1)}, bf16[8,160,256]{2,1,0:T(8,128)(2,1)}, u32[]{:S(2)}) copy-start(bf16[8,160,256]{2,1,0:T(8,128)(2,1)} %copy-done.19) | copy-start | bytes 1966084
  100.2 16.4 %collective-permute-start.3 = (bf16[12,16,256]{2,1,0:T(8,128)(2,1)S(1)}, bf16[12,16,256]{2,1,0:T(8,128)(2,1)S(1)}, u32[]{:S(2)}, u32[]{:S(2)}) collective-permute-start(bf16[12,16,256]{2,1,0:T(8,128)(2,1)S(1)} %get-tuple-element.83), channel_id=1, source_target_pairs={{32,0},{64,32},{96,64},{128,96},{160,128},{192,160},{224,192},{33,... | collective-permute-start | bytes 294920 | tf_op jit(solution)/shard_map/ppermute | solution.py:475
  (21 other events, 28.9 us)

commit v10 on v8

--- a/solution.py
+++ b/solution.py
@@ -16,7 +16,7 @@
 ROWS = 8
 BLOCK_ROWS = 64
 LEAD = SHEAR // LANES + 1
-SPLIT = 1024
+SPLIT = 1152
 VMEM = 60 * 1024 * 1024
 BANDS_VMEM = 20 * 1024 * 1024
 RESTORE_VMEM = 30 * 1024 * 1024
@@ -149,13 +149,14 @@
         size = -(-(hi - lo) // (2 * parts)) * 2
         return [(at, min(size, hi - at)) for at in range(lo, hi, size)]
 
-    inner, outer = [], []
+    inner, below, above = [], [], []
     for stage in range(1, 2 * ITERS + 1):
         reach = stage * half
         lo, hi = halo + reach, total - halo - reach
         inner.append([cut(lo, hi, GROUP)])
-        outer.append([cut(reach, lo, GROUP), cut(hi, total - reach, GROUP)])
-    return inner, outer
+        below.append([cut(reach, lo, GROUP)])
+        above.append([cut(hi, total - reach, GROUP)])
+    return inner, below, above
 
 
 def flat(stage):
@@ -233,7 +234,7 @@
     return pl.pallas_call(
         functools.partial(bands_kernel, psf_bank.shape[1], lateral_psf.shape[0], plans),
         in_specs=[smem, smem, vmem],
-        out_specs=[vmem] * 6,
+        out_specs=[vmem] * (len(counts) + 2),
         out_shape=[
             jax.ShapeDtypeStruct((n, GROUP * ROWS, SPAN * ROWS), jnp.bfloat16) for n in counts
         ]
@@ -246,7 +247,8 @@
     )(psf_bank, lateral_psf, index)
 
 
-def restore_kernel(plan, inside, counts, cut, *refs):
+def restore_kernel(plan, side, half, counts, cut, *refs):
+    inside = side == 0
     parts = []
     for count in counts:
         parts.append(refs[:count])
@@ -255,7 +257,6 @@
     refs = refs[4:]
     f32 = jnp.float32
     bf16 = jnp.bfloat16
-    half = plan[0][0][0][0] if not inside else plan[1][0][0][0] - plan[0][0][0][0]
     halo = 2 * ITERS * half
     if not inside:
         q_in, e_in = refs[:2]
@@ -268,25 +269,35 @@
         canvas = refs[-9]
     size, columns = mf.shape
     total = size // ROWS
-    tiles = columns // TILE
+    tiles = -(-columns // TILE)
 
     for buffer in (pad, pad_back):
         buffer[:, :LANES] = jnp.zeros((size, LANES), bf16)
         buffer[:, LANES + columns :] = jnp.zeros((size, LANES), bf16)
 
     at_column = 0
+    reach = (2 * ITERS - 1) * half
     for part in parts:
         width = part[0].shape[-1] if part is parts[-1] else 2 * LANES
         skip = part[0].shape[-1] - width
-        at_row = halo * ROWS if inside else 0
-        for ref in part:
-            height = ref.shape[0] * ref.shape[1]
+        if inside:
+            loads = [(part[0], 0, part[0].shape[0], halo)]
+        elif side < 0:
+            loads = [(part[0], 0, part[0].shape[0], 0), (part[1], 0, reach // 2, halo)]
+        else:
+            own = part[0].shape[0]
+            loads = [
+                (part[0], own - reach // 2, own, total - halo - reach),
+                (part[1], 0, part[1].shape[0], total - halo),
+            ]
+        for ref, lo, hi, plane in loads:
+            rows = slice(plane * ROWS, plane * ROWS + (hi - lo) * ref.shape[1])
             for col in range(0, width, TILE):
-                whole = ref[:, :, skip + col : skip + col + TILE].reshape(height, TILE)
-                there = slice(at_column + col, at_column + col + TILE)
-                mb[at_row : at_row + height, there] = whole
-                mf[at_row : at_row + height, there] = whole.astype(f32)
-            at_row += height
+                end = min(col + TILE, width)
+                whole = ref[lo:hi, :, skip + col : skip + end].reshape(-1, end - col)
+                there = slice(at_column + col, at_column + end)
+                mb[rows, there] = whole
+                mf[rows, there] = whole.astype(f32)
         at_column += width
 
     q_rows = slice((halo + half) * ROWS, (total - halo - half) * ROWS)
@@ -294,25 +305,35 @@
     e_low = (halo + 2 * half) * ROWS
     e_high = (total - halo - 2 * half) * ROWS - e_width
     if not inside:
-        qb[q_rows, :] = q_in[...]
-        for number, start in enumerate((e_low, e_high)):
-            e = e_in[number * e_width : (number + 1) * e_width, :]
-            ef[start : start + e_width, :] = e
-            mb[start : start + e_width, :] = e.astype(bf16)
+        q_height = halo * ROWS
+        q_from = 0 if side < 0 else q_in.shape[0] - q_height
+        q_to = q_rows.start + q_from
+        qb[q_to : q_to + q_height, :] = q_in[q_from : q_from + q_height, :]
+        e_from, e_to = (0, e_low) if side < 0 else (e_width, e_high)
+        e_first = e_in[e_from : e_from + e_width, :]
+        ef[e_to : e_to + e_width, :] = e_first
+        mb[e_to : e_to + e_width, :] = e_first.astype(bf16)
 
     copies = []
     base = canvas.shape[-1] - columns if cut else 0
     limit = canvas.shape[-1] if cut else columns - LANES
     top = ITERS * 2 * half
 
+    def wide(tile):
+        return min(TILE, columns - tile * TILE)
+
     def columns_of(tile):
-        return slice(tile * TILE, (tile + 1) * TILE)
+        return slice(tile * TILE, tile * TILE + wide(tile))
 
     def within(tile):
-        return slice(LANES + tile * TILE, LANES + (tile + 1) * TILE)
+        return slice(LANES + tile * TILE, LANES + tile * TILE + wide(tile))
 
     def around(tile):
-        return slice(tile * TILE, (tile + 1) * TILE + 2 * LANES)
+        return slice(tile * TILE, tile * TILE + wide(tile) + 2 * LANES)
+
+    def lateral(rows, source, matrix, tile):
+        band = matrix[: wide(tile) + 2 * LANES, : wide(tile)]
+        return jnp.dot(source[rows, around(tile)], band, preferred_element_type=f32)
 
     def rows_of(groups):
         return slice(groups[0][0] * ROWS, (groups[-1][0] + groups[-1][1]) * ROWS)
@@ -338,7 +359,7 @@
             cols = columns_of(tile)
             for groups in ahead:
                 rows = rows_of(groups)
-                b = jnp.dot(pad[rows, around(tile)], tl[...], preferred_element_type=f32) + BACKGROUND
+                b = lateral(rows, pad, tl, tile) + BACKGROUND
                 guess = pl.reciprocal(b, approx=True)
                 guess = guess * (2.0 - b * guess)
                 qb[rows, cols] = (mf[rows, cols] * guess).astype(bf16)
@@ -347,7 +368,7 @@
             cols = columns_of(tile)
             for groups in back:
                 rows = rows_of(groups)
-                d = jnp.dot(pad_back[rows, around(tile)], tm[...], preferred_element_type=f32)
+                d = lateral(rows, pad_back, tm, tile)
                 e = (mf if sweep == 0 else ef)[rows, cols] * d
                 if not final:
                     ef[rows, cols] = e
@@ -355,12 +376,12 @@
                     continue
                 start = base + tile * TILE
                 drop = cut if tile == 0 else 0
-                keep = min(TILE, limit - start)
+                keep = min(wide(tile), limit - start)
                 if keep > drop:
                     first, count = groups[0][0] - top, e.shape[0] // ROWS
                     where = (slice(first, first + count), slice(None))
                     here = slice(tile * TILE + drop, tile * TILE + keep)
-                    done[where + (here,)] = e.reshape(-1, ROWS, TILE)[:, :, drop:keep].astype(bf16)
+                    done[where + (here,)] = e.reshape(-1, ROWS, wide(tile))[:, :, drop:keep].astype(bf16)
                     copy = pltpu.make_async_copy(
                         done.at[where + (here,)],
                         canvas.at[where + (slice(start + drop, start + keep),)],
@@ -387,7 +408,8 @@
         copy.wait()
 
 
-def restore(parts, matrices, state, canvas, plan, inside, planes, half, columns):
+def restore(parts, matrices, state, canvas, plan, side, planes, half, columns):
+    inside = side == 0
     later = len(parts) > 1
     width = parts[-1][0].shape[-1] + (2 * LANES if later else 0)
     halo = 2 * ITERS * half
@@ -410,7 +432,7 @@
         ]
     return pl.pallas_call(
         functools.partial(
-            restore_kernel, plan, inside, [len(part) for part in parts], LANES if later else 0
+            restore_kernel, plan, side, half, [len(part) for part in parts], LANES if later else 0
         ),
         in_specs=specs,
         out_specs=[hbm] + [vmem] * (len(results) - 1),
@@ -424,13 +446,13 @@
             pltpu.VMEM((height, width + 2 * LANES), bf16),
             pltpu.VMEM((height, width + 2 * LANES), bf16),
             pltpu.VMEM((planes, ROWS, width), bf16),
-            pltpu.SemaphoreType.DMA((2 * (width // TILE),)),
+            pltpu.SemaphoreType.DMA((-(-width // TILE),)),
         ],
         compiler_params=pltpu.CompilerParams(vmem_limit_bytes=RESTORE_VMEM),
         cost_estimate=pl.CostEstimate(
             flops=5_000_000_000, bytes_accessed=8_000_000, transcendentals=0
         ),
-        name="inside" if inside else "ends",
+        name=("low_end", "inside", "high_end")[side + 1],
     )(*operands)
 
 
@@ -450,13 +472,14 @@
     planes = shear_offset.shape[0]
     columns = raw_frames.shape[-1]
     halo = 2 * ITERS * half
-    inner, outer = stages(planes, half)
+    plans = stages(planes, half)
     count = lax.axis_size("cam")
     forward = [(i, i + 1) for i in range(count - 1)]
     backward = [(i + 1, i) for i in range(count - 1)]
     *axial, forward_lateral, backward_lateral = bands(psf_bank, lateral_psf, band_index, planes, halo)
-    inner_matrices = (*axial[:2], forward_lateral, backward_lateral)
-    outer_matrices = (*axial[2:], forward_lateral, backward_lateral)
+    matrices = [
+        (*axial[2 * which : 2 * which + 2], forward_lateral, backward_lateral) for which in range(3)
+    ]
     depth = halo // 2
     first_piece = frame_side(
         raw_frames, frame_order, dark_frame, flat_gain, stripe_band, shear_offset, shear_fraction, 0, SPLIT
@@ -474,23 +497,30 @@
         high = lax.ppermute(centre[:depth], "cam", backward)
         return low, centre, high
 
-    def inside(centres, canvas):
+    def inside(parts, canvas):
+        centres = [(centre,) for _, centre, _ in parts]
         canvas, *state = restore(
-            centres, inner_matrices, (), canvas, inner, True, planes, half, columns
+            centres, matrices[0], (), canvas, plans[0], 0, planes, half, columns
         )
         return canvas, state
 
     def ends(parts, state, canvas):
-        return restore(parts, outer_matrices, state, canvas, outer, False, planes, half, columns)[0]
-
-    first, second_piece, inner_matrices, outer_matrices = lax.optimization_barrier(
-        (exchange(first_piece), second_piece, inner_matrices, outer_matrices)
+        lower = [(low, centre) for low, centre, _ in parts]
+        upper = [(centre, high) for _, centre, high in parts]
+        for which, side, given in ((1, -1, lower), (2, 1, upper)):
+            (canvas,) = restore(
+                given, matrices[which], state, canvas, plans[which], side, planes, half, columns
+            )
+        return canvas
+
+    first, second_piece, matrices = lax.optimization_barrier(
+        (exchange(first_piece), second_piece, matrices)
     )
     first_part = with_halo(first)
-    canvas, first_state = inside([(first,)], None)
+    canvas, first_state = inside([first_part], None)
     second, first_state = lax.optimization_barrier((exchange(second_piece), first_state))
     second_part = with_halo(second)
-    canvas, second_state = inside([(first,), (second,)], canvas)
+    canvas, second_state = inside([first_part, second_part], canvas)
     canvas = ends([first_part], first_state, canvas)
     return ends([first_part, second_part], second_state, canvas)
 

time: 108 us -> 109 us (level)
  Pallas kernels: 30.3 us -> 35.7 us
  waiting for transfers between devices: 30.4 us -> 25.5 us
    pallas_call x4 -> x6, Pallas kernels: 15.6 us -> 21 us  [restore(): pl.pallas_call(functools.partial(restore_kernel, plan, side, half, [len(p...]
    ppermute x2, waiting for transfers between devices: 3.61 us -> 0.01 us  [with_halo(): high = lax.ppermute(centre[:depth], 'cam', backward)]
    all_to_all x2, waiting for transfers between devices: 26.8 us -> 25.5 us  [exchange(): lax.all_to_all(piece, 'brick', split_axis=0, concat_axis=0, tiled=True)]
    unnamed x56 -> x62, local copies, waits for them, and re-layouts: 13.2 us -> 12.6 us
  transfers between devices with their start and end apart: 6 -> 6, of which waited for: 3 -> 2; matrix products, arithmetic and copies ran while one was open for 1% -> 1% of each run, Pallas kernels for 19% -> 24%
where the time goes in v10:
time: 109 us; the launch traced here: 107 us
  Pallas kernels  35.7 us (33%)
  starting transfers between devices  31.5 us (29%)
  waiting for transfers between devices  25.5 us (23%)
  local copies, waits for them, and re-layouts  14 us (13%)
    all_to_all x2, waiting for transfers between devices, exchange(): lax.all_to_all(piece, 'brick', split_axis=0, concat_axis=0, tiled=True)  25.5 us
    pallas_call x6, Pallas kernels, restore(): pl.pallas_call(functools.partial(restore_kernel, plan, side, half, [len(p...  21 us
    all_to_all x2, starting transfers between devices, exchange(): lax.all_to_all(piece, 'brick', split_axis=0, concat_axis=0, tiled=True)  14.9 us
    unnamed x62, local copies, waits for them, and re-layouts  12.6 us
    pallas_call x2, Pallas kernels, frame_side(): pl.pallas_call(functools.partial(frame_kernel, first, count), grid=(steps...  11.7 us
    ppermute x2, starting transfers between devices, with_halo(): high = lax.ppermute(centre[:depth], 'cam', backward)  8.8 us
    ppermute x2, starting transfers between devices, with_halo(): low = lax.ppermute(centre[-depth:], 'cam', forward)  7.86 us
    pallas_call x1, Pallas kernels, bands(): pl.pallas_call(functools.partial(bands_kernel, psf_bank.shape[1], lateral...  3.03 us
  transfers between devices with their start and end apart: 6, of which 2 were waited for; matrix products, arithmetic and copies ran while one was open for 1% of the time, Pallas kernels for 24%

profile of v10, /device:TPU:14, one launch (start us, length us, event | category | flops | bytes accessed | tf_op | source)
XLA Modules:
  0.0 107.3 jit_solution(17130296734005558336)
XLA Ops:
  0.0 6.1 %frame_side.2 = bf16[32,16,1152]{2,1,0:T(8,128)(2,1)} custom-call(s32[1,2]{1,0:T(1,128)} %order_ref.2, s32[64]{0:T(128)} %offset_ref.3, f32[64]{0:T(128)} %fraction_ref.3, bf16[2,256,2048]{2,1,0:T(8,128)(2,1)} %raw_next.3, bf16[2,256,2048]{2,1,0:T(8,128)(2,1)} %raw_next.3, bf16[2,256,2048]{2,1,0:T(8,128)(2,1)} %raw_next.3, bf16[256,2048]{1,0:T(8,128)(2,1)} %dark_next.3, ...), custom_call_target="tpu_custom_call" | custom-call | flops 8000000000 | bytes 6500000 | tf_op jit(solution)/shard_map/frame_side/pallas_call | solution.py:123
  6.2 10.2 %all-to-all-start = ((bf16[32,16,1152]{2,1,0:T(8,128)(2,1)}), bf16[32,16,1152]{2,1,0:T(8,128)(2,1)S(1)}, u32[]{:S(2)}, u32[]{:S(2)}) async-start(bf16[32,16,1152]{2,1,0:T(8,128)(2,1)} %frame_side.2), calls=%async_computation | async-start | bytes 2359296 | tf_op jit(solution)/shard_map/all_to_all | solution.py:493
  16.8 3.0 %bands.1 = (bf16[5,160,256]{2,1,0:T(8,128)(2,1)S(1)}, bf16[3,160,256]{2,1,0:T(8,128)(2,1)S(1)}, bf16[4,160,256]{2,1,0:T(8,128)(2,1)S(1)}, bf16[4,160,256]{2,1,0:...) custom-call(f32[8,13]{1,0:T(8,128)S(1)} %copy-done.4, ...), custom_call_target="tpu_custom_call" | custom-call | flops 2000000000 | bytes 2000000 | tf_op jit(solution)/shard_map/bands/pallas_call | solution.py:234
  19.8 0.7 copy-done.13
  20.6 0.7 copy-done.15
  21.3 0.7 copy-done.17
  22.0 0.7 copy-done.19
  22.8 0.7 copy-done.21
  23.5 0.7 copy-done.24
  24.9 5.6 %frame_side.3 = bf16[32,16,896]{2,1,0:T(8,128)(2,1)} custom-call(s32[1,2]{1,0:T(1,128)S(1)} %copy-done.6, s32[64]{0:T(128)S(1)} %copy-done.7, f32[64]{0:T(128)S(1)} %copy-done.8, bf16[2,256,2048]{2,1,0:T(8,128)(2,1)S(1)} %copy-done, bf16[2,256,2048]{2,1,0:T(8,128)(2,1)S(1)} %copy-done, bf16[2,256,2048]{2,1,0:T(8,128)(2,1)S(1)} %copy-done, ...), custom_call_target="tpu_custom_call" | custom-call | flops 8000000000 | bytes 6500000 | tf_op jit(solution)/shard_map/frame_side/pallas_call | solution.py:123
  30.5 17.0 %all-to-all-done.refs_0_.refs_1_ = bf16[32,16,1152]{2,1,0:T(8,128)(2,1)S(1)} async-done(((bf16[32,16,1152]{2,1,0:T(8,128)(2,1)}), bf16[32,16,1152]{2,1,0:T(8,128)(2,1)S(1)}, u32[]{:S(2)}, u32[]{:S(2)}) %all-to-all-start) | async-done | bytes 1179680 | tf_op jit(solution)/shard_map/all_to_all | solution.py:493
  47.5 4.6 %all-to-all-start.1 = ((bf16[32,16,896]{2,1,0:T(8,128)(2,1)}), bf16[32,16,896]{2,1,0:T(8,128)(2,1)S(1)}, u32[]{:S(2)}, u32[]{:S(2)}) async-start(bf16[32,16,896]{2,1,0:T(8,128)(2,1)} %frame_side.3), calls=%async_computation.1 | async-start | bytes 1835008 | tf_op jit(solution)/shard_map/all_to_all | solution.py:493
  52.1 1.0 fusion
  53.1 4.2 %collective-permute-start.2 = (bf16[12,16,1152]{2,1,0:T(8,128)(2,1)}, bf16[12,16,1152]{2,1,0:T(8,128)(2,1)S(1)}, u32[]{:S(2)}, u32[]{:S(2)}) collective-permute-start(bf16[12,16,1152]{2,1,0:T(8,128)(2,1)} %get-tuple-element.71), channel_id=1, source_target_pairs={{0,32},{32,64},{64,96},{96,128},{128,160},{160,192},{192,224},{1,3... | collective-permute-start | bytes 1327112 | tf_op jit(solution)/shard_map/ppermute | solution.py:496
  57.3 4.0 %collective-permute-start = (bf16[12,16,1152]{2,1,0:T(8,128)(2,1)}, bf16[12,16,1152]{2,1,0:T(8,128)(2,1)S(1)}, u32[]{:S(2)}, u32[]{:S(2)}) collective-permute-start(bf16[12,16,1152]{2,1,0:T(8,128)(2,1)} %get-tuple-element.72), channel_id=1, source_target_pairs={{32,0},{64,32},{96,64},{128,96},{160,128},{192,160},{224,192},{33,... | collective-permute-start | bytes 1327112 | tf_op jit(solution)/shard_map/ppermute | solution.py:497
  61.4 0.9 copy-done.22
  62.3 0.9 copy-done.25
  63.3 0.9 copy-done.28
  64.2 3.7 %inside.2 = (bf16[64,8,2048]{2,1,0:T(8,128)(2,1)}, bf16[416,1152]{1,0:T(8,128)(2,1)S(1)}, f32[192,1152]{1,0:T(8,128)S(1)}) custom-call(bf16[32,16,1152]{2,1,0:T(8,128)(2,1)S(1)} %all-to-all-done.refs_0_.refs_1_, bf16[5,160,256]{2,1,0:T(8,128)(2,1)S(1)} %get-tuple-element.50.refs_1_.refs_2_, bf16[3,160,256]{2,1,0:T(8,128)(2,1)S(1)} %copy-done.28, ...), custom_call_target="tpu_custom_call" | custom-call | flops 5000000000 | bytes 8000000 | tf_op jit(solution)/shard_map/inside/pallas_call | solution.py:433
  67.9 0.9 copy-done.9
  68.9 0.9 copy-done.11
  69.8 8.5 %all-to-all-done.1.refs_1_.refs_3_.refs_2_ = bf16[32,16,896]{2,1,0:T(8,128)(2,1)S(1)} async-done(((bf16[32,16,896]{2,1,0:T(8,128)(2,1)}), bf16[32,16,896]{2,1,0:T(8,128)(2,1)S(1)}, u32[]{:S(2)}, u32[]{:S(2)}) %all-to-all-start.1) | async-done | bytes 917536 | tf_op jit(solution)/shard_map/all_to_all | solution.py:493
  78.4 3.7 %collective-permute-start.3 = (bf16[12,16,896]{2,1,0:T(8,128)(2,1)S(1)}, bf16[12,16,896]{2,1,0:T(8,128)(2,1)S(1)}, u32[]{:S(2)}, u32[]{:S(2)}) collective-permute-start(bf16[12,16,896]{2,1,0:T(8,128)(2,1)S(1)} %get-tuple-element.73), channel_id=1, source_target_pairs={{0,32},{32,64},{64,96},{96,128},{128,160},{160,192},{192,224},{1,3... | collective-permute-start | bytes 1032200 | tf_op jit(solution)/shard_map/ppermute | solution.py:496
  82.0 4.8 %collective-permute-start.1 = (bf16[12,16,896]{2,1,0:T(8,128)(2,1)S(1)}, bf16[12,16,896]{2,1,0:T(8,128)(2,1)S(1)}, u32[]{:S(2)}, u32[]{:S(2)}) collective-permute-start(bf16[12,16,896]{2,1,0:T(8,128)(2,1)S(1)} %get-tuple-element.74), channel_id=1, source_target_pairs={{32,0},{64,32},{96,64},{128,96},{160,128},{192,160},{224,192},{33,... | collective-permute-start | bytes 1032200 | tf_op jit(solution)/shard_map/ppermute | solution.py:497
  86.8 0.9 copy-done.23
  87.8 0.9 copy-done.26
  88.7 0.9 copy-done.29
  89.7 3.7 %inside.3 = (bf16[64,8,2048]{2,1,0:T(8,128)(2,1)}, bf16[416,1152]{1,0:T(8,128)(2,1)S(1)}, f32[192,1152]{1,0:T(8,128)S(1)}) custom-call(bf16[32,16,1152]{2,1,0:T(8,128)(2,1)S(1)} %all-to-all-done.refs_0_.refs_1_, bf16[32,16,896]{2,1,0:T(8,128)(2,1)S(1)} %all-to-all-done.1.refs_1_.refs_3_.refs_2_, ...), custom_call_target="tpu_custom_call", output_to_operand_aliasing={{0}: (6, {})} | custom-call | flops 5000000000 | bytes 8000000 | tf_op jit(solution)/shard_map/inside/pallas_call | solution.py:433
  93.5 3.4 %low_end.2.refs_8_ = bf16[64,8,2048]{2,1,0:T(8,128)(2,1)} custom-call(bf16[12,16,1152]{2,1,0:T(8,128)(2,1)S(1)} %collective-permute-done.2.refs_0_, bf16[32,16,1152]{2,1,0:T(8,128)(2,1)S(1)} %all-to-all-done.refs_0_.refs_1_, bf16[4,160,256]{2,1,0:T(8,128)(2,1)S(1)} %copy-done.18, ...), custom_call_target="tpu_custom_call", output_to_operand_aliasing={{}: (8, {})} | custom-call | flops 5000000000 | bytes 8000000 | tf_op jit(solution)/shard_map/low_end/pallas_call | solution.py:433
  96.9 3.3 %high_end.2.refs_10_ = bf16[64,8,2048]{2,1,0:T(8,128)(2,1)} custom-call(bf16[32,16,1152]{2,1,0:T(8,128)(2,1)S(1)} %all-to-all-done.refs_0_.refs_1_, bf16[12,16,1152]{2,1,0:T(8,128)(2,1)S(1)} %collective-permute-done.refs_1_, bf16[4,160,256]{2,1,0:T(8,128)(2,1)S(1)} %copy-done.14, ...), custom_call_target="tpu_custom_call", output_to_operand_aliasing={{}: (8, {})} | custom-call | flops 5000000000 | bytes 8000000 | tf_op jit(solution)/shard_map/high_end/pallas_call | solution.py:433
  100.3 3.5 %low_end.3.refs_10_ = bf16[64,8,2048]{2,1,0:T(8,128)(2,1)} custom-call(bf16[12,16,1152]{2,1,0:T(8,128)(2,1)S(1)} %collective-permute-done.2.refs_0_, bf16[32,16,1152]{2,1,0:T(8,128)(2,1)S(1)} %all-to-all-done.refs_0_.refs_1_, bf16[12,16,896]{2,1,0:T(8,128)(2,1)S(1)} %collective-permute-done.3.refs_2_, ...), custom_call_target="tpu_custom_call", output_to_operand_aliasing={{}: (10, {})} | custom-call | flops 5000000000 | bytes 8000000 | tf_op jit(solution)/shard_map/low_end/pallas_call | solution.py:433
  103.8 3.3 %high_end.3 = bf16[64,8,2048]{2,1,0:T(8,128)(2,1)} custom-call(bf16[32,16,1152]{2,1,0:T(8,128)(2,1)S(1)} %all-to-all-done.refs_0_.refs_1_, bf16[12,16,1152]{2,1,0:T(8,128)(2,1)S(1)} %collective-permute-done.refs_1_, bf16[32,16,896]{2,1,0:T(8,128)(2,1)S(1)} %all-to-all-done.1.refs_1_.refs_3_.refs_2_, ...), custom_call_target="tpu_custom_call", output_to_operand_aliasing={{}: (10, {})} | custom-call | flops 5000000000 | bytes 8000000 | tf_op jit(solution)/shard_map/high_end/pallas_call | solution.py:433
  (56 shorter events, 1.1 us)
Async XLA Ops:
  6.1 10.3 %copy-start.30 = (s32[512]{0:T(512)S(1)}, s32[512]{0:T(512)}, u32[]{:S(2)}) copy-start(s32[512]{0:T(512)} %param.17) | copy-start | bytes 6148
  6.1 10.6 %copy-start.4 = (f32[8,13]{1,0:T(8,128)S(1)}, f32[8,13]{1,0:T(8,128)}, u32[]{:S(2)}) copy-start(f32[8,13]{1,0:T(8,128)} %psf_ref.1) | copy-start | bytes 1252
  6.1 10.6 %copy-start.5 = (f32[9]{0:T(128)S(1)}, f32[9]{0:T(128)}, u32[]{:S(2)}) copy-start(f32[9]{0:T(128)} %lateral_ref.1) | copy-start | bytes 112
  6.2 41.3 %all-to-all-start = ((bf16[32,16,1152]{2,1,0:T(8,128)(2,1)}), bf16[32,16,1152]{2,1,0:T(8,128)(2,1)S(1)}, u32[]{:S(2)}, u32[]{:S(2)}) async-start(bf16[32,16,1152]{2,1,0:T(8,128)(2,1)} %frame_side.2), calls=%async_computation | async-start | bytes 2359296 | tf_op jit(solution)/shard_map/all_to_all | solution.py:493
  16.7 8.2 %copy-start = (bf16[2,256,2048]{2,1,0:T(8,128)(2,1)S(1)}, bf16[2,256,2048]{2,1,0:T(8,128)(2,1)}, u32[]{:S(2)}) copy-start(bf16[2,256,2048]{2,1,0:T(8,128)(2,1)} %raw_next.3) | copy-start | bytes 6291460
  16.7 8.2 %copy-start.1 = (bf16[256,2048]{1,0:T(8,128)(2,1)S(1)}, bf16[256,2048]{1,0:T(8,128)(2,1)}, u32[]{:S(2)}) copy-start(bf16[256,2048]{1,0:T(8,128)(2,1)} %dark_next.3) | copy-start | bytes 3145732
  16.7 8.1 %copy-start.2 = (bf16[256,2048]{1,0:T(8,128)(2,1)S(1)}, bf16[256,2048]{1,0:T(8,128)(2,1)}, u32[]{:S(2)}) copy-start(bf16[256,2048]{1,0:T(8,128)(2,1)} %gain_next.3) | copy-start | bytes 3145732
  16.7 8.1 %copy-start.3 = (f32[9,2048]{1,0:T(8,128)S(1)}, f32[9,2048]{1,0:T(8,128)}, u32[]{:S(2)}) copy-start(f32[9,2048]{1,0:T(8,128)} %band_ref.3) | copy-start | bytes 221188
  16.8 8.1 %copy-start.6 = (s32[1,2]{1,0:T(1,128)S(1)}, s32[1,2]{1,0:T(1,128)}, u32[]{:S(2)}) copy-start(s32[1,2]{1,0:T(1,128)} %order_ref.2) | copy-start | bytes 28
  16.8 8.1 %copy-start.7 = (s32[64]{0:T(128)S(1)}, s32[64]{0:T(128)}, u32[]{:S(2)}) copy-start(s32[64]{0:T(128)} %offset_ref.3) | copy-start | bytes 772
  16.8 8.1 %copy-start.8 = (f32[64]{0:T(128)S(1)}, f32[64]{0:T(128)}, u32[]{:S(2)}) copy-start(f32[64]{0:T(128)} %fraction_ref.3) | copy-start | bytes 772
  21.3 0.7 copy-start.17
  22.0 0.7 copy-start.19
  47.5 30.9 %all-to-all-start.1 = ((bf16[32,16,896]{2,1,0:T(8,128)(2,1)}), bf16[32,16,896]{2,1,0:T(8,128)(2,1)S(1)}, u32[]{:S(2)}, u32[]{:S(2)}) async-start(bf16[32,16,896]{2,1,0:T(8,128)(2,1)} %frame_side.3), calls=%async_computation.1 | async-start | bytes 1835008 | tf_op jit(solution)/shard_map/all_to_all | solution.py:493
  53.1 40.3 %collective-permute-start.2 = (bf16[12,16,1152]{2,1,0:T(8,128)(2,1)}, bf16[12,16,1152]{2,1,0:T(8,128)(2,1)S(1)}, u32[]{:S(2)}, u32[]{:S(2)}) collective-permute-start(bf16[12,16,1152]{2,1,0:T(8,128)(2,1)} %get-tuple-element.71), channel_id=1, source_target_pairs={{0,32},{32,64},{64,96},{96,128},{128,160},{160,192},{192,224},{1,3... | collective-permute-start | bytes 1327112 | tf_op jit(solution)/shard_map/ppermute | solution.py:496
  57.3 39.6 %collective-permute-start = (bf16[12,16,1152]{2,1,0:T(8,128)(2,1)}, bf16[12,16,1152]{2,1,0:T(8,128)(2,1)S(1)}, u32[]{:S(2)}, u32[]{:S(2)}) collective-permute-start(bf16[12,16,1152]{2,1,0:T(8,128)(2,1)} %get-tuple-element.72), channel_id=1, source_target_pairs={{32,0},{64,32},{96,64},{128,96},{160,128},{192,160},{224,192},{33,... | collective-permute-start | bytes 1327112 | tf_op jit(solution)/shard_map/ppermute | solution.py:497
  61.4 1.0 copy-start.22
  62.3 0.9 copy-start.25
  63.3 0.9 copy-start.28
  67.9 0.9 copy-start.9
  68.9 0.9 copy-start.11
  78.4 21.9 %collective-permute-start.3 = (bf16[12,16,896]{2,1,0:T(8,128)(2,1)S(1)}, bf16[12,16,896]{2,1,0:T(8,128)(2,1)S(1)}, u32[]{:S(2)}, u32[]{:S(2)}) collective-permute-start(bf16[12,16,896]{2,1,0:T(8,128)(2,1)S(1)} %get-tuple-element.73), channel_id=1, source_target_pairs={{0,32},{32,64},{64,96},{96,128},{128,160},{160,192},{192,224},{1,3... | collective-permute-start | bytes 1032200 | tf_op jit(solution)/shard_map/ppermute | solution.py:496
  82.0 21.7 %collective-permute-start.1 = (bf16[12,16,896]{2,1,0:T(8,128)(2,1)S(1)}, bf16[12,16,896]{2,1,0:T(8,128)(2,1)S(1)}, u32[]{:S(2)}, u32[]{:S(2)}) collective-permute-start(bf16[12,16,896]{2,1,0:T(8,128)(2,1)S(1)} %get-tuple-element.74), channel_id=1, source_target_pairs={{32,0},{64,32},{96,64},{128,96},{160,128},{192,160},{224,192},{33,... | collective-permute-start | bytes 1032200 | tf_op jit(solution)/shard_map/ppermute | solution.py:497
  86.8 1.0 copy-start.23
  87.8 0.9 copy-start.26
  88.7 0.9 copy-start.29
  89.7 3.8 %copy-start.10 = (bf16[416,1152]{1,0:T(8,128)(2,1)S(1)}, bf16[416,1152]{1,0:T(8,128)(2,1)}, u32[]{:S(2)}) copy-start(bf16[416,1152]{1,0:T(8,128)(2,1)} %copy-done.9) | copy-start | bytes 2875396
  89.7 3.8 %copy-start.12 = (f32[192,1152]{1,0:T(8,128)S(1)}, f32[192,1152]{1,0:T(8,128)}, u32[]{:S(2)}) copy-start(f32[192,1152]{1,0:T(8,128)} %copy-done.11) | copy-start | bytes 2654212
  89.7 3.8 %copy-start.18 = (bf16[4,160,256]{2,1,0:T(8,128)(2,1)S(1)}, bf16[4,160,256]{2,1,0:T(8,128)(2,1)}, u32[]{:S(2)}) copy-start(bf16[4,160,256]{2,1,0:T(8,128)(2,1)} %copy-done.17) | copy-start | bytes 983044
  89.7 3.8 %copy-start.20 = (bf16[4,160,256]{2,1,0:T(8,128)(2,1)S(1)}, bf16[4,160,256]{2,1,0:T(8,128)(2,1)}, u32[]{:S(2)}) copy-start(bf16[4,160,256]{2,1,0:T(8,128)(2,1)} %copy-done.19) | copy-start | bytes 983044
  93.4 3.5 %copy-start.14 = (bf16[4,160,256]{2,1,0:T(8,128)(2,1)S(1)}, bf16[4,160,256]{2,1,0:T(8,128)(2,1)}, u32[]{:S(2)}) copy-start(bf16[4,160,256]{2,1,0:T(8,128)(2,1)} %copy-done.13) | copy-start | bytes 983044
  93.5 3.5 %copy-start.16 = (bf16[4,160,256]{2,1,0:T(8,128)(2,1)S(1)}, bf16[4,160,256]{2,1,0:T(8,128)(2,1)}, u32[]{:S(2)}) copy-start(bf16[4,160,256]{2,1,0:T(8,128)(2,1)} %copy-done.15) | copy-start | bytes 983044
  (5 other events, 3.6 us)

commit v11 on v10

--- a/solution.py
+++ b/solution.py
@@ -14,12 +14,12 @@
 LANES = 128
 TILE = 256
 ROWS = 8
-BLOCK_ROWS = 64
+BLOCK_ROWS = 128
 LEAD = SHEAR // LANES + 1
 SPLIT = 1152
 VMEM = 60 * 1024 * 1024
 BANDS_VMEM = 20 * 1024 * 1024
-RESTORE_VMEM = 30 * 1024 * 1024
+RESTORE_VMEM = 26 * 1024 * 1024
 LATER_VMEM = 20 * 1024 * 1024
 GROUP = 20
 SPAN = 32
@@ -149,14 +149,13 @@
         size = -(-(hi - lo) // (2 * parts)) * 2
         return [(at, min(size, hi - at)) for at in range(lo, hi, size)]
 
-    inner, below, above = [], [], []
+    inner, outer = [], []
     for stage in range(1, 2 * ITERS + 1):
         reach = stage * half
         lo, hi = halo + reach, total - halo - reach
         inner.append([cut(lo, hi, GROUP)])
-        below.append([cut(reach, lo, GROUP)])
-        above.append([cut(hi, total - reach, GROUP)])
-    return inner, below, above
+        outer.append([cut(reach, lo, GROUP), cut(hi, total - reach, GROUP)])
+    return inner, outer
 
 
 def flat(stage):
@@ -247,8 +246,7 @@
     )(psf_bank, lateral_psf, index)
 
 
-def restore_kernel(plan, side, half, counts, cut, *refs):
-    inside = side == 0
+def restore_kernel(plan, inside, half, counts, cut, *refs):
     parts = []
     for count in counts:
         parts.append(refs[:count])
@@ -282,13 +280,14 @@
         skip = part[0].shape[-1] - width
         if inside:
             loads = [(part[0], 0, part[0].shape[0], halo)]
-        elif side < 0:
-            loads = [(part[0], 0, part[0].shape[0], 0), (part[1], 0, reach // 2, halo)]
         else:
-            own = part[0].shape[0]
+            low, own, high = part
+            count = own.shape[0]
             loads = [
-                (part[0], own - reach // 2, own, total - halo - reach),
-                (part[1], 0, part[1].shape[0], total - halo),
+                (low, 0, low.shape[0], 0),
+                (own, 0, reach // 2, halo),
+                (own, count - reach // 2, count, total - halo - reach),
+                (high, 0, high.shape[0], total - halo),
             ]
         for ref, lo, hi, plane in loads:
             rows = slice(plane * ROWS, plane * ROWS + (hi - lo) * ref.shape[1])
@@ -306,13 +305,13 @@
     e_high = (total - halo - 2 * half) * ROWS - e_width
     if not inside:
         q_height = halo * ROWS
-        q_from = 0 if side < 0 else q_in.shape[0] - q_height
-        q_to = q_rows.start + q_from
-        qb[q_to : q_to + q_height, :] = q_in[q_from : q_from + q_height, :]
-        e_from, e_to = (0, e_low) if side < 0 else (e_width, e_high)
-        e_first = e_in[e_from : e_from + e_width, :]
-        ef[e_to : e_to + e_width, :] = e_first
-        mb[e_to : e_to + e_width, :] = e_first.astype(bf16)
+        for q_from in (0, q_in.shape[0] - q_height):
+            q_to = q_rows.start + q_from
+            qb[q_to : q_to + q_height, :] = q_in[q_from : q_from + q_height, :]
+        for e_from, e_to in ((0, e_low), (e_width, e_high)):
+            e_first = e_in[e_from : e_from + e_width, :]
+            ef[e_to : e_to + e_width, :] = e_first
+            mb[e_to : e_to + e_width, :] = e_first.astype(bf16)
 
     copies = []
     base = canvas.shape[-1] - columns if cut else 0
@@ -408,8 +407,7 @@
         copy.wait()
 
 
-def restore(parts, matrices, state, canvas, plan, side, planes, half, columns):
-    inside = side == 0
+def restore(parts, matrices, state, canvas, plan, inside, planes, half, columns):
     later = len(parts) > 1
     width = parts[-1][0].shape[-1] + (2 * LANES if later else 0)
     halo = 2 * ITERS * half
@@ -432,7 +430,7 @@
         ]
     return pl.pallas_call(
         functools.partial(
-            restore_kernel, plan, side, half, [len(part) for part in parts], LANES if later else 0
+            restore_kernel, plan, inside, half, [len(part) for part in parts], LANES if later else 0
         ),
         in_specs=specs,
         out_specs=[hbm] + [vmem] * (len(results) - 1),
@@ -446,13 +444,13 @@
             pltpu.VMEM((height, width + 2 * LANES), bf16),
             pltpu.VMEM((height, width + 2 * LANES), bf16),
             pltpu.VMEM((planes, ROWS, width), bf16),
-            pltpu.SemaphoreType.DMA((-(-width // TILE),)),
+            pltpu.SemaphoreType.DMA((-(-width // TILE) * (1 if inside else 2),)),
         ],
         compiler_params=pltpu.CompilerParams(vmem_limit_bytes=RESTORE_VMEM),
         cost_estimate=pl.CostEstimate(
             flops=5_000_000_000, bytes_accessed=8_000_000, transcendentals=0
         ),
-        name=("low_end", "inside", "high_end")[side + 1],
+        name="inside" if inside else "ends",
     )(*operands)
 
 
@@ -478,7 +476,7 @@
     backward = [(i + 1, i) for i in range(count - 1)]
     *axial, forward_lateral, backward_lateral = bands(psf_bank, lateral_psf, band_index, planes, halo)
     matrices = [
-        (*axial[2 * which : 2 * which + 2], forward_lateral, backward_lateral) for which in range(3)
+        (*axial[2 * which : 2 * which + 2], forward_lateral, backward_lateral) for which in range(2)
     ]
     depth = halo // 2
     first_piece = frame_side(
@@ -500,18 +498,14 @@
     def inside(parts, canvas):
         centres = [(centre,) for _, centre, _ in parts]
         canvas, *state = restore(
-            centres, matrices[0], (), canvas, plans[0], 0, planes, half, columns
+            centres, matrices[0], (), canvas, plans[0], True, planes, half, columns
         )
         return canvas, state
 
     def ends(parts, state, canvas):
-        lower = [(low, centre) for low, centre, _ in parts]
-        upper = [(centre, high) for _, centre, high in parts]
-        for which, side, given in ((1, -1, lower), (2, 1, upper)):
-            (canvas,) = restore(
-                given, matrices[which], state, canvas, plans[which], side, planes, half, columns
-            )
-        return canvas
+        return restore(
+            parts, matrices[1], state, canvas, plans[1], False, planes, half, columns
+        )[0]
 
     first, second_piece, matrices = lax.optimization_barrier(
         (exchange(first_piece), second_piece, matrices)

time: 109 us -> 107 us (0.982)
  waiting for transfers between devices: 25.5 us -> 30.6 us
  Pallas kernels: 35.7 us -> 30.9 us
  local copies, waits for them, and re-layouts: 14 us -> 12.7 us
    pallas_call x6 -> x4, Pallas kernels: 21 us -> 16.5 us  [restore(): pl.pallas_call(functools.partial(restore_kernel, plan, inside, half, [len...]
    ppermute x2, waiting for transfers between devices: 0.01 us -> 3.85 us  [with_halo(): high = lax.ppermute(centre[:depth], 'cam', backward)]
    all_to_all x2, waiting for transfers between devices: 25.5 us -> 26.7 us  [exchange(): lax.all_to_all(piece, 'brick', split_axis=0, concat_axis=0, tiled=True)]
    unnamed x62 -> x54, local copies, waits for them, and re-layouts: 12.6 us -> 11.4 us
  transfers between devices with their start and end apart: 6 -> 6, of which waited for: 2 -> 4; matrix products, arithmetic and copies ran while one was open for 1% -> 1% of each run, Pallas kernels for 24% -> 19%
where the time goes in v11:
time: 107 us; the launch traced here: 106 us
  starting transfers between devices  31.5 us (29%)
  Pallas kernels  30.9 us (29%)
  waiting for transfers between devices  30.6 us (29%)
  local copies, waits for them, and re-layouts  12.7 us (12%)
    all_to_all x2, waiting for transfers between devices, exchange(): lax.all_to_all(piece, 'brick', split_axis=0, concat_axis=0, tiled=True)  26.7 us
    pallas_call x4, Pallas kernels, restore(): pl.pallas_call(functools.partial(restore_kernel, plan, inside, half, [len...  16.5 us
    all_to_all x2, starting transfers between devices, exchange(): lax.all_to_all(piece, 'brick', split_axis=0, concat_axis=0, tiled=True)  14.9 us
    unnamed x54, local copies, waits for them, and re-layouts  11.4 us
    pallas_call x2, Pallas kernels, frame_side(): pl.pallas_call(functools.partial(frame_kernel, first, count), grid=(steps...  11.3 us
    ppermute x2, starting transfers between devices, with_halo(): high = lax.ppermute(centre[:depth], 'cam', backward)  8.8 us
    ppermute x2, starting transfers between devices, with_halo(): low = lax.ppermute(centre[-depth:], 'cam', forward)  7.86 us
    ppermute x2, waiting for transfers between devices, with_halo(): high = lax.ppermute(centre[:depth], 'cam', backward)  3.85 us
  transfers between devices with their start and end apart: 6, of which 4 were waited for; matrix products, arithmetic and copies ran while one was open for 1% of the time, Pallas kernels for 19%

profile of v11, /device:TPU:14, one launch (start us, length us, event | category | flops | bytes accessed | tf_op | source)
XLA Modules:
  0.0 106.2 jit_solution(11132811255868777282)
XLA Ops:
  0.0 5.8 %frame_side.2 = bf16[32,16,1152]{2,1,0:T(8,128)(2,1)} custom-call(s32[1,2]{1,0:T(1,128)} %order_ref.2, s32[64]{0:T(128)} %offset_ref.3, f32[64]{0:T(128)} %fraction_ref.3, bf16[2,256,2048]{2,1,0:T(8,128)(2,1)} %raw_next.3, bf16[2,256,2048]{2,1,0:T(8,128)(2,1)} %raw_next.3, bf16[2,256,2048]{2,1,0:T(8,128)(2,1)} %raw_next.3, bf16[256,2048]{1,0:T(8,128)(2,1)} %dark_next.3, ...), custom_call_target="tpu_custom_call" | custom-call | flops 8000000000 | bytes 6500000 | tf_op jit(solution)/shard_map/frame_side/pallas_call | solution.py:123
  5.8 10.2 %all-to-all-start = ((bf16[32,16,1152]{2,1,0:T(8,128)(2,1)}), bf16[32,16,1152]{2,1,0:T(8,128)(2,1)S(1)}, u32[]{:S(2)}, u32[]{:S(2)}) async-start(bf16[32,16,1152]{2,1,0:T(8,128)(2,1)} %frame_side.2), calls=%async_computation | async-start | bytes 2359296 | tf_op jit(solution)/shard_map/all_to_all | solution.py:491
  16.2 0.1 reshape.4.index_ref
  16.4 3.0 %bands.1 = (bf16[5,160,256]{2,1,0:T(8,128)(2,1)S(1)}, bf16[3,160,256]{2,1,0:T(8,128)(2,1)S(1)}, bf16[8,160,256]{2,1,0:T(8,128)(2,1)S(1)}, bf16[8,160,256]{2,1,0:...) custom-call(f32[8,13]{1,0:T(8,128)S(1)} %copy-done.4, f32[9]{0:T(128)S(1)} %copy-done.5, ...), custom_call_target="tpu_custom_call" | custom-call | flops 2000000000 | bytes 2000000 | tf_op jit(solution)/shard_map/bands/pallas_call | solution.py:233
  19.5 0.8 copy-done.9
  20.3 0.8 copy-done.11
  21.2 0.7 copy-done.17
  21.9 0.7 copy-done.20
  22.6 0.7 copy-done.23
  23.3 5.6 %frame_side.3 = bf16[32,16,896]{2,1,0:T(8,128)(2,1)} custom-call(s32[1,2]{1,0:T(1,128)S(1)} %copy-done.6, s32[64]{0:T(128)S(1)} %copy-done.7, f32[64]{0:T(128)S(1)} %copy-done.8, bf16[2,256,2048]{2,1,0:T(8,128)(2,1)S(1)} %copy-done, bf16[2,256,2048]{2,1,0:T(8,128)(2,1)S(1)} %copy-done, bf16[2,256,2048]{2,1,0:T(8,128)(2,1)S(1)} %copy-done, ...), custom_call_target="tpu_custom_call" | custom-call | flops 8000000000 | bytes 6500000 | tf_op jit(solution)/shard_map/frame_side/pallas_call | solution.py:123
  28.9 18.2 %all-to-all-done.refs_0_.refs_1_ = bf16[32,16,1152]{2,1,0:T(8,128)(2,1)S(1)} async-done(((bf16[32,16,1152]{2,1,0:T(8,128)(2,1)}), bf16[32,16,1152]{2,1,0:T(8,128)(2,1)S(1)}, u32[]{:S(2)}, u32[]{:S(2)}) %all-to-all-start) | async-done | bytes 1179680 | tf_op jit(solution)/shard_map/all_to_all | solution.py:491
  47.1 4.6 %all-to-all-start.1 = ((bf16[32,16,896]{2,1,0:T(8,128)(2,1)}), bf16[32,16,896]{2,1,0:T(8,128)(2,1)S(1)}, u32[]{:S(2)}, u32[]{:S(2)}) async-start(bf16[32,16,896]{2,1,0:T(8,128)(2,1)} %frame_side.3), calls=%async_computation.1 | async-start | bytes 1835008 | tf_op jit(solution)/shard_map/all_to_all | solution.py:491
  51.7 1.0 fusion
  52.7 4.2 %collective-permute-start = (bf16[12,16,1152]{2,1,0:T(8,128)(2,1)}, bf16[12,16,1152]{2,1,0:T(8,128)(2,1)S(1)}, u32[]{:S(2)}, u32[]{:S(2)}) collective-permute-start(bf16[12,16,1152]{2,1,0:T(8,128)(2,1)} %get-tuple-element.60), channel_id=1, source_target_pairs={{0,32},{32,64},{64,96},{96,128},{128,160},{160,192},{192,224},{1,3... | collective-permute-start | bytes 1327112 | tf_op jit(solution)/shard_map/ppermute | solution.py:494
  56.9 4.0 %collective-permute-start.1 = (bf16[12,16,1152]{2,1,0:T(8,128)(2,1)}, bf16[12,16,1152]{2,1,0:T(8,128)(2,1)S(1)}, u32[]{:S(2)}, u32[]{:S(2)}) collective-permute-start(bf16[12,16,1152]{2,1,0:T(8,128)(2,1)} %get-tuple-element.59), channel_id=1, source_target_pairs={{32,0},{64,32},{96,64},{128,96},{160,128},{192,160},{224,192},{33,... | collective-permute-start | bytes 1327112 | tf_op jit(solution)/shard_map/ppermute | solution.py:495
  61.0 0.9 copy-done.18
  61.9 0.9 copy-done.21
  62.9 0.9 copy-done.24
  63.8 3.7 %inside.2 = (bf16[64,8,2048]{2,1,0:T(8,128)(2,1)}, bf16[416,1152]{1,0:T(8,128)(2,1)S(1)}, f32[192,1152]{1,0:T(8,128)S(1)}) custom-call(bf16[32,16,1152]{2,1,0:T(8,128)(2,1)S(1)} %all-to-all-done.refs_0_.refs_1_, bf16[5,160,256]{2,1,0:T(8,128)(2,1)S(1)} %get-tuple-element.42.refs_1_.refs_2_, bf16[3,160,256]{2,1,0:T(8,128)(2,1)S(1)} %copy-done.24, ...), custom_call_target="tpu_custom_call" | custom-call | flops 5000000000 | bytes 8000000 | tf_op jit(solution)/shard_map/inside/pallas_call | solution.py:431
  67.6 1.0 copy-done.13
  68.5 0.9 copy-done.15
  69.4 8.5 %all-to-all-done.1.refs_1_.refs_4_ = bf16[32,16,896]{2,1,0:T(8,128)(2,1)S(1)} async-done(((bf16[32,16,896]{2,1,0:T(8,128)(2,1)}), bf16[32,16,896]{2,1,0:T(8,128)(2,1)S(1)}, u32[]{:S(2)}, u32[]{:S(2)}) %all-to-all-start.1) | async-done | bytes 917536 | tf_op jit(solution)/shard_map/all_to_all | solution.py:491
  78.0 3.7 %collective-permute-start.2 = (bf16[12,16,896]{2,1,0:T(8,128)(2,1)S(1)}, bf16[12,16,896]{2,1,0:T(8,128)(2,1)S(1)}, u32[]{:S(2)}, u32[]{:S(2)}) collective-permute-start(bf16[12,16,896]{2,1,0:T(8,128)(2,1)S(1)} %get-tuple-element.62), channel_id=1, source_target_pairs={{0,32},{32,64},{64,96},{96,128},{128,160},{160,192},{192,224},{1,3... | collective-permute-start | bytes 1032200 | tf_op jit(solution)/shard_map/ppermute | solution.py:494
  81.7 4.8 %collective-permute-start.3 = (bf16[12,16,896]{2,1,0:T(8,128)(2,1)S(1)}, bf16[12,16,896]{2,1,0:T(8,128)(2,1)S(1)}, u32[]{:S(2)}, u32[]{:S(2)}) collective-permute-start(bf16[12,16,896]{2,1,0:T(8,128)(2,1)S(1)} %get-tuple-element.61), channel_id=1, source_target_pairs={{32,0},{64,32},{96,64},{128,96},{160,128},{192,160},{224,192},{33,... | collective-permute-start | bytes 1032200 | tf_op jit(solution)/shard_map/ppermute | solution.py:495
  86.5 0.9 copy-done.19
  87.4 0.9 copy-done.22
  88.3 0.9 copy-done.25
  89.3 3.7 %inside.3 = (bf16[64,8,2048]{2,1,0:T(8,128)(2,1)}, bf16[416,1152]{1,0:T(8,128)(2,1)S(1)}, f32[192,1152]{1,0:T(8,128)S(1)}) custom-call(bf16[32,16,1152]{2,1,0:T(8,128)(2,1)S(1)} %all-to-all-done.refs_0_.refs_1_, bf16[32,16,896]{2,1,0:T(8,128)(2,1)S(1)} %all-to-all-done.1.refs_1_.refs_4_, ...), custom_call_target="tpu_custom_call", output_to_operand_aliasing={{0}: (6, {})} | custom-call | flops 5000000000 | bytes 8000000 | tf_op jit(solution)/shard_map/inside/pallas_call | solution.py:431
  93.0 1.2 %collective-permute-done.1.refs_2_ = bf16[12,16,1152]{2,1,0:T(8,128)(2,1)S(1)} collective-permute-done((bf16[12,16,1152]{2,1,0:T(8,128)(2,1)}, bf16[12,16,1152]{2,1,0:T(8,128)(2,1)S(1)}, u32[]{:S(2)}, u32[]{:S(2)}) %collective-permute-start.1) | collective-permute-done | bytes 442400 | tf_op jit(solution)/shard_map/ppermute | solution.py:495
  94.2 4.5 %ends.2.refs_12_ = bf16[64,8,2048]{2,1,0:T(8,128)(2,1)} custom-call(bf16[12,16,1152]{2,1,0:T(8,128)(2,1)S(1)} %collective-permute-done.refs_0_, bf16[32,16,1152]{2,1,0:T(8,128)(2,1)S(1)} %all-to-all-done.refs_0_.refs_1_, bf16[12,16,1152]{2,1,0:T(8,128)(2,1)S(1)} %collective-permute-done.1.refs_2_, ...), custom_call_target="tpu_custom_call", output_to_operand_aliasing={{}: (9, {})} | custom-call | flops 5000000000 | bytes 8000000 | tf_op jit(solution)/shard_map/ends/pallas_call | solution.py:431
  98.8 2.7 %collective-permute-done.3.refs_5_ = bf16[12,16,896]{2,1,0:T(8,128)(2,1)S(1)} collective-permute-done((bf16[12,16,896]{2,1,0:T(8,128)(2,1)S(1)}, bf16[12,16,896]{2,1,0:T(8,128)(2,1)S(1)}, u32[]{:S(2)}, u32[]{:S(2)}) %collective-permute-start.3) | collective-permute-done | bytes 344096 | tf_op jit(solution)/shard_map/ppermute | solution.py:495
  101.5 4.6 %ends.3 = bf16[64,8,2048]{2,1,0:T(8,128)(2,1)} custom-call(bf16[12,16,1152]{2,1,0:T(8,128)(2,1)S(1)} %collective-permute-done.refs_0_, bf16[32,16,1152]{2,1,0:T(8,128)(2,1)S(1)} %all-to-all-done.refs_0_.refs_1_, bf16[12,16,1152]{2,1,0:T(8,128)(2,1)S(1)} %collective-permute-done.1.refs_2_, ...), custom_call_target="tpu_custom_call", output_to_operand_aliasing={{}: (12, {})} | custom-call | flops 5000000000 | bytes 8000000 | tf_op jit(solution)/shard_map/ends/pallas_call | solution.py:431
  (46 shorter events, 0.3 us)
Async XLA Ops:
  5.8 10.3 %copy-start.26 = (s32[512]{0:T(512)S(1)}, s32[512]{0:T(512)}, u32[]{:S(2)}) copy-start(s32[512]{0:T(512)} %param.17) | copy-start | bytes 6148
  5.8 10.6 %copy-start.4 = (f32[8,13]{1,0:T(8,128)S(1)}, f32[8,13]{1,0:T(8,128)}, u32[]{:S(2)}) copy-start(f32[8,13]{1,0:T(8,128)} %psf_ref.1) | copy-start | bytes 1252
  5.8 10.6 %copy-start.5 = (f32[9]{0:T(128)S(1)}, f32[9]{0:T(128)}, u32[]{:S(2)}) copy-start(f32[9]{0:T(128)} %lateral_ref.1) | copy-start | bytes 112
  5.8 41.3 %all-to-all-start = ((bf16[32,16,1152]{2,1,0:T(8,128)(2,1)}), bf16[32,16,1152]{2,1,0:T(8,128)(2,1)S(1)}, u32[]{:S(2)}, u32[]{:S(2)}) async-start(bf16[32,16,1152]{2,1,0:T(8,128)(2,1)} %frame_side.2), calls=%async_computation | async-start | bytes 2359296 | tf_op jit(solution)/shard_map/all_to_all | solution.py:491
  16.3 6.9 %copy-start = (bf16[2,256,2048]{2,1,0:T(8,128)(2,1)S(1)}, bf16[2,256,2048]{2,1,0:T(8,128)(2,1)}, u32[]{:S(2)}) copy-start(bf16[2,256,2048]{2,1,0:T(8,128)(2,1)} %raw_next.3) | copy-start | bytes 6291460
  16.4 6.9 %copy-start.1 = (bf16[256,2048]{1,0:T(8,128)(2,1)S(1)}, bf16[256,2048]{1,0:T(8,128)(2,1)}, u32[]{:S(2)}) copy-start(bf16[256,2048]{1,0:T(8,128)(2,1)} %dark_next.3) | copy-start | bytes 3145732
  16.4 6.9 %copy-start.2 = (bf16[256,2048]{1,0:T(8,128)(2,1)S(1)}, bf16[256,2048]{1,0:T(8,128)(2,1)}, u32[]{:S(2)}) copy-start(bf16[256,2048]{1,0:T(8,128)(2,1)} %gain_next.3) | copy-start | bytes 3145732
  16.4 6.9 %copy-start.3 = (f32[9,2048]{1,0:T(8,128)S(1)}, f32[9,2048]{1,0:T(8,128)}, u32[]{:S(2)}) copy-start(f32[9,2048]{1,0:T(8,128)} %band_ref.3) | copy-start | bytes 221188
  16.4 6.9 %copy-start.6 = (s32[1,2]{1,0:T(1,128)S(1)}, s32[1,2]{1,0:T(1,128)}, u32[]{:S(2)}) copy-start(s32[1,2]{1,0:T(1,128)} %order_ref.2) | copy-start | bytes 28
  16.4 6.9 %copy-start.7 = (s32[64]{0:T(128)S(1)}, s32[64]{0:T(128)}, u32[]{:S(2)}) copy-start(s32[64]{0:T(128)} %offset_ref.3) | copy-start | bytes 772
  16.4 6.9 %copy-start.8 = (f32[64]{0:T(128)S(1)}, f32[64]{0:T(128)}, u32[]{:S(2)}) copy-start(f32[64]{0:T(128)} %fraction_ref.3) | copy-start | bytes 772
  19.5 0.8 copy-start.9
  20.3 0.8 copy-start.11
  21.2 0.7 copy-start.17
  21.9 0.7 copy-start.20
  47.1 30.8 %all-to-all-start.1 = ((bf16[32,16,896]{2,1,0:T(8,128)(2,1)}), bf16[32,16,896]{2,1,0:T(8,128)(2,1)S(1)}, u32[]{:S(2)}, u32[]{:S(2)}) async-start(bf16[32,16,896]{2,1,0:T(8,128)(2,1)} %frame_side.3), calls=%async_computation.1 | async-start | bytes 1835008 | tf_op jit(solution)/shard_map/all_to_all | solution.py:491
  52.7 40.3 %collective-permute-start = (bf16[12,16,1152]{2,1,0:T(8,128)(2,1)}, bf16[12,16,1152]{2,1,0:T(8,128)(2,1)S(1)}, u32[]{:S(2)}, u32[]{:S(2)}) collective-permute-start(bf16[12,16,1152]{2,1,0:T(8,128)(2,1)} %get-tuple-element.60), channel_id=1, source_target_pairs={{0,32},{32,64},{64,96},{96,128},{128,160},{160,192},{192,224},{1,3... | collective-permute-start | bytes 1327112 | tf_op jit(solution)/shard_map/ppermute | solution.py:494
  56.9 37.2 %collective-permute-start.1 = (bf16[12,16,1152]{2,1,0:T(8,128)(2,1)}, bf16[12,16,1152]{2,1,0:T(8,128)(2,1)S(1)}, u32[]{:S(2)}, u32[]{:S(2)}) collective-permute-start(bf16[12,16,1152]{2,1,0:T(8,128)(2,1)} %get-tuple-element.59), channel_id=1, source_target_pairs={{32,0},{64,32},{96,64},{128,96},{160,128},{192,160},{224,192},{33,... | collective-permute-start | bytes 1327112 | tf_op jit(solution)/shard_map/ppermute | solution.py:495
  61.0 1.0 copy-start.18
  61.9 0.9 copy-start.21
  62.9 0.9 copy-start.24
  67.6 1.0 copy-start.13
  68.5 0.9 copy-start.15
  78.0 20.7 %collective-permute-start.2 = (bf16[12,16,896]{2,1,0:T(8,128)(2,1)S(1)}, bf16[12,16,896]{2,1,0:T(8,128)(2,1)S(1)}, u32[]{:S(2)}, u32[]{:S(2)}) collective-permute-start(bf16[12,16,896]{2,1,0:T(8,128)(2,1)S(1)} %get-tuple-element.62), channel_id=1, source_target_pairs={{0,32},{32,64},{64,96},{96,128},{128,160},{160,192},{192,224},{1,3... | collective-permute-start | bytes 1032200 | tf_op jit(solution)/shard_map/ppermute | solution.py:494
  81.7 19.8 %collective-permute-start.3 = (bf16[12,16,896]{2,1,0:T(8,128)(2,1)S(1)}, bf16[12,16,896]{2,1,0:T(8,128)(2,1)S(1)}, u32[]{:S(2)}, u32[]{:S(2)}) collective-permute-start(bf16[12,16,896]{2,1,0:T(8,128)(2,1)S(1)} %get-tuple-element.61), channel_id=1, source_target_pairs={{32,0},{64,32},{96,64},{128,96},{160,128},{192,160},{224,192},{33,... | collective-permute-start | bytes 1032200 | tf_op jit(solution)/shard_map/ppermute | solution.py:495
  86.4 1.0 copy-start.19
  87.4 0.9 copy-start.22
  88.3 0.9 copy-start.25
  89.3 4.9 %copy-start.10 = (bf16[8,160,256]{2,1,0:T(8,128)(2,1)S(1)}, bf16[8,160,256]{2,1,0:T(8,128)(2,1)}, u32[]{:S(2)}) copy-start(bf16[8,160,256]{2,1,0:T(8,128)(2,1)} %copy-done.9) | copy-start | bytes 1966084
  89.3 4.9 %copy-start.12 = (bf16[8,160,256]{2,1,0:T(8,128)(2,1)S(1)}, bf16[8,160,256]{2,1,0:T(8,128)(2,1)}, u32[]{:S(2)}) copy-start(bf16[8,160,256]{2,1,0:T(8,128)(2,1)} %copy-done.11) | copy-start | bytes 1966084
  89.3 4.9 %copy-start.14 = (bf16[416,1152]{1,0:T(8,128)(2,1)S(1)}, bf16[416,1152]{1,0:T(8,128)(2,1)}, u32[]{:S(2)}) copy-start(bf16[416,1152]{1,0:T(8,128)(2,1)} %copy-done.13) | copy-start | bytes 2875396
  89.3 4.9 %copy-start.16 = (f32[192,1152]{1,0:T(8,128)S(1)}, f32[192,1152]{1,0:T(8,128)}, u32[]{:S(2)}) copy-start(f32[192,1152]{1,0:T(8,128)} %copy-done.15) | copy-start | bytes 2654212
  (1 other events, 0.7 us)

commit v12 on v11

--- a/solution.py
+++ b/solution.py
@@ -348,7 +348,7 @@
             )
             target[first * ROWS : (first + count) * ROWS, within(tile)] = r.astype(bf16)
 
-    for sweep in range(ITERS):
+    def calls(sweep):
         ahead, back = plan[2 * sweep], plan[2 * sweep + 1]
         skip_ahead = sum(len(flat(stage)) for stage in plan[0 : 2 * sweep : 2])
         skip_back = sum(len(flat(stage)) for stage in plan[1 : 2 * sweep : 2])
@@ -389,15 +389,18 @@
                     copy.start()
                     copies.append(copy)
 
-        for step in range(tiles + 5):
-            if step < tiles:
-                axial(g, skip_ahead, ahead, mb, pad, step)
-            if 0 <= step - 2 < tiles:
-                ratio(step - 2)
-            if 0 <= step - 3 < tiles:
-                axial(gt, skip_back, back, qb, pad_back, step - 3)
-            if 0 <= step - 5 < tiles:
-                update(step - 5)
+        return (
+            (0, functools.partial(axial, g, skip_ahead, ahead, mb, pad)),
+            (2, ratio),
+            (3, functools.partial(axial, gt, skip_back, back, qb, pad_back)),
+            (5, update),
+        )
+
+    waves = [(6 * sweep + lag, call) for sweep in range(ITERS) for lag, call in calls(sweep)]
+    for step in range(tiles + max(lag for lag, _ in waves)):
+        for lag, call in waves:
+            if 0 <= step - lag < tiles:
+                call(step - lag)
 
     if inside:
         q_out[...] = qb[q_rows, :]

time: 107 us -> 107 us (level)
  transfers between devices with their start and end apart: 6 -> 6, of which waited for: 4 -> 4; matrix products, arithmetic and copies ran while one was open for 1% -> 1% of each run, Pallas kernels for 19% -> 20%
where the time goes in v12:
time: 107 us; the launch traced here: 106 us
  starting transfers between devices  31.5 us (29%)
  Pallas kernels  31.1 us (29%)
  waiting for transfers between devices  30.4 us (28%)
  local copies, waits for them, and re-layouts  12.7 us (12%)
    all_to_all x2, waiting for transfers between devices, exchange(): lax.all_to_all(piece, 'brick', split_axis=0, concat_axis=0, tiled=True)  26.6 us
    pallas_call x4, Pallas kernels, restore(): pl.pallas_call(functools.partial(restore_kernel, plan, inside, half, [len...  16.7 us
    all_to_all x2, starting transfers between devices, exchange(): lax.all_to_all(piece, 'brick', split_axis=0, concat_axis=0, tiled=True)  14.9 us
    unnamed x54, local copies, waits for them, and re-layouts  11.4 us
    pallas_call x2, Pallas kernels, frame_side(): pl.pallas_call(functools.partial(frame_kernel, first, count), grid=(steps...  11.3 us
    ppermute x2, starting transfers between devices, with_halo(): high = lax.ppermute(centre[:depth], 'cam', backward)  8.8 us
    ppermute x2, starting transfers between devices, with_halo(): low = lax.ppermute(centre[-depth:], 'cam', forward)  7.86 us
    ppermute x2, waiting for transfers between devices, with_halo(): high = lax.ppermute(centre[:depth], 'cam', backward)  3.74 us
  transfers between devices with their start and end apart: 6, of which 4 were waited for; matrix products, arithmetic and copies ran while one was open for 1% of the time, Pallas kernels for 20%

profile of v12, /device:TPU:14, one launch (start us, length us, event | category | flops | bytes accessed | tf_op | source)
XLA Modules:
  0.0 106.2 jit_solution(14530060210219726383)
XLA Ops:
  0.0 5.8 %frame_side.2 = bf16[32,16,1152]{2,1,0:T(8,128)(2,1)} custom-call(s32[1,2]{1,0:T(1,128)} %order_ref.2, s32[64]{0:T(128)} %offset_ref.3, f32[64]{0:T(128)} %fraction_ref.3, bf16[2,256,2048]{2,1,0:T(8,128)(2,1)} %raw_next.3, bf16[2,256,2048]{2,1,0:T(8,128)(2,1)} %raw_next.3, bf16[2,256,2048]{2,1,0:T(8,128)(2,1)} %raw_next.3, bf16[256,2048]{1,0:T(8,128)(2,1)} %dark_next.3, ...), custom_call_target="tpu_custom_call" | custom-call | flops 8000000000 | bytes 6500000 | tf_op jit(solution)/shard_map/frame_side/pallas_call | solution.py:123
  5.8 10.2 %all-to-all-start = ((bf16[32,16,1152]{2,1,0:T(8,128)(2,1)}), bf16[32,16,1152]{2,1,0:T(8,128)(2,1)S(1)}, u32[]{:S(2)}, u32[]{:S(2)}) async-start(bf16[32,16,1152]{2,1,0:T(8,128)(2,1)} %frame_side.2), calls=%async_computation | async-start | bytes 2359296 | tf_op jit(solution)/shard_map/all_to_all | solution.py:494
  16.2 0.1 reshape.4.index_ref
  16.4 3.0 %bands.1 = (bf16[5,160,256]{2,1,0:T(8,128)(2,1)S(1)}, bf16[3,160,256]{2,1,0:T(8,128)(2,1)S(1)}, bf16[8,160,256]{2,1,0:T(8,128)(2,1)S(1)}, bf16[8,160,256]{2,1,0:...) custom-call(f32[8,13]{1,0:T(8,128)S(1)} %copy-done.4, f32[9]{0:T(128)S(1)} %copy-done.5, ...), custom_call_target="tpu_custom_call" | custom-call | flops 2000000000 | bytes 2000000 | tf_op jit(solution)/shard_map/bands/pallas_call | solution.py:233
  19.5 0.8 copy-done.9
  20.3 0.8 copy-done.11
  21.2 0.7 copy-done.17
  21.9 0.7 copy-done.20
  22.6 0.7 copy-done.23
  23.3 5.6 %frame_side.3 = bf16[32,16,896]{2,1,0:T(8,128)(2,1)} custom-call(s32[1,2]{1,0:T(1,128)S(1)} %copy-done.6, s32[64]{0:T(128)S(1)} %copy-done.7, f32[64]{0:T(128)S(1)} %copy-done.8, bf16[2,256,2048]{2,1,0:T(8,128)(2,1)S(1)} %copy-done, bf16[2,256,2048]{2,1,0:T(8,128)(2,1)S(1)} %copy-done, bf16[2,256,2048]{2,1,0:T(8,128)(2,1)S(1)} %copy-done, ...), custom_call_target="tpu_custom_call" | custom-call | flops 8000000000 | bytes 6500000 | tf_op jit(solution)/shard_map/frame_side/pallas_call | solution.py:123
  28.9 18.2 %all-to-all-done.refs_0_.refs_1_ = bf16[32,16,1152]{2,1,0:T(8,128)(2,1)S(1)} async-done(((bf16[32,16,1152]{2,1,0:T(8,128)(2,1)}), bf16[32,16,1152]{2,1,0:T(8,128)(2,1)S(1)}, u32[]{:S(2)}, u32[]{:S(2)}) %all-to-all-start) | async-done | bytes 1179680 | tf_op jit(solution)/shard_map/all_to_all | solution.py:494
  47.1 4.6 %all-to-all-start.1 = ((bf16[32,16,896]{2,1,0:T(8,128)(2,1)}), bf16[32,16,896]{2,1,0:T(8,128)(2,1)S(1)}, u32[]{:S(2)}, u32[]{:S(2)}) async-start(bf16[32,16,896]{2,1,0:T(8,128)(2,1)} %frame_side.3), calls=%async_computation.1 | async-start | bytes 1835008 | tf_op jit(solution)/shard_map/all_to_all | solution.py:494
  51.7 1.0 fusion
  52.7 4.2 %collective-permute-start = (bf16[12,16,1152]{2,1,0:T(8,128)(2,1)}, bf16[12,16,1152]{2,1,0:T(8,128)(2,1)S(1)}, u32[]{:S(2)}, u32[]{:S(2)}) collective-permute-start(bf16[12,16,1152]{2,1,0:T(8,128)(2,1)} %get-tuple-element.60), channel_id=1, source_target_pairs={{0,32},{32,64},{64,96},{96,128},{128,160},{160,192},{192,224},{1,3... | collective-permute-start | bytes 1327112 | tf_op jit(solution)/shard_map/ppermute | solution.py:497
  56.9 4.0 %collective-permute-start.1 = (bf16[12,16,1152]{2,1,0:T(8,128)(2,1)}, bf16[12,16,1152]{2,1,0:T(8,128)(2,1)S(1)}, u32[]{:S(2)}, u32[]{:S(2)}) collective-permute-start(bf16[12,16,1152]{2,1,0:T(8,128)(2,1)} %get-tuple-element.59), channel_id=1, source_target_pairs={{32,0},{64,32},{96,64},{128,96},{160,128},{192,160},{224,192},{33,... | collective-permute-start | bytes 1327112 | tf_op jit(solution)/shard_map/ppermute | solution.py:498
  61.0 0.9 copy-done.18
  61.9 0.9 copy-done.21
  62.9 0.9 copy-done.24
  63.8 3.8 %inside.2 = (bf16[64,8,2048]{2,1,0:T(8,128)(2,1)}, bf16[416,1152]{1,0:T(8,128)(2,1)S(1)}, f32[192,1152]{1,0:T(8,128)S(1)}) custom-call(bf16[32,16,1152]{2,1,0:T(8,128)(2,1)S(1)} %all-to-all-done.refs_0_.refs_1_, bf16[5,160,256]{2,1,0:T(8,128)(2,1)S(1)} %get-tuple-element.42.refs_1_.refs_2_, bf16[3,160,256]{2,1,0:T(8,128)(2,1)S(1)} %copy-done.24, ...), custom_call_target="tpu_custom_call" | custom-call | flops 5000000000 | bytes 8000000 | tf_op jit(solution)/shard_map/inside/pallas_call | solution.py:434
  67.7 1.0 copy-done.13
  68.6 0.9 copy-done.15
  69.5 8.4 %all-to-all-done.1.refs_1_.refs_4_ = bf16[32,16,896]{2,1,0:T(8,128)(2,1)S(1)} async-done(((bf16[32,16,896]{2,1,0:T(8,128)(2,1)}), bf16[32,16,896]{2,1,0:T(8,128)(2,1)S(1)}, u32[]{:S(2)}, u32[]{:S(2)}) %all-to-all-start.1) | async-done | bytes 917536 | tf_op jit(solution)/shard_map/all_to_all | solution.py:494
  78.0 3.7 %collective-permute-start.2 = (bf16[12,16,896]{2,1,0:T(8,128)(2,1)S(1)}, bf16[12,16,896]{2,1,0:T(8,128)(2,1)S(1)}, u32[]{:S(2)}, u32[]{:S(2)}) collective-permute-start(bf16[12,16,896]{2,1,0:T(8,128)(2,1)S(1)} %get-tuple-element.62), channel_id=1, source_target_pairs={{0,32},{32,64},{64,96},{96,128},{128,160},{160,192},{192,224},{1,3... | collective-permute-start | bytes 1032200 | tf_op jit(solution)/shard_map/ppermute | solution.py:497
  81.7 4.8 %collective-permute-start.3 = (bf16[12,16,896]{2,1,0:T(8,128)(2,1)S(1)}, bf16[12,16,896]{2,1,0:T(8,128)(2,1)S(1)}, u32[]{:S(2)}, u32[]{:S(2)}) collective-permute-start(bf16[12,16,896]{2,1,0:T(8,128)(2,1)S(1)} %get-tuple-element.61), channel_id=1, source_target_pairs={{32,0},{64,32},{96,64},{128,96},{160,128},{192,160},{224,192},{33,... | collective-permute-start | bytes 1032200 | tf_op jit(solution)/shard_map/ppermute | solution.py:498
  86.5 0.9 copy-done.19
  87.4 0.9 copy-done.22
  88.3 0.9 copy-done.25
  89.3 3.8 %inside.3 = (bf16[64,8,2048]{2,1,0:T(8,128)(2,1)}, bf16[416,1152]{1,0:T(8,128)(2,1)S(1)}, f32[192,1152]{1,0:T(8,128)S(1)}) custom-call(bf16[32,16,1152]{2,1,0:T(8,128)(2,1)S(1)} %all-to-all-done.refs_0_.refs_1_, bf16[32,16,896]{2,1,0:T(8,128)(2,1)S(1)} %all-to-all-done.1.refs_1_.refs_4_, ...), custom_call_target="tpu_custom_call", output_to_operand_aliasing={{0}: (6, {})} | custom-call | flops 5000000000 | bytes 8000000 | tf_op jit(solution)/shard_map/inside/pallas_call | solution.py:434
  93.1 1.1 collective-permute-done.1.refs_2_
  94.2 4.6 %ends.2.refs_12_ = bf16[64,8,2048]{2,1,0:T(8,128)(2,1)} custom-call(bf16[12,16,1152]{2,1,0:T(8,128)(2,1)S(1)} %collective-permute-done.refs_0_, bf16[32,16,1152]{2,1,0:T(8,128)(2,1)S(1)} %all-to-all-done.refs_0_.refs_1_, bf16[12,16,1152]{2,1,0:T(8,128)(2,1)S(1)} %collective-permute-done.1.refs_2_, ...), custom_call_target="tpu_custom_call", output_to_operand_aliasing={{}: (9, {})} | custom-call | flops 5000000000 | bytes 8000000 | tf_op jit(solution)/shard_map/ends/pallas_call | solution.py:434
  98.8 2.7 %collective-permute-done.3.refs_5_ = bf16[12,16,896]{2,1,0:T(8,128)(2,1)S(1)} collective-permute-done((bf16[12,16,896]{2,1,0:T(8,128)(2,1)S(1)}, bf16[12,16,896]{2,1,0:T(8,128)(2,1)S(1)}, u32[]{:S(2)}, u32[]{:S(2)}) %collective-permute-start.3) | collective-permute-done | bytes 344096 | tf_op jit(solution)/shard_map/ppermute | solution.py:498
  101.5 4.6 %ends.3 = bf16[64,8,2048]{2,1,0:T(8,128)(2,1)} custom-call(bf16[12,16,1152]{2,1,0:T(8,128)(2,1)S(1)} %collective-permute-done.refs_0_, bf16[32,16,1152]{2,1,0:T(8,128)(2,1)S(1)} %all-to-all-done.refs_0_.refs_1_, bf16[12,16,1152]{2,1,0:T(8,128)(2,1)S(1)} %collective-permute-done.1.refs_2_, ...), custom_call_target="tpu_custom_call", output_to_operand_aliasing={{}: (12, {})} | custom-call | flops 5000000000 | bytes 8000000 | tf_op jit(solution)/shard_map/ends/pallas_call | solution.py:434
  (46 shorter events, 0.3 us)
Async XLA Ops:
  5.8 10.3 %copy-start.26 = (s32[512]{0:T(512)S(1)}, s32[512]{0:T(512)}, u32[]{:S(2)}) copy-start(s32[512]{0:T(512)} %param.17) | copy-start | bytes 6148
  5.8 10.6 %copy-start.4 = (f32[8,13]{1,0:T(8,128)S(1)}, f32[8,13]{1,0:T(8,128)}, u32[]{:S(2)}) copy-start(f32[8,13]{1,0:T(8,128)} %psf_ref.1) | copy-start | bytes 1252
  5.8 10.6 %copy-start.5 = (f32[9]{0:T(128)S(1)}, f32[9]{0:T(128)}, u32[]{:S(2)}) copy-start(f32[9]{0:T(128)} %lateral_ref.1) | copy-start | bytes 112
  5.8 41.3 %all-to-all-start = ((bf16[32,16,1152]{2,1,0:T(8,128)(2,1)}), bf16[32,16,1152]{2,1,0:T(8,128)(2,1)S(1)}, u32[]{:S(2)}, u32[]{:S(2)}) async-start(bf16[32,16,1152]{2,1,0:T(8,128)(2,1)} %frame_side.2), calls=%async_computation | async-start | bytes 2359296 | tf_op jit(solution)/shard_map/all_to_all | solution.py:494
  16.3 6.9 %copy-start = (bf16[2,256,2048]{2,1,0:T(8,128)(2,1)S(1)}, bf16[2,256,2048]{2,1,0:T(8,128)(2,1)}, u32[]{:S(2)}) copy-start(bf16[2,256,2048]{2,1,0:T(8,128)(2,1)} %raw_next.3) | copy-start | bytes 6291460
  16.4 6.9 %copy-start.1 = (bf16[256,2048]{1,0:T(8,128)(2,1)S(1)}, bf16[256,2048]{1,0:T(8,128)(2,1)}, u32[]{:S(2)}) copy-start(bf16[256,2048]{1,0:T(8,128)(2,1)} %dark_next.3) | copy-start | bytes 3145732
  16.4 6.9 %copy-start.2 = (bf16[256,2048]{1,0:T(8,128)(2,1)S(1)}, bf16[256,2048]{1,0:T(8,128)(2,1)}, u32[]{:S(2)}) copy-start(bf16[256,2048]{1,0:T(8,128)(2,1)} %gain_next.3) | copy-start | bytes 3145732
  16.4 6.9 %copy-start.3 = (f32[9,2048]{1,0:T(8,128)S(1)}, f32[9,2048]{1,0:T(8,128)}, u32[]{:S(2)}) copy-start(f32[9,2048]{1,0:T(8,128)} %band_ref.3) | copy-start | bytes 221188
  16.4 6.9 %copy-start.6 = (s32[1,2]{1,0:T(1,128)S(1)}, s32[1,2]{1,0:T(1,128)}, u32[]{:S(2)}) copy-start(s32[1,2]{1,0:T(1,128)} %order_ref.2) | copy-start | bytes 28
  16.4 6.9 %copy-start.7 = (s32[64]{0:T(128)S(1)}, s32[64]{0:T(128)}, u32[]{:S(2)}) copy-start(s32[64]{0:T(128)} %offset_ref.3) | copy-start | bytes 772
  16.4 6.9 %copy-start.8 = (f32[64]{0:T(128)S(1)}, f32[64]{0:T(128)}, u32[]{:S(2)}) copy-start(f32[64]{0:T(128)} %fraction_ref.3) | copy-start | bytes 772
  19.5 0.8 copy-start.9
  20.3 0.8 copy-start.11
  21.2 0.7 copy-start.17
  21.9 0.7 copy-start.20
  47.1 30.8 %all-to-all-start.1 = ((bf16[32,16,896]{2,1,0:T(8,128)(2,1)}), bf16[32,16,896]{2,1,0:T(8,128)(2,1)S(1)}, u32[]{:S(2)}, u32[]{:S(2)}) async-start(bf16[32,16,896]{2,1,0:T(8,128)(2,1)} %frame_side.3), calls=%async_computation.1 | async-start | bytes 1835008 | tf_op jit(solution)/shard_map/all_to_all | solution.py:494
  52.7 40.4 %collective-permute-start = (bf16[12,16,1152]{2,1,0:T(8,128)(2,1)}, bf16[12,16,1152]{2,1,0:T(8,128)(2,1)S(1)}, u32[]{:S(2)}, u32[]{:S(2)}) collective-permute-start(bf16[12,16,1152]{2,1,0:T(8,128)(2,1)} %get-tuple-element.60), channel_id=1, source_target_pairs={{0,32},{32,64},{64,96},{96,128},{128,160},{160,192},{192,224},{1,3... | collective-permute-start | bytes 1327112 | tf_op jit(solution)/shard_map/ppermute | solution.py:497
  56.9 37.2 %collective-permute-start.1 = (bf16[12,16,1152]{2,1,0:T(8,128)(2,1)}, bf16[12,16,1152]{2,1,0:T(8,128)(2,1)S(1)}, u32[]{:S(2)}, u32[]{:S(2)}) collective-permute-start(bf16[12,16,1152]{2,1,0:T(8,128)(2,1)} %get-tuple-element.59), channel_id=1, source_target_pairs={{32,0},{64,32},{96,64},{128,96},{160,128},{192,160},{224,192},{33,... | collective-permute-start | bytes 1327112 | tf_op jit(solution)/shard_map/ppermute | solution.py:498
  61.0 1.0 copy-start.18
  61.9 0.9 copy-start.21
  62.9 0.9 copy-start.24
  67.6 1.0 copy-start.13
  68.6 0.9 copy-start.15
  78.0 20.8 %collective-permute-start.2 = (bf16[12,16,896]{2,1,0:T(8,128)(2,1)S(1)}, bf16[12,16,896]{2,1,0:T(8,128)(2,1)S(1)}, u32[]{:S(2)}, u32[]{:S(2)}) collective-permute-start(bf16[12,16,896]{2,1,0:T(8,128)(2,1)S(1)} %get-tuple-element.62), channel_id=1, source_target_pairs={{0,32},{32,64},{64,96},{96,128},{128,160},{160,192},{192,224},{1,3... | collective-permute-start | bytes 1032200 | tf_op jit(solution)/shard_map/ppermute | solution.py:497
  81.7 19.8 %collective-permute-start.3 = (bf16[12,16,896]{2,1,0:T(8,128)(2,1)S(1)}, bf16[12,16,896]{2,1,0:T(8,128)(2,1)S(1)}, u32[]{:S(2)}, u32[]{:S(2)}) collective-permute-start(bf16[12,16,896]{2,1,0:T(8,128)(2,1)S(1)} %get-tuple-element.61), channel_id=1, source_target_pairs={{32,0},{64,32},{96,64},{128,96},{160,128},{192,160},{224,192},{33,... | collective-permute-start | bytes 1032200 | tf_op jit(solution)/shard_map/ppermute | solution.py:498
  86.4 1.0 copy-start.19
  87.4 0.9 copy-start.22
  88.3 0.9 copy-start.25
  89.3 4.9 %copy-start.10 = (bf16[8,160,256]{2,1,0:T(8,128)(2,1)S(1)}, bf16[8,160,256]{2,1,0:T(8,128)(2,1)}, u32[]{:S(2)}) copy-start(bf16[8,160,256]{2,1,0:T(8,128)(2,1)} %copy-done.9) | copy-start | bytes 1966084
  89.3 4.9 %copy-start.12 = (bf16[8,160,256]{2,1,0:T(8,128)(2,1)S(1)}, bf16[8,160,256]{2,1,0:T(8,128)(2,1)}, u32[]{:S(2)}) copy-start(bf16[8,160,256]{2,1,0:T(8,128)(2,1)} %copy-done.11) | copy-start | bytes 1966084
  89.3 4.9 %copy-start.14 = (bf16[416,1152]{1,0:T(8,128)(2,1)S(1)}, bf16[416,1152]{1,0:T(8,128)(2,1)}, u32[]{:S(2)}) copy-start(bf16[416,1152]{1,0:T(8,128)(2,1)} %copy-done.13) | copy-start | bytes 2875396
  89.3 4.9 %copy-start.16 = (f32[192,1152]{1,0:T(8,128)S(1)}, f32[192,1152]{1,0:T(8,128)}, u32[]{:S(2)}) copy-start(f32[192,1152]{1,0:T(8,128)} %copy-done.15) | copy-start | bytes 2654212
  (1 other events, 0.7 us)

commit v13 on v12

--- a/solution.py
+++ b/solution.py
@@ -270,8 +270,9 @@
     tiles = -(-columns // TILE)
 
     for buffer in (pad, pad_back):
-        buffer[:, :LANES] = jnp.zeros((size, LANES), bf16)
-        buffer[:, LANES + columns :] = jnp.zeros((size, LANES), bf16)
+        edge = jnp.zeros((buffer.shape[0], LANES), bf16)
+        buffer[:, :LANES] = edge
+        buffer[:, LANES + columns :] = edge
 
     at_column = 0
     reach = (2 * ITERS - 1) * half
@@ -330,14 +331,22 @@
     def around(tile):
         return slice(tile * TILE, tile * TILE + wide(tile) + 2 * LANES)
 
-    def lateral(rows, source, matrix, tile):
+    def lateral(stage, source, matrix, tile):
         band = matrix[: wide(tile) + 2 * LANES, : wide(tile)]
-        return jnp.dot(source[rows, around(tile)], band, preferred_element_type=f32)
+        height = sum(count for _, count in flat(stage)) * ROWS
+        whole = jnp.dot(source[:height, around(tile)], band, preferred_element_type=f32)
+        start = 0
+        for groups in stage:
+            rows = rows_of(groups)
+            stop = start + rows.stop - rows.start
+            yield groups, rows, whole[start:stop]
+            start = stop
 
     def rows_of(groups):
         return slice(groups[0][0] * ROWS, (groups[-1][0] + groups[-1][1]) * ROWS)
 
     def axial(matrices, skip, stage, source, target, tile):
+        place = 0
         for number, (first, count) in enumerate(flat(stage)):
             low = (first - half) * ROWS
             high = (first + count + half) * ROWS
@@ -346,7 +355,8 @@
                 source[low:high, columns_of(tile)],
                 preferred_element_type=f32,
             )
-            target[first * ROWS : (first + count) * ROWS, within(tile)] = r.astype(bf16)
+            target[place : place + count * ROWS, within(tile)] = r.astype(bf16)
+            place += count * ROWS
 
     def calls(sweep):
         ahead, back = plan[2 * sweep], plan[2 * sweep + 1]
@@ -356,18 +366,15 @@
 
         def ratio(tile):
             cols = columns_of(tile)
-            for groups in ahead:
-                rows = rows_of(groups)
-                b = lateral(rows, pad, tl, tile) + BACKGROUND
+            for _, rows, blurred in lateral(ahead, pad, tl, tile):
+                b = blurred + BACKGROUND
                 guess = pl.reciprocal(b, approx=True)
                 guess = guess * (2.0 - b * guess)
                 qb[rows, cols] = (mf[rows, cols] * guess).astype(bf16)
 
         def update(tile):
             cols = columns_of(tile)
-            for groups in back:
-                rows = rows_of(groups)
-                d = lateral(rows, pad_back, tm, tile)
+            for groups, rows, d in lateral(back, pad_back, tm, tile):
                 e = (mf if sweep == 0 else ef)[rows, cols] * d
                 if not final:
                     ef[rows, cols] = e
@@ -425,6 +432,7 @@
         aliases = {len(operands): 0}
         operands.append(canvas)
         specs.append(hbm)
+    tallest = max(sum(count for _, count in flat(stage)) for stage in plan) * ROWS
     results = [jax.ShapeDtypeStruct((planes, ROWS, columns), bf16)]
     if inside:
         results += [
@@ -444,8 +452,8 @@
             pltpu.VMEM((height, width), jnp.float32),
             pltpu.VMEM((height, width), bf16),
             pltpu.VMEM((height, width), bf16),
-            pltpu.VMEM((height, width + 2 * LANES), bf16),
-            pltpu.VMEM((height, width + 2 * LANES), bf16),
+            pltpu.VMEM((tallest, width + 2 * LANES), bf16),
+            pltpu.VMEM((tallest, width + 2 * LANES), bf16),
             pltpu.VMEM((planes, ROWS, width), bf16),
             pltpu.SemaphoreType.DMA((-(-width // TILE) * (1 if inside else 2),)),
         ],

time: 107 us -> 107 us (level)
  no operation moved by 1% of the time
where the time goes in v13:
time: 107 us; the launch traced here: 106 us
  starting transfers between devices  31.5 us (29%)
  Pallas kernels  31.2 us (29%)
  waiting for transfers between devices  30.3 us (28%)
  local copies, waits for them, and re-layouts  12.7 us (12%)
    all_to_all x2, waiting for transfers between devices, exchange(): lax.all_to_all(piece, 'brick', split_axis=0, concat_axis=0, tiled=True)  26.6 us
    pallas_call x4, Pallas kernels, restore(): pl.pallas_call(functools.partial(restore_kernel, plan, inside, half, [len...  16.9 us
    all_to_all x2, starting transfers between devices, exchange(): lax.all_to_all(piece, 'brick', split_axis=0, concat_axis=0, tiled=True)  14.9 us
    unnamed x54, local copies, waits for them, and re-layouts  11.4 us
    pallas_call x2, Pallas kernels, frame_side(): pl.pallas_call(functools.partial(frame_kernel, first, count), grid=(steps...  11.3 us
    ppermute x2, starting transfers between devices, with_halo(): high = lax.ppermute(centre[:depth], 'cam', backward)  8.79 us
    ppermute x2, starting transfers between devices, with_halo(): low = lax.ppermute(centre[-depth:], 'cam', forward)  7.87 us
    ppermute x2, waiting for transfers between devices, with_halo(): high = lax.ppermute(centre[:depth], 'cam', backward)  3.69 us
  transfers between devices with their start and end apart: 6, of which 4 were waited for; matrix products, arithmetic and copies ran while one was open for 1% of the time, Pallas kernels for 20%

profile of v13, /device:TPU:14, one launch (start us, length us, event | category | flops | bytes accessed | tf_op | source)
XLA Modules:
  0.0 106.3 jit_solution(1403688627998985367)
XLA Ops:
  0.0 5.8 %frame_side.2 = bf16[32,16,1152]{2,1,0:T(8,128)(2,1)} custom-call(s32[1,2]{1,0:T(1,128)} %order_ref.2, s32[64]{0:T(128)} %offset_ref.3, f32[64]{0:T(128)} %fraction_ref.3, bf16[2,256,2048]{2,1,0:T(8,128)(2,1)} %raw_next.3, bf16[2,256,2048]{2,1,0:T(8,128)(2,1)} %raw_next.3, bf16[2,256,2048]{2,1,0:T(8,128)(2,1)} %raw_next.3, bf16[256,2048]{1,0:T(8,128)(2,1)} %dark_next.3, ...), custom_call_target="tpu_custom_call" | custom-call | flops 8000000000 | bytes 6500000 | tf_op jit(solution)/shard_map/frame_side/pallas_call | solution.py:123
  5.8 10.2 %all-to-all-start = ((bf16[32,16,1152]{2,1,0:T(8,128)(2,1)}), bf16[32,16,1152]{2,1,0:T(8,128)(2,1)S(1)}, u32[]{:S(2)}, u32[]{:S(2)}) async-start(bf16[32,16,1152]{2,1,0:T(8,128)(2,1)} %frame_side.2), calls=%async_computation | async-start | bytes 2359296 | tf_op jit(solution)/shard_map/all_to_all | solution.py:502
  16.2 0.1 reshape.4.index_ref
  16.4 3.0 %bands.1 = (bf16[5,160,256]{2,1,0:T(8,128)(2,1)S(1)}, bf16[3,160,256]{2,1,0:T(8,128)(2,1)S(1)}, bf16[8,160,256]{2,1,0:T(8,128)(2,1)S(1)}, bf16[8,160,256]{2,1,0:...) custom-call(f32[8,13]{1,0:T(8,128)S(1)} %copy-done.4, f32[9]{0:T(128)S(1)} %copy-done.5, ...), custom_call_target="tpu_custom_call" | custom-call | flops 2000000000 | bytes 2000000 | tf_op jit(solution)/shard_map/bands/pallas_call | solution.py:233
  19.5 0.8 copy-done.9
  20.3 0.8 copy-done.11
  21.2 0.7 copy-done.17
  21.9 0.7 copy-done.20
  22.6 0.7 copy-done.23
  23.3 5.6 %frame_side.3 = bf16[32,16,896]{2,1,0:T(8,128)(2,1)} custom-call(s32[1,2]{1,0:T(1,128)S(1)} %copy-done.6, s32[64]{0:T(128)S(1)} %copy-done.7, f32[64]{0:T(128)S(1)} %copy-done.8, bf16[2,256,2048]{2,1,0:T(8,128)(2,1)S(1)} %copy-done, bf16[2,256,2048]{2,1,0:T(8,128)(2,1)S(1)} %copy-done, bf16[2,256,2048]{2,1,0:T(8,128)(2,1)S(1)} %copy-done, ...), custom_call_target="tpu_custom_call" | custom-call | flops 8000000000 | bytes 6500000 | tf_op jit(solution)/shard_map/frame_side/pallas_call | solution.py:123
  28.9 18.2 %all-to-all-done.refs_0_.refs_1_ = bf16[32,16,1152]{2,1,0:T(8,128)(2,1)S(1)} async-done(((bf16[32,16,1152]{2,1,0:T(8,128)(2,1)}), bf16[32,16,1152]{2,1,0:T(8,128)(2,1)S(1)}, u32[]{:S(2)}, u32[]{:S(2)}) %all-to-all-start) | async-done | bytes 1179680 | tf_op jit(solution)/shard_map/all_to_all | solution.py:502
  47.1 4.6 %all-to-all-start.1 = ((bf16[32,16,896]{2,1,0:T(8,128)(2,1)}), bf16[32,16,896]{2,1,0:T(8,128)(2,1)S(1)}, u32[]{:S(2)}, u32[]{:S(2)}) async-start(bf16[32,16,896]{2,1,0:T(8,128)(2,1)} %frame_side.3), calls=%async_computation.1 | async-start | bytes 1835008 | tf_op jit(solution)/shard_map/all_to_all | solution.py:502
  51.7 1.0 fusion
  52.7 4.2 %collective-permute-start = (bf16[12,16,1152]{2,1,0:T(8,128)(2,1)}, bf16[12,16,1152]{2,1,0:T(8,128)(2,1)S(1)}, u32[]{:S(2)}, u32[]{:S(2)}) collective-permute-start(bf16[12,16,1152]{2,1,0:T(8,128)(2,1)} %get-tuple-element.60), channel_id=1, source_target_pairs={{0,32},{32,64},{64,96},{96,128},{128,160},{160,192},{192,224},{1,3... | collective-permute-start | bytes 1327112 | tf_op jit(solution)/shard_map/ppermute | solution.py:505
  56.9 4.0 %collective-permute-start.1 = (bf16[12,16,1152]{2,1,0:T(8,128)(2,1)}, bf16[12,16,1152]{2,1,0:T(8,128)(2,1)S(1)}, u32[]{:S(2)}, u32[]{:S(2)}) collective-permute-start(bf16[12,16,1152]{2,1,0:T(8,128)(2,1)} %get-tuple-element.59), channel_id=1, source_target_pairs={{32,0},{64,32},{96,64},{128,96},{160,128},{192,160},{224,192},{33,... | collective-permute-start | bytes 1327112 | tf_op jit(solution)/shard_map/ppermute | solution.py:506
  61.0 0.9 copy-done.18
  61.9 0.9 copy-done.21
  62.9 0.9 copy-done.24
  63.8 3.8 %inside.2 = (bf16[64,8,2048]{2,1,0:T(8,128)(2,1)}, bf16[416,1152]{1,0:T(8,128)(2,1)S(1)}, f32[192,1152]{1,0:T(8,128)S(1)}) custom-call(bf16[32,16,1152]{2,1,0:T(8,128)(2,1)S(1)} %all-to-all-done.refs_0_.refs_1_, bf16[5,160,256]{2,1,0:T(8,128)(2,1)S(1)} %get-tuple-element.42.refs_1_.refs_2_, bf16[3,160,256]{2,1,0:T(8,128)(2,1)S(1)} %copy-done.24, ...), custom_call_target="tpu_custom_call" | custom-call | flops 5000000000 | bytes 8000000 | tf_op jit(solution)/shard_map/inside/pallas_call | solution.py:442
  67.7 1.0 copy-done.13
  68.6 0.9 copy-done.15
  69.5 8.4 %all-to-all-done.1.refs_1_.refs_4_ = bf16[32,16,896]{2,1,0:T(8,128)(2,1)S(1)} async-done(((bf16[32,16,896]{2,1,0:T(8,128)(2,1)}), bf16[32,16,896]{2,1,0:T(8,128)(2,1)S(1)}, u32[]{:S(2)}, u32[]{:S(2)}) %all-to-all-start.1) | async-done | bytes 917536 | tf_op jit(solution)/shard_map/all_to_all | solution.py:502
  78.0 3.7 %collective-permute-start.2 = (bf16[12,16,896]{2,1,0:T(8,128)(2,1)S(1)}, bf16[12,16,896]{2,1,0:T(8,128)(2,1)S(1)}, u32[]{:S(2)}, u32[]{:S(2)}) collective-permute-start(bf16[12,16,896]{2,1,0:T(8,128)(2,1)S(1)} %get-tuple-element.62), channel_id=1, source_target_pairs={{0,32},{32,64},{64,96},{96,128},{128,160},{160,192},{192,224},{1,3... | collective-permute-start | bytes 1032200 | tf_op jit(solution)/shard_map/ppermute | solution.py:505
  81.7 4.8 %collective-permute-start.3 = (bf16[12,16,896]{2,1,0:T(8,128)(2,1)S(1)}, bf16[12,16,896]{2,1,0:T(8,128)(2,1)S(1)}, u32[]{:S(2)}, u32[]{:S(2)}) collective-permute-start(bf16[12,16,896]{2,1,0:T(8,128)(2,1)S(1)} %get-tuple-element.61), channel_id=1, source_target_pairs={{32,0},{64,32},{96,64},{128,96},{160,128},{192,160},{224,192},{33,... | collective-permute-start | bytes 1032200 | tf_op jit(solution)/shard_map/ppermute | solution.py:506
  86.5 0.9 copy-done.19
  87.4 0.9 copy-done.22
  88.3 0.9 copy-done.25
  89.3 3.8 %inside.3 = (bf16[64,8,2048]{2,1,0:T(8,128)(2,1)}, bf16[416,1152]{1,0:T(8,128)(2,1)S(1)}, f32[192,1152]{1,0:T(8,128)S(1)}) custom-call(bf16[32,16,1152]{2,1,0:T(8,128)(2,1)S(1)} %all-to-all-done.refs_0_.refs_1_, bf16[32,16,896]{2,1,0:T(8,128)(2,1)S(1)} %all-to-all-done.1.refs_1_.refs_4_, ...), custom_call_target="tpu_custom_call", output_to_operand_aliasing={{0}: (6, {})} | custom-call | flops 5000000000 | bytes 8000000 | tf_op jit(solution)/shard_map/inside/pallas_call | solution.py:442
  93.1 1.1 %collective-permute-done.1.refs_2_ = bf16[12,16,1152]{2,1,0:T(8,128)(2,1)S(1)} collective-permute-done((bf16[12,16,1152]{2,1,0:T(8,128)(2,1)}, bf16[12,16,1152]{2,1,0:T(8,128)(2,1)S(1)}, u32[]{:S(2)}, u32[]{:S(2)}) %collective-permute-start.1) | collective-permute-done | bytes 442400 | tf_op jit(solution)/shard_map/ppermute | solution.py:506
  94.2 4.6 %ends.2.refs_12_ = bf16[64,8,2048]{2,1,0:T(8,128)(2,1)} custom-call(bf16[12,16,1152]{2,1,0:T(8,128)(2,1)S(1)} %collective-permute-done.refs_0_, bf16[32,16,1152]{2,1,0:T(8,128)(2,1)S(1)} %all-to-all-done.refs_0_.refs_1_, bf16[12,16,1152]{2,1,0:T(8,128)(2,1)S(1)} %collective-permute-done.1.refs_2_, ...), custom_call_target="tpu_custom_call", output_to_operand_aliasing={{}: (9, {})} | custom-call | flops 5000000000 | bytes 8000000 | tf_op jit(solution)/shard_map/ends/pallas_call | solution.py:442
  98.8 2.6 %collective-permute-done.3.refs_5_ = bf16[12,16,896]{2,1,0:T(8,128)(2,1)S(1)} collective-permute-done((bf16[12,16,896]{2,1,0:T(8,128)(2,1)S(1)}, bf16[12,16,896]{2,1,0:T(8,128)(2,1)S(1)}, u32[]{:S(2)}, u32[]{:S(2)}) %collective-permute-start.3) | collective-permute-done | bytes 344096 | tf_op jit(solution)/shard_map/ppermute | solution.py:506
  101.5 4.7 %ends.3 = bf16[64,8,2048]{2,1,0:T(8,128)(2,1)} custom-call(bf16[12,16,1152]{2,1,0:T(8,128)(2,1)S(1)} %collective-permute-done.refs_0_, bf16[32,16,1152]{2,1,0:T(8,128)(2,1)S(1)} %all-to-all-done.refs_0_.refs_1_, bf16[12,16,1152]{2,1,0:T(8,128)(2,1)S(1)} %collective-permute-done.1.refs_2_, ...), custom_call_target="tpu_custom_call", output_to_operand_aliasing={{}: (12, {})} | custom-call | flops 5000000000 | bytes 8000000 | tf_op jit(solution)/shard_map/ends/pallas_call | solution.py:442
  (46 shorter events, 0.3 us)
Async XLA Ops:
  5.8 10.3 %copy-start.26 = (s32[512]{0:T(512)S(1)}, s32[512]{0:T(512)}, u32[]{:S(2)}) copy-start(s32[512]{0:T(512)} %param.17) | copy-start | bytes 6148
  5.8 10.6 %copy-start.4 = (f32[8,13]{1,0:T(8,128)S(1)}, f32[8,13]{1,0:T(8,128)}, u32[]{:S(2)}) copy-start(f32[8,13]{1,0:T(8,128)} %psf_ref.1) | copy-start | bytes 1252
  5.8 10.6 %copy-start.5 = (f32[9]{0:T(128)S(1)}, f32[9]{0:T(128)}, u32[]{:S(2)}) copy-start(f32[9]{0:T(128)} %lateral_ref.1) | copy-start | bytes 112
  5.8 41.3 %all-to-all-start = ((bf16[32,16,1152]{2,1,0:T(8,128)(2,1)}), bf16[32,16,1152]{2,1,0:T(8,128)(2,1)S(1)}, u32[]{:S(2)}, u32[]{:S(2)}) async-start(bf16[32,16,1152]{2,1,0:T(8,128)(2,1)} %frame_side.2), calls=%async_computation | async-start | bytes 2359296 | tf_op jit(solution)/shard_map/all_to_all | solution.py:502
  16.3 6.9 %copy-start = (bf16[2,256,2048]{2,1,0:T(8,128)(2,1)S(1)}, bf16[2,256,2048]{2,1,0:T(8,128)(2,1)}, u32[]{:S(2)}) copy-start(bf16[2,256,2048]{2,1,0:T(8,128)(2,1)} %raw_next.3) | copy-start | bytes 6291460
  16.4 6.9 %copy-start.1 = (bf16[256,2048]{1,0:T(8,128)(2,1)S(1)}, bf16[256,2048]{1,0:T(8,128)(2,1)}, u32[]{:S(2)}) copy-start(bf16[256,2048]{1,0:T(8,128)(2,1)} %dark_next.3) | copy-start | bytes 3145732
  16.4 6.9 %copy-start.2 = (bf16[256,2048]{1,0:T(8,128)(2,1)S(1)}, bf16[256,2048]{1,0:T(8,128)(2,1)}, u32[]{:S(2)}) copy-start(bf16[256,2048]{1,0:T(8,128)(2,1)} %gain_next.3) | copy-start | bytes 3145732
  16.4 6.9 %copy-start.3 = (f32[9,2048]{1,0:T(8,128)S(1)}, f32[9,2048]{1,0:T(8,128)}, u32[]{:S(2)}) copy-start(f32[9,2048]{1,0:T(8,128)} %band_ref.3) | copy-start | bytes 221188
  16.4 6.9 %copy-start.6 = (s32[1,2]{1,0:T(1,128)S(1)}, s32[1,2]{1,0:T(1,128)}, u32[]{:S(2)}) copy-start(s32[1,2]{1,0:T(1,128)} %order_ref.2) | copy-start | bytes 28
  16.4 6.9 %copy-start.7 = (s32[64]{0:T(128)S(1)}, s32[64]{0:T(128)}, u32[]{:S(2)}) copy-start(s32[64]{0:T(128)} %offset_ref.3) | copy-start | bytes 772
  16.4 6.9 %copy-start.8 = (f32[64]{0:T(128)S(1)}, f32[64]{0:T(128)}, u32[]{:S(2)}) copy-start(f32[64]{0:T(128)} %fraction_ref.3) | copy-start | bytes 772
  19.5 0.8 copy-start.9
  20.3 0.8 copy-start.11
  21.2 0.7 copy-start.17
  21.9 0.7 copy-start.20
  47.1 30.8 %all-to-all-start.1 = ((bf16[32,16,896]{2,1,0:T(8,128)(2,1)}), bf16[32,16,896]{2,1,0:T(8,128)(2,1)S(1)}, u32[]{:S(2)}, u32[]{:S(2)}) async-start(bf16[32,16,896]{2,1,0:T(8,128)(2,1)} %frame_side.3), calls=%async_computation.1 | async-start | bytes 1835008 | tf_op jit(solution)/shard_map/all_to_all | solution.py:502
  52.7 40.4 %collective-permute-start = (bf16[12,16,1152]{2,1,0:T(8,128)(2,1)}, bf16[12,16,1152]{2,1,0:T(8,128)(2,1)S(1)}, u32[]{:S(2)}, u32[]{:S(2)}) collective-permute-start(bf16[12,16,1152]{2,1,0:T(8,128)(2,1)} %get-tuple-element.60), channel_id=1, source_target_pairs={{0,32},{32,64},{64,96},{96,128},{128,160},{160,192},{192,224},{1,3... | collective-permute-start | bytes 1327112 | tf_op jit(solution)/shard_map/ppermute | solution.py:505
  56.9 37.2 %collective-permute-start.1 = (bf16[12,16,1152]{2,1,0:T(8,128)(2,1)}, bf16[12,16,1152]{2,1,0:T(8,128)(2,1)S(1)}, u32[]{:S(2)}, u32[]{:S(2)}) collective-permute-start(bf16[12,16,1152]{2,1,0:T(8,128)(2,1)} %get-tuple-element.59), channel_id=1, source_target_pairs={{32,0},{64,32},{96,64},{128,96},{160,128},{192,160},{224,192},{33,... | collective-permute-start | bytes 1327112 | tf_op jit(solution)/shard_map/ppermute | solution.py:506
  61.0 1.0 copy-start.18
  61.9 0.9 copy-start.21
  62.9 0.9 copy-start.24
  67.6 1.0 copy-start.13
  68.6 0.9 copy-start.15
  78.0 20.8 %collective-permute-start.2 = (bf16[12,16,896]{2,1,0:T(8,128)(2,1)S(1)}, bf16[12,16,896]{2,1,0:T(8,128)(2,1)S(1)}, u32[]{:S(2)}, u32[]{:S(2)}) collective-permute-start(bf16[12,16,896]{2,1,0:T(8,128)(2,1)S(1)} %get-tuple-element.62), channel_id=1, source_target_pairs={{0,32},{32,64},{64,96},{96,128},{128,160},{160,192},{192,224},{1,3... | collective-permute-start | bytes 1032200 | tf_op jit(solution)/shard_map/ppermute | solution.py:505
  81.7 19.8 %collective-permute-start.3 = (bf16[12,16,896]{2,1,0:T(8,128)(2,1)S(1)}, bf16[12,16,896]{2,1,0:T(8,128)(2,1)S(1)}, u32[]{:S(2)}, u32[]{:S(2)}) collective-permute-start(bf16[12,16,896]{2,1,0:T(8,128)(2,1)S(1)} %get-tuple-element.61), channel_id=1, source_target_pairs={{32,0},{64,32},{96,64},{128,96},{160,128},{192,160},{224,192},{33,... | collective-permute-start | bytes 1032200 | tf_op jit(solution)/shard_map/ppermute | solution.py:506
  86.4 1.0 copy-start.19
  87.4 0.9 copy-start.22
  88.3 0.9 copy-start.25
  89.3 4.9 %copy-start.10 = (bf16[8,160,256]{2,1,0:T(8,128)(2,1)S(1)}, bf16[8,160,256]{2,1,0:T(8,128)(2,1)}, u32[]{:S(2)}) copy-start(bf16[8,160,256]{2,1,0:T(8,128)(2,1)} %copy-done.9) | copy-start | bytes 1966084
  89.3 4.9 %copy-start.12 = (bf16[8,160,256]{2,1,0:T(8,128)(2,1)S(1)}, bf16[8,160,256]{2,1,0:T(8,128)(2,1)}, u32[]{:S(2)}) copy-start(bf16[8,160,256]{2,1,0:T(8,128)(2,1)} %copy-done.11) | copy-start | bytes 1966084
  89.3 4.9 %copy-start.14 = (bf16[416,1152]{1,0:T(8,128)(2,1)S(1)}, bf16[416,1152]{1,0:T(8,128)(2,1)}, u32[]{:S(2)}) copy-start(bf16[416,1152]{1,0:T(8,128)(2,1)} %copy-done.13) | copy-start | bytes 2875396
  89.3 4.9 %copy-start.16 = (f32[192,1152]{1,0:T(8,128)S(1)}, f32[192,1152]{1,0:T(8,128)}, u32[]{:S(2)}) copy-start(f32[192,1152]{1,0:T(8,128)} %copy-done.15) | copy-start | bytes 2654212
  (1 other events, 0.7 us)

commit v14 on v13

--- a/solution.py
+++ b/solution.py
@@ -16,7 +16,7 @@
 ROWS = 8
 BLOCK_ROWS = 128
 LEAD = SHEAR // LANES + 1
-SPLIT = 1152
+SPLIT = 1280
 VMEM = 60 * 1024 * 1024
 BANDS_VMEM = 20 * 1024 * 1024
 RESTORE_VMEM = 26 * 1024 * 1024

time: 107 us -> 108 us (level)
  waiting for transfers between devices: 30.3 us -> 32.3 us
  Pallas kernels: 31.2 us -> 30.1 us
    ppermute x2, waiting for transfers between devices: 3.69 us -> 5.62 us  [with_halo(): high = lax.ppermute(centre[:depth], 'cam', backward)]
  transfers between devices with their start and end apart: 6 -> 6, of which waited for: 4 -> 4; matrix products, arithmetic and copies ran while one was open for 1% -> 1% of each run, Pallas kernels for 20% -> 19%
where the time goes in v14:
time: 108 us; the launch traced here: 107 us
  waiting for transfers between devices  32.3 us (30%)
  starting transfers between devices  31.2 us (29%)
  Pallas kernels  30.1 us (28%)
  local copies, waits for them, and re-layouts  12.9 us (12%)
    all_to_all x2, waiting for transfers between devices, exchange(): lax.all_to_all(piece, 'brick', split_axis=0, concat_axis=0, tiled=True)  26.6 us
    pallas_call x4, Pallas kernels, restore(): pl.pallas_call(functools.partial(restore_kernel, plan, inside, half, [len...  15.8 us
    all_to_all x2, starting transfers between devices, exchange(): lax.all_to_all(piece, 'brick', split_axis=0, concat_axis=0, tiled=True)  14.5 us
    unnamed x54, local copies, waits for them, and re-layouts  11.5 us
    pallas_call x2, Pallas kernels, frame_side(): pl.pallas_call(functools.partial(frame_kernel, first, count), grid=(steps...  11.2 us
    ppermute x2, starting transfers between devices, with_halo(): low = lax.ppermute(centre[-depth:], 'cam', forward)  8.39 us
    ppermute x2, starting transfers between devices, with_halo(): high = lax.ppermute(centre[:depth], 'cam', backward)  8.26 us
    ppermute x2, waiting for transfers between devices, with_halo(): high = lax.ppermute(centre[:depth], 'cam', backward)  5.62 us
  transfers between devices with their start and end apart: 6, of which 4 were waited for; matrix products, arithmetic and copies ran while one was open for 1% of the time, Pallas kernels for 19%

profile of v14, /device:TPU:14, one launch (start us, length us, event | category | flops | bytes accessed | tf_op | source)
XLA Modules:
  0.0 106.8 jit_solution(13485290436196051201)
XLA Ops:
  0.0 6.2 %frame_side.2 = bf16[32,16,1280]{2,1,0:T(8,128)(2,1)} custom-call(s32[1,2]{1,0:T(1,128)} %order_ref.2, s32[64]{0:T(128)} %offset_ref.3, f32[64]{0:T(128)} %fraction_ref.3, bf16[2,256,2048]{2,1,0:T(8,128)(2,1)} %raw_next.3, bf16[2,256,2048]{2,1,0:T(8,128)(2,1)} %raw_next.3, bf16[2,256,2048]{2,1,0:T(8,128)(2,1)} %raw_next.3, bf16[256,2048]{1,0:T(8,128)(2,1)} %dark_next.3, ...), custom_call_target="tpu_custom_call" | custom-call | flops 8000000000 | bytes 6500000 | tf_op jit(solution)/shard_map/frame_side/pallas_call | solution.py:123
  6.2 10.2 %all-to-all-start = ((bf16[32,16,1280]{2,1,0:T(8,128)(2,1)}), bf16[32,16,1280]{2,1,0:T(8,128)(2,1)S(1)}, u32[]{:S(2)}, u32[]{:S(2)}) async-start(bf16[32,16,1280]{2,1,0:T(8,128)(2,1)} %frame_side.2), calls=%async_computation | async-start | bytes 2621440 | tf_op jit(solution)/shard_map/all_to_all | solution.py:502
  16.6 0.1 reshape.4.index_ref
  16.8 3.0 %bands.1 = (bf16[5,160,256]{2,1,0:T(8,128)(2,1)S(1)}, bf16[3,160,256]{2,1,0:T(8,128)(2,1)S(1)}, bf16[8,160,256]{2,1,0:T(8,128)(2,1)S(1)}, bf16[8,160,256]{2,1,0:...) custom-call(f32[8,13]{1,0:T(8,128)S(1)} %copy-done.4, f32[9]{0:T(128)S(1)} %copy-done.5, ...), custom_call_target="tpu_custom_call" | custom-call | flops 2000000000 | bytes 2000000 | tf_op jit(solution)/shard_map/bands/pallas_call | solution.py:233
  19.9 0.8 copy-done.13
  20.7 0.9 copy-done.15
  21.6 0.7 copy-done.17
  22.3 0.7 copy-done.20
  23.0 0.7 copy-done.23
  23.8 5.0 %frame_side.3 = bf16[32,16,768]{2,1,0:T(8,128)(2,1)} custom-call(s32[1,2]{1,0:T(1,128)S(1)} %copy-done.6, s32[64]{0:T(128)S(1)} %copy-done.7, f32[64]{0:T(128)S(1)} %copy-done.8, bf16[2,256,2048]{2,1,0:T(8,128)(2,1)S(1)} %copy-done, bf16[2,256,2048]{2,1,0:T(8,128)(2,1)S(1)} %copy-done, bf16[2,256,2048]{2,1,0:T(8,128)(2,1)S(1)} %copy-done, ...), custom_call_target="tpu_custom_call" | custom-call | flops 8000000000 | bytes 6500000 | tf_op jit(solution)/shard_map/frame_side/pallas_call | solution.py:123
  28.8 21.4 %all-to-all-done.refs_0_.refs_1_ = bf16[32,16,1280]{2,1,0:T(8,128)(2,1)S(1)} async-done(((bf16[32,16,1280]{2,1,0:T(8,128)(2,1)}), bf16[32,16,1280]{2,1,0:T(8,128)(2,1)S(1)}, u32[]{:S(2)}, u32[]{:S(2)}) %all-to-all-start) | async-done | bytes 1310752 | tf_op jit(solution)/shard_map/all_to_all | solution.py:502
  50.2 4.3 %all-to-all-start.1 = ((bf16[32,16,768]{2,1,0:T(8,128)(2,1)}), bf16[32,16,768]{2,1,0:T(8,128)(2,1)S(1)}, u32[]{:S(2)}, u32[]{:S(2)}) async-start(bf16[32,16,768]{2,1,0:T(8,128)(2,1)} %frame_side.3), calls=%async_computation.1 | async-start | bytes 1572864 | tf_op jit(solution)/shard_map/all_to_all | solution.py:502
  54.5 1.1 fusion
  55.5 4.2 %collective-permute-start = (bf16[12,16,1280]{2,1,0:T(8,128)(2,1)}, bf16[12,16,1280]{2,1,0:T(8,128)(2,1)S(1)}, u32[]{:S(2)}, u32[]{:S(2)}) collective-permute-start(bf16[12,16,1280]{2,1,0:T(8,128)(2,1)} %get-tuple-element.60), channel_id=1, source_target_pairs={{0,32},{32,64},{64,96},{96,128},{128,160},{160,192},{192,224},{1,3... | collective-permute-start | bytes 1474568 | tf_op jit(solution)/shard_map/ppermute | solution.py:505
  59.7 4.0 %collective-permute-start.1 = (bf16[12,16,1280]{2,1,0:T(8,128)(2,1)}, bf16[12,16,1280]{2,1,0:T(8,128)(2,1)S(1)}, u32[]{:S(2)}, u32[]{:S(2)}) collective-permute-start(bf16[12,16,1280]{2,1,0:T(8,128)(2,1)} %get-tuple-element.59), channel_id=1, source_target_pairs={{32,0},{64,32},{96,64},{128,96},{160,128},{192,160},{224,192},{33,... | collective-permute-start | bytes 1474568 | tf_op jit(solution)/shard_map/ppermute | solution.py:506
  63.8 0.9 copy-done.18
  64.7 0.9 copy-done.21
  65.7 0.9 copy-done.24
  66.6 4.0 %inside.2 = (bf16[64,8,2048]{2,1,0:T(8,128)(2,1)}, bf16[416,1280]{1,0:T(8,128)(2,1)S(1)}, f32[192,1280]{1,0:T(8,128)S(1)}) custom-call(bf16[32,16,1280]{2,1,0:T(8,128)(2,1)S(1)} %all-to-all-done.refs_0_.refs_1_, bf16[5,160,256]{2,1,0:T(8,128)(2,1)S(1)} %get-tuple-element.42.refs_1_.refs_2_, bf16[3,160,256]{2,1,0:T(8,128)(2,1)S(1)} %copy-done.24, ...), custom_call_target="tpu_custom_call" | custom-call | flops 5000000000 | bytes 8000000 | tf_op jit(solution)/shard_map/inside/pallas_call | solution.py:442
  70.6 1.0 copy-done.9
  71.6 0.9 copy-done.11
  72.5 5.3 %all-to-all-done.1.refs_1_.refs_4_ = bf16[32,16,768]{2,1,0:T(8,128)(2,1)S(1)} async-done(((bf16[32,16,768]{2,1,0:T(8,128)(2,1)}), bf16[32,16,768]{2,1,0:T(8,128)(2,1)S(1)}, u32[]{:S(2)}, u32[]{:S(2)}) %all-to-all-start.1) | async-done | bytes 786464 | tf_op jit(solution)/shard_map/all_to_all | solution.py:502
  77.8 4.2 %collective-permute-start.2 = (bf16[12,16,768]{2,1,0:T(8,128)(2,1)S(1)}, bf16[12,16,768]{2,1,0:T(8,128)(2,1)S(1)}, u32[]{:S(2)}, u32[]{:S(2)}) collective-permute-start(bf16[12,16,768]{2,1,0:T(8,128)(2,1)S(1)} %get-tuple-element.62), channel_id=1, source_target_pairs={{0,32},{32,64},{64,96},{96,128},{128,160},{160,192},{192,224},{1,3... | collective-permute-start | bytes 884744 | tf_op jit(solution)/shard_map/ppermute | solution.py:505
  82.1 4.2 %collective-permute-start.3 = (bf16[12,16,768]{2,1,0:T(8,128)(2,1)S(1)}, bf16[12,16,768]{2,1,0:T(8,128)(2,1)S(1)}, u32[]{:S(2)}, u32[]{:S(2)}) collective-permute-start(bf16[12,16,768]{2,1,0:T(8,128)(2,1)S(1)} %get-tuple-element.61), channel_id=1, source_target_pairs={{32,0},{64,32},{96,64},{128,96},{160,128},{192,160},{224,192},{33,... | collective-permute-start | bytes 884744 | tf_op jit(solution)/shard_map/ppermute | solution.py:506
  86.3 0.9 copy-done.19
  87.2 0.9 copy-done.22
  88.2 0.9 copy-done.25
  89.1 3.3 %inside.3 = (bf16[64,8,2048]{2,1,0:T(8,128)(2,1)}, bf16[416,1024]{1,0:T(8,128)(2,1)S(1)}, f32[192,1024]{1,0:T(8,128)S(1)}) custom-call(bf16[32,16,1280]{2,1,0:T(8,128)(2,1)S(1)} %all-to-all-done.refs_0_.refs_1_, bf16[32,16,768]{2,1,0:T(8,128)(2,1)S(1)} %all-to-all-done.1.refs_1_.refs_4_, ...), custom_call_target="tpu_custom_call", output_to_operand_aliasing={{0}: (6, {})} | custom-call | flops 5000000000 | bytes 8000000 | tf_op jit(solution)/shard_map/inside/pallas_call | solution.py:442
  92.5 3.9 %collective-permute-done.1.refs_2_ = bf16[12,16,1280]{2,1,0:T(8,128)(2,1)S(1)} collective-permute-done((bf16[12,16,1280]{2,1,0:T(8,128)(2,1)}, bf16[12,16,1280]{2,1,0:T(8,128)(2,1)S(1)}, u32[]{:S(2)}, u32[]{:S(2)}) %collective-permute-start.1) | collective-permute-done | bytes 491552 | tf_op jit(solution)/shard_map/ppermute | solution.py:506
  96.5 4.5 %ends.2.refs_12_ = bf16[64,8,2048]{2,1,0:T(8,128)(2,1)} custom-call(bf16[12,16,1280]{2,1,0:T(8,128)(2,1)S(1)} %collective-permute-done.refs_0_, bf16[32,16,1280]{2,1,0:T(8,128)(2,1)S(1)} %all-to-all-done.refs_0_.refs_1_, bf16[12,16,1280]{2,1,0:T(8,128)(2,1)S(1)} %collective-permute-done.1.refs_2_, ...), custom_call_target="tpu_custom_call", output_to_operand_aliasing={{}: (9, {})} | custom-call | flops 5000000000 | bytes 8000000 | tf_op jit(solution)/shard_map/ends/pallas_call | solution.py:442
  101.0 1.7 %collective-permute-done.3.refs_5_ = bf16[12,16,768]{2,1,0:T(8,128)(2,1)S(1)} collective-permute-done((bf16[12,16,768]{2,1,0:T(8,128)(2,1)S(1)}, bf16[12,16,768]{2,1,0:T(8,128)(2,1)S(1)}, u32[]{:S(2)}, u32[]{:S(2)}) %collective-permute-start.3) | collective-permute-done | bytes 294944 | tf_op jit(solution)/shard_map/ppermute | solution.py:506
  102.7 4.0 %ends.3 = bf16[64,8,2048]{2,1,0:T(8,128)(2,1)} custom-call(bf16[12,16,1280]{2,1,0:T(8,128)(2,1)S(1)} %collective-permute-done.refs_0_, bf16[32,16,1280]{2,1,0:T(8,128)(2,1)S(1)} %all-to-all-done.refs_0_.refs_1_, bf16[12,16,1280]{2,1,0:T(8,128)(2,1)S(1)} %collective-permute-done.1.refs_2_, ...), custom_call_target="tpu_custom_call", output_to_operand_aliasing={{}: (12, {})} | custom-call | flops 5000000000 | bytes 8000000 | tf_op jit(solution)/shard_map/ends/pallas_call | solution.py:442
  (46 shorter events, 0.3 us)
Async XLA Ops:
  6.2 10.3 %copy-start.26 = (s32[512]{0:T(512)S(1)}, s32[512]{0:T(512)}, u32[]{:S(2)}) copy-start(s32[512]{0:T(512)} %param.17) | copy-start | bytes 6148
  6.2 10.6 %copy-start.4 = (f32[8,13]{1,0:T(8,128)S(1)}, f32[8,13]{1,0:T(8,128)}, u32[]{:S(2)}) copy-start(f32[8,13]{1,0:T(8,128)} %psf_ref.1) | copy-start | bytes 1252
  6.2 10.6 %copy-start.5 = (f32[9]{0:T(128)S(1)}, f32[9]{0:T(128)}, u32[]{:S(2)}) copy-start(f32[9]{0:T(128)} %lateral_ref.1) | copy-start | bytes 112
  6.2 44.0 %all-to-all-start = ((bf16[32,16,1280]{2,1,0:T(8,128)(2,1)}), bf16[32,16,1280]{2,1,0:T(8,128)(2,1)S(1)}, u32[]{:S(2)}, u32[]{:S(2)}) async-start(bf16[32,16,1280]{2,1,0:T(8,128)(2,1)} %frame_side.2), calls=%async_computation | async-start | bytes 2621440 | tf_op jit(solution)/shard_map/all_to_all | solution.py:502
  16.8 7.0 %copy-start = (bf16[2,256,2048]{2,1,0:T(8,128)(2,1)S(1)}, bf16[2,256,2048]{2,1,0:T(8,128)(2,1)}, u32[]{:S(2)}) copy-start(bf16[2,256,2048]{2,1,0:T(8,128)(2,1)} %raw_next.3) | copy-start | bytes 6291460
  16.8 7.0 %copy-start.1 = (bf16[256,2048]{1,0:T(8,128)(2,1)S(1)}, bf16[256,2048]{1,0:T(8,128)(2,1)}, u32[]{:S(2)}) copy-start(bf16[256,2048]{1,0:T(8,128)(2,1)} %dark_next.3) | copy-start | bytes 3145732
  16.8 7.0 %copy-start.2 = (bf16[256,2048]{1,0:T(8,128)(2,1)S(1)}, bf16[256,2048]{1,0:T(8,128)(2,1)}, u32[]{:S(2)}) copy-start(bf16[256,2048]{1,0:T(8,128)(2,1)} %gain_next.3) | copy-start | bytes 3145732
  16.8 7.0 %copy-start.3 = (f32[9,2048]{1,0:T(8,128)S(1)}, f32[9,2048]{1,0:T(8,128)}, u32[]{:S(2)}) copy-start(f32[9,2048]{1,0:T(8,128)} %band_ref.3) | copy-start | bytes 221188
  16.8 6.9 %copy-start.6 = (s32[1,2]{1,0:T(1,128)S(1)}, s32[1,2]{1,0:T(1,128)}, u32[]{:S(2)}) copy-start(s32[1,2]{1,0:T(1,128)} %order_ref.2) | copy-start | bytes 28
  16.8 6.9 %copy-start.7 = (s32[64]{0:T(128)S(1)}, s32[64]{0:T(128)}, u32[]{:S(2)}) copy-start(s32[64]{0:T(128)} %offset_ref.3) | copy-start | bytes 772
  16.8 6.9 %copy-start.8 = (f32[64]{0:T(128)S(1)}, f32[64]{0:T(128)}, u32[]{:S(2)}) copy-start(f32[64]{0:T(128)} %fraction_ref.3) | copy-start | bytes 772
  19.9 0.8 copy-start.13
  20.7 0.9 copy-start.15
  21.6 0.7 copy-start.17
  22.3 0.7 copy-start.20
  50.2 27.6 %all-to-all-start.1 = ((bf16[32,16,768]{2,1,0:T(8,128)(2,1)}), bf16[32,16,768]{2,1,0:T(8,128)(2,1)S(1)}, u32[]{:S(2)}, u32[]{:S(2)}) async-start(bf16[32,16,768]{2,1,0:T(8,128)(2,1)} %frame_side.3), calls=%async_computation.1 | async-start | bytes 1572864 | tf_op jit(solution)/shard_map/all_to_all | solution.py:502
  55.5 37.0 %collective-permute-start = (bf16[12,16,1280]{2,1,0:T(8,128)(2,1)}, bf16[12,16,1280]{2,1,0:T(8,128)(2,1)S(1)}, u32[]{:S(2)}, u32[]{:S(2)}) collective-permute-start(bf16[12,16,1280]{2,1,0:T(8,128)(2,1)} %get-tuple-element.60), channel_id=1, source_target_pairs={{0,32},{32,64},{64,96},{96,128},{128,160},{160,192},{192,224},{1,3... | collective-permute-start | bytes 1474568 | tf_op jit(solution)/shard_map/ppermute | solution.py:505
  59.7 36.7 %collective-permute-start.1 = (bf16[12,16,1280]{2,1,0:T(8,128)(2,1)}, bf16[12,16,1280]{2,1,0:T(8,128)(2,1)S(1)}, u32[]{:S(2)}, u32[]{:S(2)}) collective-permute-start(bf16[12,16,1280]{2,1,0:T(8,128)(2,1)} %get-tuple-element.59), channel_id=1, source_target_pairs={{32,0},{64,32},{96,64},{128,96},{160,128},{192,160},{224,192},{33,... | collective-permute-start | bytes 1474568 | tf_op jit(solution)/shard_map/ppermute | solution.py:506
  63.8 1.0 copy-start.18
  64.7 0.9 copy-start.21
  65.7 0.9 copy-start.24
  70.6 1.0 copy-start.9
  71.6 0.9 copy-start.11
  77.8 23.1 %collective-permute-start.2 = (bf16[12,16,768]{2,1,0:T(8,128)(2,1)S(1)}, bf16[12,16,768]{2,1,0:T(8,128)(2,1)S(1)}, u32[]{:S(2)}, u32[]{:S(2)}) collective-permute-start(bf16[12,16,768]{2,1,0:T(8,128)(2,1)S(1)} %get-tuple-element.62), channel_id=1, source_target_pairs={{0,32},{32,64},{64,96},{96,128},{128,160},{160,192},{192,224},{1,3... | collective-permute-start | bytes 884744 | tf_op jit(solution)/shard_map/ppermute | solution.py:505
  82.1 20.6 %collective-permute-start.3 = (bf16[12,16,768]{2,1,0:T(8,128)(2,1)S(1)}, bf16[12,16,768]{2,1,0:T(8,128)(2,1)S(1)}, u32[]{:S(2)}, u32[]{:S(2)}) collective-permute-start(bf16[12,16,768]{2,1,0:T(8,128)(2,1)S(1)} %get-tuple-element.61), channel_id=1, source_target_pairs={{32,0},{64,32},{96,64},{128,96},{160,128},{192,160},{224,192},{33,... | collective-permute-start | bytes 884744 | tf_op jit(solution)/shard_map/ppermute | solution.py:506
  86.3 1.0 copy-start.19
  87.2 0.9 copy-start.22
  88.2 0.9 copy-start.25
  89.1 7.3 %copy-start.10 = (bf16[416,1280]{1,0:T(8,128)(2,1)S(1)}, bf16[416,1280]{1,0:T(8,128)(2,1)}, u32[]{:S(2)}) copy-start(bf16[416,1280]{1,0:T(8,128)(2,1)} %copy-done.9) | copy-start | bytes 3194884
  89.1 7.3 %copy-start.12 = (f32[192,1280]{1,0:T(8,128)S(1)}, f32[192,1280]{1,0:T(8,128)}, u32[]{:S(2)}) copy-start(f32[192,1280]{1,0:T(8,128)} %copy-done.11) | copy-start | bytes 2949124
  89.1 7.3 %copy-start.14 = (bf16[8,160,256]{2,1,0:T(8,128)(2,1)S(1)}, bf16[8,160,256]{2,1,0:T(8,128)(2,1)}, u32[]{:S(2)}) copy-start(bf16[8,160,256]{2,1,0:T(8,128)(2,1)} %copy-done.13) | copy-start | bytes 1966084
  89.1 7.3 %copy-start.16 = (bf16[8,160,256]{2,1,0:T(8,128)(2,1)S(1)}, bf16[8,160,256]{2,1,0:T(8,128)(2,1)}, u32[]{:S(2)}) copy-start(bf16[8,160,256]{2,1,0:T(8,128)(2,1)} %copy-done.15) | copy-start | bytes 1966084
  (1 other events, 0.7 us)

commit v15 on v14

--- a/solution.py
+++ b/solution.py
@@ -16,7 +16,7 @@
 ROWS = 8
 BLOCK_ROWS = 128
 LEAD = SHEAR // LANES + 1
-SPLIT = 1280
+SPLIT = 1024
 VMEM = 60 * 1024 * 1024
 BANDS_VMEM = 20 * 1024 * 1024
 RESTORE_VMEM = 26 * 1024 * 1024

time: 108 us -> 107 us (level)
  waiting for transfers between devices: 32.3 us -> 30.3 us
  local copies, waits for them, and re-layouts: 12.9 us -> 14.5 us
    ppermute x2, waiting for transfers between devices: 5.62 us -> 3.48 us  [with_halo(): high = lax.ppermute(centre[:depth], 'cam', backward)]
    unnamed x54 -> x56, local copies, waits for them, and re-layouts: 11.5 us -> 13.2 us
  transfers between devices with their start and end apart: 6 -> 6, of which waited for: 4 -> 3; matrix products, arithmetic and copies ran while one was open for 1% -> 1% of each run, Pallas kernels for 19% -> 19%
where the time goes in v15:
time: 107 us; the launch traced here: 106 us
  starting transfers between devices  30.9 us (29%)
  waiting for transfers between devices  30.3 us (28%)
  Pallas kernels  30.1 us (28%)
  local copies, waits for them, and re-layouts  14.5 us (14%)
    all_to_all x2, waiting for transfers between devices, exchange(): lax.all_to_all(piece, 'brick', split_axis=0, concat_axis=0, tiled=True)  26.8 us
    pallas_call x4, Pallas kernels, restore(): pl.pallas_call(functools.partial(restore_kernel, plan, inside, half, [len...  15.8 us
    all_to_all x2, starting transfers between devices, exchange(): lax.all_to_all(piece, 'brick', split_axis=0, concat_axis=0, tiled=True)  14.2 us
    unnamed x56, local copies, waits for them, and re-layouts  13.2 us
    pallas_call x2, Pallas kernels, frame_side(): pl.pallas_call(functools.partial(frame_kernel, first, count), grid=(steps...  11.3 us
    ppermute x2, starting transfers between devices, with_halo(): high = lax.ppermute(centre[:depth], 'cam', backward)  8.85 us
    ppermute x2, starting transfers between devices, with_halo(): low = lax.ppermute(centre[-depth:], 'cam', forward)  7.81 us
    ppermute x2, waiting for transfers between devices, with_halo(): high = lax.ppermute(centre[:depth], 'cam', backward)  3.48 us
  transfers between devices with their start and end apart: 6, of which 3 were waited for; matrix products, arithmetic and copies ran while one was open for 1% of the time, Pallas kernels for 19%

profile of v15, /device:TPU:14, one launch (start us, length us, event | category | flops | bytes accessed | tf_op | source)
XLA Modules:
  0.0 106.2 jit_solution(13579562620863370275)
XLA Ops:
  0.0 5.4 %frame_side.2 = bf16[32,16,1024]{2,1,0:T(8,128)(2,1)} custom-call(s32[1,2]{1,0:T(1,128)} %order_ref.2, s32[64]{0:T(128)} %offset_ref.3, f32[64]{0:T(128)} %fraction_ref.3, bf16[2,256,2048]{2,1,0:T(8,128)(2,1)} %raw_next.3, bf16[2,256,2048]{2,1,0:T(8,128)(2,1)} %raw_next.3, bf16[2,256,2048]{2,1,0:T(8,128)(2,1)} %raw_next.3, bf16[256,2048]{1,0:T(8,128)(2,1)} %dark_next.3, ...), custom_call_target="tpu_custom_call" | custom-call | flops 8000000000 | bytes 6500000 | tf_op jit(solution)/shard_map/frame_side/pallas_call | solution.py:123
  5.5 10.2 %all-to-all-start = ((bf16[32,16,1024]{2,1,0:T(8,128)(2,1)}), bf16[32,16,1024]{2,1,0:T(8,128)(2,1)S(1)}, u32[]{:S(2)}, u32[]{:S(2)}) async-start(bf16[32,16,1024]{2,1,0:T(8,128)(2,1)} %frame_side.2), calls=%async_computation | async-start | bytes 2097152 | tf_op jit(solution)/shard_map/all_to_all | solution.py:502
  16.1 3.0 %bands.1 = (bf16[5,160,256]{2,1,0:T(8,128)(2,1)S(1)}, bf16[3,160,256]{2,1,0:T(8,128)(2,1)S(1)}, bf16[8,160,256]{2,1,0:T(8,128)(2,1)S(1)}, bf16[8,160,256]{2,1,0:...) custom-call(f32[8,13]{1,0:T(8,128)S(1)} %copy-done.4, f32[9]{0:T(128)S(1)} %copy-done.5, ...), custom_call_target="tpu_custom_call" | custom-call | flops 2000000000 | bytes 2000000 | tf_op jit(solution)/shard_map/bands/pallas_call | solution.py:233
  19.2 0.8 copy-done.9
  20.0 0.7 copy-done.15
  20.7 0.7 copy-done.18
  21.4 0.7 copy-done.21
  22.2 0.7 copy-done.24
  22.9 5.8 %frame_side.3 = bf16[32,16,1024]{2,1,0:T(8,128)(2,1)} custom-call(s32[1,2]{1,0:T(1,128)S(1)} %copy-done.6, s32[64]{0:T(128)S(1)} %copy-done.7, f32[64]{0:T(128)S(1)} %copy-done.8, bf16[2,256,2048]{2,1,0:T(8,128)(2,1)S(1)} %copy-done, bf16[2,256,2048]{2,1,0:T(8,128)(2,1)S(1)} %copy-done, bf16[2,256,2048]{2,1,0:T(8,128)(2,1)S(1)} %copy-done, ...), custom_call_target="tpu_custom_call" | custom-call | flops 8000000000 | bytes 6500000 | tf_op jit(solution)/shard_map/frame_side/pallas_call | solution.py:123
  28.7 15.9 %all-to-all-done.refs_0_.refs_1_ = bf16[32,16,1024]{2,1,0:T(8,128)(2,1)S(1)} async-done(((bf16[32,16,1024]{2,1,0:T(8,128)(2,1)}), bf16[32,16,1024]{2,1,0:T(8,128)(2,1)S(1)}, u32[]{:S(2)}, u32[]{:S(2)}) %all-to-all-start) | async-done | bytes 1048608 | tf_op jit(solution)/shard_map/all_to_all | solution.py:502
  44.7 4.0 %all-to-all-start.1 = ((bf16[32,16,1024]{2,1,0:T(8,128)(2,1)}), bf16[32,16,1024]{2,1,0:T(8,128)(2,1)S(1)}, u32[]{:S(2)}, u32[]{:S(2)}) async-start(bf16[32,16,1024]{2,1,0:T(8,128)(2,1)} %frame_side.3), calls=%async_computation.1 | async-start | bytes 2097152 | tf_op jit(solution)/shard_map/all_to_all | solution.py:502
  48.7 0.9 fusion.1
  49.6 4.2 %collective-permute-start = (bf16[12,16,1024]{2,1,0:T(8,128)(2,1)}, bf16[12,16,1024]{2,1,0:T(8,128)(2,1)S(1)}, u32[]{:S(2)}, u32[]{:S(2)}) collective-permute-start(bf16[12,16,1024]{2,1,0:T(8,128)(2,1)} %get-tuple-element.62), channel_id=1, source_target_pairs={{0,32},{32,64},{64,96},{96,128},{128,160},{160,192},{192,224},{1,3... | collective-permute-start | bytes 1179656 | tf_op jit(solution)/shard_map/ppermute | solution.py:505
  53.8 4.0 %collective-permute-start.1 = (bf16[12,16,1024]{2,1,0:T(8,128)(2,1)}, bf16[12,16,1024]{2,1,0:T(8,128)(2,1)S(1)}, u32[]{:S(2)}, u32[]{:S(2)}) collective-permute-start(bf16[12,16,1024]{2,1,0:T(8,128)(2,1)} %get-tuple-element.61), channel_id=1, source_target_pairs={{32,0},{64,32},{96,64},{128,96},{160,128},{192,160},{224,192},{33,... | collective-permute-start | bytes 1179656 | tf_op jit(solution)/shard_map/ppermute | solution.py:506
  57.9 1.0 copy-done.16
  58.9 0.9 copy-done.19
  59.8 0.9 copy-done.22
  60.8 0.9 copy-done.25
  61.7 3.3 %inside.2 = (bf16[64,8,2048]{2,1,0:T(8,128)(2,1)}, bf16[416,1024]{1,0:T(8,128)(2,1)S(1)}, f32[192,1024]{1,0:T(8,128)S(1)}) custom-call(bf16[32,16,1024]{2,1,0:T(8,128)(2,1)S(1)} %all-to-all-done.refs_0_.refs_1_, bf16[5,160,256]{2,1,0:T(8,128)(2,1)S(1)} %copy-done.16, bf16[3,160,256]{2,1,0:T(8,128)(2,1)S(1)} %copy-done.25, bf16[512,256]{1,0:T(8,128)(2,1)S(1)} %copy-done.19, ...), custom_call_target="tpu_custom_call" | custom-call | flops 5000000000 | bytes 8000000 | tf_op jit(solution)/shard_map/inside/pallas_call | solution.py:442
  65.0 0.9 copy-done.11
  65.9 0.9 copy-done.13
  66.8 10.9 %all-to-all-done.1.refs_1_.refs_4_ = bf16[32,16,1024]{2,1,0:T(8,128)(2,1)S(1)} async-done(((bf16[32,16,1024]{2,1,0:T(8,128)(2,1)}), bf16[32,16,1024]{2,1,0:T(8,128)(2,1)S(1)}, u32[]{:S(2)}, u32[]{:S(2)}) %all-to-all-start.1) | async-done | bytes 1048608 | tf_op jit(solution)/shard_map/all_to_all | solution.py:502
  77.7 3.6 %collective-permute-start.2 = (bf16[12,16,1024]{2,1,0:T(8,128)(2,1)S(1)}, bf16[12,16,1024]{2,1,0:T(8,128)(2,1)S(1)}, u32[]{:S(2)}, u32[]{:S(2)}) collective-permute-start(bf16[12,16,1024]{2,1,0:T(8,128)(2,1)S(1)} %get-tuple-element.60), channel_id=1, source_target_pairs={{0,32},{32,64},{64,96},{96,128},{128,160},{160,192},{192,224},{1,3... | collective-permute-start | bytes 1179656 | tf_op jit(solution)/shard_map/ppermute | solution.py:505
  81.4 4.8 %collective-permute-start.3 = (bf16[12,16,1024]{2,1,0:T(8,128)(2,1)S(1)}, bf16[12,16,1024]{2,1,0:T(8,128)(2,1)S(1)}, u32[]{:S(2)}, u32[]{:S(2)}) collective-permute-start(bf16[12,16,1024]{2,1,0:T(8,128)(2,1)S(1)} %get-tuple-element.59), channel_id=1, source_target_pairs={{32,0},{64,32},{96,64},{128,96},{160,128},{192,160},{224,192},{33,... | collective-permute-start | bytes 1179656 | tf_op jit(solution)/shard_map/ppermute | solution.py:506
  86.2 1.0 copy-done.17
  87.2 0.9 copy-done.20
  88.1 0.9 copy-done.23
  89.1 0.9 copy-done.26
  90.0 4.0 %inside.3 = (bf16[64,8,2048]{2,1,0:T(8,128)(2,1)}, bf16[416,1280]{1,0:T(8,128)(2,1)S(1)}, f32[192,1280]{1,0:T(8,128)S(1)}) custom-call(bf16[32,16,1024]{2,1,0:T(8,128)(2,1)S(1)} %all-to-all-done.refs_0_.refs_1_, bf16[32,16,1024]{2,1,0:T(8,128)(2,1)S(1)} %all-to-all-done.1.refs_1_.refs_4_, ...), custom_call_target="tpu_custom_call", output_to_operand_aliasing={{0}: (6, {})} | custom-call | flops 5000000000 | bytes 8000000 | tf_op jit(solution)/shard_map/inside/pallas_call | solution.py:442
  94.1 4.0 %ends.2.refs_12_ = bf16[64,8,2048]{2,1,0:T(8,128)(2,1)} custom-call(bf16[12,16,1024]{2,1,0:T(8,128)(2,1)S(1)} %collective-permute-done.refs_0_, bf16[32,16,1024]{2,1,0:T(8,128)(2,1)S(1)} %all-to-all-done.refs_0_.refs_1_, bf16[12,16,1024]{2,1,0:T(8,128)(2,1)S(1)} %collective-permute-done.1.refs_2_, ...), custom_call_target="tpu_custom_call", output_to_operand_aliasing={{}: (9, {})} | custom-call | flops 5000000000 | bytes 8000000 | tf_op jit(solution)/shard_map/ends/pallas_call | solution.py:442
  98.1 3.5 %collective-permute-done.3.refs_5_ = bf16[12,16,1024]{2,1,0:T(8,128)(2,1)S(1)} collective-permute-done((bf16[12,16,1024]{2,1,0:T(8,128)(2,1)S(1)}, bf16[12,16,1024]{2,1,0:T(8,128)(2,1)S(1)}, u32[]{:S(2)}, u32[]{:S(2)}) %collective-permute-start.3) | collective-permute-done | bytes 393248 | tf_op jit(solution)/shard_map/ppermute | solution.py:506
  101.6 4.5 %ends.3 = bf16[64,8,2048]{2,1,0:T(8,128)(2,1)} custom-call(bf16[12,16,1024]{2,1,0:T(8,128)(2,1)S(1)} %collective-permute-done.refs_0_, bf16[32,16,1024]{2,1,0:T(8,128)(2,1)S(1)} %all-to-all-done.refs_0_.refs_1_, bf16[12,16,1024]{2,1,0:T(8,128)(2,1)S(1)} %collective-permute-done.1.refs_2_, ...), custom_call_target="tpu_custom_call", output_to_operand_aliasing={{}: (12, {})} | custom-call | flops 5000000000 | bytes 8000000 | tf_op jit(solution)/shard_map/ends/pallas_call | solution.py:442
  (48 shorter events, 0.5 us)
Async XLA Ops:
  5.5 10.3 %copy-start.27 = (s32[512]{0:T(512)S(1)}, s32[512]{0:T(512)}, u32[]{:S(2)}) copy-start(s32[512]{0:T(512)} %param.17) | copy-start | bytes 6148
  5.5 10.6 %copy-start.4 = (f32[8,13]{1,0:T(8,128)S(1)}, f32[8,13]{1,0:T(8,128)}, u32[]{:S(2)}) copy-start(f32[8,13]{1,0:T(8,128)} %psf_ref.1) | copy-start | bytes 1252
  5.5 10.6 %copy-start.5 = (f32[9]{0:T(128)S(1)}, f32[9]{0:T(128)}, u32[]{:S(2)}) copy-start(f32[9]{0:T(128)} %lateral_ref.1) | copy-start | bytes 112
  5.5 39.2 %all-to-all-start = ((bf16[32,16,1024]{2,1,0:T(8,128)(2,1)}), bf16[32,16,1024]{2,1,0:T(8,128)(2,1)S(1)}, u32[]{:S(2)}, u32[]{:S(2)}) async-start(bf16[32,16,1024]{2,1,0:T(8,128)(2,1)} %frame_side.2), calls=%async_computation | async-start | bytes 2097152 | tf_op jit(solution)/shard_map/all_to_all | solution.py:502
  16.0 6.8 %copy-start = (bf16[2,256,2048]{2,1,0:T(8,128)(2,1)S(1)}, bf16[2,256,2048]{2,1,0:T(8,128)(2,1)}, u32[]{:S(2)}) copy-start(bf16[2,256,2048]{2,1,0:T(8,128)(2,1)} %raw_next.3) | copy-start | bytes 6291460
  16.0 6.8 %copy-start.1 = (bf16[256,2048]{1,0:T(8,128)(2,1)S(1)}, bf16[256,2048]{1,0:T(8,128)(2,1)}, u32[]{:S(2)}) copy-start(bf16[256,2048]{1,0:T(8,128)(2,1)} %dark_next.3) | copy-start | bytes 3145732
  16.1 6.8 %copy-start.2 = (bf16[256,2048]{1,0:T(8,128)(2,1)S(1)}, bf16[256,2048]{1,0:T(8,128)(2,1)}, u32[]{:S(2)}) copy-start(bf16[256,2048]{1,0:T(8,128)(2,1)} %gain_next.3) | copy-start | bytes 3145732
  16.1 6.8 %copy-start.3 = (f32[9,2048]{1,0:T(8,128)S(1)}, f32[9,2048]{1,0:T(8,128)}, u32[]{:S(2)}) copy-start(f32[9,2048]{1,0:T(8,128)} %band_ref.3) | copy-start | bytes 221188
  16.1 6.8 %copy-start.6 = (s32[1,2]{1,0:T(1,128)S(1)}, s32[1,2]{1,0:T(1,128)}, u32[]{:S(2)}) copy-start(s32[1,2]{1,0:T(1,128)} %order_ref.2) | copy-start | bytes 28
  16.1 6.8 %copy-start.7 = (s32[64]{0:T(128)S(1)}, s32[64]{0:T(128)}, u32[]{:S(2)}) copy-start(s32[64]{0:T(128)} %offset_ref.3) | copy-start | bytes 772
  16.1 6.8 %copy-start.8 = (f32[64]{0:T(128)S(1)}, f32[64]{0:T(128)}, u32[]{:S(2)}) copy-start(f32[64]{0:T(128)} %fraction_ref.3) | copy-start | bytes 772
  19.2 0.8 copy-start.9
  20.0 0.7 copy-start.15
  21.4 0.7 copy-start.21
  44.7 33.0 %all-to-all-start.1 = ((bf16[32,16,1024]{2,1,0:T(8,128)(2,1)}), bf16[32,16,1024]{2,1,0:T(8,128)(2,1)S(1)}, u32[]{:S(2)}, u32[]{:S(2)}) async-start(bf16[32,16,1024]{2,1,0:T(8,128)(2,1)} %frame_side.3), calls=%async_computation.1 | async-start | bytes 2097152 | tf_op jit(solution)/shard_map/all_to_all | solution.py:502
  49.6 44.4 %collective-permute-start = (bf16[12,16,1024]{2,1,0:T(8,128)(2,1)}, bf16[12,16,1024]{2,1,0:T(8,128)(2,1)S(1)}, u32[]{:S(2)}, u32[]{:S(2)}) collective-permute-start(bf16[12,16,1024]{2,1,0:T(8,128)(2,1)} %get-tuple-element.62), channel_id=1, source_target_pairs={{0,32},{32,64},{64,96},{96,128},{128,160},{160,192},{192,224},{1,3... | collective-permute-start | bytes 1179656 | tf_op jit(solution)/shard_map/ppermute | solution.py:505
  53.8 40.2 %collective-permute-start.1 = (bf16[12,16,1024]{2,1,0:T(8,128)(2,1)}, bf16[12,16,1024]{2,1,0:T(8,128)(2,1)S(1)}, u32[]{:S(2)}, u32[]{:S(2)}) collective-permute-start(bf16[12,16,1024]{2,1,0:T(8,128)(2,1)} %get-tuple-element.61), channel_id=1, source_target_pairs={{32,0},{64,32},{96,64},{128,96},{160,128},{192,160},{224,192},{33,... | collective-permute-start | bytes 1179656 | tf_op jit(solution)/shard_map/ppermute | solution.py:506
  57.9 1.0 copy-start.16
  58.9 0.9 copy-start.19
  59.8 0.9 copy-start.22
  60.8 0.9 copy-start.25
  65.0 0.9 copy-start.11
  65.9 0.9 copy-start.13
  77.7 20.3 %collective-permute-start.2 = (bf16[12,16,1024]{2,1,0:T(8,128)(2,1)S(1)}, bf16[12,16,1024]{2,1,0:T(8,128)(2,1)S(1)}, u32[]{:S(2)}, u32[]{:S(2)}) collective-permute-start(bf16[12,16,1024]{2,1,0:T(8,128)(2,1)S(1)} %get-tuple-element.60), channel_id=1, source_target_pairs={{0,32},{32,64},{64,96},{96,128},{128,160},{160,192},{192,224},{1,3... | collective-permute-start | bytes 1179656 | tf_op jit(solution)/shard_map/ppermute | solution.py:505
  81.4 20.2 %collective-permute-start.3 = (bf16[12,16,1024]{2,1,0:T(8,128)(2,1)S(1)}, bf16[12,16,1024]{2,1,0:T(8,128)(2,1)S(1)}, u32[]{:S(2)}, u32[]{:S(2)}) collective-permute-start(bf16[12,16,1024]{2,1,0:T(8,128)(2,1)S(1)} %get-tuple-element.59), channel_id=1, source_target_pairs={{32,0},{64,32},{96,64},{128,96},{160,128},{192,160},{224,192},{33,... | collective-permute-start | bytes 1179656 | tf_op jit(solution)/shard_map/ppermute | solution.py:506
  86.2 1.0 copy-start.17
  87.2 0.9 copy-start.20
  88.1 0.9 copy-start.23
  89.1 0.9 copy-start.26
  90.0 4.0 %copy-start.10 = (bf16[8,160,256]{2,1,0:T(8,128)(2,1)S(1)}, bf16[8,160,256]{2,1,0:T(8,128)(2,1)}, u32[]{:S(2)}) copy-start(bf16[8,160,256]{2,1,0:T(8,128)(2,1)} %copy-done.9) | copy-start | bytes 1966084
  90.0 4.0 %copy-start.12 = (bf16[416,1024]{1,0:T(8,128)(2,1)S(1)}, bf16[416,1024]{1,0:T(8,128)(2,1)}, u32[]{:S(2)}) copy-start(bf16[416,1024]{1,0:T(8,128)(2,1)} %copy-done.11) | copy-start | bytes 2555908
  90.0 4.0 %copy-start.14 = (f32[192,1024]{1,0:T(8,128)S(1)}, f32[192,1024]{1,0:T(8,128)}, u32[]{:S(2)}) copy-start(f32[192,1024]{1,0:T(8,128)} %copy-done.13) | copy-start | bytes 2359300
  (2 other events, 1.4 us)

commit v16 on v13

--- a/solution.py
+++ b/solution.py
@@ -21,8 +21,8 @@
 BANDS_VMEM = 20 * 1024 * 1024
 RESTORE_VMEM = 26 * 1024 * 1024
 LATER_VMEM = 20 * 1024 * 1024
-GROUP = 20
-SPAN = 32
+GROUP = 24
+SPAN = 36
 
 
 def frame_kernel(

time: 107 us -> 108 us (level)
  Pallas kernels: 31.2 us -> 33 us
  waiting for transfers between devices: 30.3 us -> 28.8 us
    pallas_call x4, Pallas kernels: 16.9 us -> 18.4 us  [restore(): pl.pallas_call(functools.partial(restore_kernel, plan, inside, half, [len...]
where the time goes in v16:
time: 108 us; the launch traced here: 107 us
  Pallas kernels  33 us (31%)
  starting transfers between devices  31.5 us (29%)
  waiting for transfers between devices  28.8 us (27%)
  local copies, waits for them, and re-layouts  13.2 us (12%)
    all_to_all x2, waiting for transfers between devices, exchange(): lax.all_to_all(piece, 'brick', split_axis=0, concat_axis=0, tiled=True)  26.1 us
    pallas_call x4, Pallas kernels, restore(): pl.pallas_call(functools.partial(restore_kernel, plan, inside, half, [len...  18.4 us
    all_to_all x2, starting transfers between devices, exchange(): lax.all_to_all(piece, 'brick', split_axis=0, concat_axis=0, tiled=True)  14.9 us
    unnamed x54, local copies, waits for them, and re-layouts  11.9 us
    pallas_call x2, Pallas kernels, frame_side(): pl.pallas_call(functools.partial(frame_kernel, first, count), grid=(steps...  11.3 us
    ppermute x2, starting transfers between devices, with_halo(): high = lax.ppermute(centre[:depth], 'cam', backward)  8.78 us
    ppermute x2, starting transfers between devices, with_halo(): low = lax.ppermute(centre[-depth:], 'cam', forward)  7.87 us
    pallas_call x1, Pallas kernels, bands(): pl.pallas_call(functools.partial(bands_kernel, psf_bank.shape[1], lateral...  3.29 us
  transfers between devices with their start and end apart: 6, of which 4 were waited for; matrix products, arithmetic and copies ran while one was open for 1% of the time, Pallas kernels for 20%

profile of v16, /device:TPU:14, one launch (start us, length us, event | category | flops | bytes accessed | tf_op | source)
XLA Modules:
  0.0 107.0 jit_solution(10156707195591181173)
XLA Ops:
  0.0 5.8 %frame_side.2 = bf16[32,16,1152]{2,1,0:T(8,128)(2,1)} custom-call(s32[1,2]{1,0:T(1,128)} %order_ref.2, s32[64]{0:T(128)} %offset_ref.3, f32[64]{0:T(128)} %fraction_ref.3, bf16[2,256,2048]{2,1,0:T(8,128)(2,1)} %raw_next.3, bf16[2,256,2048]{2,1,0:T(8,128)(2,1)} %raw_next.3, bf16[2,256,2048]{2,1,0:T(8,128)(2,1)} %raw_next.3, bf16[256,2048]{1,0:T(8,128)(2,1)} %dark_next.3, ...), custom_call_target="tpu_custom_call" | custom-call | flops 8000000000 | bytes 6500000 | tf_op jit(solution)/shard_map/frame_side/pallas_call | solution.py:123
  5.8 10.2 %all-to-all-start = ((bf16[32,16,1152]{2,1,0:T(8,128)(2,1)}), bf16[32,16,1152]{2,1,0:T(8,128)(2,1)S(1)}, u32[]{:S(2)}, u32[]{:S(2)}) async-start(bf16[32,16,1152]{2,1,0:T(8,128)(2,1)} %frame_side.2), calls=%async_computation | async-start | bytes 2359296 | tf_op jit(solution)/shard_map/all_to_all | solution.py:502
  16.2 0.1 reshape.4.index_ref
  16.4 3.3 %bands.1 = (bf16[5,192,288]{2,1,0:T(8,128)(2,1)S(1)}, bf16[3,192,288]{2,1,0:T(8,128)(2,1)S(1)}, bf16[4,192,288]{2,1,0:T(8,128)(2,1)S(1)}, bf16[4,192,288]{2,1,0:...) custom-call(f32[8,13]{1,0:T(8,128)S(1)} %copy-done.4, f32[9]{0:T(128)S(1)} %copy-done.5, ...), custom_call_target="tpu_custom_call" | custom-call | flops 2000000000 | bytes 2000000 | tf_op jit(solution)/shard_map/bands/pallas_call | solution.py:233
  19.7 0.9 copy-done.9
  20.6 0.8 copy-done.14
  21.4 0.8 copy-done.16
  22.2 0.7 copy-done.20
  22.9 0.7 copy-done.23
  23.7 5.6 %frame_side.3 = bf16[32,16,896]{2,1,0:T(8,128)(2,1)} custom-call(s32[1,2]{1,0:T(1,128)S(1)} %copy-done.6, s32[64]{0:T(128)S(1)} %copy-done.7, f32[64]{0:T(128)S(1)} %copy-done.8, bf16[2,256,2048]{2,1,0:T(8,128)(2,1)S(1)} %copy-done, bf16[2,256,2048]{2,1,0:T(8,128)(2,1)S(1)} %copy-done, bf16[2,256,2048]{2,1,0:T(8,128)(2,1)S(1)} %copy-done, ...), custom_call_target="tpu_custom_call" | custom-call | flops 8000000000 | bytes 6500000 | tf_op jit(solution)/shard_map/frame_side/pallas_call | solution.py:123
  29.2 17.8 %all-to-all-done.refs_0_.refs_1_ = bf16[32,16,1152]{2,1,0:T(8,128)(2,1)S(1)} async-done(((bf16[32,16,1152]{2,1,0:T(8,128)(2,1)}), bf16[32,16,1152]{2,1,0:T(8,128)(2,1)S(1)}, u32[]{:S(2)}, u32[]{:S(2)}) %all-to-all-start) | async-done | bytes 1179680 | tf_op jit(solution)/shard_map/all_to_all | solution.py:502
  47.1 4.6 %all-to-all-start.1 = ((bf16[32,16,896]{2,1,0:T(8,128)(2,1)}), bf16[32,16,896]{2,1,0:T(8,128)(2,1)S(1)}, u32[]{:S(2)}, u32[]{:S(2)}) async-start(bf16[32,16,896]{2,1,0:T(8,128)(2,1)} %frame_side.3), calls=%async_computation.1 | async-start | bytes 1835008 | tf_op jit(solution)/shard_map/all_to_all | solution.py:502
  51.7 1.0 fusion
  52.7 4.2 %collective-permute-start = (bf16[12,16,1152]{2,1,0:T(8,128)(2,1)}, bf16[12,16,1152]{2,1,0:T(8,128)(2,1)S(1)}, u32[]{:S(2)}, u32[]{:S(2)}) collective-permute-start(bf16[12,16,1152]{2,1,0:T(8,128)(2,1)} %get-tuple-element.60), channel_id=1, source_target_pairs={{0,32},{32,64},{64,96},{96,128},{128,160},{160,192},{192,224},{1,3... | collective-permute-start | bytes 1327112 | tf_op jit(solution)/shard_map/ppermute | solution.py:505
  57.0 4.0 %collective-permute-start.1 = (bf16[12,16,1152]{2,1,0:T(8,128)(2,1)}, bf16[12,16,1152]{2,1,0:T(8,128)(2,1)S(1)}, u32[]{:S(2)}, u32[]{:S(2)}) collective-permute-start(bf16[12,16,1152]{2,1,0:T(8,128)(2,1)} %get-tuple-element.59), channel_id=1, source_target_pairs={{32,0},{64,32},{96,64},{128,96},{160,128},{192,160},{224,192},{33,... | collective-permute-start | bytes 1327112 | tf_op jit(solution)/shard_map/ppermute | solution.py:506
  61.0 1.1 %copy-done.10 = bf16[5,192,288]{2,1,0:T(8,128)(2,1)S(1)} copy-done((bf16[5,192,288]{2,1,0:T(8,128)(2,1)S(1)}, bf16[5,192,288]{2,1,0:T(8,128)(2,1)}, u32[]{:S(2)}) %copy-start.10) | copy-done | bytes 552984
  62.1 0.9 copy-done.21
  63.1 0.9 copy-done.24
  64.0 3.8 %inside.2 = (bf16[64,8,2048]{2,1,0:T(8,128)(2,1)}, bf16[416,1152]{1,0:T(8,128)(2,1)S(1)}, f32[192,1152]{1,0:T(8,128)S(1)}) custom-call(bf16[32,16,1152]{2,1,0:T(8,128)(2,1)S(1)} %all-to-all-done.refs_0_.refs_1_, bf16[5,192,288]{2,1,0:T(8,128)(2,1)S(1)} %copy-done.10, bf16[3,192,288]{2,1,0:T(8,128)(2,1)S(1)} %get-tuple-element.43.refs_2_.refs_3_, ...), custom_call_target="tpu_custom_call" | custom-call | flops 5000000000 | bytes 8000000 | tf_op jit(solution)/shard_map/inside/pallas_call | solution.py:442
  67.8 1.0 copy-done.12
  68.8 0.9 copy-done.18
  69.7 8.2 %all-to-all-done.1.refs_1_.refs_4_ = bf16[32,16,896]{2,1,0:T(8,128)(2,1)S(1)} async-done(((bf16[32,16,896]{2,1,0:T(8,128)(2,1)}), bf16[32,16,896]{2,1,0:T(8,128)(2,1)S(1)}, u32[]{:S(2)}, u32[]{:S(2)}) %all-to-all-start.1) | async-done | bytes 917536 | tf_op jit(solution)/shard_map/all_to_all | solution.py:502
  78.0 3.7 %collective-permute-start.2 = (bf16[12,16,896]{2,1,0:T(8,128)(2,1)S(1)}, bf16[12,16,896]{2,1,0:T(8,128)(2,1)S(1)}, u32[]{:S(2)}, u32[]{:S(2)}) collective-permute-start(bf16[12,16,896]{2,1,0:T(8,128)(2,1)S(1)} %get-tuple-element.62), channel_id=1, source_target_pairs={{0,32},{32,64},{64,96},{96,128},{128,160},{160,192},{192,224},{1,3... | collective-permute-start | bytes 1032200 | tf_op jit(solution)/shard_map/ppermute | solution.py:505
  81.7 4.7 %collective-permute-start.3 = (bf16[12,16,896]{2,1,0:T(8,128)(2,1)S(1)}, bf16[12,16,896]{2,1,0:T(8,128)(2,1)S(1)}, u32[]{:S(2)}, u32[]{:S(2)}) collective-permute-start(bf16[12,16,896]{2,1,0:T(8,128)(2,1)S(1)} %get-tuple-element.61), channel_id=1, source_target_pairs={{32,0},{64,32},{96,64},{128,96},{160,128},{192,160},{224,192},{33,... | collective-permute-start | bytes 1032200 | tf_op jit(solution)/shard_map/ppermute | solution.py:506
  86.5 1.1 %copy-done.11 = bf16[5,192,288]{2,1,0:T(8,128)(2,1)S(1)} copy-done((bf16[5,192,288]{2,1,0:T(8,128)(2,1)S(1)}, bf16[5,192,288]{2,1,0:T(8,128)(2,1)}, u32[]{:S(2)}) %copy-start.11) | copy-done | bytes 552984
  87.6 0.9 copy-done.22
  88.5 0.9 copy-done.25
  89.5 3.8 %inside.3 = (bf16[64,8,2048]{2,1,0:T(8,128)(2,1)}, bf16[416,1152]{1,0:T(8,128)(2,1)S(1)}, f32[192,1152]{1,0:T(8,128)S(1)}) custom-call(bf16[32,16,1152]{2,1,0:T(8,128)(2,1)S(1)} %all-to-all-done.refs_0_.refs_1_, bf16[32,16,896]{2,1,0:T(8,128)(2,1)S(1)} %all-to-all-done.1.refs_1_.refs_4_, ...), custom_call_target="tpu_custom_call", output_to_operand_aliasing={{0}: (6, {})} | custom-call | flops 5000000000 | bytes 8000000 | tf_op jit(solution)/shard_map/inside/pallas_call | solution.py:442
  93.3 0.9 collective-permute-done.1.refs_2_
  94.2 5.4 %ends.2.refs_12_ = bf16[64,8,2048]{2,1,0:T(8,128)(2,1)} custom-call(bf16[12,16,1152]{2,1,0:T(8,128)(2,1)S(1)} %collective-permute-done.refs_0_, bf16[32,16,1152]{2,1,0:T(8,128)(2,1)S(1)} %all-to-all-done.refs_0_.refs_1_, bf16[12,16,1152]{2,1,0:T(8,128)(2,1)S(1)} %collective-permute-done.1.refs_2_, ...), custom_call_target="tpu_custom_call", output_to_operand_aliasing={{}: (9, {})} | custom-call | flops 5000000000 | bytes 8000000 | tf_op jit(solution)/shard_map/ends/pallas_call | solution.py:442
  99.6 1.8 %collective-permute-done.3.refs_5_ = bf16[12,16,896]{2,1,0:T(8,128)(2,1)S(1)} collective-permute-done((bf16[12,16,896]{2,1,0:T(8,128)(2,1)S(1)}, bf16[12,16,896]{2,1,0:T(8,128)(2,1)S(1)}, u32[]{:S(2)}, u32[]{:S(2)}) %collective-permute-start.3) | collective-permute-done | bytes 344096 | tf_op jit(solution)/shard_map/ppermute | solution.py:506
  101.5 5.4 %ends.3 = bf16[64,8,2048]{2,1,0:T(8,128)(2,1)} custom-call(bf16[12,16,1152]{2,1,0:T(8,128)(2,1)S(1)} %collective-permute-done.refs_0_, bf16[32,16,1152]{2,1,0:T(8,128)(2,1)S(1)} %all-to-all-done.refs_0_.refs_1_, bf16[12,16,1152]{2,1,0:T(8,128)(2,1)S(1)} %collective-permute-done.1.refs_2_, ...), custom_call_target="tpu_custom_call", output_to_operand_aliasing={{}: (12, {})} | custom-call | flops 5000000000 | bytes 8000000 | tf_op jit(solution)/shard_map/ends/pallas_call | solution.py:442
  (46 shorter events, 0.3 us)
Async XLA Ops:
  5.8 10.3 %copy-start.26 = (s32[512]{0:T(512)S(1)}, s32[512]{0:T(512)}, u32[]{:S(2)}) copy-start(s32[512]{0:T(512)} %param.17) | copy-start | bytes 6148
  5.8 10.6 %copy-start.4 = (f32[8,13]{1,0:T(8,128)S(1)}, f32[8,13]{1,0:T(8,128)}, u32[]{:S(2)}) copy-start(f32[8,13]{1,0:T(8,128)} %psf_ref.1) | copy-start | bytes 1252
  5.8 10.6 %copy-start.5 = (f32[9]{0:T(128)S(1)}, f32[9]{0:T(128)}, u32[]{:S(2)}) copy-start(f32[9]{0:T(128)} %lateral_ref.1) | copy-start | bytes 112
  5.8 41.3 %all-to-all-start = ((bf16[32,16,1152]{2,1,0:T(8,128)(2,1)}), bf16[32,16,1152]{2,1,0:T(8,128)(2,1)S(1)}, u32[]{:S(2)}, u32[]{:S(2)}) async-start(bf16[32,16,1152]{2,1,0:T(8,128)(2,1)} %frame_side.2), calls=%async_computation | async-start | bytes 2359296 | tf_op jit(solution)/shard_map/all_to_all | solution.py:502
  16.3 7.3 %copy-start = (bf16[2,256,2048]{2,1,0:T(8,128)(2,1)S(1)}, bf16[2,256,2048]{2,1,0:T(8,128)(2,1)}, u32[]{:S(2)}) copy-start(bf16[2,256,2048]{2,1,0:T(8,128)(2,1)} %raw_next.3) | copy-start | bytes 6291460
  16.4 7.3 %copy-start.1 = (bf16[256,2048]{1,0:T(8,128)(2,1)S(1)}, bf16[256,2048]{1,0:T(8,128)(2,1)}, u32[]{:S(2)}) copy-start(bf16[256,2048]{1,0:T(8,128)(2,1)} %dark_next.3) | copy-start | bytes 3145732
  16.4 7.3 %copy-start.2 = (bf16[256,2048]{1,0:T(8,128)(2,1)S(1)}, bf16[256,2048]{1,0:T(8,128)(2,1)}, u32[]{:S(2)}) copy-start(bf16[256,2048]{1,0:T(8,128)(2,1)} %gain_next.3) | copy-start | bytes 3145732
  16.4 7.3 %copy-start.3 = (f32[9,2048]{1,0:T(8,128)S(1)}, f32[9,2048]{1,0:T(8,128)}, u32[]{:S(2)}) copy-start(f32[9,2048]{1,0:T(8,128)} %band_ref.3) | copy-start | bytes 221188
  16.4 7.3 %copy-start.6 = (s32[1,2]{1,0:T(1,128)S(1)}, s32[1,2]{1,0:T(1,128)}, u32[]{:S(2)}) copy-start(s32[1,2]{1,0:T(1,128)} %order_ref.2) | copy-start | bytes 28
  16.4 7.3 %copy-start.7 = (s32[64]{0:T(128)S(1)}, s32[64]{0:T(128)}, u32[]{:S(2)}) copy-start(s32[64]{0:T(128)} %offset_ref.3) | copy-start | bytes 772
  16.4 7.3 %copy-start.8 = (f32[64]{0:T(128)S(1)}, f32[64]{0:T(128)}, u32[]{:S(2)}) copy-start(f32[64]{0:T(128)} %fraction_ref.3) | copy-start | bytes 772
  19.7 0.9 copy-start.9
  20.6 0.8 copy-start.14
  21.4 0.8 copy-start.16
  22.9 0.7 copy-start.23
  47.1 30.8 %all-to-all-start.1 = ((bf16[32,16,896]{2,1,0:T(8,128)(2,1)}), bf16[32,16,896]{2,1,0:T(8,128)(2,1)S(1)}, u32[]{:S(2)}, u32[]{:S(2)}) async-start(bf16[32,16,896]{2,1,0:T(8,128)(2,1)} %frame_side.3), calls=%async_computation.1 | async-start | bytes 1835008 | tf_op jit(solution)/shard_map/all_to_all | solution.py:502
  52.7 40.5 %collective-permute-start = (bf16[12,16,1152]{2,1,0:T(8,128)(2,1)}, bf16[12,16,1152]{2,1,0:T(8,128)(2,1)S(1)}, u32[]{:S(2)}, u32[]{:S(2)}) collective-permute-start(bf16[12,16,1152]{2,1,0:T(8,128)(2,1)} %get-tuple-element.60), channel_id=1, source_target_pairs={{0,32},{32,64},{64,96},{96,128},{128,160},{160,192},{192,224},{1,3... | collective-permute-start | bytes 1327112 | tf_op jit(solution)/shard_map/ppermute | solution.py:505
  57.0 37.2 %collective-permute-start.1 = (bf16[12,16,1152]{2,1,0:T(8,128)(2,1)}, bf16[12,16,1152]{2,1,0:T(8,128)(2,1)S(1)}, u32[]{:S(2)}, u32[]{:S(2)}) collective-permute-start(bf16[12,16,1152]{2,1,0:T(8,128)(2,1)} %get-tuple-element.59), channel_id=1, source_target_pairs={{32,0},{64,32},{96,64},{128,96},{160,128},{192,160},{224,192},{33,... | collective-permute-start | bytes 1327112 | tf_op jit(solution)/shard_map/ppermute | solution.py:506
  61.0 1.1 %copy-start.10 = (bf16[5,192,288]{2,1,0:T(8,128)(2,1)S(1)}, bf16[5,192,288]{2,1,0:T(8,128)(2,1)}, u32[]{:S(2)}) copy-start(bf16[5,192,288]{2,1,0:T(8,128)(2,1)} %copy-done.9) | copy-start | bytes 1658884
  62.1 0.9 copy-start.21
  63.1 0.9 copy-start.24
  67.8 1.0 copy-start.12
  68.8 0.9 copy-start.18
  78.0 21.6 %collective-permute-start.2 = (bf16[12,16,896]{2,1,0:T(8,128)(2,1)S(1)}, bf16[12,16,896]{2,1,0:T(8,128)(2,1)S(1)}, u32[]{:S(2)}, u32[]{:S(2)}) collective-permute-start(bf16[12,16,896]{2,1,0:T(8,128)(2,1)S(1)} %get-tuple-element.62), channel_id=1, source_target_pairs={{0,32},{32,64},{64,96},{96,128},{128,160},{160,192},{192,224},{1,3... | collective-permute-start | bytes 1032200 | tf_op jit(solution)/shard_map/ppermute | solution.py:505
  81.7 19.8 %collective-permute-start.3 = (bf16[12,16,896]{2,1,0:T(8,128)(2,1)S(1)}, bf16[12,16,896]{2,1,0:T(8,128)(2,1)S(1)}, u32[]{:S(2)}, u32[]{:S(2)}) collective-permute-start(bf16[12,16,896]{2,1,0:T(8,128)(2,1)S(1)} %get-tuple-element.61), channel_id=1, source_target_pairs={{32,0},{64,32},{96,64},{128,96},{160,128},{192,160},{224,192},{33,... | collective-permute-start | bytes 1032200 | tf_op jit(solution)/shard_map/ppermute | solution.py:506
  86.4 1.1 %copy-start.11 = (bf16[5,192,288]{2,1,0:T(8,128)(2,1)S(1)}, bf16[5,192,288]{2,1,0:T(8,128)(2,1)}, u32[]{:S(2)}) copy-start(bf16[5,192,288]{2,1,0:T(8,128)(2,1)} %copy-done.9) | copy-start | bytes 1658884
  87.6 0.9 copy-start.22
  88.5 0.9 copy-start.25
  89.5 4.7 %copy-start.13 = (bf16[416,1152]{1,0:T(8,128)(2,1)S(1)}, bf16[416,1152]{1,0:T(8,128)(2,1)}, u32[]{:S(2)}) copy-start(bf16[416,1152]{1,0:T(8,128)(2,1)} %copy-done.12) | copy-start | bytes 2875396
  89.5 4.7 %copy-start.15 = (bf16[4,192,288]{2,1,0:T(8,128)(2,1)S(1)}, bf16[4,192,288]{2,1,0:T(8,128)(2,1)}, u32[]{:S(2)}) copy-start(bf16[4,192,288]{2,1,0:T(8,128)(2,1)} %copy-done.14) | copy-start | bytes 1327108
  89.5 4.7 %copy-start.17 = (bf16[4,192,288]{2,1,0:T(8,128)(2,1)S(1)}, bf16[4,192,288]{2,1,0:T(8,128)(2,1)}, u32[]{:S(2)}) copy-start(bf16[4,192,288]{2,1,0:T(8,128)(2,1)} %copy-done.16) | copy-start | bytes 1327108
  89.5 4.7 %copy-start.19 = (f32[192,1152]{1,0:T(8,128)S(1)}, f32[192,1152]{1,0:T(8,128)}, u32[]{:S(2)}) copy-start(f32[192,1152]{1,0:T(8,128)} %copy-done.18) | copy-start | bytes 2654212
  (1 other events, 0.7 us)
